TPU v7x, 32 devices: a whole 2x2x4 slice. The times are simulated.
32 devices in a mesh: dp: 32 (over z, y, x, core).
Axes of the slice: x: 2, y: 2, z: 4, core: 2. Of those that a mesh axis runs over, the one named last changes fastest.
Arguments:
- tokens: bfloat16 [12288, 2048], P('dp'), may hold values from -6 to 6
- seq_lengths: int32 [32, 3], P('dp'), may hold values from 1 to 256, 384 in all within a row
- ln1_gain: bfloat16 [2048], P('dp'), may hold values from 0.099609375 to 1.8984375
- ln1_bias: bfloat16 [2048], P('dp'), may hold values from -3 to 3
- ln2_gain: bfloat16 [2048], P('dp'), may hold values from 0.099609375 to 1.8984375
- ln2_bias: bfloat16 [2048], P('dp'), may hold values from -3 to 3
- qkv_weight: bfloat16 [2048, 6144], P('dp'), may hold values from -0.125 to 0.125
- qkv_bias: bfloat16 [6144], P('dp'), may hold values from -3 to 3
- dense_weight: bfloat16 [2048, 2048], P('dp'), may hold values from -0.5 to 0.5
- dense_bias: bfloat16 [2048], P('dp'), may hold values from -3 to 3
- expand_weight: bfloat16 [2048, 8192], P('dp'), may hold values from -0.125 to 0.125
- expand_bias: bfloat16 [8192], P('dp'), may hold values from -3 to 3
- contract_weight: bfloat16 [8192, 2048], P('dp'), may hold values from -0.0625 to 0.0625
- contract_bias: bfloat16 [2048], P('dp'), may hold values from -3 to 3
- cotangent: bfloat16 [12288, 2048], P('dp'), may hold values from -6 to 6
Outputs:
- layer_out: bfloat16 [12288, 2048], P('dp')
- input_grad: float32 [12288, 2048], P('dp')
- ln1_gain_grad: float32 [2048], P('dp')
- ln1_bias_grad: float32 [2048], P('dp')
- ln2_gain_grad: float32 [2048], P('dp')
- ln2_bias_grad: float32 [2048], P('dp')
- qkv_weight_grad: float32 [2048, 6144], P('dp')
- qkv_bias_grad: float32 [6144], P('dp')
- dense_weight_grad: float32 [2048, 2048], P('dp')
- dense_bias_grad: float32 [2048], P('dp')
- expand_weight_grad: float32 [2048, 8192], P('dp')
- expand_bias_grad: float32 [8192], P('dp')
- contract_weight_grad: float32 [8192, 2048], P('dp')
- contract_bias_grad: float32 [2048], P('dp')
Inputs may be any that keep to these rules, and one draw needn't show every extreme that they name: `seq_lengths`: row d lists, in order, the lengths of the sequences packed into device d's 384 slots; each row sums to 384.
All inputs are finite; a program needn't handle non-finite values.
Results may differ from a plain program's by a relative error of at most 0.011.
Values may be sent and summed in bfloat16 or wider, within the bound.
No kernel may reach another device: no remote copies, remote signals or barrier semaphores. Data moves between devices by JAX's collectives and lax.ppermute only.
A program may use at most 640 MiB of HBM per device.

v0:
```python
import math

import jax
import jax.numpy as jnp
from jax import lax
from jax.sharding import PartitionSpec as P

HEADS = 8


EPSILON = 1e-05
MASKED = -1e30
PAIRED = (((1,), (1,)), ((), ()))
LEADING = (((0,), (0,)), ((), ()))


def slot_layout(lengths, slots):
    place = jnp.arange(slots, dtype=jnp.int32)
    ends = jnp.cumsum(lengths, dtype=jnp.int32)
    after = (place[:, None] >= ends[None, :]).astype(jnp.int32)
    segment = jnp.sum(after, axis=1, dtype=jnp.int32)
    offset = jnp.sum(after * lengths[None, :], axis=1, dtype=jnp.int32)
    return (segment, place - offset)


def rotary_tables(position, rotated):
    half = rotated // 2
    ladder = jnp.arange(half, dtype=jnp.float32) * (-math.log(10000.0) / half)
    angle = position.astype(jnp.float32)[:, None] * jnp.exp(ladder)[None, :]
    return (jnp.cos(angle), jnp.sin(angle))


def rotate(value, cosine, sine, heads, rotated):
    count = value.shape[0]
    shaped = value.reshape(count, heads, -1)
    half = rotated // 2
    first = shaped[:, :, :half]
    second = shaped[:, :, half:rotated]
    across = cosine[:, None, :]
    upward = sine[:, None, :]
    turned = jnp.concatenate(
        [
            first * across - second * upward,
            second * across + first * upward,
            shaped[:, :, rotated:],
        ],
        axis=2,
    )
    return turned.reshape(count, -1)


def norm_rows(value, gain, shift):
    centre = jnp.mean(value, axis=1, keepdims=True)
    spread = value - centre
    variance = jnp.mean(spread * spread, axis=1, keepdims=True)
    return spread * lax.rsqrt(variance + EPSILON) * gain + shift


def smooth_gate(value):
    return jax.nn.gelu(value, approximate=False)


def allowed_pairs(segment):
    place = jnp.arange(segment.shape[0], dtype=jnp.int32)
    return (segment[:, None] == segment[None, :]) & (place[None, :] <= place[:, None])


def masked_scores(query_heads, key_heads, allowed, scale):
    scores = (
        jnp.einsum("qhd,khd->hqk", query_heads, key_heads, preferred_element_type=jnp.float32)
        * scale
    )
    return jnp.where(allowed[None], scores, MASKED)


def attend_forward(query, key, value, allowed, heads, scale):
    count, width = query.shape
    query_heads = query.reshape(count, heads, -1)
    key_heads = key.reshape(count, heads, -1)
    value_heads = value.reshape(count, heads, -1)
    masked = masked_scores(query_heads, key_heads, allowed, scale)
    highest = jnp.max(masked, axis=2, keepdims=True)
    raised = jnp.exp(masked - highest)
    total = jnp.sum(raised, axis=2, keepdims=True)
    weights = (raised / total).astype(jnp.bfloat16)
    mixed = jnp.einsum("hqk,khd->qhd", weights, value_heads, preferred_element_type=jnp.float32)
    return (mixed.reshape(count, width).astype(jnp.bfloat16), highest + jnp.log(total))


def attend_backward(query, key, value, allowed, log_total, grad_attn, heads, scale):
    count, width = query.shape
    query_heads = query.reshape(count, heads, -1)
    key_heads = key.reshape(count, heads, -1)
    value_heads = value.reshape(count, heads, -1)
    grad_heads = grad_attn.reshape(count, heads, -1)
    probs = jnp.exp(masked_scores(query_heads, key_heads, allowed, scale) - log_total)
    grad_probs = jnp.einsum(
        "qhd,khd->hqk", grad_heads, value_heads, preferred_element_type=jnp.float32
    )
    grad_value = jnp.einsum(
        "hqk,qhd->khd", probs.astype(jnp.bfloat16), grad_heads, preferred_element_type=jnp.float32
    )
    inner = jnp.sum(probs * grad_probs, axis=2, keepdims=True)
    grad_score = (probs * (grad_probs - inner)).astype(jnp.bfloat16)
    grad_query = (
        jnp.einsum("hqk,khd->qhd", grad_score, key_heads, preferred_element_type=jnp.float32)
        * scale
    )
    grad_key = (
        jnp.einsum("hqk,qhd->khd", grad_score, query_heads, preferred_element_type=jnp.float32)
        * scale
    )
    return (
        grad_query.reshape(count, width),
        grad_key.reshape(count, width),
        grad_value.reshape(count, width),
    )


def times_leading(left, right):
    return lax.dot_general(left, right, LEADING, preferred_element_type=jnp.float32)


def times_paired(left, right):
    return lax.dot_general(left, right, PAIRED, preferred_element_type=jnp.float32)


def per_device(
    tokens,
    seq_lengths,
    ln1_gain,
    ln1_bias,
    ln2_gain,
    ln2_bias,
    qkv_weight,
    qkv_bias,
    dense_weight,
    dense_bias,
    expand_weight,
    expand_bias,
    contract_weight,
    contract_bias,
    cotangent,
):
    slots, width = tokens.shape
    hidden_units = expand_weight.shape[1]
    head_dim = width // HEADS
    rotated = head_dim // 4
    scale = 1.0 / math.sqrt(head_dim)
    gathered = (
        lax.all_gather(ln1_gain, "dp", axis=0, tiled=True),
        lax.all_gather(ln1_bias, "dp", axis=0, tiled=True),
        lax.all_gather(ln2_gain, "dp", axis=0, tiled=True),
        lax.all_gather(ln2_bias, "dp", axis=0, tiled=True),
        lax.all_gather(qkv_bias, "dp", axis=0, tiled=True),
        lax.all_gather(dense_bias, "dp", axis=0, tiled=True),
        lax.all_gather(expand_bias, "dp", axis=0, tiled=True),
        lax.all_gather(contract_bias, "dp", axis=0, tiled=True),
    )
    gain_one, shift_one, gain_two, shift_two, bias_qkv, bias_dense, bias_expand, bias_contract = [
        item.astype(jnp.float32) for item in gathered
    ]
    inputs = tokens.astype(jnp.float32)
    segment, position = slot_layout(seq_lengths[0], slots)
    cosine, sine = rotary_tables(position, rotated)
    allowed = allowed_pairs(segment)

    def both_norms(value, first_gain, first_shift, second_gain, second_shift):
        return (
            norm_rows(value, first_gain, first_shift),
            norm_rows(value, second_gain, second_shift),
        )

    (normed_one, normed_two), norm_pull = jax.vjp(
        both_norms, inputs, gain_one, shift_one, gain_two, shift_two
    )
    low_one = normed_one.astype(jnp.bfloat16)
    low_two = normed_two.astype(jnp.bfloat16)
    pieces = (
        lax.all_gather(qkv_weight, "dp", axis=0, tiled=True),
        lax.all_gather(expand_weight, "dp", axis=0, tiled=True),
    )
    qkv_linear = jnp.dot(low_one, pieces[0], preferred_element_type=jnp.float32)
    hidden_linear = jnp.dot(low_two, pieces[1], preferred_element_type=jnp.float32)
    projected = qkv_linear + bias_qkv

    def turn_both(query_part, key_part):
        return (
            rotate(query_part, cosine, sine, HEADS, rotated),
            rotate(key_part, cosine, sine, HEADS, rotated),
        )

    (query_turned, key_turned), turn_pull = jax.vjp(
        turn_both, projected[:, :width], projected[:, width : 2 * width]
    )
    query = query_turned.astype(jnp.bfloat16)
    key = key_turned.astype(jnp.bfloat16)
    value = projected[:, 2 * width :].astype(jnp.bfloat16)
    attn, log_total = attend_forward(query, key, value, allowed, HEADS, scale)
    hidden = hidden_linear + bias_expand
    active_full, gate_pull = jax.vjp(smooth_gate, hidden)
    active = active_full.astype(jnp.bfloat16)
    full_dense, full_contract = (
        lax.all_gather(dense_weight, "dp", axis=0, tiled=True),
        lax.all_gather(contract_weight, "dp", axis=0, tiled=True),
    )
    branch_attn = jnp.dot(attn, full_dense, preferred_element_type=jnp.float32) + bias_dense
    branch_mlp = jnp.dot(active, full_contract, preferred_element_type=jnp.float32) + bias_contract
    layer_out = (inputs + branch_attn + branch_mlp).astype(jnp.bfloat16)
    grad_out = cotangent.astype(jnp.float32)
    back_dense, back_contract = (
        lax.all_gather(dense_weight, "dp", axis=0, tiled=True),
        lax.all_gather(contract_weight, "dp", axis=0, tiled=True),
    )
    grad_active = times_paired(cotangent, back_contract)
    (grad_hidden_full,) = gate_pull(grad_active)
    grad_hidden = grad_hidden_full.astype(jnp.bfloat16)
    contract_weight_grad = lax.psum_scatter(
        times_leading(active, cotangent), "dp", scatter_dimension=0, tiled=True
    )
    grad_attn = times_paired(cotangent, back_dense).astype(jnp.bfloat16)
    grad_query, grad_key, grad_value = attend_backward(
        query, key, value, allowed, log_total, grad_attn, HEADS, scale
    )
    grad_query_raw, grad_key_raw = turn_pull((grad_query, grad_key))
    grad_qkv = jnp.concatenate([grad_query_raw, grad_key_raw, grad_value], axis=1).astype(
        jnp.bfloat16
    )
    pieces = (
        lax.all_gather(qkv_weight, "dp", axis=0, tiled=True),
        lax.all_gather(expand_weight, "dp", axis=0, tiled=True),
    )
    stacked = jnp.stack([times_paired(grad_qkv, pieces[0]), times_paired(grad_hidden, pieces[1])])
    grad_inputs, grad_gain_one, grad_shift_one, grad_gain_two, grad_shift_two = norm_pull(
        (stacked[0], stacked[1])
    )
    input_grad = grad_out + grad_inputs
    rows_grad = lax.psum_scatter(
        jnp.concatenate(
            [
                times_leading(low_one, grad_qkv),
                times_leading(attn, cotangent),
                times_leading(low_two, grad_hidden),
            ],
            axis=1,
        ),
        "dp",
        scatter_dimension=0,
        tiled=True,
    )
    qkv_weight_grad = rows_grad[:, : 3 * width]
    dense_weight_grad = rows_grad[:, 3 * width : 4 * width]
    expand_weight_grad = rows_grad[:, 4 * width : 4 * width + hidden_units]
    column_out = jnp.sum(grad_out, axis=0)
    small_terms = (
        grad_gain_one,
        grad_shift_one,
        grad_gain_two,
        grad_shift_two,
        jnp.sum(grad_qkv.astype(jnp.float32), axis=0),
        column_out,
        jnp.sum(grad_hidden.astype(jnp.float32), axis=0),
        column_out,
    )
    summed = (
        lax.psum_scatter(small_terms[0], "dp", scatter_dimension=0, tiled=True),
        lax.psum_scatter(small_terms[1], "dp", scatter_dimension=0, tiled=True),
        lax.psum_scatter(small_terms[2], "dp", scatter_dimension=0, tiled=True),
        lax.psum_scatter(small_terms[3], "dp", scatter_dimension=0, tiled=True),
        lax.psum_scatter(small_terms[4], "dp", scatter_dimension=0, tiled=True),
        lax.psum_scatter(small_terms[5], "dp", scatter_dimension=0, tiled=True),
        lax.psum_scatter(small_terms[6], "dp", scatter_dimension=0, tiled=True),
        lax.psum_scatter(small_terms[7], "dp", scatter_dimension=0, tiled=True),
    )
    return (
        layer_out,
        input_grad,
        summed[0],
        summed[1],
        summed[2],
        summed[3],
        qkv_weight_grad,
        summed[4],
        dense_weight_grad,
        summed[5],
        expand_weight_grad,
        summed[6],
        contract_weight_grad,
        summed[7],
    )


def solution(mesh):
    in_specs = (
        P("dp", None),
        P("dp", None),
        P("dp"),
        P("dp"),
        P("dp"),
        P("dp"),
        P("dp", None),
        P("dp"),
        P("dp", None),
        P("dp"),
        P("dp", None),
        P("dp"),
        P("dp", None),
        P("dp"),
        P("dp", None),
    )
    out_specs = (
        P("dp", None),
        P("dp", None),
        P("dp"),
        P("dp"),
        P("dp"),
        P("dp"),
        P("dp", None),
        P("dp"),
        P("dp", None),
        P("dp"),
        P("dp", None),
        P("dp"),
        P("dp", None),
        P("dp"),
    )
    return jax.shard_map(
        per_device, mesh=mesh, in_specs=in_specs, out_specs=out_specs, check_vma=False
    )
```

profile of v0, /device:TPU:1, one launch (start us, length us, event | category | flops | bytes accessed | tf_op | source)
XLA Modules:
  0.0 3491.0 jit_solution(13240706652993735940)
XLA Ops:
  12.0 43.2 %all-reduce.22 = (bf16[2048]{0:T(1024)(128)(2,1)S(1)}, bf16[2048]{0:T(1024)(128)(2,1)S(1)}, bf16[6144]{0:T(1024)(128)(2,1)S(1)}, bf16[2048]{0:T(1024)(128)(2,1)S...) all-reduce(bf16[2048]{0:T(1024)(128)(2,1)S(1)} %dynamic-update-slic, ...), channel_id=1, replica_groups=mesh['dp'=32] {'dp'}, use_global_device_ids=true, to_apply=%add.11 | all-reduce | flops 18432 | bytes 73728
  57.5 40.7 %all-gather = bf16[32,1,256]{2,1,0:T(2,128)(2,1)S(1)} all-gather(bf16[1,1,256]{2,1,0:T(2,128)(2,1)S(1)} %reshape.272), channel_id=1, replica_groups=mesh['dp'=32] {'dp'}, dimensions={0}, use_global_device_ids=true | all-gather | bytes 16896 | tf_op jit(solution)/shard_map/all_gather | solution.py:157
  102.2 10.3 convolution_convert_fusion
  112.5 1.9 copy.120
  114.4 133.2 %all-gather.6.cloned.1.call-done = bf16[2048,6144]{1,0:T(8,128)(2,1)} async-done(((bf16[64,6144]{1,0:T(8,128)(2,1)}), bf16[2048,6144]{1,0:T(8,128)(2,1)}) %all-gather.6.cloned.1.call-update) | async-done | bytes 25165840 | tf_op jit(solution)/shard_map/all_gather | solution.py:180
  247.6 14.8 convolution_add_fusion.1
  263.1 1.4 copy.130
  264.6 1.4 copy.131
  270.1 3.1 fusion.59
  273.9 1.4 multiply_reduce_fusion
  276.3 2.1 multiply_bitcast_fusion.1
  278.5 2.5 split.24
  281.0 1.5 multiply_bitcast_fusion
  283.4 2.1 multiply_add_fusion.3
  285.5 2.9 add_convert_fusion.1
  288.4 2.8 copy.107
  291.2 5.2 add_convert_fusion.2
  296.4 2.8 copy.103
  299.3 4.2 fusion.33
  303.6 8.5 convert_reduce_fusion.1
  312.1 1.4 fusion.36
  314.6 8.3 fusion.62
  323.0 27.9 fusion.47
  350.9 92.6 %all-gather.10.cloned.1.call-done = bf16[2048,8192]{1,0:T(8,128)(2,1)} async-done(((bf16[64,8192]{1,0:T(8,128)(2,1)}), bf16[2048,8192]{1,0:T(8,128)(2,1)}) %all-gather.10.cloned.1.call-update) | async-done | bytes 33554448 | tf_op jit(solution)/shard_map/all_gather | solution.py:181
  443.5 22.2 convolution_add_fusion
  465.7 173.5 %all-gather.12.cloned.1.call-done = bf16[8192,2048]{1,0:T(8,128)(2,1)} async-done(((bf16[256,2048]{1,0:T(8,128)(2,1)}), bf16[8192,2048]{1,0:T(8,128)(2,1)}) %all-gather.12.cloned.1.call-update) | async-done | bytes 33554448 | tf_op jit(solution)/shard_map/all_gather | solution.py:205
  639.2 46.8 %convert_reduce_fusion = (f32[8192]{0:T(1024)}, bf16[384,8192]{1,0:T(8,128)(2,1)}, f32[384,8192]{1,0:T(8,128)}) fusion(f32[384,8192]{1,0:T(8,128)} %convolution_add_fusion, bf16[384,2048]{1,0:T(8,128)(2,1)S(1)} %copy-done.13, bf16[8192,2048]{1,0:T(8,128)(2,1)} %all-gather.12.cloned.1.call-done), kind=kOutput, calls=%fused_computation.3 | convolution fusion | flops 13117677568 | bytes 66617344 | tf_op jit(solution)/shard_map/dot_general | solution.py:125
  686.0 28.6 fusion.44
  714.7 20.9 fusion.61
  735.6 19.3 fusion.54
  754.9 5.1 fusion.23
  760.1 4.4 convert_reduce_fusion.3
  764.6 87.6 %pad_maximum_fusion = f32[2048,16384]{1,0:T(8,128)} fusion(f32[2048,8192]{1,0:T(8,128)} %fusion.44, f32[2048,2048]{1,0:T(8,128)} %fusion.62, f32[2048,6144]{1,0:T(8,128)} %fusion.47), kind=kLoop, calls=%fused_computation | loop fusion | flops 67108864 | bytes 268435456 | tf_op jit(solution)/shard_map/concatenate | solution.py:239
  852.3 12.0 multiply_convert_fusion
  864.3 28.5 fusion.63
  893.5 19.3 fusion.60
  912.8 8.7 fusion.28
  921.5 1.3 dynamic-slice
  923.5 1.3 dynamic-slice.1
  924.8 1.3 dynamic-slice.2
  926.0 1.3 dynamic-slice.3
  927.3 1.3 dynamic-slice.5
  928.6 1.3 dynamic-slice.7
  929.9 1842.9 %all-reduce.26.cloned.1.call-done = f32[2048,16384]{1,0:T(8,128)} async-done(((f32[2048,16384]{1,0:T(8,128)}), f32[2048,16384]{1,0:T(8,128)}) %all-reduce.26.cloned.1.call-update) | async-done | bytes 134217744
  2772.9 2.1 dynamic-slice.9
  2774.9 3.5 dynamic-slice.10
  2778.5 2.7 constant_dynamic-slice_fusion
  2781.1 702.0 %reduce-scatter.2.cloned.1.call-done = f32[256,2048]{1,0:T(8,128)} async-done(((f32[8192,2048]{1,0:T(8,128)}), f32[256,2048]{1,0:T(8,128)}) %reduce-scatter.2.cloned.1.call-update) | async-done | bytes 2097168 | tf_op jit(solution)/shard_map/reduce_scatter | solution.py:218
  (165 shorter events, 21.5 us)
Async XLA Ops:
  7.2 3.0 copy-start.38
  7.2 3.0 copy-start.39
  7.2 3.2 copy-start.40
  7.2 3.5 copy-start.41
  7.2 3.7 copy-start.42
  7.2 4.0 copy-start.43
  7.2 4.2 copy-start.44
  7.3 4.5 copy-start.45
  7.3 91.6 %copy-start.37 = (s32[1,3]{1,0:T(1,128)S(1)}, s32[1,3]{1,0:T(1,128)}, u32[]{:S(2)}) copy-start(s32[1,3]{1,0:T(1,128)} %param.16) | copy-start | bytes 40
  7.3 91.9 %copy-start = (bf16[384,2048]{1,0:T(8,128)(2,1)S(1)}, bf16[384,2048]{1,0:T(8,128)(2,1)}, u32[]{:S(2)}) copy-start(bf16[384,2048]{1,0:T(8,128)(2,1)} %param.15) | copy-start | bytes 4718596
  7.3 94.9 %all-gather.8.cloned.1.call-start = ((), (), s32[]{:S(2)}) async-start(), calls=%async_computation.2 | async-start | bytes 8650752 | tf_op jit(solution)/shard_map/all_gather | solution.py:204
  8.0 239.6 %all-gather.6.cloned.1.call-start = ((), (), s32[]{:S(2)}) async-start(), calls=%async_computation.1 | async-start | bytes 25952256 | tf_op jit(solution)/shard_map/all_gather | solution.py:180
  8.8 93.4 %copy-start.11 = (bf16[384,2048]{1,0:T(8,128)(2,1)S(1)}, bf16[384,2048]{1,0:T(8,128)(2,1)}, u32[]{:S(2)}) copy-start(bf16[384,2048]{1,0:T(8,128)(2,1)} %param.29) | copy-start | bytes 4718596
  8.8 434.8 %all-gather.10.cloned.1.call-start = ((), (), s32[]{:S(2)}) async-start(), calls=%async_computation.3 | async-start | bytes 34603008 | tf_op jit(solution)/shard_map/all_gather | solution.py:181
  9.5 629.7 %all-gather.12.cloned.1.call-start = ((), (), s32[]{:S(2)}) async-start(), calls=%async_computation.4 | async-start | bytes 34603008 | tf_op jit(solution)/shard_map/all_gather | solution.py:205
  10.1 911.4 %all-reduce.28.cloned.1.call-start = ((), (), s32[]{:S(2)}) async-start(), calls=%async_computation.7 | async-start | bytes 196608
  114.4 159.4 %copy-start.10 = (bf16[384,2048]{0,1:T(8,128)(2,1)}, bf16[384,2048]{0,1:T(8,128)(2,1)S(1)}, u32[]{:S(2)}) copy-start(bf16[384,2048]{0,1:T(8,128)(2,1)S(1)} %copy.120) | copy-start | bytes 4718596
  262.7 11.2 copy-start.19
  273.2 2.2 copy-start.2
  296.4 2.8 copy-start.26
  296.4 15.7 slice-start
  299.2 4.3 copy-start.3
  299.2 4.3 copy-start.6
  299.3 12.8 slice-start.1
  303.5 9.9 copy-start.8
  303.5 8.5 copy-start.20
  303.5 8.5 copy-start.29
  303.5 8.5 copy-start.31
  312.1 2.5 copy-start.12
  314.6 8.3 copy-start.4
  314.6 8.3 copy-start.7
  314.6 8.3 copy-start.9
  314.6 8.3 copy-start.21
  314.6 8.3 copy-start.24
  322.9 120.6 %copy-start.23 = (f32[2048]{0:T(1024)S(1)}, f32[2048]{0:T(1024)}, u32[]{:S(2)}) copy-start(f32[2048]{0:T(1024)} %convert_element_type.101) | copy-start | bytes 24580
  323.0 120.6 %copy-start.32 = (f32[32,1,256]{2,1,0:T(1,128)S(1)}, f32[32,1,256]{2,1,0:T(1,128)}, u32[]{:S(2)}) copy-start(f32[32,1,256]{2,1,0:T(1,128)} %convert_element_type.114) | copy-start | bytes 98308
  443.5 195.7 %copy-start.13 = (bf16[384,2048]{1,0:T(8,128)(2,1)S(1)}, bf16[384,2048]{1,0:T(8,128)(2,1)}, u32[]{:S(2)}) copy-start(bf16[384,2048]{1,0:T(8,128)(2,1)} %param.29) | copy-start | bytes 4718596
  714.7 20.9 copy-start.5
  714.7 20.9 copy-start.22
  735.6 19.3 copy-start.34
  754.9 5.2 copy-start.14
  754.9 5.2 copy-start.15
  754.9 5.2 copy-start.16
  764.5 2008.3 %all-reduce.26.cloned.1.call-start = ((), (), s32[]{:S(2)}) async-start(), calls=%async_computation.6 | async-start | bytes 268435456
  852.3 2630.9 %reduce-scatter.2.cloned.1.call-start = ((), (), s32[]{:S(2)}) async-start(), calls=%async_computation.5 | async-start | bytes 69206016 | tf_op jit(solution)/shard_map/reduce_scatter | solution.py:218
  893.5 19.3 copy-start.1
  893.5 19.3 copy-start.18
  923.5 2559.7 %copy-start.46 = (f32[64]{0:T(128)}, f32[64]{0:T(128)S(1)}, u32[]{:S(2)}) copy-start(f32[64]{0:T(128)S(1)} %dynamic-slice.6) | copy-start | bytes 772
  (8 other events, 9.4 us)
Sparse Core Ops, SparseCore 0:
  11.0 80.4 all-gather.7
  94.4 153.2 all-gather.5
  250.5 192.9 all-gather.9
  446.2 192.9 all-gather.11
  764.7 121.4 all-reduce.27
  893.5 1879.3 all-reduce.25
  2775.9 707.1 reduce-scatter.1
where the time goes:
time: 3500 us; the launch traced here: 3490 us
  waiting for transfers between devices  2950 us (84%)
  matrix products  269 us (8%)
  other arithmetic  136 us (4%)
  blocking collectives  83.9 us (2%)
  local copies, waits for them, and re-layouts  38.8 us (1%)
    unnamed x9, waiting for transfers between devices  1850 us
    reduce_scatter x1, waiting for transfers between devices, per_device(): lax.psum_scatter(times_leading(active, cotangent), 'dp', scatter_dimensio...  702 us
    all_gather x1, waiting for transfers between devices, per_device(): lax.all_gather(contract_weight, 'dp', axis=0, tiled=True)  173 us
    all_gather x1, waiting for transfers between devices, per_device(): lax.all_gather(qkv_weight, 'dp', axis=0, tiled=True)  133 us
    dot_general x4, matrix products, times_paired(): lax.dot_general(left, right, PAIRED, preferred_element_type=jnp.float32)  97.3 us
    dot_general x4, matrix products, times_leading(): lax.dot_general(left, right, LEADING, preferred_element_type=jnp.float32)  93.4 us
    all_gather x1, waiting for transfers between devices, per_device(): lax.all_gather(expand_weight, 'dp', axis=0, tiled=True)  92.6 us
    concatenate x1, other arithmetic, per_device(): jnp.concatenate([times_leading(low_one, grad_qkv), times_leading(attn, co...  87.6 us
  transfers between devices with their start and end apart: 7, of which 5 were waited for; matrix products, arithmetic and copies ran while one was open for 9% of the time, Pallas kernels for 0%

commit v1 on v0

v1 whole, which is shorter than its diff:
```python
import math

import jax
import jax.numpy as jnp
from jax import lax
from jax.sharding import PartitionSpec as P


HEADS = 8

EPSILON = 1e-05
MASKED = -1e30
PAIRED = (((1,), (1,)), ((), ()))
LEADING = (((0,), (0,)), ((), ()))


class Plan:
    def __init__(self, count):
        self.count = count
        self.bits = count.bit_length() - 1
        self.inner = (3, 1, 0) if count == 32 else (2, 1, 0)
        self.outer = tuple(b for b in reversed(range(self.bits)) if b not in self.inner)
        self.groups = count // HEADS

    def device(self, group, slot):
        found = 0
        for place, bit in enumerate(reversed(self.outer)):
            found |= ((group >> place) & 1) << bit
        for place, bit in enumerate(reversed(self.inner)):
            found |= ((slot >> place) & 1) << bit
        return found

    def inner_groups(self):
        return [
            [self.device(group, slot) for slot in range(HEADS)] for group in range(self.groups)
        ]

    def flip(self, bit):
        return [(d, d ^ (1 << bit)) for d in range(self.count)]


def bit_of(index, bit):
    return (index >> bit) & 1


def gather_bits(value, bits, plan):
    pieces = [(0, value)]
    for bit in bits:
        pieces += [
            (mask | (1 << bit), lax.ppermute(piece, "dp", plan.flip(bit)))
            for mask, piece in pieces
        ]
    return pieces


def place_outer(pieces, me, plan):
    shape = pieces[0][1].shape
    held = jnp.zeros((2,) * len(plan.outer) + shape, pieces[0][1].dtype)
    for mask, piece in pieces:
        start = [bit_of(me ^ mask, bit) for bit in plan.outer] + [0] * len(shape)
        held = lax.dynamic_update_slice(held, piece.reshape((1,) * len(plan.outer) + shape), start)
    return held.reshape((plan.groups,) + shape)


def place_all(pieces, me, plan):
    rest = pieces[0][1].shape[1:]
    held = jnp.zeros((2,) * plan.bits + rest, pieces[0][1].dtype)
    order = list(reversed(range(plan.bits)))
    for mask, piece in pieces:
        start = [bit_of(me ^ mask, b) if b in plan.outer else 0 for b in order] + [0] * len(rest)
        block = piece.reshape(tuple(1 if b in plan.outer else 2 for b in order) + rest)
        held = lax.dynamic_update_slice(held, block, start)
    return held.reshape((plan.count,) + rest)


def reduce_outer(value, me, plan):
    rest = value.shape[1:]
    held = value.reshape((2,) * len(plan.outer) + rest)
    for place in reversed(range(len(plan.outer))):
        bit = plan.outer[place]
        mine = bit_of(me, bit)
        kept = lax.dynamic_index_in_dim(held, mine, place, keepdims=True)
        sent = lax.dynamic_index_in_dim(held, 1 - mine, place, keepdims=True)
        got = lax.ppermute(sent.astype(jnp.bfloat16), "dp", plan.flip(bit))
        held = kept.astype(jnp.float32) + got.astype(jnp.float32)
    return held.reshape(rest)


def slot_layout(lengths, slots):
    place = jnp.arange(slots, dtype=jnp.int32)
    ends = jnp.cumsum(lengths, dtype=jnp.int32)
    after = (place[:, None] >= ends[None, :]).astype(jnp.int32)
    segment = jnp.sum(after, axis=1, dtype=jnp.int32)
    offset = jnp.sum(after * lengths[None, :], axis=1, dtype=jnp.int32)
    return (segment, place - offset)


def rotary_tables(position, rotated):
    half = rotated // 2
    ladder = jnp.arange(half, dtype=jnp.float32) * (-math.log(10000.0) / half)
    angle = position.astype(jnp.float32)[:, None] * jnp.exp(ladder)[None, :]
    return (jnp.cos(angle), jnp.sin(angle))


def rotate(value, cosine, sine, sign):
    half = cosine.shape[-1]
    first = value[:, :half]
    second = value[:, half : 2 * half]
    return jnp.concatenate(
        [
            first * cosine - sign * second * sine,
            second * cosine + sign * first * sine,
            value[:, 2 * half :],
        ],
        axis=1,
    )


def norm_terms(value):
    centre = jnp.mean(value, axis=1, keepdims=True)
    spread = value - centre
    variance = jnp.mean(spread * spread, axis=1, keepdims=True)
    scale = lax.rsqrt(variance + EPSILON)
    return (spread * scale, scale)


def times_leading(left, right):
    return lax.dot_general(left, right, LEADING, preferred_element_type=jnp.float32)


def times_paired(left, right):
    return lax.dot_general(left, right, PAIRED, preferred_element_type=jnp.float32)


def attend(query, key, value, grad_attn, segment, scale):
    place = jnp.arange(segment.shape[1], dtype=jnp.int32)
    allowed = (segment[:, :, None] == segment[:, None, :]) & (
        place[None, None, :] <= place[None, :, None]
    )

    def batched(spec, left, right):
        return jnp.einsum(spec, left, right, preferred_element_type=jnp.float32)

    scores = batched("bqd,bkd->bqk", query, key) * scale
    masked = jnp.where(allowed, scores, MASKED)
    highest = jnp.max(masked, axis=2, keepdims=True)
    raised = jnp.exp(masked - highest)
    weights = raised / jnp.sum(raised, axis=2, keepdims=True)
    probs = weights.astype(jnp.bfloat16)
    attn = batched("bqk,bkd->bqd", probs, value).astype(jnp.bfloat16)
    grad_probs = batched("bqd,bkd->bqk", grad_attn, value)
    grad_value = batched("bqk,bqd->bkd", probs, grad_attn)
    inner = jnp.sum(weights * grad_probs, axis=2, keepdims=True)
    grad_score = (weights * (grad_probs - inner)).astype(jnp.bfloat16)
    grad_query = batched("bqk,bkd->bqd", grad_score, key) * scale
    grad_key = batched("bqk,bqd->bkd", grad_score, query) * scale
    return (attn, grad_query, grad_key, grad_value)


def per_device(
    plan,
    tokens,
    seq_lengths,
    ln1_gain,
    ln1_bias,
    ln2_gain,
    ln2_bias,
    qkv_weight,
    qkv_bias,
    dense_weight,
    dense_bias,
    expand_weight,
    expand_bias,
    contract_weight,
    contract_bias,
    cotangent,
):
    slots, width = tokens.shape
    rows = qkv_weight.shape[0]
    units = contract_weight.shape[0]
    count, groups = plan.count, plan.groups
    head_dim = width // HEADS
    rotated = head_dim // 4
    scale = 1.0 / math.sqrt(head_dim)
    me = lax.axis_index("dp")
    inner_groups = plan.inner_groups()
    slot = sum(bit_of(me, bit) << place for place, bit in enumerate(reversed(plan.inner)))

    parts = [
        ln1_gain,
        ln1_bias,
        ln2_gain,
        ln2_bias,
        dense_bias,
        contract_bias,
        qkv_bias,
        expand_bias,
        seq_lengths[0].astype(jnp.bfloat16),
    ]
    sizes = [item.shape[0] for item in parts]
    total = sum(sizes)
    padded = -(-total // 1024) * 1024
    small = jnp.concatenate(parts + [jnp.zeros((padded - total,), jnp.bfloat16)])
    every = lax.all_gather(small, "dp", axis=0, tiled=False).astype(jnp.float32)
    taken, at = [], 0
    for size in sizes:
        taken.append(every[:, at : at + size])
        at += size
    gain_one, shift_one, gain_two, shift_two, bias_dense, bias_contract = [
        item.reshape(1, width) for item in taken[:6]
    ]
    bias_qkv = lax.dynamic_index_in_dim(
        taken[6].reshape(3, HEADS, head_dim), slot, 1, keepdims=False
    ).reshape(1, 3 * head_dim)

    def of_slot(value):
        rest = value.shape[1:]
        shaped = value.reshape((2,) * plan.bits + rest)
        order = list(reversed(range(plan.bits)))
        for place, bit in enumerate(order):
            if bit in plan.inner:
                shaped = lax.dynamic_slice_in_dim(shaped, bit_of(me, bit), 1, place)
        return shaped.reshape((groups,) + rest)

    def of_group(value):
        rest = value.shape[1:]
        shaped = value.reshape((2,) * plan.bits + rest)
        order = list(reversed(range(plan.bits)))
        for place, bit in enumerate(order):
            if bit in plan.outer:
                shaped = lax.dynamic_slice_in_dim(shaped, bit_of(me, bit), 1, place)
        return shaped.reshape((HEADS,) + rest)

    bias_expand = of_slot(taken[7]).reshape(1, groups * units)
    lengths = of_group(taken[8]).astype(jnp.int32)

    group_tokens = lax.all_gather(
        tokens, "dp", axis=0, tiled=True, axis_index_groups=inner_groups
    )
    group_cotangent = lax.all_gather(
        cotangent, "dp", axis=0, tiled=True, axis_index_groups=inner_groups
    )

    columns = [plan.device(group, s) for s in range(HEADS) for group in range(groups)]
    qkv_parts = qkv_weight.reshape(rows, 3, HEADS, head_dim).transpose(2, 0, 1, 3)
    expand_parts = expand_weight.reshape(rows, count, units)[:, jnp.array(columns)]
    expand_parts = expand_parts.reshape(rows, HEADS, groups * units).transpose(1, 0, 2)
    both = jnp.concatenate([qkv_parts.reshape(HEADS, rows, 3 * head_dim), expand_parts], axis=2)
    both = lax.all_to_all(both, "dp", 0, 0, tiled=True, axis_index_groups=inner_groups)
    weight_in = place_all(gather_bits(both, plan.outer, plan), me, plan).reshape(width, -1)
    weight_qkv = weight_in[:, : 3 * head_dim]
    weight_expand = weight_in[:, 3 * head_dim :]

    to_slot = [(d, plan.device(d % groups, d // groups)) for d in range(count)]
    from_slot = [(target, source) for source, target in to_slot]
    dense_part = lax.ppermute(dense_weight, "dp", to_slot)
    weight_dense = place_outer(gather_bits(dense_part, plan.outer, plan), me, plan)
    weight_dense = weight_dense.reshape(head_dim, width)
    weight_contract = place_outer(gather_bits(contract_weight, plan.outer, plan), me, plan)
    weight_contract = weight_contract.reshape(groups * units, width)

    segment, position = jax.vmap(lambda item: slot_layout(item, slots))(lengths)
    cosine, sine = rotary_tables(position.reshape(-1), rotated)
    normed, _ = norm_terms(group_tokens.astype(jnp.float32))
    low_one = (normed * gain_one + shift_one).astype(jnp.bfloat16)
    low_two = (normed * gain_two + shift_two).astype(jnp.bfloat16)
    low_normed = normed.astype(jnp.bfloat16)
    projected = jnp.dot(low_one, weight_qkv, preferred_element_type=jnp.float32) + bias_qkv
    query = rotate(projected[:, :head_dim], cosine, sine, 1.0).astype(jnp.bfloat16)
    key = rotate(projected[:, head_dim : 2 * head_dim], cosine, sine, 1.0).astype(jnp.bfloat16)
    value = projected[:, 2 * head_dim :].astype(jnp.bfloat16)
    hidden = jnp.dot(low_two, weight_expand, preferred_element_type=jnp.float32) + bias_expand
    active_full, gate_pull = jax.vjp(lambda v: jax.nn.gelu(v, approximate=False), hidden)
    active = active_full.astype(jnp.bfloat16)
    grad_attn = times_paired(group_cotangent, weight_dense).astype(jnp.bfloat16)

    def blocked(item):
        return item.reshape(HEADS, slots, head_dim)

    attn, grad_query, grad_key, grad_value = attend(
        blocked(query), blocked(key), blocked(value), blocked(grad_attn), segment, scale
    )
    attn = attn.reshape(HEADS * slots, head_dim)
    grad_query, grad_key, grad_value = [
        item.reshape(HEADS * slots, head_dim) for item in (grad_query, grad_key, grad_value)
    ]
    branch = jnp.dot(attn, weight_dense, preferred_element_type=jnp.float32) + jnp.dot(
        active, weight_contract, preferred_element_type=jnp.float32
    )
    branch = lax.psum_scatter(
        branch.astype(jnp.bfloat16),
        "dp",
        scatter_dimension=0,
        tiled=True,
        axis_index_groups=inner_groups,
    )
    inputs = tokens.astype(jnp.float32)
    layer_out = (inputs + branch.astype(jnp.float32) + bias_dense + bias_contract).astype(
        jnp.bfloat16
    )

    grad_active = times_paired(group_cotangent, weight_contract)
    (grad_hidden,) = gate_pull(grad_active)
    grad_hidden = grad_hidden.astype(jnp.bfloat16)
    grad_qkv = jnp.concatenate(
        [
            rotate(grad_query, cosine, sine, -1.0),
            rotate(grad_key, cosine, sine, -1.0),
            grad_value,
        ],
        axis=1,
    ).astype(jnp.bfloat16)
    grad_both = (
        times_paired(grad_qkv, weight_qkv) * gain_one
        + times_paired(grad_hidden, weight_expand) * gain_two
    )
    grad_both = lax.psum_scatter(
        grad_both.astype(jnp.bfloat16),
        "dp",
        scatter_dimension=0,
        tiled=True,
        axis_index_groups=inner_groups,
    ).astype(jnp.float32)
    own_normed, own_scale = norm_terms(inputs)
    input_grad = (
        cotangent.astype(jnp.float32)
        + (
            grad_both
            - jnp.mean(grad_both, axis=1, keepdims=True)
            - own_normed * jnp.mean(grad_both * own_normed, axis=1, keepdims=True)
        )
        * own_scale
    )

    contract_terms = times_leading(active, group_cotangent).astype(jnp.bfloat16)
    contract_weight_grad = reduce_outer(contract_terms.reshape(groups, units, width), me, plan)
    dense_terms = times_leading(attn, group_cotangent).astype(jnp.bfloat16)
    dense_weight_grad = reduce_outer(dense_terms.reshape(groups, rows, width), me, plan)
    dense_weight_grad = lax.ppermute(
        dense_weight_grad.astype(jnp.bfloat16), "dp", from_slot
    ).astype(jnp.float32)
    bias_out_grad = lax.psum_scatter(
        jnp.sum(cotangent.astype(jnp.float32), axis=0), "dp", scatter_dimension=0, tiled=True
    )

    def input_terms(grad):
        terms = times_leading(low_normed, grad)
        shaped = terms.reshape((2,) * plan.bits + (rows, -1))
        order = list(reversed(range(plan.bits)))
        shaped = shaped.transpose(
            [order.index(b) for b in plan.outer]
            + [order.index(b) for b in plan.inner]
            + [plan.bits, plan.bits + 1]
        ).reshape(groups, HEADS * rows, -1)
        sums = jnp.sum(grad.astype(jnp.float32), axis=0)
        sums = jnp.broadcast_to(sums, (groups, 16, sums.shape[0]))
        return jnp.concatenate([shaped, sums], axis=1).astype(jnp.bfloat16)

    def finish(reduced):
        core = reduced[: HEADS * rows].reshape(HEADS, rows, -1)
        sums = jnp.broadcast_to(reduced[None, HEADS * rows :], (HEADS, 16, reduced.shape[1]))
        sent = jnp.concatenate([core, sums], axis=1).astype(jnp.bfloat16)
        got = lax.all_to_all(sent, "dp", 0, 0, tiled=True, axis_index_groups=inner_groups)
        got = got.astype(jnp.float32)
        return got[:, :rows], got[:, rows]

    expand_got, expand_sums = finish(reduce_outer(input_terms(grad_hidden), me, plan))
    qkv_got, qkv_sums = finish(reduce_outer(input_terms(grad_qkv), me, plan))
    qkv_got = qkv_got.reshape(HEADS, rows, 3, head_dim).transpose(1, 2, 0, 3)
    qkv_got = qkv_got.reshape(rows, 3 * width)
    qkv_sums = qkv_sums.reshape(HEADS, 3, head_dim).transpose(1, 0, 2).reshape(3 * width)
    inverse = [0] * count
    for place, device in enumerate(columns):
        inverse[device] = place
    inverse = jnp.array(inverse)
    expand_got = expand_got.reshape(HEADS, rows, groups, units).transpose(1, 0, 2, 3)
    expand_got = expand_got.reshape(rows, count, units)[:, inverse].reshape(rows, count * units)
    expand_sums = expand_sums.reshape(count, units)[inverse].reshape(count * units)

    def input_grads(got, sums, weight, gain, shift):
        weight = weight.astype(jnp.float32)
        gain = gain.astype(jnp.float32)
        shift = shift.astype(jnp.float32)
        return (
            got * gain[:, None] + shift[:, None] * sums[None, :],
            jnp.sum(weight * got, axis=1),
            jnp.sum(weight * sums[None, :], axis=1),
        )

    qkv_weight_grad, ln1_gain_grad, ln1_bias_grad = input_grads(
        qkv_got, qkv_sums, qkv_weight, ln1_gain, ln1_bias
    )
    expand_weight_grad, ln2_gain_grad, ln2_bias_grad = input_grads(
        expand_got, expand_sums, expand_weight, ln2_gain, ln2_bias
    )
    per = qkv_bias.shape[0]
    return (
        layer_out,
        input_grad,
        ln1_gain_grad,
        ln1_bias_grad,
        ln2_gain_grad,
        ln2_bias_grad,
        qkv_weight_grad,
        lax.dynamic_slice_in_dim(qkv_sums, me * per, per),
        dense_weight_grad,
        bias_out_grad,
        expand_weight_grad,
        lax.dynamic_slice_in_dim(expand_sums, me * units, units),
        contract_weight_grad,
        bias_out_grad,
    )


def solution(mesh):
    in_specs = (
        P("dp", None),
        P("dp", None),
        P("dp"),
        P("dp"),
        P("dp"),
        P("dp"),
        P("dp", None),
        P("dp"),
        P("dp", None),
        P("dp"),
        P("dp", None),
        P("dp"),
        P("dp", None),
        P("dp"),
        P("dp", None),
    )
    out_specs = (
        P("dp", None),
        P("dp", None),
        P("dp"),
        P("dp"),
        P("dp"),
        P("dp"),
        P("dp", None),
        P("dp"),
        P("dp", None),
        P("dp"),
        P("dp", None),
        P("dp"),
        P("dp", None),
        P("dp"),
    )
    plan = Plan(mesh.shape["dp"])

    def layer(*arrays):
        return per_device(plan, *arrays)

    return jax.shard_map(layer, mesh=mesh, in_specs=in_specs, out_specs=out_specs, check_vma=False)
```

time: 3500 us -> 949 us (0.27)
  waiting for transfers between devices: 2950 us -> 270 us
  local copies, waits for them, and re-layouts: 38.8 us -> 130 us
  blocking collectives: 83.9 us -> 165 us
  other arithmetic: 136 us -> 67.5 us
  starting transfers between devices: 0.27 us -> 36.9 us
    unnamed x9 -> x4, waiting for transfers between devices: 1850 us -> 1.41 us
    reduce_scatter x1 -> x2, waiting for transfers between devices: 702 us -> 0.02 us  [the longest x1 0.02 us: per_device(): lax.psum_scatter(branch.astype(jnp.bfloat16), 'dp', scatter_dimension=0,...]
    all_gather x4 -> x2, waiting for transfers between devices: 399 us -> 0.01 us  [the longest x1 0.01 us: per_device(): lax.all_gather(tokens, 'dp', axis=0, tiled=True, axis_index_groups=inner_...]
    ppermute x0 -> x19, waiting for transfers between devices: none -> 250 us  [the longest x8 132 us: reduce_outer(): got = lax.ppermute(sent.astype(jnp.bfloat16), 'dp', plan.flip(bit))]
    concatenate x1 -> x5, other arithmetic: 87.6 us -> 3.98 us  [the longest x2 2.16 us: finish(): sent = jnp.concatenate([core, sums], axis=1).astype(jnp.bfloat16)]
    all_gather x1, blocking collectives: 40.7 us -> 120 us  [per_device(): every = lax.all_gather(small, 'dp', axis=0, tiled=False).astype(jnp.float32)]
    dot_general x10 -> x9, matrix products: 78.7 us -> 114 us  [the longest x1 46.5 us: per_device(): jnp.dot(low_two, weight_expand, preferred_element_type=jnp.float32)]
  transfers between devices with their start and end apart: 7 -> 26, of which waited for: 5 -> 10; matrix products, arithmetic and copies ran while one was open for 9% -> 27% of each run, Pallas kernels for 0% -> 0%
where the time goes in v1:
time: 949 us; the launch traced here: 942 us
  waiting for transfers between devices  270 us (28%)
  matrix products  258 us (27%)
  blocking collectives  165 us (17%)
  local copies, waits for them, and re-layouts  130 us (14%)
  other arithmetic  67.5 us (7%)
  starting transfers between devices  36.9 us (4%)
  between operations  15.4 us (2%)
    ppermute x8, waiting for transfers between devices, reduce_outer(): got = lax.ppermute(sent.astype(jnp.bfloat16), 'dp', plan.flip(bit))  132 us
    all_gather x1, blocking collectives, per_device(): every = lax.all_gather(small, 'dp', axis=0, tiled=False).astype(jnp.float32)  120 us
    ppermute x9, waiting for transfers between devices, gather_bits(): lax.ppermute(piece, 'dp', plan.flip(bit))  113 us
    dot_general x4, matrix products, times_paired(): lax.dot_general(left, right, PAIRED, preferred_element_type=jnp.float32)  78.6 us
    dot_general x4, matrix products, times_leading(): lax.dot_general(left, right, LEADING, preferred_element_type=jnp.float32)  58.4 us
    dot_general x1, matrix products, per_device(): jnp.dot(low_two, weight_expand, preferred_element_type=jnp.float32)  46.5 us
    unnamed x1, blocking collectives  44.4 us
    unnamed x122, local copies, waits for them, and re-layouts  23.6 us
  transfers between devices with their start and end apart: 26, of which 10 were waited for; matrix products, arithmetic and copies ran while one was open for 27% of the time, Pallas kernels for 0%

profile of v1, /device:TPU:1, one launch (start us, length us, event | category | flops | bytes accessed | tf_op | source)
XLA Modules:
  0.0 942.1 jit_solution(15652359809318747779)
XLA Ops:
  16.8 5.3 all-to-all-start
  28.6 120.3 %all-gather = bf16[32768]{0:T(1024)(128)(2,1)S(1)} all-gather(bf16[1024]{0:T(1024)(128)(2,1)S(1)} %concatenate.54), channel_id=2, replica_groups=mesh['dp'=32] {'dp'}, dimensions={0}, use_global_device_ids=true | all-gather | bytes 67584 | tf_op jit(solution)/shard_map/all_gather | solution.py:204
  159.8 11.8 %collective-permute-done.4 = bf16[64,2048]{1,0:T(8,128)(2,1)} collective-permute-done((bf16[64,2048]{1,0:T(8,128)(2,1)S(1)}, bf16[64,2048]{1,0:T(8,128)(2,1)}, u32[]{:S(2)}, u32[]{:S(2)}) %collective-permute-start.4) | collective-permute-done | bytes 262176 | tf_op jit(solution)/shard_map/ppermute | solution.py:50
  175.1 2.9 collective-permute-done.6
  178.4 71.5 %collective-permute-done = bf16[8,64,1792]{2,1,0:T(8,128)(2,1)S(1)} collective-permute-done((bf16[8,64,1792]{2,1,0:T(8,128)(2,1)S(1)}, bf16[8,64,1792]{2,1,0:T(8,128)(2,1)S(1)}, u32[]{:S(2)}, u32[]{:S(2)}) %collective-permute-start) | collective-permute-done | bytes 1835040 | tf_op jit(solution)/shard_map/ppermute | solution.py:50
  255.6 3.8 broadcast_in_dim.29
  263.7 27.1 %collective-permute-done.2 = bf16[8,64,1792]{2,1,0:T(8,128)(2,1)S(1)} collective-permute-done((bf16[8,64,1792]{2,1,0:T(8,128)(2,1)S(1)}, bf16[8,64,1792]{2,1,0:T(8,128)(2,1)S(1)}, u32[]{:S(2)}, u32[]{:S(2)}) %collective-permute-start.2) | collective-permute-done | bytes 1835040 | tf_op jit(solution)/shard_map/ppermute | solution.py:50
  292.1 6.3 convert_reduce_fusion
  298.4 8.0 fusion.10
  306.4 18.6 %fusion.119 = (bf16[3072,768]{0,1:T(8,128)(2,1)}, f32[3072,768]{0,1:T(8,128)}) fusion(f32[768]{0:T(1024)S(1)} %add.281, bf16[2048,1792]{1,0:T(8,128)(2,1)} %bitcast.10, bf16[3072,2048]{1,0:T(8,128)(2,1)} %all-gather.4.cloned.1.call-done, f32[2048]{0:T(1024)S(1)} %add.268, f32[2048]{0:T(1024)S(1)} %mul.283, f32[3072]{0:T(1024)S(1)} %add_rsqrt_fusion, ...), kind=kOutput, calls=%fused_computation.227 | convolution fusion | flops 9706143744 | bytes 29928448 | tf_op jit(solution)/shard_map/dot_general | solution.py:268
  326.6 3.2 fusion.115
  333.9 3.6 fusion.90
  345.6 9.6 %fusion.41 = bf16[3072,256]{0,1:T(8,128)(2,1)} fusion(bf16[256,2048]{1,0:T(8,128)(2,1)} %bitcast.162, bf16[3072,2048]{1,0:T(8,128)(2,1)} %all-gather.6.cloned.1.call-done), kind=kOutput, calls=%fused_computation.79 | convolution fusion | flops 3222011904 | bytes 15204352 | tf_op jit(solution)/shard_map/dot_general | solution.py:132
  355.2 3.0 copy.241
  358.2 6.9 fusion.120
  365.1 5.1 convolution_convert_fusion.5
  392.0 3.8 fusion.104
  410.3 9.8 %concatenate.64 = bf16[3072,768]{1,0:T(8,128)(2,1)} concatenate(bf16[3072,32]{1,0:T(8,128)(2,1)} %copy.215, bf16[3072,32]{1,0:T(8,128)(2,1)} %copy.216, bf16[3072,192]{1,0:T(8,128)(2,1)S(1)} %copy.217, bf16[3072,32]{1,0:T(8,128)(2,1)} %copy.218, bf16[3072,32]{1,0:T(8,128)(2,1)} %copy.219, bf16[3072,192]{1,0:T(8,128)(2,1)S(1)} %copy.220, bf16[3072,256]{1,0:T(8,128)(2,1)} %bitcast.190), dimensions={1} | concatenate | bytes 9437184 | tf_op jit(solution)/shard_map/concatenate | solution.py:305
  420.1 17.6 %fusion.53 = f32[3072,2048]{1,0:T(8,128)} fusion(bf16[3072,768]{1,0:T(8,128)(2,1)} %concatenate.64, bf16[2048,1792]{1,0:T(8,128)(2,1)} %bitcast.10), kind=kOutput, calls=%fused_computation.95 | convolution fusion | flops 9663676416 | bytes 33030144 | tf_op jit(solution)/shard_map/dot_general | solution.py:132
  437.7 46.5 %multiply_convert_fusion = (bf16[3072,1024]{1,0:T(8,128)(2,1)}, f32[3072,1024]{1,0:T(8,128)}, f32[3072,1024]{1,0:T(8,128)}) fusion(f32[1024]{0:T(1024)S(1)} %bitcast.205, bf16[2048,1792]{1,0:T(8,128)(2,1)} %bitcast.10, bf16[3072,2048]{1,0:T(8,128)(2,1)} %all-gather.4.cloned.1.call-done, f32[2048]{0:T(1024)S(1)} %copy-done.31, f32[2048]{0:T(1024)S(1)} %copy-done.30, ...), kind=kOutput, calls=%fused_computation.31 | convolution fusion | flops 13130268672 | bytes 48279552 | tf_op jit(solution)/shard_map/dot_general | solution.py:272
  484.3 29.6 %fusion.121 = (bf16[1024]{0:T(1024)(128)(2,1)S(1)}, bf16[3072,1024]{1,0:T(8,128)(2,1)}) fusion(f32[3072,1024]{1,0:T(8,128)} %get-tuple-element.23, bf16[1024,2048]{1,0:T(8,128)(2,1)} %bitcast.28, bf16[3072,2048]{1,0:T(8,128)(2,1)} %all-gather.6.cloned.1.call-done, f32[3072,1024]{1,0:T(8,128)} %get-tuple-element.57, f32[1024]{0:T(1024)S(1)} %bitcast.206), kind=kOutput, calls=%fused_computation.229 | convolution fusion | flops 12935232512 | bytes 48240640 | tf_op jit(solution)/shard_map/dot_general | solution.py:132
  513.8 21.8 %add_convert_fusion = bf16[3072,2048]{1,0:T(8,128)(2,1)} fusion(f32[3072,2048]{1,0:T(8,128)} %fusion.53, bf16[3072,1024]{1,0:T(8,128)(2,1)} %get-tuple-element.59, f32[2048]{0:T(1024)S(1)} %copy-done.30, f32[2048]{0:T(1024)S(1)} %copy-done.33, bf16[2048,1792]{1,0:T(8,128)(2,1)} %bitcast.10), kind=kOutput, calls=%fused_computation.16 | convolution fusion | flops 12910067712 | bytes 48250880 | tf_op jit(solution)/shard_map/dot_general | solution.py:132
  537.1 3.4 convolution_convert_fusion.6
  540.5 20.3 %fusion.122 = f32[3072,2048]{1,0:T(8,128)} fusion(bf16[3072,1024]{1,0:T(8,128)(2,1)} %get-tuple-element.22, bf16[1024,2048]{1,0:T(8,128)(2,1)} %bitcast.28), kind=kOutput, calls=%fused_computation.230 | convolution fusion | flops 12884901888 | bytes 35651584 | tf_op jit(solution)/shard_map/dot_general | solution.py:287
  560.9 15.2 %add_convert_fusion.1 = bf16[3072,2048]{1,0:T(8,128)(2,1)} fusion(f32[3072,2048]{1,0:T(8,128)} %fusion.122, bf16[3072,256]{1,0:T(8,128)(2,1)S(1)} %bitcast.146, bf16[256,2048]{1,0:T(8,128)(2,1)S(1)} %bitcast.163), kind=kOutput, calls=%fused_computation.17 | convolution fusion | flops 3233808384 | bytes 40370176 | tf_op jit(solution)/shard_map/dot_general | solution.py:287
  577.8 3.1 reduce
  580.9 20.4 %convolution_convert_fusion.2 = bf16[2048,1024]{1,0:T(8,128)(2,1)S(1)} fusion(bf16[3072,1024]{1,0:T(8,128)(2,1)} %get-tuple-element.59, bf16[3072,2048]{1,0:T(8,128)(2,1)} %all-gather.4.cloned.1.call-done, f32[3072]{0:T(1024)S(1)} %copy-done.29, f32[3072]{0:T(1024)S(1)} %copy-done.24), kind=kOutput, calls=%fused_computation.76 | convolution fusion | flops 12912164864 | bytes 23093248 | tf_op jit(solution)/shard_map/dot_general | solution.py:128
  604.4 18.1 %convolution_convert_fusion.3 = bf16[2048,768]{1,0:T(8,128)(2,1)} fusion(bf16[3072,768]{1,0:T(8,128)(2,1)} %concatenate.64, bf16[3072,2048]{1,0:T(8,128)(2,1)} %all-gather.4.cloned.1.call-done, f32[3072]{0:T(1024)S(1)} %copy-done.29, f32[3072]{0:T(1024)S(1)} %copy-done.24), kind=kOutput, calls=%fused_computation.83 | convolution fusion | flops 9690415104 | bytes 20471808 | tf_op jit(solution)/shard_map/dot_general | solution.py:128
  625.3 16.5 %convolution_convert_fusion.1 = bf16[1024,2048]{1,0:T(8,128)(2,1)} fusion(bf16[3072,1024]{1,0:T(8,128)(2,1)} %get-tuple-element.22, bf16[3072,2048]{1,0:T(8,128)(2,1)S(1)} %bitcast.141), kind=kOutput, calls=%fused_computation.75 | convolution fusion | flops 12886999040 | bytes 23068672 | tf_op jit(solution)/shard_map/dot_general | solution.py:128
  641.8 3.2 constant_dynamic-slice_fusion
  646.0 39.9 %collective-permute-done.10 = bf16[2,1,528,768]{3,2,1,0:T(8,128)(2,1)} collective-permute-done((bf16[2,1,528,768]{3,2,1,0:T(8,128)(2,1)S(1)}, bf16[2,1,528,768]{3,2,1,0:T(8,128)(2,1)}, u32[]{:S(2)}, u32[]{:S(2)}) %collective-permute-start.10) | collective-permute-done | bytes 1622048 | tf_op jit(solution)/shard_map/ppermute | solution.py:84
  687.8 3.4 convolution_convert_fusion.4
  701.7 42.5 %collective-permute-done.11 = bf16[1,1,528,768]{3,2,1,0:T(8,128)(2,1)S(1)} collective-permute-done((bf16[1,1,528,768]{3,2,1,0:T(8,128)(2,1)S(1)}, bf16[1,1,528,768]{3,2,1,0:T(8,128)(2,1)S(1)}, u32[]{:S(2)}, u32[]{:S(2)}) %collective-permute-start.11) | collective-permute-done | bytes 811040 | tf_op jit(solution)/shard_map/ppermute | solution.py:84
  745.5 7.6 all-to-all-start.1
  755.4 5.4 convert_add_fusion.2
  760.7 12.0 %collective-permute-done.13 = bf16[1,1,528,1024]{3,2,1,0:T(8,128)(2,1)} collective-permute-done((bf16[1,1,528,1024]{3,2,1,0:T(8,128)(2,1)}, bf16[1,1,528,1024]{3,2,1,0:T(8,128)(2,1)}, u32[]{:S(2)}, u32[]{:S(2)}) %collective-permute-start.13) | collective-permute-done | bytes 1081376 | tf_op jit(solution)/shard_map/ppermute | solution.py:84
  775.7 18.1 %all-to-all-done.1 = bf16[8,80,768]{2,1,0:T(8,128)(2,1)S(1)} async-done(((bf16[8,80,768]{2,1,0:T(8,128)(2,1)}), bf16[8,80,768]{2,1,0:T(8,128)(2,1)S(1)}, u32[]{:S(2)}, u32[]{:S(2)}) %all-to-all-start.1) | async-done | bytes 983072 | tf_op jit(solution)/shard_map/all_to_all | solution.py:363
  794.7 3.8 all-to-all-start.2
  805.9 5.1 collective-permute-done.16
  811.8 37.6 %collective-permute-done.18 = bf16[1,1,256,2048]{3,2,1,0:T(8,128)(2,1)} collective-permute-done((bf16[1,1,256,2048]{3,2,1,0:T(8,128)(2,1)}, bf16[1,1,256,2048]{3,2,1,0:T(8,128)(2,1)}, u32[]{:S(2)}, u32[]{:S(2)}) %collective-permute-start.18) | collective-permute-done | bytes 1048608 | tf_op jit(solution)/shard_map/ppermute | solution.py:84
  849.5 3.6 add_bitcast_fusion
  854.4 3.9 reshape.313
  863.5 3.8 fusion.68
  869.1 3.6 gather_fusion.1
  872.7 3.1 copy.250
  877.5 4.5 fusion.64
  884.7 5.5 convert_reduce_fusion.3
  890.1 44.4 %all-reduce = f32[2048]{0:T(1024)S(1)} all-reduce(f32[2048]{0:T(1024)S(1)} %get-tuple-element.36), channel_id=5, replica_groups=mesh['dp'=32] {'dp'}, use_global_device_ids=true, to_apply=%region_21.22.clone | all-reduce | flops 2048 | bytes 16384
  (294 shorter events, 142.6 us)
Async XLA Ops:
  7.2 284.9 %all-gather.4.cloned.1.call-start = ((), (), s32[]{:S(2)}) async-start(), calls=%async_computation.5 | async-start | bytes 14155776 | tf_op jit(solution)/shard_map/all_gather | solution.py:237
  7.9 337.7 %all-gather.6.cloned.1.call-start = ((), (), s32[]{:S(2)}) async-start(), calls=%async_computation.7 | async-start | bytes 14155776 | tf_op jit(solution)/shard_map/all_gather | solution.py:240
  16.8 140.4 %all-to-all-start = ((bf16[8,64,1792]{2,1,0:T(8,128)(2,1)}), bf16[8,64,1792]{2,1,0:T(8,128)(2,1)S(1)}, u32[]{:S(2)}, u32[]{:S(2)}) async-start(bf16[8,64,1792]{2,1,0:T(8,128)(2,1)} %copy.199), calls=%async_computation | async-start | bytes 3670016 | tf_op jit(solution)/shard_map/all_to_all | solution.py:249
  22.1 860.0 %reduce-scatter.5.cloned.1.call-start = ((), (), s32[]{:S(2)}) async-start(), calls=%async_computation.8 | async-start | bytes 14155776 | tf_op jit(solution)/shard_map/reduce_scatter | solution.py:317
  22.1 151.5 %collective-permute-start.7 = (bf16[256,2048]{1,0:T(8,128)(2,1)S(1)}, bf16[256,2048]{1,0:T(8,128)(2,1)}, u32[]{:S(2)}, u32[]{:S(2)}) collective-permute-start(bf16[256,2048]{1,0:T(8,128)(2,1)S(1)} %copy-done.19), channel_id=1, source_target_pairs={{0,16},{1,17},{2,18},{3,19},{4,20},{5,21},{6,22},{7,23},{8,24},{9,... | collective-permute-start | bytes 3145736 | tf_op jit(solution)/shard_map/ppermute | solution.py:50
  24.5 227.7 %collective-permute-start.8 = (bf16[256,2048]{1,0:T(8,128)(2,1)S(1)}, bf16[256,2048]{1,0:T(8,128)(2,1)}, u32[]{:S(2)}, u32[]{:S(2)}) collective-permute-start(bf16[256,2048]{1,0:T(8,128)(2,1)S(1)} %copy-done.19), channel_id=1, source_target_pairs={{0,4},{1,5},{2,6},{3,7},{4,0},{5,1},{6,2},{7,3},{8,12},{9,13},{10,... | collective-permute-start | bytes 3145736 | tf_op jit(solution)/shard_map/ppermute | solution.py:50
  25.7 131.5 %collective-permute-start.3 = (bf16[64,2048]{1,0:T(8,128)(2,1)}, bf16[64,2048]{1,0:T(8,128)(2,1)S(1)}, u32[]{:S(2)}, u32[]{:S(2)}) collective-permute-start(bf16[64,2048]{1,0:T(8,128)(2,1)} %param.25), channel_id=1, source_target_pairs={{0,0},{1,4},{2,16},{3,20},{4,1},{5,5},{6,17},{7,21},{8,2},{9,6},{1... | collective-permute-start | bytes 786440 | tf_op jit(solution)/shard_map/ppermute | solution.py:256
  156.5 149.9 %copy-start.32 = (f32[2048]{0:T(1024)}, f32[2048]{0:T(1024)S(1)}, u32[]{:S(2)}) copy-start(f32[2048]{0:T(1024)S(1)} %mul.283) | copy-start | bytes 24580
  157.3 14.3 %collective-permute-start.4 = (bf16[64,2048]{1,0:T(8,128)(2,1)S(1)}, bf16[64,2048]{1,0:T(8,128)(2,1)}, u32[]{:S(2)}, u32[]{:S(2)}) collective-permute-start(bf16[64,2048]{1,0:T(8,128)(2,1)S(1)} %collective-permute-done.3), channel_id=1, source_target_pairs={{0,16},{1,17},{2,18},{3,19},{4,20},{5,21},{6,22},{7,23},{8,24},{9,... | collective-permute-start | bytes 786440 | tf_op jit(solution)/shard_map/ppermute | solution.py:50
  157.3 15.3 %collective-permute-start.5 = (bf16[64,2048]{1,0:T(8,128)(2,1)S(1)}, bf16[64,2048]{1,0:T(8,128)(2,1)}, u32[]{:S(2)}, u32[]{:S(2)}) collective-permute-start(bf16[64,2048]{1,0:T(8,128)(2,1)S(1)} %collective-permute-done.3), channel_id=1, source_target_pairs={{0,4},{1,5},{2,6},{3,7},{4,0},{5,1},{6,2},{7,3},{8,12},{9,13},{10,... | collective-permute-start | bytes 786440 | tf_op jit(solution)/shard_map/ppermute | solution.py:50
  157.3 92.6 %collective-permute-start = (bf16[8,64,1792]{2,1,0:T(8,128)(2,1)S(1)}, bf16[8,64,1792]{2,1,0:T(8,128)(2,1)S(1)}, u32[]{:S(2)}, u32[]{:S(2)}) collective-permute-start(bf16[8,64,1792]{2,1,0:T(8,128)(2,1)S(1)} %all-to-all-done), channel_id=1, source_target_pairs={{0,16},{1,17},{2,18},{3,19},{4,20},{5,21},{6,22},{7,23},{8,24},{9,... | collective-permute-start | bytes 5505032 | tf_op jit(solution)/shard_map/ppermute | solution.py:50
  171.6 6.4 collective-permute-start.6
  173.6 80.9 %collective-permute-start.9 = (bf16[256,2048]{1,0:T(8,128)(2,1)}, bf16[256,2048]{1,0:T(8,128)(2,1)S(1)}, u32[]{:S(2)}, u32[]{:S(2)}) collective-permute-start(bf16[256,2048]{1,0:T(8,128)(2,1)} %collective-permute-done.7), channel_id=1, source_target_pairs={{0,4},{1,5},{2,6},{3,7},{4,0},{5,1},{6,2},{7,3},{8,12},{9,13},{10,... | collective-permute-start | bytes 3145736 | tf_op jit(solution)/shard_map/ppermute | solution.py:50
  178.0 71.9 %copy-start.8 = (bf16[2,2,64,2048]{3,2,1,0:T(8,128)(2,1)}, bf16[2,2,64,2048]{3,2,1,0:T(8,128)(2,1)S(1)}, u32[]{:S(2)}) copy-start(bf16[2,2,64,2048]{3,2,1,0:T(8,128)(2,1)S(1)} %bitcast_dynamic-update-slice_fusion.4) | copy-start | bytes 3145732
  178.0 84.2 %collective-permute-start.1 = (bf16[8,64,1792]{2,1,0:T(8,128)(2,1)S(1)}, bf16[8,64,1792]{2,1,0:T(8,128)(2,1)S(1)}, u32[]{:S(2)}, u32[]{:S(2)}) collective-permute-start(bf16[8,64,1792]{2,1,0:T(8,128)(2,1)S(1)} %all-to-all-done), channel_id=1, source_target_pairs={{0,4},{1,5},{2,6},{3,7},{4,0},{5,1},{6,2},{7,3},{8,12},{9,13},{10,... | collective-permute-start | bytes 5505032 | tf_op jit(solution)/shard_map/ppermute | solution.py:50
  249.9 40.8 %collective-permute-start.2 = (bf16[8,64,1792]{2,1,0:T(8,128)(2,1)S(1)}, bf16[8,64,1792]{2,1,0:T(8,128)(2,1)S(1)}, u32[]{:S(2)}, u32[]{:S(2)}) collective-permute-start(bf16[8,64,1792]{2,1,0:T(8,128)(2,1)S(1)} %collective-permute-done), channel_id=1, source_target_pairs={{0,4},{1,5},{2,6},{3,7},{4,0},{5,1},{6,2},{7,3},{8,12},{9,13},{10,... | collective-permute-start | bytes 5505032 | tf_op jit(solution)/shard_map/ppermute | solution.py:50
  306.4 18.7 %copy-start.28 = (f32[3072]{0:T(1024)}, f32[3072]{0:T(1024)S(1)}, u32[]{:S(2)}) copy-start(f32[3072]{0:T(1024)S(1)} %add_rsqrt_fusion) | copy-start | bytes 36868
  420.1 17.6 %copy-start.24 = (f32[3072]{0:T(1024)S(1)}, f32[3072]{0:T(1024)}, u32[]{:S(2)}) copy-start(f32[3072]{0:T(1024)} %copy-done.23) | copy-start | bytes 36868
  420.1 17.6 %copy-start.29 = (f32[3072]{0:T(1024)S(1)}, f32[3072]{0:T(1024)}, u32[]{:S(2)}) copy-start(f32[3072]{0:T(1024)} %copy-done.28) | copy-start | bytes 36868
  420.1 17.6 %copy-start.30 = (f32[2048]{0:T(1024)S(1)}, f32[2048]{0:T(1024)}, u32[]{:S(2)}) copy-start(f32[2048]{0:T(1024)} %mul.303) | copy-start | bytes 24580
  420.1 17.6 %copy-start.31 = (f32[2048]{0:T(1024)S(1)}, f32[2048]{0:T(1024)}, u32[]{:S(2)}) copy-start(f32[2048]{0:T(1024)} %add.286) | copy-start | bytes 24580
  484.3 29.6 %copy-start.33 = (f32[2048]{0:T(1024)S(1)}, f32[2048]{0:T(1024)}, u32[]{:S(2)}) copy-start(f32[2048]{0:T(1024)} %copy-done.32) | copy-start | bytes 24580
  535.7 348.9 %reduce-scatter.3.cloned.1.call-start = ((), (), s32[]{:S(2)}) async-start(), calls=%async_computation.6 | async-start | bytes 14155776 | tf_op jit(solution)/shard_map/reduce_scatter | solution.py:290
  540.5 20.3 %copy-start.9 = (bf16[2,2,64,2048]{3,2,1,0:T(8,128)(2,1)S(1)}, bf16[2,2,64,2048]{3,2,1,0:T(8,128)(2,1)}, u32[]{:S(2)}) copy-start(bf16[2,2,64,2048]{3,2,1,0:T(8,128)(2,1)} %copy-done.8) | copy-start | bytes 3145732
  601.7 23.6 %slice-start = ((s8[12582912]{0:T(1024)(128)(4,1)}), s8[4194304]{0:T(1024)(128)(4,1)S(1)}, s32[]{:S(2)}) async-start(s8[12582912]{0:T(1024)(128)(4,1)} %bitcast.140), calls=%async_computation.9 | async-start | bytes 8388608
  603.3 22.0 %slice-start.1 = ((s8[12582912]{0:T(1024)(128)(4,1)}), s8[4194304]{0:T(1024)(128)(4,1)S(1)}, s32[]{:S(2)}) async-start(s8[12582912]{0:T(1024)(128)(4,1)} %bitcast.140), calls=%async_computation.10 | async-start | bytes 8388608
  603.3 22.0 %slice-start.2 = ((s8[12582912]{0:T(1024)(128)(4,1)}), s8[4194304]{0:T(1024)(128)(4,1)S(1)}, s32[]{:S(2)}) async-start(s8[12582912]{0:T(1024)(128)(4,1)} %bitcast.140), calls=%async_computation.11 | async-start | bytes 8388608
  603.3 90.3 %collective-permute-start.12 = (bf16[2,1,528,1024]{3,2,1,0:T(8,128)(2,1)}, bf16[2,1,528,1024]{3,2,1,0:T(8,128)(2,1)}, u32[]{:S(2)}, u32[]{:S(2)}) collective-permute-start(bf16[2,1,528,1024]{3,2,1,0:T(8,128)(2,1)} %fusion.61), channel_id=1, source_target_pairs={{0,4},{1,5},{2,6},{3,7},{4,0},{5,1},{6,2},{7,3},{8,12},{9,13},{10,... | collective-permute-start | bytes 6488072 | tf_op jit(solution)/shard_map/ppermute | solution.py:84
  624.8 61.1 %collective-permute-start.10 = (bf16[2,1,528,768]{3,2,1,0:T(8,128)(2,1)S(1)}, bf16[2,1,528,768]{3,2,1,0:T(8,128)(2,1)}, u32[]{:S(2)}, u32[]{:S(2)}) collective-permute-start(bf16[2,1,528,768]{3,2,1,0:T(8,128)(2,1)S(1)} %fusion.65), channel_id=1, source_target_pairs={{0,4},{1,5},{2,6},{3,7},{4,0},{5,1},{6,2},{7,3},{8,12},{9,13},{10,... | collective-permute-start | bytes 4866056 | tf_op jit(solution)/shard_map/ppermute | solution.py:84
  645.0 110.3 %collective-permute-start.17 = (bf16[2,1,256,2048]{3,2,1,0:T(8,128)(2,1)}, bf16[2,1,256,2048]{3,2,1,0:T(8,128)(2,1)}, u32[]{:S(2)}, u32[]{:S(2)}) collective-permute-start(bf16[2,1,256,2048]{3,2,1,0:T(8,128)(2,1)} %constant_dynamic-slice_fusion), channel_id=1, source_target_pairs={{0,4},{1,5},{2,6},{3,7},{4,0},{5,1},{6,2},{7,3},{8,12},{9,13},{10,... | collective-permute-start | bytes 6291464 | tf_op jit(solution)/shard_map/ppermute | solution.py:84
  687.7 56.5 %collective-permute-start.11 = (bf16[1,1,528,768]{3,2,1,0:T(8,128)(2,1)S(1)}, bf16[1,1,528,768]{3,2,1,0:T(8,128)(2,1)S(1)}, u32[]{:S(2)}, u32[]{:S(2)}) collective-permute-start(bf16[1,1,528,768]{3,2,1,0:T(8,128)(2,1)S(1)} %dynamic-slice_convert_fusion.2), channel_id=1, source_target_pairs={{0,16},{1,17},{2,18},{3,19},{4,20},{5,21},{6,22},{7,23},{8,24},{9,... | collective-permute-start | bytes 2433032 | tf_op jit(solution)/shard_map/ppermute | solution.py:84
  692.2 60.9 %collective-permute-start.14 = (bf16[2,1,64,2048]{3,2,1,0:T(8,128)(2,1)}, bf16[2,1,64,2048]{3,2,1,0:T(8,128)(2,1)S(1)}, u32[]{:S(2)}, u32[]{:S(2)}) collective-permute-start(bf16[2,1,64,2048]{3,2,1,0:T(8,128)(2,1)} %constant_dynamic-slice_fusion.1), channel_id=1, source_target_pairs={{0,4},{1,5},{2,6},{3,7},{4,0},{5,1},{6,2},{7,3},{8,12},{9,13},{10,... | collective-permute-start | bytes 1572872 | tf_op jit(solution)/shard_map/ppermute | solution.py:84
  699.4 73.4 %collective-permute-start.13 = (bf16[1,1,528,1024]{3,2,1,0:T(8,128)(2,1)}, bf16[1,1,528,1024]{3,2,1,0:T(8,128)(2,1)}, u32[]{:S(2)}, u32[]{:S(2)}) collective-permute-start(bf16[1,1,528,1024]{3,2,1,0:T(8,128)(2,1)} %dynamic-slice_convert_fusion), channel_id=1, source_target_pairs={{0,16},{1,17},{2,18},{3,19},{4,20},{5,21},{6,22},{7,23},{8,24},{9,... | collective-permute-start | bytes 3244040 | tf_op jit(solution)/shard_map/ppermute | solution.py:84
  745.5 48.2 %all-to-all-start.1 = ((bf16[8,80,768]{2,1,0:T(8,128)(2,1)}), bf16[8,80,768]{2,1,0:T(8,128)(2,1)S(1)}, u32[]{:S(2)}, u32[]{:S(2)}) async-start(bf16[8,80,768]{2,1,0:T(8,128)(2,1)} %pad_maximum_fusion.4), calls=%async_computation.3 | async-start | bytes 1966080 | tf_op jit(solution)/shard_map/all_to_all | solution.py:363
  755.2 17.5 %slice-start.3 = ((s8[4325376]{0:T(1024)(128)(4,1)}), s8[4194304]{0:T(1024)(128)(4,1)S(1)}, s32[]{:S(2)}) async-start(s8[4325376]{0:T(1024)(128)(4,1)} %bitcast.148), calls=%async_computation.12 | async-start | bytes 8388608
  755.3 17.5 %slice-start.4 = ((s8[4325376]{0:T(1024)(128)(4,1)}), s8[131072]{0:T(1024)(128)(4,1)S(1)}, s32[]{:S(2)}) async-start(s8[4325376]{0:T(1024)(128)(4,1)} %bitcast.148), calls=%async_computation.13 | async-start | bytes 262144
  755.3 46.5 %collective-permute-start.15 = (bf16[1,1,64,2048]{3,2,1,0:T(8,128)(2,1)S(1)}, bf16[1,1,64,2048]{3,2,1,0:T(8,128)(2,1)}, u32[]{:S(2)}, u32[]{:S(2)}) collective-permute-start(bf16[1,1,64,2048]{3,2,1,0:T(8,128)(2,1)S(1)} %dynamic-slice_convert_fusion.3), channel_id=1, source_target_pairs={{0,16},{1,17},{2,18},{3,19},{4,20},{5,21},{6,22},{7,23},{8,24},{9,... | collective-permute-start | bytes 786440 | tf_op jit(solution)/shard_map/ppermute | solution.py:84
  775.7 30.0 %copy-start.46 = (s32[32]{0:T(128)S(1)}, s32[32]{0:T(128)}, u32[]{:S(2)}) copy-start(s32[32]{0:T(128)} %constant.281) | copy-start | bytes 388
  775.7 30.0 %copy-start.39 = (bf16[64]{0:T(256)(128)(2,1)S(1)}, bf16[64]{0:T(256)(128)(2,1)}, u32[]{:S(2)}) copy-start(bf16[64]{0:T(256)(128)(2,1)} %param.21) | copy-start | bytes 388
  775.7 30.0 %copy-start.41 = (bf16[64]{0:T(256)(128)(2,1)S(1)}, bf16[64]{0:T(256)(128)(2,1)}, u32[]{:S(2)}) copy-start(bf16[64]{0:T(256)(128)(2,1)} %param.22) | copy-start | bytes 388
  775.7 30.0 %copy-start.43 = (bf16[64]{0:T(256)(128)(2,1)S(1)}, bf16[64]{0:T(256)(128)(2,1)}, u32[]{:S(2)}) copy-start(bf16[64]{0:T(256)(128)(2,1)} %param.19) | copy-start | bytes 388
  775.7 30.0 %copy-start.45 = (bf16[64]{0:T(256)(128)(2,1)S(1)}, bf16[64]{0:T(256)(128)(2,1)}, u32[]{:S(2)}) copy-start(bf16[64]{0:T(256)(128)(2,1)} %param.20) | copy-start | bytes 388
  775.7 30.1 %copy-start.22 = (f32[32,64]{1,0:T(8,128)S(1)}, f32[32,64]{1,0:T(8,128)}, u32[]{:S(2)}) copy-start(f32[32,64]{1,0:T(8,128)} %get-tuple-element.43) | copy-start | bytes 24580
  775.7 30.1 %copy-start.21 = (f32[32,64]{1,0:T(8,128)S(1)}, f32[32,64]{1,0:T(8,128)}, u32[]{:S(2)}) copy-start(f32[32,64]{1,0:T(8,128)} %get-tuple-element.44) | copy-start | bytes 24580
  794.7 72.6 %all-to-all-start.2 = ((bf16[8,80,1024]{2,1,0:T(8,128)(2,1)}), bf16[8,80,1024]{2,1,0:T(8,128)(2,1)S(1)}, u32[]{:S(2)}, u32[]{:S(2)}) async-start(bf16[8,80,1024]{2,1,0:T(8,128)(2,1)} %pad_maximum_fusion.3), calls=%async_computation.4 | async-start | bytes 2621440 | tf_op jit(solution)/shard_map/all_to_all | solution.py:363
  801.2 48.3 %collective-permute-start.18 = (bf16[1,1,256,2048]{3,2,1,0:T(8,128)(2,1)}, bf16[1,1,256,2048]{3,2,1,0:T(8,128)(2,1)}, u32[]{:S(2)}, u32[]{:S(2)}) collective-permute-start(bf16[1,1,256,2048]{3,2,1,0:T(8,128)(2,1)} %dynamic-slice_convert_fusion.1), channel_id=1, source_target_pairs={{0,16},{1,17},{2,18},{3,19},{4,20},{5,21},{6,22},{7,23},{8,24},{9,... | collective-permute-start | bytes 3145736 | tf_op jit(solution)/shard_map/ppermute | solution.py:84
  802.9 8.1 collective-permute-start.16
  805.9 47.2 %copy-start.3 = (bf16[8,80,768]{2,1,0:T(8,128)(2,1)S(1)}, bf16[8,80,768]{2,1,0:T(8,128)(2,1)}, u32[]{:S(2)}) copy-start(bf16[8,80,768]{2,1,0:T(8,128)(2,1)} %copy-done.2) | copy-start | bytes 2949124
  (33 other events, 228.8 us)
Sparse Core Ops, SparseCore 0:
  9.7 114.4 all-gather.3
  125.8 91.1 all-gather.5
  535.8 126.8 reduce-scatter.4
  664.9 131.5 reduce-scatter.2

commit v2 on v1

v2 whole, which is shorter than its diff:
```python
import math

import jax
import jax.numpy as jnp
from jax import lax
from jax.experimental import pallas as pl
from jax.experimental.pallas import tpu as pltpu
from jax.sharding import PartitionSpec as P


HEADS = 8

EPSILON = 1e-05
MASKED = -1e30
PAIRED = (((1,), (1,)), ((), ()))
LEADING = (((0,), (0,)), ((), ()))
VMEM_LIMIT = 60 * 2**20


class Plan:
    def __init__(self, count):
        self.count = count
        self.bits = count.bit_length() - 1
        self.inner = (3, 1, 0) if count == 32 else (2, 1, 0)
        self.outer = (2, 4) if count == 32 else tuple(range(self.bits - 1, 2, -1))
        self.order = tuple(reversed(range(self.bits)))
        self.groups = count // HEADS

    def device(self, group, slot):
        found = 0
        for place, bit in enumerate(reversed(self.outer)):
            found |= ((group >> place) & 1) << bit
        for place, bit in enumerate(reversed(self.inner)):
            found |= ((slot >> place) & 1) << bit
        return found

    def inner_groups(self):
        return [
            [self.device(group, slot) for slot in range(HEADS)] for group in range(self.groups)
        ]

    def flip(self, bit):
        return [(d, d ^ (1 << bit)) for d in range(self.count)]


def bit_of(index, bit):
    return (index >> bit) & 1


def swap(value, bit, plan):
    return lax.ppermute(value, "dp", plan.flip(bit))


def gather_outer(value, plan):
    pieces = [(0, value)]
    for bit in reversed(plan.outer):
        pieces += [(mask | (1 << bit), swap(piece, bit, plan)) for mask, piece in pieces]
    return pieces


def gather_small(value, bits, me, plan):
    for bit in reversed(bits):
        got = swap(value, bit, plan)
        low = bit_of(me, bit) == 0
        value = jnp.where(
            low, jnp.concatenate([value, got]), jnp.concatenate([got, value])
        )
    return value


def place_outer(pieces, me, plan):
    shape = pieces[0][1].shape
    held = jnp.zeros((2,) * len(plan.outer) + shape, pieces[0][1].dtype)
    for mask, piece in pieces:
        start = [bit_of(me ^ mask, bit) for bit in plan.outer] + [0] * len(shape)
        held = lax.dynamic_update_slice(held, piece.reshape((1,) * len(plan.outer) + shape), start)
    return held.reshape((plan.groups,) + shape)


def place_all(pieces, me, plan):
    rest = pieces[0][1].shape[1:]
    held = jnp.zeros((2,) * plan.bits + rest, pieces[0][1].dtype)
    for mask, piece in pieces:
        start = [bit_of(me ^ mask, b) if b in plan.outer else 0 for b in plan.order]
        block = piece.reshape(tuple(1 if b in plan.outer else 2 for b in plan.order) + rest)
        held = lax.dynamic_update_slice(held, block, start + [0] * len(rest))
    return held.reshape((plan.count,) + rest)


def reduce_rest(kept, got, me, plan):
    rest = kept.shape[1:]
    shape = (2,) * (len(plan.outer) - 1) + rest
    held = kept.reshape(shape).astype(jnp.float32) + got.reshape(shape).astype(jnp.float32)
    for bit in plan.outer[1:]:
        mine = bit_of(me, bit)
        sent = lax.dynamic_index_in_dim(held, 1 - mine, 0, keepdims=False).astype(jnp.bfloat16)
        held = lax.dynamic_index_in_dim(held, mine, 0, keepdims=False)
        held = held + swap(sent, bit, plan).astype(jnp.float32)
    return held


def slot_layout(lengths, slots):
    place = jnp.arange(slots, dtype=jnp.int32)
    ends = jnp.cumsum(lengths, dtype=jnp.int32)
    after = (place[:, None] >= ends[None, :]).astype(jnp.int32)
    segment = jnp.sum(after, axis=1, dtype=jnp.int32)
    offset = jnp.sum(after * lengths[None, :], axis=1, dtype=jnp.int32)
    return (segment, place - offset)


def rotary_tables(position, rotated, lanes):
    half = rotated // 2
    ladder = jnp.arange(half, dtype=jnp.float32) * (-math.log(10000.0) / half)
    angle = position.astype(jnp.float32)[:, None] * jnp.exp(ladder)[None, :]
    cosine, sine = jnp.cos(angle), jnp.sin(angle)
    rest = (position.shape[0], lanes - rotated)
    return (
        jnp.concatenate([cosine, cosine, jnp.ones(rest, jnp.float32)], axis=1),
        jnp.concatenate([-sine, sine, jnp.zeros(rest, jnp.float32)], axis=1),
    )


def norm_terms(value):
    centre = jnp.mean(value, axis=1, keepdims=True)
    spread = value - centre
    variance = jnp.mean(spread * spread, axis=1, keepdims=True)
    scale = lax.rsqrt(variance + EPSILON)
    return (spread * scale, scale)


def times(left, right):
    return jnp.dot(left, right, preferred_element_type=jnp.float32)


def times_leading(left, right):
    return lax.dot_general(left, right, LEADING, preferred_element_type=jnp.float32)


def times_paired(left, right):
    return lax.dot_general(left, right, PAIRED, preferred_element_type=jnp.float32)


def over_blocks(kernel, slots, blocked, whole, outs, flops):
    count = blocked[0].shape[0] // slots
    held = sum(item.size * item.dtype.itemsize for item in blocked + whole)
    made = sum(count * slots * columns * jnp.dtype(kind).itemsize for columns, kind in outs)
    return pl.pallas_call(
        kernel,
        grid=(count,),
        in_specs=[pl.BlockSpec((slots, item.shape[1]), lambda i: (i, 0)) for item in blocked]
        + [pl.BlockSpec(item.shape, lambda i: (0, 0)) for item in whole],
        out_specs=[pl.BlockSpec((slots, columns), lambda i: (i, 0)) for columns, _ in outs],
        out_shape=[jax.ShapeDtypeStruct((count * slots, columns), kind) for columns, kind in outs],
        compiler_params=pltpu.CompilerParams(vmem_limit_bytes=VMEM_LIMIT),
        cost_estimate=pl.CostEstimate(flops=flops, bytes_accessed=held + made, transcendentals=0),
    )(*blocked, *whole)


def turn(value, cosine, sine, half):
    lane = lax.broadcasted_iota(jnp.int32, value.shape, 1)
    lanes = value.shape[1]
    swapped = jnp.where(
        lane < half, pltpu.roll(value, lanes - half, 1), pltpu.roll(value, half, 1)
    )
    return value * cosine + swapped * sine


def turn_into(out, at, value, cosine, sine, half):
    lanes = cosine.shape[1]
    turned = turn(value[:, :lanes], cosine, sine, half)
    out[:, at : at + lanes] = turned.astype(jnp.bfloat16)
    out[:, at + lanes : at + value.shape[1]] = value[:, lanes:].astype(jnp.bfloat16)


def qkv_kernel(head_dim, x, cosine, sine, weight, bias, out):
    projected = times(x[...], weight[...]) + bias[...]
    half = head_dim // 8
    for part in range(2):
        at = part * head_dim
        turn_into(out, at, projected[:, at : at + head_dim], cosine[...], sine[...], half)
    out[:, 2 * head_dim :] = projected[:, 2 * head_dim :].astype(jnp.bfloat16)


def expand_kernel(x, weight, bias, active, slope):
    hidden = times(x[...], weight[...]) + bias[...]
    below = 0.5 * (1.0 + lax.erf(hidden * math.sqrt(0.5)))
    density = jnp.exp(-0.5 * hidden * hidden) * (1.0 / math.sqrt(2.0 * math.pi))
    active[...] = (hidden * below).astype(jnp.bfloat16)
    slope[...] = below + hidden * density


def grad_hidden_kernel(cotangent, slope, weight, out):
    out[...] = (times_paired(cotangent[...], weight[...]) * slope[...]).astype(jnp.bfloat16)


def branch_kernel(attn, active, dense, contract, out):
    total = times(attn[...], dense[...]) + times(active[...], contract[...])
    out[...] = total.astype(jnp.bfloat16)


def grad_norm_kernel(grad_qkv, grad_hidden, qkv, expand, gain_one, gain_two, out):
    total = (
        times_paired(grad_qkv[...], qkv[...]) * gain_one[...]
        + times_paired(grad_hidden[...], expand[...]) * gain_two[...]
    )
    out[...] = total.astype(jnp.bfloat16)


def attend_kernel(
    head_dim, qkv, cotangent, cosine, sine, segment, dense, segments, attn, grad_qkv
):
    scale = 1.0 / math.sqrt(head_dim)
    query = qkv[:, :head_dim]
    key = qkv[:, head_dim : 2 * head_dim]
    value = qkv[:, 2 * head_dim :]
    grad_attn = times_paired(cotangent[...], dense[...]).astype(jnp.bfloat16)
    slots = query.shape[0]
    row = lax.broadcasted_iota(jnp.int32, (slots, slots), 0)
    column = lax.broadcasted_iota(jnp.int32, (slots, slots), 1)
    block = pl.program_id(0)
    allowed = (segment[...] == segments[pl.ds(block, 1), :]) & (column <= row)
    masked = jnp.where(allowed, times_paired(query, key) * scale, MASKED)
    raised = jnp.exp(masked - jnp.max(masked, axis=1, keepdims=True))
    weights = raised / jnp.sum(raised, axis=1, keepdims=True)
    probs = weights.astype(jnp.bfloat16)
    attn[...] = times(probs, value).astype(jnp.bfloat16)
    grad_probs = times_paired(grad_attn, value)
    grad_value = times_leading(probs, grad_attn)
    inner = jnp.sum(weights * grad_probs, axis=1, keepdims=True)
    grad_score = (weights * (grad_probs - inner)).astype(jnp.bfloat16)
    half = head_dim // 8
    back = -sine[...]
    grad_query = times(grad_score, key) * scale
    turn_into(grad_qkv, 0, grad_query, cosine[...], back, half)
    grad_key = times_leading(grad_score, query) * scale
    turn_into(grad_qkv, head_dim, grad_key, cosine[...], back, half)
    grad_qkv[:, 2 * head_dim :] = grad_value.astype(jnp.bfloat16)


def input_terms_kernel(_, left, right, out):
    out[...] = times_leading(left[...], right[...]).astype(jnp.bfloat16)


def input_terms(normed, grad, blocks, block):
    depth, width = normed.shape
    columns = grad.shape[1]
    count = blocks.shape[0]
    rows = count * block
    return pl.pallas_call(
        input_terms_kernel,
        grid_spec=pltpu.PrefetchScalarGridSpec(
            num_scalar_prefetch=1,
            grid=(count,),
            in_specs=[
                pl.BlockSpec((depth, block), lambda i, blocks: (0, blocks[i])),
                pl.BlockSpec(
                    (depth, columns), lambda i, blocks: (0, 0), pipeline_mode=pl.Buffered(1)
                ),
            ],
            out_specs=pl.BlockSpec((block, columns), lambda i, blocks: (i, 0)),
        ),
        out_shape=jax.ShapeDtypeStruct((rows, columns), jnp.bfloat16),
        compiler_params=pltpu.CompilerParams(vmem_limit_bytes=VMEM_LIMIT),
        cost_estimate=pl.CostEstimate(
            flops=2 * depth * rows * columns,
            bytes_accessed=2 * (depth * (rows + columns) + rows * columns),
            transcendentals=0,
        ),
    )(blocks, normed, grad)


def unpack_kernel(places, got, sums, weight, gain, shift, grad, gain_grad, shift_grad):
    by_gain = jnp.zeros(gain.shape, jnp.float32)
    by_shift = jnp.zeros(gain.shape, jnp.float32)
    for slot, start, at, many in places:
        terms = got[slot, :, start : start + many].astype(jnp.float32)
        total = sums[slot : slot + 1, start : start + many]
        parts = weight[:, at : at + many].astype(jnp.float32)
        grad[:, at : at + many] = terms * gain[...] + total * shift[...]
        by_gain += jnp.sum(parts * terms, axis=1, keepdims=True)
        by_shift += jnp.sum(parts * total, axis=1, keepdims=True)
    gain_grad[...] = by_gain
    shift_grad[...] = by_shift


def unpack(places, got, sums, weight, gain, shift):
    rows, columns = weight.shape
    gain = gain.astype(jnp.float32).reshape(rows, 1)
    shift = shift.astype(jnp.float32).reshape(rows, 1)
    grad, gain_grad, shift_grad = pl.pallas_call(
        lambda *refs: unpack_kernel(places, *refs),
        out_shape=[
            jax.ShapeDtypeStruct((rows, columns), jnp.float32),
            jax.ShapeDtypeStruct((rows, 1), jnp.float32),
            jax.ShapeDtypeStruct((rows, 1), jnp.float32),
        ],
        compiler_params=pltpu.CompilerParams(vmem_limit_bytes=VMEM_LIMIT),
    )(got, sums, weight, gain, shift)
    return grad, gain_grad.reshape(rows), shift_grad.reshape(rows)


def per_device(
    plan,
    tokens,
    seq_lengths,
    ln1_gain,
    ln1_bias,
    ln2_gain,
    ln2_bias,
    qkv_weight,
    qkv_bias,
    dense_weight,
    dense_bias,
    expand_weight,
    expand_bias,
    contract_weight,
    contract_bias,
    cotangent,
):
    slots, width = tokens.shape
    rows = qkv_weight.shape[0]
    units = contract_weight.shape[0]
    count, groups = plan.count, plan.groups
    head_dim = width // HEADS
    rotated = head_dim // 4
    hidden_units = groups * units
    shared = HEADS * slots
    me = lax.axis_index("dp")
    inner_groups = plan.inner_groups()
    slot = sum(bit_of(me, bit) << place for place, bit in enumerate(reversed(plan.inner)))

    group_tokens = lax.all_gather(tokens, "dp", axis=0, tiled=True, axis_index_groups=inner_groups)
    group_cotangent = lax.all_gather(
        cotangent, "dp", axis=0, tiled=True, axis_index_groups=inner_groups
    )

    parts = [
        ln1_gain,
        ln1_bias,
        ln2_gain,
        ln2_bias,
        dense_bias,
        contract_bias,
        qkv_bias,
        expand_bias,
        seq_lengths[0].astype(jnp.bfloat16),
    ]
    sizes = [item.shape[0] for item in parts]
    total = sum(sizes)
    lines = -(-total // 1024) * 8
    small = jnp.concatenate(parts + [jnp.zeros((lines * 128 - total,), jnp.bfloat16)])
    every = gather_small(small.reshape(1, lines, 128), plan.order, me, plan)
    every = every.reshape(count, lines * 128).astype(jnp.float32)
    taken, at = [], 0
    for size in sizes:
        taken.append(every[:, at : at + size])
        at += size
    gain_one, shift_one, gain_two, shift_two, bias_dense, bias_contract = [
        item.reshape(1, width) for item in taken[:6]
    ]
    bias_qkv = lax.dynamic_index_in_dim(
        taken[6].reshape(3, HEADS, head_dim), slot, 1, keepdims=False
    ).reshape(1, 3 * head_dim)

    def fixed(value, bits):
        rest = value.shape[1:]
        value = value.reshape((2,) * plan.bits + rest)
        for place, bit in enumerate(plan.order):
            if bit in bits:
                value = lax.dynamic_slice_in_dim(value, bit_of(me, bit), 1, place)
        return value

    bias_expand = fixed(taken[7], plan.inner)
    kept = [bit for bit in plan.order if bit in plan.outer]
    bias_expand = bias_expand.reshape((2,) * len(kept) + (units,))
    bias_expand = bias_expand.transpose([kept.index(b) for b in plan.outer] + [len(kept)])
    bias_expand = bias_expand.reshape(1, hidden_units)
    lengths = fixed(taken[8], plan.outer).reshape(HEADS, -1).astype(jnp.int32)

    expand_places = [
        (s, group * units, plan.device(group, s) * units, units)
        for s in range(HEADS)
        for group in range(groups)
    ]
    qkv_places = [
        (s, part * head_dim, part * width + s * head_dim, head_dim)
        for s in range(HEADS)
        for part in range(3)
    ]

    def to_slots(weight, places):
        own = [
            jnp.concatenate(
                [weight[:, at : at + many] for s, _, at, many in places if s == which], axis=1
            )
            for which in range(HEADS)
        ]
        sent = jnp.stack(own)
        got = lax.all_to_all(sent, "dp", 0, 0, tiled=True, axis_index_groups=inner_groups)
        return place_all(gather_outer(got, plan), me, plan).reshape(width, -1)

    weight_expand = to_slots(expand_weight, expand_places)
    weight_qkv = to_slots(qkv_weight, qkv_places)

    to_slot = [(d, plan.device(d % groups, d // groups)) for d in range(count)]
    from_slot = [(target, source) for source, target in to_slot]
    weight_contract = place_outer(gather_outer(contract_weight, plan), me, plan)
    weight_contract = weight_contract.reshape(hidden_units, width)
    dense_part = lax.ppermute(dense_weight, "dp", to_slot)
    weight_dense = place_outer(gather_outer(dense_part, plan), me, plan)
    weight_dense = weight_dense.reshape(head_dim, width)

    segment, position = jax.vmap(lambda item: slot_layout(item, slots))(lengths)
    cosine, sine = rotary_tables(position.reshape(-1), rotated, head_dim // 2)
    normed, _ = norm_terms(group_tokens.astype(jnp.float32))
    low_one = (normed * gain_one + shift_one).astype(jnp.bfloat16)
    low_two = (normed * gain_two + shift_two).astype(jnp.bfloat16)
    low_normed = normed.astype(jnp.bfloat16)
    active, slope = over_blocks(
        expand_kernel,
        slots,
        [low_two],
        [weight_expand, bias_expand],
        [(hidden_units, jnp.bfloat16), (hidden_units, jnp.float32)],
        2 * shared * width * hidden_units,
    )
    (qkv,) = over_blocks(
        lambda *refs: qkv_kernel(head_dim, *refs),
        slots,
        [low_one, cosine, sine],
        [weight_qkv, bias_qkv],
        [(3 * head_dim, jnp.bfloat16)],
        2 * shared * width * 3 * head_dim,
    )

    first = bit_of(me, plan.outer[0])

    def reduce_output(left, width_of):
        def half_of(which):
            columns = left.shape[1] // 2
            taken = lax.dynamic_slice_in_dim(left, which * columns, columns, 1)
            terms = times_leading(taken, group_cotangent).astype(jnp.bfloat16)
            return terms.reshape(groups // 2, width_of, width)

        sent = swap(half_of(1 - first), plan.outer[0], plan)
        return reduce_rest(half_of(first), sent, me, plan)

    contract_weight_grad = reduce_output(active, units)

    (grad_hidden,) = over_blocks(
        grad_hidden_kernel,
        slots,
        [group_cotangent, slope],
        [weight_contract],
        [(hidden_units, jnp.bfloat16)],
        2 * shared * width * hidden_units,
    )

    block = 256
    numbers = jnp.arange(width // block // 2, dtype=jnp.int32)
    reach = (rows << plan.outer[0]) // block

    def reduce_input(grad):
        def half_of(which):
            blocks = (numbers // reach) * (2 * reach) + which * reach + numbers % reach
            terms = input_terms(low_normed, grad, blocks, block)
            return terms.reshape(groups // 2, HEADS * rows, grad.shape[1])

        sent = swap(half_of(1 - first), plan.outer[0], plan)
        reduced = reduce_rest(half_of(first), sent, me, plan)
        reduced = reduced.reshape(HEADS, rows, -1).astype(jnp.bfloat16)
        return lax.all_to_all(reduced, "dp", 0, 0, tiled=True, axis_index_groups=inner_groups)

    expand_got = reduce_input(grad_hidden)

    attn, grad_qkv = over_blocks(
        lambda *refs: attend_kernel(head_dim, *refs),
        slots,
        [qkv, group_cotangent, cosine, sine, segment.reshape(-1, 1)],
        [weight_dense, segment],
        [(head_dim, jnp.bfloat16), (3 * head_dim, jnp.bfloat16)],
        2 * shared * head_dim * (width + 7 * slots),
    )
    qkv_got = reduce_input(grad_qkv)
    dense_weight_grad = reduce_output(attn, rows)
    dense_weight_grad = lax.ppermute(
        dense_weight_grad.astype(jnp.bfloat16), "dp", from_slot
    ).astype(jnp.float32)

    sums = jnp.concatenate(
        [
            jnp.sum(grad_qkv.astype(jnp.float32), axis=0),
            jnp.sum(grad_hidden.astype(jnp.float32), axis=0),
            jnp.sum(group_cotangent.astype(jnp.float32), axis=0),
        ]
    ).reshape(-1, 128)
    for bit in plan.outer:
        sums = sums + swap(sums, bit, plan)
    own_sums = 3 * head_dim + hidden_units
    bias_out_grad = lax.dynamic_slice_in_dim(
        sums.reshape(-1), own_sums + me * (width // count), width // count
    )
    all_sums = gather_small(sums[None, : own_sums // 128], plan.inner, me, plan)
    all_sums = all_sums.reshape(HEADS, own_sums)
    qkv_sums, expand_sums = all_sums[:, : 3 * head_dim], all_sums[:, 3 * head_dim :]

    (branch,) = over_blocks(
        branch_kernel,
        slots,
        [attn, active],
        [weight_dense, weight_contract],
        [(width, jnp.bfloat16)],
        2 * shared * width * (head_dim + hidden_units),
    )
    branch = lax.psum_scatter(
        branch, "dp", scatter_dimension=0, tiled=True, axis_index_groups=inner_groups
    )
    inputs = tokens.astype(jnp.float32)
    layer_out = (inputs + branch.astype(jnp.float32) + bias_dense + bias_contract).astype(
        jnp.bfloat16
    )

    (grad_both,) = over_blocks(
        grad_norm_kernel,
        slots,
        [grad_qkv, grad_hidden],
        [weight_qkv, weight_expand, gain_one, gain_two],
        [(width, jnp.bfloat16)],
        2 * shared * width * (3 * head_dim + hidden_units),
    )
    grad_both = lax.psum_scatter(
        grad_both, "dp", scatter_dimension=0, tiled=True, axis_index_groups=inner_groups
    ).astype(jnp.float32)
    own_normed, own_scale = norm_terms(inputs)
    input_grad = (
        cotangent.astype(jnp.float32)
        + (
            grad_both
            - jnp.mean(grad_both, axis=1, keepdims=True)
            - own_normed * jnp.mean(grad_both * own_normed, axis=1, keepdims=True)
        )
        * own_scale
    )

    qkv_weight_grad, ln1_gain_grad, ln1_bias_grad = unpack(
        qkv_places, qkv_got, qkv_sums, qkv_weight, ln1_gain, ln1_bias
    )
    expand_weight_grad, ln2_gain_grad, ln2_bias_grad = unpack(
        expand_places, expand_got, expand_sums, expand_weight, ln2_gain, ln2_bias
    )
    qkv_bias_grad = qkv_sums.reshape(HEADS, 3, head_dim).transpose(1, 0, 2).reshape(3 * width)
    per = qkv_bias.shape[0]
    qkv_bias_grad = lax.dynamic_slice_in_dim(qkv_bias_grad, me * per, per)
    group = sum(bit_of(me, bit) << place for place, bit in enumerate(reversed(plan.outer)))
    expand_bias_grad = lax.dynamic_slice(expand_sums, (slot, group * units), (1, units))
    return (
        layer_out,
        input_grad,
        ln1_gain_grad,
        ln1_bias_grad,
        ln2_gain_grad,
        ln2_bias_grad,
        qkv_weight_grad,
        qkv_bias_grad,
        dense_weight_grad,
        bias_out_grad,
        expand_weight_grad,
        expand_bias_grad.reshape(units),
        contract_weight_grad,
        bias_out_grad,
    )


def solution(mesh):
    in_specs = (
        P("dp", None),
        P("dp", None),
        P("dp"),
        P("dp"),
        P("dp"),
        P("dp"),
        P("dp", None),
        P("dp"),
        P("dp", None),
        P("dp"),
        P("dp", None),
        P("dp"),
        P("dp", None),
        P("dp"),
        P("dp", None),
    )
    out_specs = (
        P("dp", None),
        P("dp", None),
        P("dp"),
        P("dp"),
        P("dp"),
        P("dp"),
        P("dp", None),
        P("dp"),
        P("dp", None),
        P("dp"),
        P("dp", None),
        P("dp"),
        P("dp", None),
        P("dp"),
    )
    plan = Plan(mesh.shape["dp"])

    def layer(*arrays):
        return per_device(plan, *arrays)

    return jax.shard_map(layer, mesh=mesh, in_specs=in_specs, out_specs=out_specs, check_vma=False)
```

time: 949 us -> 691 us (0.73)
  matrix products: 258 us -> 38.2 us
  Pallas kernels: 0 us -> 181 us
  blocking collectives: 165 us -> 0 us
  local copies, waits for them, and re-layouts: 130 us -> 43.4 us
  other arithmetic: 67.5 us -> 99.4 us
  waiting for transfers between devices: 270 us -> 239 us
  starting transfers between devices: 36.9 us -> 61 us
    dot_general x13 -> x0, matrix products: 193 us -> none  [the longest x4 78.6 us: times_paired(): lax.dot_general(left, right, PAIRED, preferred_element_type=jnp.float32)]
    pallas_call x0 -> x12, Pallas kernels: none -> 181 us  [the longest x6 129 us: over_blocks(): pl.pallas_call(kernel, grid=(count,), in_specs=[pl.BlockSpec((slots, item...]
    all_gather x1 -> x0, blocking collectives: 120 us -> none  [per_device(): every = lax.all_gather(small, 'dp', axis=0, tiled=False).astype(jnp.float32)]
    unnamed x1 -> x0, blocking collectives: 44.4 us -> none
    ppermute x17 -> x30, waiting for transfers between devices: 245 us -> 203 us  [swap(): return lax.ppermute(value, 'dp', plan.flip(bit))]
    concatenate x9 -> x3, local copies, waits for them, and re-layouts: 22.1 us -> 0.25 us  [the longest x1 0.09 us: per_device(): jnp.concatenate(parts + [jnp.zeros((lines * 128 - total,), jnp.bfloat16)])]
    convert_element_type x8 -> x5, other arithmetic: 1.28 us -> 22.8 us  [the longest x1 19.2 us: per_device(): low_normed = normed.astype(jnp.bfloat16)]
    dot_general x4, matrix products: 58.4 us -> 38.2 us  [times_leading(): lax.dot_general(left, right, LEADING, preferred_element_type=jnp.float32)]
  transfers between devices with their start and end apart: 26 -> 40, of which waited for: 10 -> 15; matrix products, arithmetic and copies ran while one was open for 27% -> 26% of each run, Pallas kernels for 0% -> 17%
where the time goes in v2:
time: 691 us; the launch traced here: 678 us
  waiting for transfers between devices  239 us (35%)
  Pallas kernels  181 us (26%)
  other arithmetic  99.4 us (14%)
  starting transfers between devices  61 us (9%)
  local copies, waits for them, and re-layouts  43.4 us (6%)
  matrix products  38.2 us (6%)
  between operations  15 us (2%)
    ppermute x30, waiting for transfers between devices, swap(): return lax.ppermute(value, 'dp', plan.flip(bit))  203 us
    pallas_call x6, Pallas kernels, over_blocks(): pl.pallas_call(kernel, grid=(count,), in_specs=[pl.BlockSpec((slots, item...  129 us
    pallas_call x4, Pallas kernels, input_terms(): pl.pallas_call(input_terms_kernel, grid_spec=pltpu.PrefetchScalarGridSpec...  44.9 us
    dot_general x4, matrix products, times_leading(): lax.dot_general(left, right, LEADING, preferred_element_type=jnp.float32)  38.2 us
    ppermute x30, starting transfers between devices, swap(): return lax.ppermute(value, 'dp', plan.flip(bit))  34.1 us
    all_to_all x2, waiting for transfers between devices, to_slots(): lax.all_to_all(sent, 'dp', 0, 0, tiled=True, axis_index_groups=inner_groups)  20.4 us
    convert_element_type x1, other arithmetic, per_device(): low_normed = normed.astype(jnp.bfloat16)  19.2 us
  transfers between devices with their start and end apart: 40, of which 15 were waited for; matrix products, arithmetic and copies ran while one was open for 26% of the time, Pallas kernels for 17%

profile of v2, /device:TPU:1, one launch (start us, length us, event | category | flops | bytes accessed | tf_op | source)
XLA Modules:
  0.0 677.6 jit_solution(12274114742250638330)
XLA Ops:
  8.8 3.2 collective-permute-start.15
  19.9 3.9 all-to-all-start
  31.2 2.6 broadcast_in_dim.42
  44.0 28.7 %collective-permute-done.3 = bf16[8,8,128]{2,1,0:T(8,128)(2,1)S(1)} collective-permute-done((bf16[8,8,128]{2,1,0:T(8,128)(2,1)S(1)}, bf16[8,8,128]{2,1,0:T(8,128)(2,1)S(1)}, u32[]{:S(2)}, u32[]{:S(2)}) %collective-permute-start.3) | collective-permute-done | bytes 16416 | tf_op jit(solution)/shard_map/ppermute | solution.py:51
  72.7 3.7 collective-permute-done.4
  77.0 5.8 fusion.39
  82.8 2.5 maximum_maximum_fusion
  91.8 8.9 %all-to-all-start.1 = ((bf16[8,64,1024]{2,1,0:T(8,128)(2,1)}), bf16[8,64,1024]{2,1,0:T(8,128)(2,1)S(1)}, u32[]{:S(2)}, u32[]{:S(2)}) async-start(bf16[8,64,1024]{2,1,0:T(8,128)(2,1)} %fusion.48), calls=%async_computation.1 | async-start | bytes 2097152 | tf_op jit(solution)/shard_map/all_to_all | solution.py:399
  102.7 4.1 collective-permute-done.11
  107.5 3.0 collective-permute-start.5
  110.5 20.4 %all-to-all-done.1 = bf16[8,64,1024]{2,1,0:T(8,128)(2,1)S(1)} async-done(((bf16[8,64,1024]{2,1,0:T(8,128)(2,1)}), bf16[8,64,1024]{2,1,0:T(8,128)(2,1)S(1)}, u32[]{:S(2)}, u32[]{:S(2)}) %all-to-all-start.1) | async-done | bytes 1048608 | tf_op jit(solution)/shard_map/all_to_all | solution.py:399
  140.0 2.6 broadcast_in_dim.41
  143.7 10.8 %collective-permute-done.5 = bf16[8,64,768]{2,1,0:T(8,128)(2,1)} collective-permute-done((bf16[8,64,768]{2,1,0:T(8,128)(2,1)S(1)}, bf16[8,64,768]{2,1,0:T(8,128)(2,1)}, u32[]{:S(2)}, u32[]{:S(2)}) %collective-permute-start.5) | collective-permute-done | bytes 786464 | tf_op jit(solution)/shard_map/ppermute | solution.py:51
  156.6 27.5 %collective-permute-done.12 = bf16[8,64,1024]{2,1,0:T(8,128)(2,1)S(1)} collective-permute-done((bf16[8,64,1024]{2,1,0:T(8,128)(2,1)S(1)}, bf16[8,64,1024]{2,1,0:T(8,128)(2,1)S(1)}, u32[]{:S(2)}, u32[]{:S(2)}) %collective-permute-start.12) | collective-permute-done | bytes 1048608 | tf_op jit(solution)/shard_map/ppermute | solution.py:51
  194.6 21.5 %collective-permute-done.14 = bf16[8,64,1024]{2,1,0:T(8,128)(2,1)S(1)} collective-permute-done((bf16[8,64,1024]{2,1,0:T(8,128)(2,1)S(1)}, bf16[8,64,1024]{2,1,0:T(8,128)(2,1)S(1)}, u32[]{:S(2)}, u32[]{:S(2)}) %collective-permute-start.14) | collective-permute-done | bytes 1048608 | tf_op jit(solution)/shard_map/ppermute | solution.py:51
  217.2 6.4 convert_reduce_fusion
  223.6 8.0 %fusion.9 = f32[3072]{0:T(1024)S(1)} fusion(bf16[3072,2048]{1,0:T(8,128)(2,1)} %all-gather.3.cloned.1.call-done, f32[3072]{0:T(1024)S(1)} %broadcast_multiply_fusion), kind=kLoop, calls=%fused_computation.11 | loop fusion | flops 25162752 | bytes 12607488 | tf_op jit(solution)/shard_map/reduce_sum | solution.py:126
  231.6 19.2 %fusion.2 = (bf16[3072,2048]{1,0:T(8,128)(2,1)}, bf16[3072,2048]{1,0:T(8,128)(2,1)}, bf16[3072,2048]{1,0:T(8,128)(2,1)}) fusion(bf16[3072,2048]{1,0:T(8,128)(2,1)} %all-gather.3.cloned.1.call-done, f32[3072]{0:T(1024)S(1)} %add_rsqrt_fusion, f32[3072]{0:T(1024)S(1)} %broadcast_multiply_fusion, f32[2048]{0:T(1024)S(1)} %add.278, f32[2048]{0:T(1024)S(1)} %mul.132, ...), kind=kLoop, calls=%fused_computation.4 | loop fusion | flops 62914560 | bytes 50388992 | tf_op jit(solution)/shard_map/convert_element_type | solution.py:418
  250.8 16.1 %shard_map.254.refs_0_ = bf16[3072,768]{1,0:T(8,128)(2,1)} custom-call(bf16[3072,2048]{1,0:T(8,128)(2,1)} %get-tuple-element.40.refs_0_, f32[3072,128]{1,0:T(8,128)} %get-tuple-element.110.refs_1_.refs_2_, f32[3072,128]{1,0:T(8,128)} %get-tuple-element.111.refs_2_.refs_3_, bf16[2048,768]{1,0:T(8,128)(2,1)} %bitcast.20.refs_3_.qkv, f32[1,768]{1,0:T(1,128)} %bitcast.273), custom_call_target="tpu_custom_call" | custom-call | flops 9663676416 | bytes 23596032 | tf_op jit(solution)/shard_map/pallas_call | solution.py:147
  266.9 22.5 %shard_map.256 = (bf16[3072,1024]{1,0:T(8,128)(2,1)}, f32[3072,1024]{1,0:T(8,128)}) custom-call(bf16[3072,2048]{1,0:T(8,128)(2,1)} %get-tuple-element.39.x, bf16[2048,1024]{1,0:T(8,128)(2,1)} %bitcast.43.weight.expand, f32[1,1024]{1,0:T(1,128)} %reshape.314.bias), custom_call_target="tpu_custom_call" | custom-call | flops 12884901888 | bytes 35655680 | tf_op jit(solution)/shard_map/pallas_call | solution.py:147
  289.4 19.9 %shard_map.258.grad_hidden.right = bf16[3072,1024]{1,0:T(8,128)(2,1)} custom-call(bf16[3072,2048]{1,0:T(8,128)(2,1)} %all-gather.5.cloned.1.call-done.refs_1_.cotangent, f32[3072,1024]{1,0:T(8,128)} %get-tuple-element.27.slope, bf16[1024,2048]{1,0:T(8,128)(2,1)} %bitcast.49.contract.weight), custom_call_target="tpu_custom_call" | custom-call | flops 12884901888 | bytes 35651584 | tf_op jit(solution)/shard_map/pallas_call | solution.py:147
  309.4 18.7 %shard_map.255 = (bf16[3072,256]{1,0:T(8,128)(2,1)}, bf16[3072,768]{1,0:T(8,128)(2,1)}) custom-call(bf16[3072,768]{1,0:T(8,128)(2,1)} %shard_map.254.refs_0_, bf16[3072,2048]{1,0:T(8,128)(2,1)} %all-gather.5.cloned.1.call-done.refs_1_.cotangent, f32[3072,128]{1,0:T(8,128)} %get-tuple-element.110.refs_1_.refs_2_, ...), custom_call_target="tpu_custom_call" | custom-call | flops 7449083904 | bytes 27811840 | tf_op jit(solution)/shard_map/pallas_call | solution.py:147
  328.1 29.5 %shard_map.259 = bf16[3072,2048]{1,0:T(8,128)(2,1)} custom-call(bf16[3072,768]{1,0:T(8,128)(2,1)} %get-tuple-element.26.grad_qkv.right, bf16[3072,1024]{1,0:T(8,128)(2,1)} %shard_map.258.grad_hidden.right, bf16[2048,768]{1,0:T(8,128)(2,1)} %bitcast.20.refs_3_.qkv, bf16[2048,1024]{1,0:T(8,128)(2,1)} %bitcast.43.weight.expand, f32[1,2048]{1,0:T(1,128)} %reshape.319.gain_one, ...), custom_call_target="tpu_custom_call" | custom-call | flops 22548578304 | bytes 30949376 | tf_op jit(solution)/shard_map/pallas_call | solution.py:147
  357.6 22.0 %shard_map.257 = bf16[3072,2048]{1,0:T(8,128)(2,1)} custom-call(bf16[3072,256]{1,0:T(8,128)(2,1)} %get-tuple-element.24.attn, bf16[3072,1024]{1,0:T(8,128)(2,1)} %get-tuple-element.25.active, bf16[256,2048]{1,0:T(8,128)(2,1)} %bitcast.239, bf16[1024,2048]{1,0:T(8,128)(2,1)} %bitcast.49.contract.weight), custom_call_target="tpu_custom_call" | custom-call | flops 16106127360 | bytes 25690112 | tf_op jit(solution)/shard_map/pallas_call | solution.py:147
  384.5 10.2 %shard_map.261 = bf16[1024,768]{1,0:T(8,128)(2,1)} custom-call(s32[4]{0:T(128)} %fusion.63._, bf16[3072,2048]{1,0:T(8,128)(2,1)} %get-tuple-element.38.left, bf16[3072,768]{1,0:T(8,128)(2,1)} %get-tuple-element.26.grad_qkv.right), custom_call_target="tpu_custom_call" | custom-call | flops 4831838208 | bytes 12582912 | tf_op jit(solution)/shard_map/pallas_call | solution.py:249
  395.7 3.1 convert_reduce_fusion.3
  398.8 3.7 convert_reduce_fusion.2
  402.5 6.7 convert_reduce_fusion.1
  409.7 12.4 %shard_map.264 = bf16[1024,1024]{1,0:T(8,128)(2,1)} custom-call(s32[4]{0:T(128)} %fusion.63._, bf16[3072,2048]{1,0:T(8,128)(2,1)} %get-tuple-element.38.left, bf16[3072,1024]{1,0:T(8,128)(2,1)} %shard_map.258.grad_hidden.right), custom_call_target="tpu_custom_call" | custom-call | flops 6442450944 | bytes 14680064 | tf_op jit(solution)/shard_map/pallas_call | solution.py:249
  423.0 8.0 %convolution_convert_fusion = bf16[128,2048]{1,0:T(8,128)(2,1)} fusion(bf16[3072,2048]{1,0:T(8,128)(2,1)} %all-gather.5.cloned.1.call-done.refs_1_.cotangent, bf16[3072,256]{1,0:T(8,128)(2,1)S(1)} %copy-done.10, s32[]{:T(128)S(6)} %select_n.264), kind=kOutput, calls=%fused_computation.41 | convolution fusion | flops 1610874880 | bytes 13893636 | tf_op jit(solution)/shard_map/dot_general | solution.py:136
  431.1 10.9 %fusion.28 = bf16[512,2048]{1,0:T(8,128)(2,1)} fusion(bf16[3072,2048]{1,0:T(8,128)(2,1)} %all-gather.5.cloned.1.call-done.refs_1_.cotangent, bf16[3072,1024]{1,0:T(8,128)(2,1)S(1)} %bitcast.277, s32[]{:T(128)S(6)} %select_n.268), kind=kOutput, calls=%fused_computation.40 | convolution fusion | flops 6443499520 | bytes 17825796 | tf_op jit(solution)/shard_map/dot_general | solution.py:136
  443.4 12.1 %shard_map.263 = bf16[1024,1024]{1,0:T(8,128)(2,1)} custom-call(s32[4]{0:T(128)} %fusion.64._, bf16[3072,2048]{1,0:T(8,128)(2,1)} %get-tuple-element.38.left, bf16[3072,1024]{1,0:T(8,128)(2,1)} %shard_map.258.grad_hidden.right), custom_call_target="tpu_custom_call" | custom-call | flops 6442450944 | bytes 14680064 | tf_op jit(solution)/shard_map/pallas_call | solution.py:249
  455.6 11.7 %fusion.25 = bf16[512,2048]{1,0:T(8,128)(2,1)} fusion(bf16[3072,2048]{1,0:T(8,128)(2,1)} %all-gather.5.cloned.1.call-done.refs_1_.cotangent, bf16[3072,1024]{1,0:T(8,128)(2,1)} %get-tuple-element.25.active, s32[]{:T(128)S(6)} %select_n.267), kind=kOutput, calls=%fused_computation.39 | convolution fusion | flops 6443499520 | bytes 17825796 | tf_op jit(solution)/shard_map/dot_general | solution.py:136
  469.1 10.2 %shard_map.260 = bf16[1024,768]{1,0:T(8,128)(2,1)} custom-call(s32[4]{0:T(128)} %fusion.64._, bf16[3072,2048]{1,0:T(8,128)(2,1)} %get-tuple-element.38.left, bf16[3072,768]{1,0:T(8,128)(2,1)} %get-tuple-element.26.grad_qkv.right), custom_call_target="tpu_custom_call" | custom-call | flops 4831838208 | bytes 12582912 | tf_op jit(solution)/shard_map/pallas_call | solution.py:249
  479.3 3.5 collective-permute-start.22
  485.3 7.6 %convolution_convert_fusion.1 = bf16[128,2048]{1,0:T(8,128)(2,1)} fusion(bf16[3072,2048]{1,0:T(8,128)(2,1)} %all-gather.5.cloned.1.call-done.refs_1_.cotangent, bf16[3072,256]{1,0:T(8,128)(2,1)S(1)} %copy-done.10, s32[]{:T(128)S(6)} %select_n.263), kind=kOutput, calls=%fused_computation.42 | convolution fusion | flops 1610874880 | bytes 13893636 | tf_op jit(solution)/shard_map/dot_general | solution.py:136
  501.6 43.2 %collective-permute-done.19 = bf16[512,768]{1,0:T(8,128)(2,1)S(1)} collective-permute-done((bf16[512,768]{1,0:T(8,128)(2,1)S(1)}, bf16[512,768]{1,0:T(8,128)(2,1)S(1)}, u32[]{:S(2)}, u32[]{:S(2)}) %collective-permute-start.19) | collective-permute-done | bytes 786464 | tf_op jit(solution)/shard_map/ppermute | solution.py:51
  545.8 4.7 all-to-all-start.2
  552.9 4.5 convert_add_fusion.1
  557.4 15.7 %collective-permute-done.26 = bf16[512,1024]{1,0:T(8,128)(2,1)} collective-permute-done((bf16[512,1024]{1,0:T(8,128)(2,1)}, bf16[512,1024]{1,0:T(8,128)(2,1)}, u32[]{:S(2)}, u32[]{:S(2)}) %collective-permute-start.26) | collective-permute-done | bytes 1048608 | tf_op jit(solution)/shard_map/ppermute | solution.py:51
  575.6 10.5 %all-to-all-done.2.refs_0_ = bf16[8,64,768]{2,1,0:T(8,128)(2,1)S(1)} async-done(((bf16[8,64,768]{2,1,0:T(8,128)(2,1)}), bf16[8,64,768]{2,1,0:T(8,128)(2,1)S(1)}, u32[]{:S(2)}, u32[]{:S(2)}) %all-to-all-start.2) | async-done | bytes 786464 | tf_op jit(solution)/shard_map/all_to_all | solution.py:472
  586.1 4.4 all-to-all-start.3
  595.1 2.7 collective-permute-start.29
  597.8 43.9 %collective-permute-done.24 = f32[4,14,128]{2,1,0:T(8,128)S(1)} collective-permute-done((f32[4,14,128]{2,1,0:T(8,128)S(1)}, f32[4,14,128]{2,1,0:T(8,128)S(1)}, u32[]{:S(2)}, u32[]{:S(2)}) %collective-permute-start.24) | collective-permute-done | bytes 28704 | tf_op jit(solution)/shard_map/ppermute | solution.py:51
  643.1 3.7 collective-permute-done.29
  649.2 3.5 shard_map.262
  655.6 4.1 shard_map.265
  665.1 5.1 fusion.15
  (261 shorter events, 105.1 us)
Async XLA Ops:
  7.3 209.9 %all-gather.3.cloned.1.call-start = ((), (), s32[]{:S(2)}) async-start(), calls=%async_computation.6 | async-start | bytes 14155776 | tf_op jit(solution)/shard_map/all_gather | solution.py:332
  8.0 17.8 %copy-start.5 = (bf16[64,8192]{1,0:T(8,128)(2,1)S(1)}, bf16[64,8192]{1,0:T(8,128)(2,1)}, u32[]{:S(2)}) copy-start(bf16[64,8192]{1,0:T(8,128)(2,1)} %refs_2_.3) | copy-start | bytes 3145732
  8.0 281.4 %all-gather.5.cloned.1.call-start = ((), (), s32[]{:S(2)}) async-start(), calls=%async_computation.7 | async-start | bytes 14155776 | tf_op jit(solution)/shard_map/all_gather | solution.py:333
  8.8 98.1 %collective-permute-start.15 = (bf16[256,2048]{1,0:T(8,128)(2,1)}, bf16[256,2048]{1,0:T(8,128)(2,1)}, u32[]{:S(2)}, u32[]{:S(2)}) collective-permute-start(bf16[256,2048]{1,0:T(8,128)(2,1)} %param.27), channel_id=1, source_target_pairs={{0,16},{1,17},{2,18},{3,19},{4,20},{5,21},{6,22},{7,23},{8,24},{9,... | collective-permute-start | bytes 3145736 | tf_op jit(solution)/shard_map/ppermute | solution.py:51
  12.0 121.2 %collective-permute-start.16 = (bf16[256,2048]{1,0:T(8,128)(2,1)}, bf16[256,2048]{1,0:T(8,128)(2,1)}, u32[]{:S(2)}, u32[]{:S(2)}) collective-permute-start(bf16[256,2048]{1,0:T(8,128)(2,1)} %param.27), channel_id=1, source_target_pairs={{0,4},{1,5},{2,6},{3,7},{4,0},{5,1},{6,2},{7,3},{8,12},{9,13},{10,... | collective-permute-start | bytes 3145736 | tf_op jit(solution)/shard_map/ppermute | solution.py:51
  13.4 22.9 %collective-permute-start = (bf16[1,8,128]{2,1,0:T(8,128)(2,1)S(1)}, bf16[1,8,128]{2,1,0:T(8,128)(2,1)S(1)}, u32[]{:S(2)}, u32[]{:S(2)}) collective-permute-start(bf16[1,8,128]{2,1,0:T(8,128)(2,1)S(1)} %bitcast.266), channel_id=1, source_target_pairs={{0,1},{1,0},{2,3},{3,2},{4,5},{5,4},{6,7},{7,6},{8,9},{9,8},{10,11... | collective-permute-start | bytes 6152 | tf_op jit(solution)/shard_map/ppermute | solution.py:51
  19.9 71.9 %all-to-all-start = ((bf16[8,64,768]{2,1,0:T(8,128)(2,1)}), bf16[8,64,768]{2,1,0:T(8,128)(2,1)S(1)}, u32[]{:S(2)}, u32[]{:S(2)}) async-start(bf16[8,64,768]{2,1,0:T(8,128)(2,1)} %fusion.56), calls=%async_computation | async-start | bytes 1572864 | tf_op jit(solution)/shard_map/all_to_all | solution.py:399
  23.8 66.3 %collective-permute-start.8 = (bf16[64,2048]{1,0:T(8,128)(2,1)}, bf16[64,2048]{1,0:T(8,128)(2,1)S(1)}, u32[]{:S(2)}, u32[]{:S(2)}) collective-permute-start(bf16[64,2048]{1,0:T(8,128)(2,1)} %param.23), channel_id=1, source_target_pairs={{0,0},{1,16},{2,4},{3,20},{4,1},{5,17},{6,5},{7,21},{8,2},{9,18},{... | collective-permute-start | bytes 786440 | tf_op jit(solution)/shard_map/ppermute | solution.py:409
  36.4 3.1 collective-permute-start.1
  39.4 2.9 collective-permute-start.2
  42.3 30.3 %collective-permute-start.3 = (bf16[8,8,128]{2,1,0:T(8,128)(2,1)S(1)}, bf16[8,8,128]{2,1,0:T(8,128)(2,1)S(1)}, u32[]{:S(2)}, u32[]{:S(2)}) collective-permute-start(bf16[8,8,128]{2,1,0:T(8,128)(2,1)S(1)} %maximum_select_fusion.7), channel_id=1, source_target_pairs={{0,8},{1,9},{2,10},{3,11},{4,12},{5,13},{6,14},{7,15},{8,0},{9,1},... | collective-permute-start | bytes 49160 | tf_op jit(solution)/shard_map/ppermute | solution.py:51
  72.7 3.8 collective-permute-start.4
  90.1 11.0 %collective-permute-start.9 = (bf16[64,2048]{1,0:T(8,128)(2,1)S(1)}, bf16[64,2048]{1,0:T(8,128)(2,1)S(1)}, u32[]{:S(2)}, u32[]{:S(2)}) collective-permute-start(bf16[64,2048]{1,0:T(8,128)(2,1)S(1)} %collective-permute-done.8), channel_id=1, source_target_pairs={{0,16},{1,17},{2,18},{3,19},{4,20},{5,21},{6,22},{7,23},{8,24},{9,... | collective-permute-start | bytes 786440 | tf_op jit(solution)/shard_map/ppermute | solution.py:51
  90.7 11.0 %collective-permute-start.10 = (bf16[64,2048]{1,0:T(8,128)(2,1)S(1)}, bf16[64,2048]{1,0:T(8,128)(2,1)}, u32[]{:S(2)}, u32[]{:S(2)}) collective-permute-start(bf16[64,2048]{1,0:T(8,128)(2,1)S(1)} %collective-permute-done.8), channel_id=1, source_target_pairs={{0,4},{1,5},{2,6},{3,7},{4,0},{5,1},{6,2},{7,3},{8,12},{9,13},{10,... | collective-permute-start | bytes 786440 | tf_op jit(solution)/shard_map/ppermute | solution.py:51
  91.8 39.1 %all-to-all-start.1 = ((bf16[8,64,1024]{2,1,0:T(8,128)(2,1)}), bf16[8,64,1024]{2,1,0:T(8,128)(2,1)S(1)}, u32[]{:S(2)}, u32[]{:S(2)}) async-start(bf16[8,64,1024]{2,1,0:T(8,128)(2,1)} %fusion.48), calls=%async_computation.1 | async-start | bytes 2097152 | tf_op jit(solution)/shard_map/all_to_all | solution.py:399
  100.7 561.8 %reduce-scatter.5.cloned.1.call-start = ((), (), s32[]{:S(2)}) async-start(), calls=%async_computation.9 | async-start | bytes 14155776 | tf_op jit(solution)/shard_map/reduce_scatter | solution.py:531
  101.1 5.7 collective-permute-start.11
  106.8 32.2 %copy-start.11 = (bf16[2,2,64,2048]{3,2,1,0:T(8,128)(2,1)}, bf16[2,2,64,2048]{3,2,1,0:T(8,128)(2,1)S(1)}, u32[]{:S(2)}) copy-start(bf16[2,2,64,2048]{3,2,1,0:T(8,128)(2,1)S(1)} %bitcast_dynamic-update-slice_fusion.4) | copy-start | bytes 3145732
  106.9 78.0 %collective-permute-start.17 = (bf16[256,2048]{1,0:T(8,128)(2,1)}, bf16[256,2048]{1,0:T(8,128)(2,1)}, u32[]{:S(2)}, u32[]{:S(2)}) collective-permute-start(bf16[256,2048]{1,0:T(8,128)(2,1)} %collective-permute-done.15), channel_id=1, source_target_pairs={{0,4},{1,5},{2,6},{3,7},{4,0},{5,1},{6,2},{7,3},{8,12},{9,13},{10,... | collective-permute-start | bytes 3145736 | tf_op jit(solution)/shard_map/ppermute | solution.py:51
  107.5 47.0 %collective-permute-start.5 = (bf16[8,64,768]{2,1,0:T(8,128)(2,1)S(1)}, bf16[8,64,768]{2,1,0:T(8,128)(2,1)}, u32[]{:S(2)}, u32[]{:S(2)}) collective-permute-start(bf16[8,64,768]{2,1,0:T(8,128)(2,1)S(1)} %all-to-all-done), channel_id=1, source_target_pairs={{0,16},{1,17},{2,18},{3,19},{4,20},{5,21},{6,22},{7,23},{8,24},{9,... | collective-permute-start | bytes 2359304 | tf_op jit(solution)/shard_map/ppermute | solution.py:51
  130.9 53.2 %collective-permute-start.12 = (bf16[8,64,1024]{2,1,0:T(8,128)(2,1)S(1)}, bf16[8,64,1024]{2,1,0:T(8,128)(2,1)S(1)}, u32[]{:S(2)}, u32[]{:S(2)}) collective-permute-start(bf16[8,64,1024]{2,1,0:T(8,128)(2,1)S(1)} %all-to-all-done.1), channel_id=1, source_target_pairs={{0,16},{1,17},{2,18},{3,19},{4,20},{5,21},{6,22},{7,23},{8,24},{9,... | collective-permute-start | bytes 3145736 | tf_op jit(solution)/shard_map/ppermute | solution.py:51
  135.6 53.6 %collective-permute-start.6 = (bf16[8,64,768]{2,1,0:T(8,128)(2,1)S(1)}, bf16[8,64,768]{2,1,0:T(8,128)(2,1)S(1)}, u32[]{:S(2)}, u32[]{:S(2)}) collective-permute-start(bf16[8,64,768]{2,1,0:T(8,128)(2,1)S(1)} %all-to-all-done), channel_id=1, source_target_pairs={{0,4},{1,5},{2,6},{3,7},{4,0},{5,1},{6,2},{7,3},{8,12},{9,13},{10,... | collective-permute-start | bytes 2359304 | tf_op jit(solution)/shard_map/ppermute | solution.py:51
  136.5 54.8 %collective-permute-start.13 = (bf16[8,64,1024]{2,1,0:T(8,128)(2,1)S(1)}, bf16[8,64,1024]{2,1,0:T(8,128)(2,1)S(1)}, u32[]{:S(2)}, u32[]{:S(2)}) collective-permute-start(bf16[8,64,1024]{2,1,0:T(8,128)(2,1)S(1)} %all-to-all-done.1), channel_id=1, source_target_pairs={{0,4},{1,5},{2,6},{3,7},{4,0},{5,1},{6,2},{7,3},{8,12},{9,13},{10,... | collective-permute-start | bytes 3145736 | tf_op jit(solution)/shard_map/ppermute | solution.py:51
  154.5 39.2 %collective-permute-start.7 = (bf16[8,64,768]{2,1,0:T(8,128)(2,1)}, bf16[8,64,768]{2,1,0:T(8,128)(2,1)S(1)}, u32[]{:S(2)}, u32[]{:S(2)}) collective-permute-start(bf16[8,64,768]{2,1,0:T(8,128)(2,1)} %collective-permute-done.5), channel_id=1, source_target_pairs={{0,4},{1,5},{2,6},{3,7},{4,0},{5,1},{6,2},{7,3},{8,12},{9,13},{10,... | collective-permute-start | bytes 2359304 | tf_op jit(solution)/shard_map/ppermute | solution.py:51
  184.1 32.0 %collective-permute-start.14 = (bf16[8,64,1024]{2,1,0:T(8,128)(2,1)S(1)}, bf16[8,64,1024]{2,1,0:T(8,128)(2,1)S(1)}, u32[]{:S(2)}, u32[]{:S(2)}) collective-permute-start(bf16[8,64,1024]{2,1,0:T(8,128)(2,1)S(1)} %collective-permute-done.12), channel_id=1, source_target_pairs={{0,4},{1,5},{2,6},{3,7},{4,0},{5,1},{6,2},{7,3},{8,12},{9,13},{10,... | collective-permute-start | bytes 3145736 | tf_op jit(solution)/shard_map/ppermute | solution.py:51
  357.6 307.5 %reduce-scatter.3.cloned.1.call-start = ((), (), s32[]{:S(2)}) async-start(), calls=%async_computation.8 | async-start | bytes 14155776 | tf_op jit(solution)/shard_map/reduce_scatter | solution.py:515
  394.7 88.1 %collective-permute-start.18 = (bf16[2,512,768]{2,1,0:T(8,128)(2,1)}, bf16[2,512,768]{2,1,0:T(8,128)(2,1)}, u32[]{:S(2)}, u32[]{:S(2)}) collective-permute-start(bf16[2,512,768]{2,1,0:T(8,128)(2,1)} %bitcast.237), channel_id=1, source_target_pairs={{0,4},{1,5},{2,6},{3,7},{4,0},{5,1},{6,2},{7,3},{8,12},{9,13},{10,... | collective-permute-start | bytes 4718600 | tf_op jit(solution)/shard_map/ppermute | solution.py:51
  409.3 13.8 %copy-start.10 = (bf16[3072,256]{1,0:T(8,128)(2,1)S(1)}, bf16[3072,256]{1,0:T(8,128)(2,1)}, u32[]{:S(2)}) copy-start(bf16[3072,256]{1,0:T(8,128)(2,1)} %get-tuple-element.24.attn) | copy-start | bytes 4718596
  409.3 58.0 %collective-permute-start.20 = (f32[30,128]{1,0:T(8,128)S(1)}, f32[30,128]{1,0:T(8,128)S(1)}, u32[]{:S(2)}, u32[]{:S(2)}) collective-permute-start(f32[30,128]{1,0:T(8,128)S(1)} %maximum_bitcast_fusion.16), channel_id=1, source_target_pairs={{0,4},{1,5},{2,6},{3,7},{4,0},{5,1},{6,2},{7,3},{8,12},{9,13},{10,... | collective-permute-start | bytes 46088 | tf_op jit(solution)/shard_map/ppermute | solution.py:51
  422.1 71.9 %collective-permute-start.25 = (bf16[2,512,1024]{2,1,0:T(8,128)(2,1)}, bf16[2,512,1024]{2,1,0:T(8,128)(2,1)}, u32[]{:S(2)}, u32[]{:S(2)}) collective-permute-start(bf16[2,512,1024]{2,1,0:T(8,128)(2,1)} %bitcast.275), channel_id=1, source_target_pairs={{0,4},{1,5},{2,6},{3,7},{4,0},{5,1},{6,2},{7,3},{8,12},{9,13},{10,... | collective-permute-start | bytes 6291464 | tf_op jit(solution)/shard_map/ppermute | solution.py:51
  431.0 119.5 %collective-permute-start.27 = (bf16[2,64,2048]{2,1,0:T(8,128)(2,1)}, bf16[2,64,2048]{2,1,0:T(8,128)(2,1)}, u32[]{:S(2)}, u32[]{:S(2)}) collective-permute-start(bf16[2,64,2048]{2,1,0:T(8,128)(2,1)} %bitcast.69), channel_id=1, source_target_pairs={{0,4},{1,5},{2,6},{3,7},{4,0},{5,1},{6,2},{7,3},{8,12},{9,13},{10,... | collective-permute-start | bytes 1572872 | tf_op jit(solution)/shard_map/ppermute | solution.py:51
  442.0 110.8 %collective-permute-start.30 = (bf16[2,256,2048]{2,1,0:T(8,128)(2,1)}, bf16[2,256,2048]{2,1,0:T(8,128)(2,1)}, u32[]{:S(2)}, u32[]{:S(2)}) collective-permute-start(bf16[2,256,2048]{2,1,0:T(8,128)(2,1)} %bitcast.75), channel_id=1, source_target_pairs={{0,4},{1,5},{2,6},{3,7},{4,0},{5,1},{6,2},{7,3},{8,12},{9,13},{10,... | collective-permute-start | bytes 6291464 | tf_op jit(solution)/shard_map/ppermute | solution.py:51
  467.3 12.0 %collective-permute-start.21 = (f32[30,128]{1,0:T(8,128)S(1)}, f32[30,128]{1,0:T(8,128)S(1)}, u32[]{:S(2)}, u32[]{:S(2)}) collective-permute-start(f32[30,128]{1,0:T(8,128)S(1)} %fusion.65), channel_id=1, source_target_pairs={{0,16},{1,17},{2,18},{3,19},{4,20},{5,21},{6,22},{7,23},{8,24},{9,... | collective-permute-start | bytes 46088 | tf_op jit(solution)/shard_map/ppermute | solution.py:51
  479.3 13.7 %collective-permute-start.22 = (f32[1,14,128]{2,1,0:T(8,128)S(1)}, f32[1,14,128]{2,1,0:T(8,128)S(1)}, u32[]{:S(2)}, u32[]{:S(2)}) collective-permute-start(f32[1,14,128]{2,1,0:T(8,128)S(1)} %get-tuple-element.106), channel_id=1, source_target_pairs={{0,1},{1,0},{2,3},{3,2},{4,5},{5,4},{6,7},{7,6},{8,9},{9,8},{10,11... | collective-permute-start | bytes 21512 | tf_op jit(solution)/shard_map/ppermute | solution.py:51
  485.2 59.6 %collective-permute-start.19 = (bf16[512,768]{1,0:T(8,128)(2,1)S(1)}, bf16[512,768]{1,0:T(8,128)(2,1)S(1)}, u32[]{:S(2)}, u32[]{:S(2)}) collective-permute-start(bf16[512,768]{1,0:T(8,128)(2,1)S(1)} %fusion.35), channel_id=1, source_target_pairs={{0,16},{1,17},{2,18},{3,19},{4,20},{5,21},{6,22},{7,23},{8,24},{9,... | collective-permute-start | bytes 2359304 | tf_op jit(solution)/shard_map/ppermute | solution.py:51
  493.0 177.2 %copy-start.24 = (f32[64]{0:T(128)}, f32[64]{0:T(128)S(1)}, u32[]{:S(2)}) copy-start(f32[64]{0:T(128)S(1)} %dynamic_slice.76) | copy-start | bytes 772
  493.0 99.5 %collective-permute-start.23 = (f32[2,14,128]{2,1,0:T(8,128)S(1)}, f32[2,14,128]{2,1,0:T(8,128)S(1)}, u32[]{:S(2)}, u32[]{:S(2)}) collective-permute-start(f32[2,14,128]{2,1,0:T(8,128)S(1)} %maximum_select_fusion.8), channel_id=1, source_target_pairs={{0,2},{1,3},{2,0},{3,1},{4,6},{5,7},{6,4},{7,5},{8,10},{9,11},{10,... | collective-permute-start | bytes 43016 | tf_op jit(solution)/shard_map/ppermute | solution.py:51
  499.6 73.5 %collective-permute-start.26 = (bf16[512,1024]{1,0:T(8,128)(2,1)}, bf16[512,1024]{1,0:T(8,128)(2,1)}, u32[]{:S(2)}, u32[]{:S(2)}) collective-permute-start(bf16[512,1024]{1,0:T(8,128)(2,1)} %fusion.33), channel_id=1, source_target_pairs={{0,16},{1,17},{2,18},{3,19},{4,20},{5,21},{6,22},{7,23},{8,24},{9,... | collective-permute-start | bytes 3145736 | tf_op jit(solution)/shard_map/ppermute | solution.py:51
  545.8 40.3 %all-to-all-start.2 = ((bf16[8,64,768]{2,1,0:T(8,128)(2,1)}), bf16[8,64,768]{2,1,0:T(8,128)(2,1)S(1)}, u32[]{:S(2)}, u32[]{:S(2)}) async-start(bf16[8,64,768]{2,1,0:T(8,128)(2,1)} %bitcast.54), calls=%async_computation.4 | async-start | bytes 1572864 | tf_op jit(solution)/shard_map/all_to_all | solution.py:472
  552.8 41.3 %collective-permute-start.28 = (bf16[64,2048]{1,0:T(8,128)(2,1)}, bf16[64,2048]{1,0:T(8,128)(2,1)}, u32[]{:S(2)}, u32[]{:S(2)}) collective-permute-start(bf16[64,2048]{1,0:T(8,128)(2,1)} %fusion.40), channel_id=1, source_target_pairs={{0,16},{1,17},{2,18},{3,19},{4,20},{5,21},{6,22},{7,23},{8,24},{9,... | collective-permute-start | bytes 786440 | tf_op jit(solution)/shard_map/ppermute | solution.py:51
  552.8 20.2 %copy-start.3 = (f32[2,512,1024]{2,1,0:T(8,128)S(1)}, f32[2,512,1024]{2,1,0:T(8,128)}, u32[]{:S(2)}) copy-start(f32[2,512,1024]{2,1,0:T(8,128)} %copy-done.2) | copy-start | bytes 12582916
  586.1 61.5 %copy-start.7 = (bf16[8,64,768]{2,1,0:T(8,128)(2,1)}, bf16[8,64,768]{2,1,0:T(8,128)(2,1)S(1)}, u32[]{:S(2)}) copy-start(bf16[8,64,768]{2,1,0:T(8,128)(2,1)S(1)} %all-to-all-done.2.refs_0_) | copy-start | bytes 2359300
  586.1 69.5 %all-to-all-start.3 = ((bf16[8,64,1024]{2,1,0:T(8,128)(2,1)}), bf16[8,64,1024]{2,1,0:T(8,128)(2,1)}, u32[]{:S(2)}, u32[]{:S(2)}) async-start(bf16[8,64,1024]{2,1,0:T(8,128)(2,1)} %bitcast.63), calls=%async_computation.5 | async-start | bytes 2097152 | tf_op jit(solution)/shard_map/all_to_all | solution.py:472
  590.5 57.1 %copy-start.1 = (f32[2,256,2048]{2,1,0:T(8,128)S(1)}, f32[2,256,2048]{2,1,0:T(8,128)}, u32[]{:S(2)}) copy-start(f32[2,256,2048]{2,1,0:T(8,128)} %convert_add_fusion.1) | copy-start | bytes 12582916
  592.4 55.2 %collective-permute-start.31 = (bf16[256,2048]{1,0:T(8,128)(2,1)S(1)}, bf16[256,2048]{1,0:T(8,128)(2,1)S(1)}, u32[]{:S(2)}, u32[]{:S(2)}) collective-permute-start(bf16[256,2048]{1,0:T(8,128)(2,1)S(1)} %fusion.34), channel_id=1, source_target_pairs={{0,16},{1,17},{2,18},{3,19},{4,20},{5,21},{6,22},{7,23},{8,24},{9,... | collective-permute-start | bytes 3145736 | tf_op jit(solution)/shard_map/ppermute | solution.py:51
  592.6 49.2 %collective-permute-start.24 = (f32[4,14,128]{2,1,0:T(8,128)S(1)}, f32[4,14,128]{2,1,0:T(8,128)S(1)}, u32[]{:S(2)}, u32[]{:S(2)}) collective-permute-start(f32[4,14,128]{2,1,0:T(8,128)S(1)} %maximum_select_fusion.4), channel_id=1, source_target_pairs={{0,8},{1,9},{2,10},{3,11},{4,12},{5,13},{6,14},{7,15},{8,0},{9,1},... | collective-permute-start | bytes 86024 | tf_op jit(solution)/shard_map/ppermute | solution.py:51
  595.1 51.7 %collective-permute-start.29 = (bf16[64,2048]{1,0:T(8,128)(2,1)S(1)}, bf16[64,2048]{1,0:T(8,128)(2,1)S(1)}, u32[]{:S(2)}, u32[]{:S(2)}) collective-permute-start(bf16[64,2048]{1,0:T(8,128)(2,1)S(1)} %fusion.38), channel_id=1, source_target_pairs={{0,0},{16,1},{4,2},{20,3},{1,4},{17,5},{5,6},{21,7},{2,8},{18,9},{... | collective-permute-start | bytes 786440 | tf_op jit(solution)/shard_map/ppermute | solution.py:486
  652.7 12.4 %copy-start.4 = (bf16[384,2048]{1,0:T(8,128)(2,1)S(1)}, bf16[384,2048]{1,0:T(8,128)(2,1)}, u32[]{:S(2)}) copy-start(bf16[384,2048]{1,0:T(8,128)(2,1)} %param.29) | copy-start | bytes 4718596
  (19 other events, 125.5 us)
Sparse Core Ops, SparseCore 0:
  9.8 122.1 all-gather.2
  133.6 95.8 all-gather.4
  357.7 130.8 reduce-scatter.4
  490.7 158.5 reduce-scatter.2

commit v3 on v2

v3 whole, which is shorter than its diff:
```python
import math

import jax
import jax.numpy as jnp
from jax import lax
from jax.experimental import pallas as pl
from jax.experimental.pallas import tpu as pltpu
from jax.sharding import PartitionSpec as P


HEADS = 8

EPSILON = 1e-05
MASKED = -1e30
PAIRED = (((1,), (1,)), ((), ()))
LEADING = (((0,), (0,)), ((), ()))
VMEM_LIMIT = 60 * 2**20
ORDER = (0, 2, 4, 6, 1, 3, 5, 7)
BRIEF = pl.CostEstimate(flops=1, bytes_accessed=1, transcendentals=0)


class Plan:
    def __init__(self, count):
        self.count = count
        self.bits = count.bit_length() - 1
        self.groups = count // HEADS

    def device(self, group, slot):
        return group * HEADS + slot

    def sharing(self):
        return [[self.device(g, s) for s in range(HEADS)] for g in range(self.groups)]

    def across(self):
        return [[self.device(g, s) for g in range(self.groups)] for s in range(HEADS)]

    def flip(self, bit):
        return [(d, d ^ (1 << bit)) for d in range(self.count)]


def swap(value, bit, plan):
    return lax.ppermute(value, "dp", plan.flip(bit))


def gather_small(value, bits, me, plan):
    rest = value.shape
    order = sorted(bits, reverse=True)
    value = value.reshape((1,) * len(bits) + rest)
    for bit in bits:
        got = swap(value, bit, plan)
        place = order.index(bit)
        value = jnp.where(
            (me >> bit) & 1 == 0,
            jnp.concatenate([value, got], axis=place),
            jnp.concatenate([got, value], axis=place),
        )
    return value.reshape((-1,) + rest)


def gather_tokens(value, plan, last):
    pieces = {0: value}
    for bit in (1, 2):
        pieces[1 << bit] = swap(value, bit, plan)
    pieces[6] = swap(pieces[1 << (3 - last)], last, plan)
    for mask in (0, 2, 4, 6):
        pieces[mask | 1] = swap(pieces[mask], 0, plan)
    return jnp.concatenate([pieces[mask] for mask in ORDER])


class Chain:
    def __init__(self):
        self.waits = []

    def settle(self, *values):
        self.waits += values

    def launch(self, kernel, inputs, in_specs, outs, out_specs, grid=(1,), prefetch=(), **options):
        known = len(prefetch) + len(inputs)
        waits = self.waits

        def body(*refs):
            kernel(*refs[:known], *refs[known + len(waits) :])

        made = pl.pallas_call(
            body,
            grid_spec=pltpu.PrefetchScalarGridSpec(
                num_scalar_prefetch=len(prefetch),
                grid=grid,
                in_specs=in_specs + [pl.BlockSpec(memory_space=pl.ANY)] * len(waits),
                out_specs=out_specs,
                **options,
            ),
            out_shape=[jax.ShapeDtypeStruct(shape, kind) for shape, kind in outs],
            compiler_params=pltpu.CompilerParams(vmem_limit_bytes=VMEM_LIMIT),
            cost_estimate=BRIEF,
        )(*prefetch, *inputs, *waits)
        self.waits = [made[0]]
        return made


def whole(item):
    return pl.BlockSpec(item.shape, lambda i, *_: (0,) * len(item.shape))


def slot_layout(lengths, slots):
    place = jnp.arange(slots, dtype=jnp.int32)
    ends = jnp.cumsum(lengths, dtype=jnp.int32)
    after = (place[:, None] >= ends[None, :]).astype(jnp.int32)
    segment = jnp.sum(after, axis=1, dtype=jnp.int32)
    offset = jnp.sum(after * lengths[None, :], axis=1, dtype=jnp.int32)
    return (segment, place - offset)


def rotary_tables(position, rotated, lanes):
    half = rotated // 2
    ladder = jnp.arange(half, dtype=jnp.float32) * (-math.log(10000.0) / half)
    angle = position.astype(jnp.float32)[:, None] * jnp.exp(ladder)[None, :]
    cosine, sine = jnp.cos(angle), jnp.sin(angle)
    rest = (position.shape[0], lanes - rotated)
    return (
        jnp.concatenate([cosine, cosine, jnp.ones(rest, jnp.float32)], axis=1),
        jnp.concatenate([-sine, sine, jnp.zeros(rest, jnp.float32)], axis=1),
    )


def norm_terms(value):
    centre = jnp.mean(value, axis=1, keepdims=True)
    spread = value - centre
    variance = jnp.mean(spread * spread, axis=1, keepdims=True)
    scale = lax.rsqrt(variance + EPSILON)
    return (spread * scale, scale)


def times(left, right):
    return jnp.dot(left, right, preferred_element_type=jnp.float32)


def times_leading(left, right):
    return lax.dot_general(left, right, LEADING, preferred_element_type=jnp.float32)


def times_paired(left, right):
    return lax.dot_general(left, right, PAIRED, preferred_element_type=jnp.float32)


def over_blocks(chain, kernel, slots, blocked, known, outs, sums=(), rows=None):
    count = blocked[0].shape[0] // slots
    gathered, runs = rows or (None, [])
    extra = [gathered] if runs else []

    def body(*refs):
        given = len(blocked) + len(known)
        if not runs:
            kernel(*refs)
            return
        weight = refs[-1]

        @pl.when(pl.program_id(0) == 0)
        def _():
            place = 0
            for start, many in runs:
                weight[place : place + many, :] = refs[given][start : start + many, :]
                place += many

        kernel(*refs[:given], weight, *refs[given + 1 : -1])

    def moving(width):
        return pl.BlockSpec((slots, width), lambda i: (i, 0))

    shapes = [((count * slots, width), kind) for width, kind in outs]
    shapes += [((1, width), jnp.float32) for width in sums]
    specs = [moving(width) for width, _ in outs]
    specs += [pl.BlockSpec((1, width), lambda i: (0, 0)) for width in sums]
    if runs:
        shape = (sum(many for _, many in runs), gathered.shape[1])
        shapes.append((shape, jnp.bfloat16))
        specs.append(pl.BlockSpec(shape, lambda i: (0, 0)))
    return chain.launch(
        body,
        [*blocked, *known, *extra],
        [moving(item.shape[1]) for item in blocked]
        + [whole(item) for item in known]
        + [
            pl.BlockSpec(item.shape, lambda i: (0, 0), pipeline_mode=pl.Buffered(1))
            for item in extra
        ],
        shapes,
        specs,
        (count,),
    )


def add_columns(out, value):
    total = jnp.sum(value.astype(jnp.float32), axis=0, keepdims=True)
    block = pl.program_id(0)

    @pl.when(block == 0)
    def _():
        out[...] = total

    @pl.when(block > 0)
    def _():
        out[...] += total


def terms_of(chain, compute, slots, width, place, blocked, known, added, split):
    extra = [] if added is None else [added]

    def kernel(*refs):
        values = [ref[...] for ref in refs[: len(blocked) + len(known)]]
        total = compute(*values)
        if extra:
            total += refs[len(values)][...].astype(jnp.float32)
        outs = refs[len(values) + len(extra) :]
        if not split:
            outs[0][...] = total.astype(jnp.bfloat16)
            return
        for step, out in enumerate(outs):

            @pl.when(pl.program_id(0) == step)
            def _(out=out):
                out[...] = total.astype(jnp.bfloat16)

    outs = 4 if split else 1
    shape = (slots if split else 4 * slots, width)
    return chain.launch(
        kernel,
        [*blocked, *known, *extra],
        [pl.BlockSpec((slots, item.shape[1]), lambda i: (i + 4 * place, 0)) for item in blocked]
        + [whole(item) for item in known]
        + [pl.BlockSpec((slots, width), lambda i: (i, 0)) for _ in extra],
        [(shape, jnp.bfloat16)] * outs,
        [pl.BlockSpec((slots, width), lambda i: (0 if split else i, 0)) for _ in range(outs)],
        (4,),
    )


def join(chain, one, two, kind):
    rows, width = one.shape
    tile = rows // 2 if rows % 32 == 0 else rows

    def kernel(one, two, out):
        out[...] = (one[...].astype(jnp.float32) + two[...].astype(jnp.float32)).astype(kind)

    spec = pl.BlockSpec((tile, width), lambda i: (i, 0))
    return chain.launch(
        kernel, [one, two], [spec, spec], [((rows, width), kind)], [spec], (rows // tile,)
    )[0]


def split_output(chain, reduced, units, rows):
    width = reduced.shape[1]

    def kernel(reduced, contract, dense):
        contract[...] = reduced[:units].astype(jnp.float32)
        dense[...] = reduced[units:]

    shapes = [(units, width), (rows, width)]
    return chain.launch(
        kernel,
        [reduced],
        [whole(reduced)],
        list(zip(shapes, [jnp.float32, jnp.bfloat16])),
        [pl.BlockSpec(shape, lambda i: (0, 0)) for shape in shapes],
    )


def finish_input(chain, cotangent, tokens, own, one, two):
    slots, width = tokens.shape
    tile = slots // 4

    def kernel(cotangent, tokens, own, one, two, out):
        normed, scale = norm_terms(tokens[...].astype(jnp.float32))
        grad = own[...].astype(jnp.float32) + one[...].astype(jnp.float32)
        grad += two[...].astype(jnp.float32)
        along = jnp.mean(grad * normed, axis=1, keepdims=True)
        grad = grad - jnp.mean(grad, axis=1, keepdims=True) - normed * along
        out[...] = cotangent[...].astype(jnp.float32) + grad * scale

    spec = pl.BlockSpec((tile, width), lambda i: (i, 0))
    return chain.launch(
        kernel,
        [cotangent, tokens, own, one, two],
        [spec] * 5,
        [((slots, width), jnp.float32)],
        [spec],
        (slots // tile,),
    )[0]


def finish_output(chain, tokens, own, one, two, bias_one, bias_two):
    slots, width = tokens.shape
    tile = slots // 4

    def kernel(tokens, own, one, two, bias_one, bias_two, out):
        total = tokens[...].astype(jnp.float32) + own[...].astype(jnp.float32)
        total += one[...].astype(jnp.float32) + two[...].astype(jnp.float32)
        out[...] = (total + bias_one[...] + bias_two[...]).astype(jnp.bfloat16)

    spec = pl.BlockSpec((tile, width), lambda i: (i, 0))
    return chain.launch(
        kernel,
        [tokens, own, one, two, bias_one, bias_two],
        [spec] * 4 + [whole(bias_one), whole(bias_two)],
        [((slots, width), jnp.bfloat16)],
        [spec],
        (slots // tile,),
    )[0]


def norm_kernel(rows, out):
    out[...] = norm_terms(rows[...].astype(jnp.float32))[0].astype(jnp.bfloat16)


def scaled(normed, gain, shift):
    return (normed[...].astype(jnp.float32) * gain[...] + shift[...]).astype(jnp.bfloat16)


def turn(value, cosine, sine, half):
    lane = lax.broadcasted_iota(jnp.int32, value.shape, 1)
    lanes = value.shape[1]
    swapped = jnp.where(
        lane < half, pltpu.roll(value, lanes - half, 1), pltpu.roll(value, half, 1)
    )
    return value * cosine + swapped * sine


def turn_into(out, at, value, cosine, sine, half):
    lanes = cosine.shape[1]
    turned = turn(value[:, :lanes], cosine, sine, half)
    out[:, at : at + lanes] = turned.astype(jnp.bfloat16)
    out[:, at + lanes : at + value.shape[1]] = value[:, lanes:].astype(jnp.bfloat16)


def qkv_kernel(head_dim, normed, cosine, sine, gain, shift, bias, weight, out):
    projected = times(scaled(normed, gain, shift), weight[...]) + bias[...]
    half = head_dim // 8
    for part in range(2):
        at = part * head_dim
        turn_into(out, at, projected[:, at : at + head_dim], cosine[...], sine[...], half)
    out[:, 2 * head_dim :] = projected[:, 2 * head_dim :].astype(jnp.bfloat16)


def expand_kernel(normed, gain, shift, bias, weight, active, slope):
    hidden = times(scaled(normed, gain, shift), weight[...]) + bias[...]
    below = 0.5 * (1.0 + lax.erf(hidden * math.sqrt(0.5)))
    density = jnp.exp(-0.5 * hidden * hidden) * (1.0 / math.sqrt(2.0 * math.pi))
    active[...] = (hidden * below).astype(jnp.bfloat16)
    slope[...] = below + hidden * density


def grad_hidden_kernel(cotangent, slope, weight, out, out_sum, cotangent_sum):
    grad = (times_paired(cotangent[...], weight[...]) * slope[...]).astype(jnp.bfloat16)
    out[...] = grad
    add_columns(out_sum, grad)
    add_columns(cotangent_sum, cotangent[...])


def branch_terms(attn, active, dense, contract):
    return times(attn, dense) + times(active, contract)


def norm_grad_terms(grad_qkv, grad_hidden, qkv, expand, gain_one, gain_two):
    return times_paired(grad_qkv, qkv) * gain_one + times_paired(grad_hidden, expand) * gain_two


def attend_kernel(
    head_dim, qkv, cotangent, cosine, sine, segment, segments, dense, attn, grad_qkv, grad_sum
):
    scale = 1.0 / math.sqrt(head_dim)
    query = qkv[:, :head_dim]
    key = qkv[:, head_dim : 2 * head_dim]
    value = qkv[:, 2 * head_dim :]
    grad_attn = times_paired(cotangent[...], dense[...]).astype(jnp.bfloat16)
    slots = query.shape[0]
    row = lax.broadcasted_iota(jnp.int32, (slots, slots), 0)
    column = lax.broadcasted_iota(jnp.int32, (slots, slots), 1)
    block = pl.program_id(0)
    allowed = (segment[...] == segments[pl.ds(block, 1), :]) & (column <= row)
    masked = jnp.where(allowed, times_paired(query, key) * scale, MASKED)
    raised = jnp.exp(masked - jnp.max(masked, axis=1, keepdims=True))
    weights = raised / jnp.sum(raised, axis=1, keepdims=True)
    probs = weights.astype(jnp.bfloat16)
    attn[...] = times(probs, value).astype(jnp.bfloat16)
    grad_probs = times_paired(grad_attn, value)
    grad_value = times_leading(probs, grad_attn)
    inner = jnp.sum(weights * grad_probs, axis=1, keepdims=True)
    grad_score = (weights * (grad_probs - inner)).astype(jnp.bfloat16)
    half = head_dim // 8
    back = -sine[...]
    grad_query = times(grad_score, key) * scale
    turn_into(grad_qkv, 0, grad_query, cosine[...], back, half)
    grad_key = times_leading(grad_score, query) * scale
    turn_into(grad_qkv, head_dim, grad_key, cosine[...], back, half)
    grad_qkv[:, 2 * head_dim :] = grad_value.astype(jnp.bfloat16)
    add_columns(grad_sum, grad_qkv[...])


def input_terms(chain, normed, grad):
    depth, width = normed.shape
    columns = grad.shape[1]
    block = 256

    def kernel(left, right, out):
        out[...] = times_leading(left[...], right[...]).astype(jnp.bfloat16)

    return chain.launch(
        kernel,
        [normed, grad],
        [
            pl.BlockSpec((depth, block), lambda i: (0, i)),
            pl.BlockSpec((depth, columns), lambda i: (0, 0), pipeline_mode=pl.Buffered(1)),
        ],
        [((width, columns), jnp.bfloat16)],
        [pl.BlockSpec((block, columns), lambda i: (i, 0))],
        (width // block,),
    )[0]


def output_terms(chain, active, attn, groups, right):
    depth, width = right.shape
    tile = width // 4
    lefts = [active, attn]
    own = [item.shape[1] // groups for item in lefts]
    stride = sum(own)

    def kernel(active, attn, right, out):
        before = 0
        for left, many in zip((active, attn), own):
            terms = times_leading(left[...], right[...]).astype(jnp.bfloat16)
            for group in range(groups):
                at = group * stride + before
                out[at : at + many, :] = terms[group * many : (group + 1) * many]
            before = many

    return chain.launch(
        kernel,
        [active, attn, right],
        [
            pl.BlockSpec(item.shape, lambda i: (0, 0), pipeline_mode=pl.Buffered(1))
            for item in lefts
        ]
        + [pl.BlockSpec((depth, tile), lambda i: (0, i))],
        [((groups * stride, width), jnp.bfloat16)],
        [pl.BlockSpec((groups * stride, tile), lambda i: (0, i))],
        (width // tile,),
    )[0]


def pack(chain, arrays, moves, columns):
    rows = arrays[0].shape[0]

    def kernel(*refs):
        for slot, at, which, column, many in moves:
            refs[-1][slot, :, at : at + many] = refs[which][:, column : column + many]

    shape = (HEADS, rows, columns)
    return chain.launch(
        kernel,
        arrays,
        [whole(item) for item in arrays],
        [(shape, jnp.bfloat16)],
        [pl.BlockSpec(shape, lambda i: (0, 0, 0))],
    )[0]


def unpack(chain, places, got, sums, weight, gain, shift):
    rows, width = weight.shape
    gain = gain.astype(jnp.float32).reshape(rows, 1)
    shift = shift.astype(jnp.float32).reshape(rows, 1)

    def kernel(got, sums, weight, gain, shift, grad, gain_grad, shift_grad):
        by_gain = jnp.zeros((rows, 1), jnp.float32)
        by_shift = jnp.zeros((rows, 1), jnp.float32)
        for slot, start, at, many in places:
            terms = got[slot, :, start : start + many].astype(jnp.float32)
            total = sums[slot : slot + 1, start : start + many]
            parts = weight[:, at : at + many].astype(jnp.float32)
            grad[:, at : at + many] = terms * gain[...] + total * shift[...]
            by_gain += jnp.sum(parts * terms, axis=1, keepdims=True)
            by_shift += jnp.sum(parts * total, axis=1, keepdims=True)
        gain_grad[...] = by_gain
        shift_grad[...] = by_shift

    inputs = [got, sums, weight, gain, shift]
    shapes = [(rows, width), (rows, 1), (rows, 1)]
    grad, gain_grad, shift_grad = chain.launch(
        kernel,
        inputs,
        [whole(item) for item in inputs],
        [(shape, jnp.float32) for shape in shapes],
        [pl.BlockSpec(shape, lambda i: (0, 0)) for shape in shapes],
    )
    return grad, gain_grad.reshape(rows), shift_grad.reshape(rows)


def per_device(
    plan,
    tokens,
    seq_lengths,
    ln1_gain,
    ln1_bias,
    ln2_gain,
    ln2_bias,
    qkv_weight,
    qkv_bias,
    dense_weight,
    dense_bias,
    expand_weight,
    expand_bias,
    contract_weight,
    contract_bias,
    cotangent,
):
    slots, width = tokens.shape
    rows = qkv_weight.shape[0]
    units = contract_weight.shape[0]
    count, groups = plan.count, plan.groups
    head_dim = width // HEADS
    rotated = head_dim // 4
    hidden_units = groups * units
    me = lax.axis_index("dp")
    slot = me % HEADS
    sharing, across = plan.sharing(), plan.across()
    outer_bits = tuple(range(3, plan.bits))
    chain = Chain()

    def gather(value):
        return lax.all_gather(value, "dp", axis=0, tiled=True, axis_index_groups=across)

    def reduce(value):
        return lax.psum_scatter(
            value, "dp", scatter_dimension=0, tiled=True, axis_index_groups=across
        )

    def exchange(value):
        return lax.all_to_all(value, "dp", 0, 0, tiled=True, axis_index_groups=sharing)

    to_slot = [(d, plan.device(d % groups, d // groups)) for d in range(count)]
    from_slot = [(target, source) for source, target in to_slot]
    dense_part = lax.ppermute(dense_weight, "dp", to_slot)
    weight_out = gather(jnp.concatenate([contract_weight, dense_part]))
    contract_runs = [(group * (units + rows), units) for group in range(groups)]
    dense_runs = [(group * (units + rows) + units, rows) for group in range(groups)]

    expand_places = [
        (s, group * units, plan.device(group, s) * units, units)
        for s in range(HEADS)
        for group in range(groups)
    ]
    qkv_places = [
        (s, part * head_dim, part * width + s * head_dim, head_dim)
        for s in range(HEADS)
        for part in range(3)
    ]
    split = 3 * head_dim
    moves = [(s, at, 0, column, many) for s, at, column, many in qkv_places]
    moves += [(s, split + at, 1, column, many) for s, at, column, many in expand_places]
    own = exchange(pack(chain, [qkv_weight, expand_weight], moves, split + hidden_units))
    own = own.reshape(HEADS * rows, -1)
    weight_qkv = gather(own[:, :split])
    weight_expand = gather(own[:, split:])

    tile = slots // 4
    own_normed = chain.launch(
        norm_kernel,
        [tokens],
        [pl.BlockSpec((tile, width), lambda i: (i, 0))],
        [((slots, width), jnp.bfloat16)],
        [pl.BlockSpec((tile, width), lambda i: (i, 0))],
        (slots // tile,),
    )[0]
    normed = gather_tokens(own_normed, plan, 1)
    group_cotangent = gather_tokens(cotangent, plan, 2)

    parts = [
        ln1_gain,
        ln1_bias,
        ln2_gain,
        ln2_bias,
        dense_bias,
        contract_bias,
        qkv_bias,
        expand_bias,
        seq_lengths[0].astype(jnp.bfloat16),
    ]
    sizes = [item.shape[0] for item in parts]
    lines = -(-sum(sizes) // 1024) * 8
    small = jnp.concatenate(parts + [jnp.zeros((lines * 128 - sum(sizes),), jnp.bfloat16)])
    every = gather_small(small.reshape(lines, 128), outer_bits + (0, 1, 2), me, plan)
    every = every.reshape(count, lines * 128).astype(jnp.float32)
    taken, at = [], 0
    for size in sizes:
        taken.append(every[:, at : at + size])
        at += size
    gain_one, shift_one, gain_two, shift_two, bias_dense, bias_contract = [
        item.reshape(1, width) for item in taken[:6]
    ]
    bias_qkv = lax.dynamic_index_in_dim(
        taken[6].reshape(3, HEADS, head_dim), slot, 1, keepdims=False
    ).reshape(1, split)
    bias_expand = lax.dynamic_index_in_dim(
        taken[7].reshape(groups, HEADS, units), slot, 1, keepdims=False
    ).reshape(1, hidden_units)
    lengths = jnp.concatenate(
        [lax.dynamic_slice_in_dim(taken[8], me ^ mask, 1) for mask in ORDER]
    ).astype(jnp.int32)
    segment, position = jax.vmap(lambda item: slot_layout(item, slots))(lengths)
    cosine, sine = rotary_tables(position.reshape(-1), rotated, head_dim // 2)

    def sum_begin(compute, blocked, known):
        terms = terms_of(chain, compute, slots, width, 1, blocked, known, None, False)[0]
        return swap(terms, 0, plan)

    def sum_next(compute, blocked, known, got, near):
        own, of_x, of_y, of_both = terms_of(
            chain, compute, slots, width, 0, blocked, known, got, True
        )
        of_near, of_far = (of_x, of_y) if near == 1 else (of_y, of_x)
        return own, swap(of_both, near, plan), swap(of_near, near, plan), of_far

    def sum_last(own, from_both, from_near, of_far, near):
        of_far = join(chain, of_far, from_both, jnp.bfloat16)
        return own, from_near, swap(of_far, 3 - near, plan)

    (qkv,) = over_blocks(
        chain,
        lambda *refs: qkv_kernel(head_dim, *refs),
        slots,
        [normed, cosine, sine],
        [gain_one, shift_one, bias_qkv, weight_qkv],
        [(split, jnp.bfloat16)],
    )
    attn, grad_qkv, qkv_sum, weight_dense = over_blocks(
        chain,
        lambda *refs: attend_kernel(head_dim, *refs),
        slots,
        [qkv, group_cotangent, cosine, sine, segment.reshape(-1, 1)],
        [segment],
        [(head_dim, jnp.bfloat16), (split, jnp.bfloat16)],
        [split],
        (weight_out, dense_runs),
    )
    qkv_got = reduce(input_terms(chain, normed, grad_qkv))
    active, slope = over_blocks(
        chain,
        expand_kernel,
        slots,
        [normed],
        [gain_two, shift_two, bias_expand, weight_expand],
        [(hidden_units, jnp.bfloat16), (hidden_units, jnp.float32)],
    )
    output_got = reduce(output_terms(chain, active, attn, groups, group_cotangent))
    grad_hidden, hidden_sum, cotangent_sum, weight_contract = over_blocks(
        chain,
        grad_hidden_kernel,
        slots,
        [group_cotangent, slope],
        [],
        [(hidden_units, jnp.bfloat16)],
        [hidden_units, width],
        (weight_out, contract_runs),
    )
    expand_got = reduce(input_terms(chain, normed, grad_hidden))

    sums = jnp.concatenate([qkv_sum, hidden_sum, cotangent_sum], axis=1).reshape(-1, 128)
    for bit in outer_bits:
        sums = sums + swap(sums, bit, plan)
    own_lines = (split + hidden_units) // 128
    bias_out_grad = lax.dynamic_slice_in_dim(
        sums[own_lines:].reshape(-1), me * (width // count), width // count
    )
    sums = gather_small(sums[:own_lines], (0, 1, 2), me, plan).reshape(HEADS, -1)
    qkv_sums, expand_sums = sums[:, :split], sums[:, split:]

    branch_of = branch_terms, [attn, active], [weight_dense, weight_contract]
    norm_of = (
        norm_grad_terms,
        [grad_qkv, grad_hidden],
        [weight_qkv, weight_expand, gain_one, gain_two],
    )
    branch_got = sum_begin(*branch_of)
    norm_got = sum_begin(*norm_of)
    branch = sum_next(*branch_of, branch_got, 1)
    norm_parts = sum_next(*norm_of, norm_got, 2)
    branch = sum_last(*branch, 1)
    norm_parts = sum_last(*norm_parts, 2)
    layer_out = finish_output(chain, tokens, *branch, bias_dense, bias_contract)
    input_grad = finish_input(chain, cotangent, tokens, *norm_parts)

    qkv_got = exchange(qkv_got.reshape(HEADS, rows, split))
    qkv_weight_grad, ln1_gain_grad, ln1_bias_grad = unpack(
        chain, qkv_places, qkv_got, qkv_sums, qkv_weight, ln1_gain, ln1_bias
    )
    contract_weight_grad, dense_grad = split_output(chain, output_got, units, rows)
    dense_weight_grad = lax.ppermute(dense_grad, "dp", from_slot).astype(jnp.float32)
    expand_got = exchange(expand_got.reshape(HEADS, rows, hidden_units))
    expand_weight_grad, ln2_gain_grad, ln2_bias_grad = unpack(
        chain, expand_places, expand_got, expand_sums, expand_weight, ln2_gain, ln2_bias
    )
    qkv_bias_grad = qkv_sums.reshape(HEADS, 3, head_dim).transpose(1, 0, 2).reshape(3 * width)
    per = qkv_bias.shape[0]
    qkv_bias_grad = lax.dynamic_slice_in_dim(qkv_bias_grad, me * per, per)
    expand_bias_grad = lax.dynamic_slice(
        expand_sums, (slot, (me // HEADS) * units), (1, units)
    ).reshape(units)
    return (
        layer_out,
        input_grad,
        ln1_gain_grad,
        ln1_bias_grad,
        ln2_gain_grad,
        ln2_bias_grad,
        qkv_weight_grad,
        qkv_bias_grad,
        dense_weight_grad,
        bias_out_grad,
        expand_weight_grad,
        expand_bias_grad,
        contract_weight_grad,
        bias_out_grad,
    )


def solution(mesh):
    in_specs = (
        P("dp", None),
        P("dp", None),
        P("dp"),
        P("dp"),
        P("dp"),
        P("dp"),
        P("dp", None),
        P("dp"),
        P("dp", None),
        P("dp"),
        P("dp", None),
        P("dp"),
        P("dp", None),
        P("dp"),
        P("dp", None),
    )
    out_specs = (
        P("dp", None),
        P("dp", None),
        P("dp"),
        P("dp"),
        P("dp"),
        P("dp"),
        P("dp", None),
        P("dp"),
        P("dp", None),
        P("dp"),
        P("dp", None),
        P("dp"),
        P("dp", None),
        P("dp"),
    )
    plan = Plan(mesh.shape["dp"])

    def layer(*arrays):
        return per_device(plan, *arrays)

    return jax.shard_map(layer, mesh=mesh, in_specs=in_specs, out_specs=out_specs, check_vma=False)
```

time: 691 us -> 618 us (0.89); the launches traced: 678 us -> 614 us
  other arithmetic: 99.4 us -> 14.8 us
  waiting for transfers between devices: 239 us -> 178 us
  Pallas kernels: 181 us -> 241 us
  matrix products: 38.2 us -> 0 us
  blocking collectives: 0 us -> 27.7 us
  starting transfers between devices: 61 us -> 86.3 us
  local copies, waits for them, and re-layouts: 43.4 us -> 50.9 us
    ppermute x30 -> x32, waiting for transfers between devices: 203 us -> 139 us  [swap(): return lax.ppermute(value, 'dp', plan.flip(bit))]
    pallas_call x12 -> x20, Pallas kernels: 181 us -> 241 us  [launch(): pl.pallas_call(body, grid_spec=pltpu.PrefetchScalarGridSpec(num_scalar_pr...]
    dot_general x4 -> x0, matrix products: 38.2 us -> none  [times_leading(): lax.dot_general(left, right, LEADING, preferred_element_type=jnp.float32)]
    ppermute x30 -> x32, starting transfers between devices: 34.1 us -> 66.1 us  [swap(): return lax.ppermute(value, 'dp', plan.flip(bit))]
    reduce_sum x8 -> x0, other arithmetic: 31.3 us -> none  [the longest x2 8.52 us: norm_terms(): variance = jnp.mean(spread * spread, axis=1, keepdims=True)]
    unnamed x68 -> x70, local copies, waits for them, and re-layouts: 4.35 us -> 35.3 us
    all_to_all x0 -> x1, blocking collectives: none -> 27.7 us  [exchange(): lax.all_to_all(value, 'dp', 0, 0, tiled=True, axis_index_groups=sharing)]
    convert_element_type x6 -> x2, other arithmetic: 24.6 us -> 0.84 us  [the longest x1 0.83 us: per_device(): lax.ppermute(dense_grad, 'dp', from_slot).astype(jnp.float32)]
  transfers between devices with their start and end apart: 40 -> 42, of which waited for: 15 -> 15; matrix products, arithmetic and copies ran while one was open for 26% -> 10% of each run, Pallas kernels for 17% -> 39%
where the time goes in v3:
time: 618 us; the launch traced here: 614 us
  Pallas kernels  241 us (39%)
  waiting for transfers between devices  178 us (29%)
  starting transfers between devices  86.3 us (14%)
  local copies, waits for them, and re-layouts  50.9 us (8%)
  blocking collectives  27.7 us (4%)
  between operations  14.9 us (2%)
  other arithmetic  14.8 us (2%)
    pallas_call x20, Pallas kernels, launch(): pl.pallas_call(body, grid_spec=pltpu.PrefetchScalarGridSpec(num_scalar_pr...  241 us
    ppermute x32, waiting for transfers between devices, swap(): return lax.ppermute(value, 'dp', plan.flip(bit))  139 us
    ppermute x32, starting transfers between devices, swap(): return lax.ppermute(value, 'dp', plan.flip(bit))  66.1 us
    unnamed x70, local copies, waits for them, and re-layouts  35.3 us
    all_to_all x1, blocking collectives, exchange(): lax.all_to_all(value, 'dp', 0, 0, tiled=True, axis_index_groups=sharing)  27.7 us
    all_to_all x2, waiting for transfers between devices, exchange(): lax.all_to_all(value, 'dp', 0, 0, tiled=True, axis_index_groups=sharing)  19.8 us
  transfers between devices with their start and end apart: 42, of which 15 were waited for; matrix products, arithmetic and copies ran while one was open for 10% of the time, Pallas kernels for 39%

profile of v3, /device:TPU:1, one launch (start us, length us, event | category | flops | bytes accessed | tf_op | source)
XLA Modules:
  0.0 613.6 jit_solution(6675706887193617207)
XLA Ops:
  7.2 2.8 shard_map.254.refs_1_
  10.1 27.7 %all_to_all.15 = bf16[8,64,1792]{2,1,0:T(8,128)(2,1)S(1)} all-to-all(bf16[8,64,1792]{2,1,0:T(8,128)(2,1)} %shard_map.254.refs_1_), channel_id=1, replica_groups={{0,1,2,3,4,5,6,7},{8,9,10,11,12,13,14,15},{16,17,18,19,20,21,22,23},{24..., dimensions={0} | all-to-all | bytes 3670016 | tf_op jit(solution)/shard_map/all_to_all | solution.py:537
  38.8 4.4 collective-permute-start.19
  43.2 3.3 collective-permute-done.19
  47.8 22.8 %collective-permute-start.13 = (bf16[384,2048]{1,0:T(8,128)(2,1)}, bf16[384,2048]{1,0:T(8,128)(2,1)}, u32[]{:S(2)}, u32[]{:S(2)}) collective-permute-start(bf16[384,2048]{1,0:T(8,128)(2,1)} %refs_0_.7), channel_id=1, source_target_pairs={{0,4},{1,5},{2,6},{3,7},{4,0},{5,1},{6,2},{7,3},{8,12},{9,13},{10,... | collective-permute-start | bytes 4718600 | tf_op jit(solution)/shard_map/ppermute | solution.py:42
  70.7 4.1 shard_map.255.refs_7_
  74.8 5.1 collective-permute-start.3
  82.8 2.8 constant_dynamic-update-slice_fusion.15
  85.6 2.8 collective-permute-start.8
  89.9 3.5 collective-permute-start.9
  96.6 5.5 collective-permute-done.10
  102.7 32.6 %collective-permute-done.11 = bf16[2,2,1,2,2,8,128]{6,5,4,3,2,1,0:T(8,128)(2,1)S(1)} collective-permute-done((bf16[2,2,1,2,2,8,128]{6,5,4,3,2,1,0:T(8,128)(2,1)S(1)}, bf16[2,2,1,2,2,8,128]{6,5,4,3,2,1,0:T(8,128)(2,1)S(1)}, u32[]{:S(2)}, u32[]{:S(2)}) %collective-permute-start.11) | collective-permute-done | bytes 32800 | tf_op jit(solution)/shard_map/ppermute | solution.py:42
  135.9 5.8 fusion
  150.9 15.1 %collective-permute-done = bf16[384,2048]{1,0:T(8,128)(2,1)S(1)} collective-permute-done((bf16[384,2048]{1,0:T(8,128)(2,1)S(1)}, bf16[384,2048]{1,0:T(8,128)(2,1)S(1)}, u32[]{:S(2)}, u32[]{:S(2)}) %collective-permute-start) | collective-permute-done | bytes 1572896 | tf_op jit(solution)/shard_map/ppermute | solution.py:42
  166.0 12.0 %collective-permute-start.5 = (bf16[384,2048]{1,0:T(8,128)(2,1)}, bf16[384,2048]{1,0:T(8,128)(2,1)S(1)}, u32[]{:S(2)}, u32[]{:S(2)}) collective-permute-start(bf16[384,2048]{1,0:T(8,128)(2,1)} %collective-permute-done.1), channel_id=1, source_target_pairs={{0,1},{1,0},{2,3},{3,2},{4,5},{5,4},{6,7},{7,6},{8,9},{9,8},{10,11... | collective-permute-start | bytes 4718600 | tf_op jit(solution)/shard_map/ppermute | solution.py:42
  179.2 2.8 constant_dynamic-update-slice_fusion.5
  185.2 2.8 constant_dynamic-update-slice_fusion.13
  188.0 11.7 %collective-permute-done.2 = bf16[384,2048]{1,0:T(8,128)(2,1)} collective-permute-done((bf16[384,2048]{1,0:T(8,128)(2,1)}, bf16[384,2048]{1,0:T(8,128)(2,1)}, u32[]{:S(2)}, u32[]{:S(2)}) %collective-permute-start.2) | collective-permute-done | bytes 1572896 | tf_op jit(solution)/shard_map/ppermute | solution.py:42
  199.7 6.3 %collective-permute-start.16 = (bf16[384,2048]{1,0:T(8,128)(2,1)}, bf16[384,2048]{1,0:T(8,128)(2,1)S(1)}, u32[]{:S(2)}, u32[]{:S(2)}) collective-permute-start(bf16[384,2048]{1,0:T(8,128)(2,1)} %collective-permute-done.12), channel_id=1, source_target_pairs={{0,1},{1,0},{2,3},{3,2},{4,5},{5,4},{6,7},{7,6},{8,9},{9,8},{10,11... | collective-permute-start | bytes 4718600 | tf_op jit(solution)/shard_map/ppermute | solution.py:42
  211.9 2.8 constant_dynamic-update-slice_fusion.12
  223.8 16.1 %shard_map.256.refs_0_.refs_7_ = bf16[3072,768]{1,0:T(8,128)(2,1)} custom-call(bf16[3072,2048]{1,0:T(8,128)(2,1)} %constant_dynamic-update-slice_fusion.refs_0_, f32[3072,128]{1,0:T(8,128)} %get-tuple-element.91.refs_1_.refs_2_, f32[3072,128]{1,0:T(8,128)} %get-tuple-element.92.refs_2_.refs_3_, f32[1,2048]{1,0:T(1,128)} %reshape.1209.refs_3_.refs_4_, ...), custom_call_target="tpu_custom_call" | custom-call | flops 1 | bytes 1 | tf_op jit(solution)/shard_map/pallas_call | solution.py:84
  239.9 20.7 %shard_map.257 = (bf16[3072,256]{1,0:T(8,128)(2,1)}, bf16[3072,768]{1,0:T(8,128)(2,1)}, f32[1,768]{1,0:T(1,128)}, bf16[256,2048]{1,0:T(8,128)(2,1)}) custom-call(bf16[3072,768]{1,0:T(8,128)(2,1)} %shard_map.256.refs_0_.refs_7_, bf16[3072,2048]{1,0:T(8,128)(2,1)} %constant_dynamic-update-slice_fusion.8.refs_1_.refs_2_.refs_0_, ...), custom_call_target="tpu_custom_call" | custom-call | flops 1 | bytes 1 | tf_op jit(solution)/shard_map/pallas_call | solution.py:84
  260.6 15.6 %shard_map.258.refs_5_ = bf16[2048,768]{1,0:T(8,128)(2,1)} custom-call(bf16[3072,2048]{1,0:T(8,128)(2,1)} %constant_dynamic-update-slice_fusion.refs_0_, bf16[3072,768]{1,0:T(8,128)(2,1)} %get-tuple-element.41.refs_1_.refs_0_, bf16[3072,256]{1,0:T(8,128)(2,1)} %get-tuple-element.40.refs_2_.refs_1_.refs_0_), custom_call_target="tpu_custom_call" | custom-call | flops 1 | bytes 1 | tf_op jit(solution)/shard_map/pallas_call | solution.py:84
  278.4 9.7 %all-gather.8.cloned.1.call-done.refs_4_.refs_3_ = bf16[2048,1024]{1,0:T(8,128)(2,1)} async-done(((bf16[512,1024]{1,0:T(8,128)(2,1)}), bf16[2048,1024]{1,0:T(8,128)(2,1)}) %all-gather.8.cloned.1.call-update) | async-done | bytes 4194320 | tf_op jit(solution)/shard_map/all_gather | solution.py:529
  288.2 22.5 %shard_map.259 = (bf16[3072,1024]{1,0:T(8,128)(2,1)}, f32[3072,1024]{1,0:T(8,128)}) custom-call(bf16[3072,2048]{1,0:T(8,128)(2,1)} %constant_dynamic-update-slice_fusion.refs_0_, f32[1,2048]{1,0:T(1,128)} %reshape.1215.refs_1_.refs_5_, f32[1,2048]{1,0:T(1,128)} %reshape.1216.refs_2_, f32[1,1024]{1,0:T(1,128)} %bitcast.96, ...), custom_call_target="tpu_custom_call" | custom-call | flops 1 | bytes 1 | tf_op jit(solution)/shard_map/pallas_call | solution.py:84
  310.6 22.4 %shard_map.260.refs_3_ = bf16[1280,2048]{1,0:T(8,128)(2,1)} custom-call(bf16[3072,1024]{1,0:T(8,128)(2,1)} %get-tuple-element.42.refs_0_.refs_3_.refs_1_, bf16[3072,256]{1,0:T(8,128)(2,1)} %get-tuple-element.40.refs_2_.refs_1_.refs_0_, bf16[3072,2048]{1,0:T(8,128)(2,1)} %constant_dynamic-update-slice_fusion.8.refs_1_.refs_2_.refs_0_, ...), custom_call_target="tpu_custom_call" | custom-call | flops 1 | bytes 1 | tf_op jit(solution)/shard_map/pallas_call | solution.py:84
  333.1 23.5 %shard_map.261 = (bf16[3072,1024]{1,0:T(8,128)(2,1)}, f32[1,1024]{1,0:T(1,128)}, f32[1,2048]{1,0:T(1,128)}, bf16[1024,2048]{1,0:T(8,128)(2,1)}) custom-call(bf16[3072,2048]{1,0:T(8,128)(2,1)} %constant_dynamic-update-slice_fusion.8.refs_1_.refs_2_.refs_0_, f32[3072,1024]{1,0:T(8,128)} %get-tuple-element.44.refs_1_, ...), custom_call_target="tpu_custom_call" | custom-call | flops 1 | bytes 1 | tf_op jit(solution)/shard_map/pallas_call | solution.py:84
  356.6 18.8 %shard_map.262.refs_4_ = bf16[2048,1024]{1,0:T(8,128)(2,1)} custom-call(bf16[3072,2048]{1,0:T(8,128)(2,1)} %constant_dynamic-update-slice_fusion.refs_0_, bf16[3072,1024]{1,0:T(8,128)(2,1)} %get-tuple-element.46.refs_1_.refs_2_, bf16[3072,1024]{1,0:T(8,128)(2,1)} %get-tuple-element.46.refs_1_.refs_2_), custom_call_target="tpu_custom_call" | custom-call | flops 1 | bytes 1 | tf_op jit(solution)/shard_map/pallas_call | solution.py:84
  376.0 13.0 %shard_map.263.refs_6_ = bf16[1536,2048]{1,0:T(8,128)(2,1)} custom-call(bf16[3072,256]{1,0:T(8,128)(2,1)} %get-tuple-element.40.refs_2_.refs_1_.refs_0_, bf16[3072,1024]{1,0:T(8,128)(2,1)} %get-tuple-element.42.refs_0_.refs_3_.refs_1_, bf16[256,2048]{1,0:T(8,128)(2,1)} %get-tuple-element.43.refs_2_, bf16[1024,2048]{1,0:T(8,128)(2,1)} %get-tuple-element.45.refs_3_, ...), custom_call_target="tpu_custom_call" | custom-call | flops 1 | bytes 1 | tf_op jit(solution)/shard_map/pallas_call | solution.py:84
  389.7 17.1 %shard_map.264.refs_5_ = bf16[1536,2048]{1,0:T(8,128)(2,1)} custom-call(bf16[3072,768]{1,0:T(8,128)(2,1)} %get-tuple-element.41.refs_1_.refs_0_, bf16[3072,1024]{1,0:T(8,128)(2,1)} %get-tuple-element.46.refs_1_.refs_2_, bf16[2048,768]{1,0:T(8,128)(2,1)} %all-gather.4.cloned.1.call-done.refs_6_.refs_2_, ...), custom_call_target="tpu_custom_call" | custom-call | flops 1 | bytes 1 | tf_op jit(solution)/shard_map/pallas_call | solution.py:84
  406.8 15.9 %shard_map.265 = (bf16[384,2048]{1,0:T(8,128)(2,1)}, bf16[384,2048]{1,0:T(8,128)(2,1)}, bf16[384,2048]{1,0:T(8,128)(2,1)}, bf16[384,2048]{1,0:T(8,128)(2,1)}) custom-call(bf16[3072,256]{1,0:T(8,128)(2,1)} %get-tuple-element.40.refs_2_.refs_1_.refs_0_, bf16[3072,1024]{1,0:T(8,128)(2,1)} %get-tuple-element.42.refs_0_.refs_3_.refs_1_, ...), custom_call_target="tpu_custom_call" | custom-call | flops 1 | bytes 1 | tf_op jit(solution)/shard_map/pallas_call | solution.py:84
  423.9 20.6 %shard_map.266 = (bf16[384,2048]{1,0:T(8,128)(2,1)}, bf16[384,2048]{1,0:T(8,128)(2,1)}, bf16[384,2048]{1,0:T(8,128)(2,1)}, bf16[384,2048]{1,0:T(8,128)(2,1)}) custom-call(bf16[3072,768]{1,0:T(8,128)(2,1)} %get-tuple-element.41.refs_1_.refs_0_, bf16[3072,1024]{1,0:T(8,128)(2,1)} %get-tuple-element.46.refs_1_.refs_2_, ...), custom_call_target="tpu_custom_call" | custom-call | flops 1 | bytes 1 | tf_op jit(solution)/shard_map/pallas_call | solution.py:84
  446.4 12.2 %collective-permute-done.22.refs_1_ = bf16[384,2048]{1,0:T(8,128)(2,1)S(1)} collective-permute-done((bf16[384,2048]{1,0:T(8,128)(2,1)}, bf16[384,2048]{1,0:T(8,128)(2,1)S(1)}, u32[]{:S(2)}, u32[]{:S(2)}) %collective-permute-start.22) | collective-permute-done | bytes 1572896 | tf_op jit(solution)/shard_map/ppermute | solution.py:42
  459.7 3.8 shard_map.267.refs_2_
  464.7 15.3 %collective-permute-done.25.refs_1_ = bf16[384,2048]{1,0:T(8,128)(2,1)} collective-permute-done((bf16[384,2048]{1,0:T(8,128)(2,1)}, bf16[384,2048]{1,0:T(8,128)(2,1)}, u32[]{:S(2)}, u32[]{:S(2)}) %collective-permute-start.25) | collective-permute-done | bytes 1572896 | tf_op jit(solution)/shard_map/ppermute | solution.py:42
  480.1 2.9 shard_map.268.refs_6_
  484.0 5.7 collective-permute-done.29
  489.7 5.3 all-to-all-start.1
  497.6 37.2 %collective-permute-done.31 = f32[1,1,2,14,128]{4,3,2,1,0:T(8,128)S(1)} collective-permute-done((f32[1,1,2,14,128]{4,3,2,1,0:T(8,128)S(1)}, f32[1,1,2,14,128]{4,3,2,1,0:T(8,128)S(1)}, u32[]{:S(2)}, u32[]{:S(2)}) %collective-permute-start.31) | collective-permute-done | bytes 14368 | tf_op jit(solution)/shard_map/ppermute | solution.py:42
  536.0 19.7 %all-to-all-done.1.refs_0_ = bf16[8,64,768]{2,1,0:T(8,128)(2,1)S(1)} async-done(((bf16[8,64,768]{2,1,0:T(8,128)(2,1)}), bf16[8,64,768]{2,1,0:T(8,128)(2,1)S(1)}, u32[]{:S(2)}, u32[]{:S(2)}) %all-to-all-start.1) | async-done | bytes 786464 | tf_op jit(solution)/shard_map/all_to_all | solution.py:537
  555.8 5.7 all-to-all-start.2
  564.9 4.8 shard_map.269.refs_5_
  570.9 6.4 %shard_map.270.refs_5_ = f32[384,2048]{1,0:T(8,128)} custom-call(bf16[384,2048]{1,0:T(8,128)(2,1)} %refs_0_.7, bf16[384,2048]{1,0:T(8,128)(2,1)} %refs_1_.3, bf16[384,2048]{1,0:T(8,128)(2,1)} %get-tuple-element.51.refs_2_, bf16[384,2048]{1,0:T(8,128)(2,1)} %copy-done.3, bf16[384,2048]{1,0:T(8,128)(2,1)} %collective-permute-done.27.refs_4_, ...), custom_call_target="tpu_custom_call" | custom-call | flops 1 | bytes 1 | tf_op jit(solution)/shard_map/pallas_call | solution.py:84
  577.3 3.5 shard_map.271
  580.8 2.9 shard_map.272
  583.7 3.5 collective-permute-start.33
  592.3 4.1 shard_map.273
  599.2 5.9 collective-permute-done.33
  (205 shorter events, 67.4 us)
Async XLA Ops:
  7.2 216.6 %all-gather.4.cloned.1.call-start = ((), (), s32[]{:S(2)}) async-start(), calls=%async_computation.6 | async-start | bytes 3932160 | tf_op jit(solution)/shard_map/all_gather | solution.py:529
  38.7 201.1 %all-gather.6.cloned.1.call-start = ((), (), s32[]{:S(2)}) async-start(), calls=%async_computation.7 | async-start | bytes 6553600 | tf_op jit(solution)/shard_map/all_gather | solution.py:529
  38.8 7.7 %collective-permute-start.19 = (bf16[64,2048]{1,0:T(8,128)(2,1)S(1)}, bf16[64,2048]{1,0:T(8,128)(2,1)S(1)}, u32[]{:S(2)}, u32[]{:S(2)}) collective-permute-start(bf16[64,2048]{1,0:T(8,128)(2,1)S(1)} %copy-done.22), channel_id=1, source_target_pairs={{0,0},{1,8},{2,16},{3,24},{4,1},{5,9},{6,17},{7,25},{8,2},{9,10},{... | collective-permute-start | bytes 786440 | tf_op jit(solution)/shard_map/ppermute | solution.py:541
  47.7 32.2 %copy-start.23 = (s32[1,3]{1,0:T(1,128)S(1)}, s32[1,3]{1,0:T(1,128)}, u32[]{:S(2)}) copy-start(s32[1,3]{1,0:T(1,128)} %param.16) | copy-start | bytes 40
  47.7 32.2 %copy-start.14 = (bf16[64]{0:T(256)(128)(2,1)S(1)}, bf16[64]{0:T(256)(128)(2,1)}, u32[]{:S(2)}) copy-start(bf16[64]{0:T(256)(128)(2,1)} %param.24) | copy-start | bytes 388
  47.7 32.2 %copy-start.15 = (bf16[64]{0:T(256)(128)(2,1)S(1)}, bf16[64]{0:T(256)(128)(2,1)}, u32[]{:S(2)}) copy-start(bf16[64]{0:T(256)(128)(2,1)} %param.28) | copy-start | bytes 388
  47.7 32.2 %copy-start.16 = (bf16[192]{0:T(256)(128)(2,1)S(1)}, bf16[192]{0:T(256)(128)(2,1)}, u32[]{:S(2)}) copy-start(bf16[192]{0:T(256)(128)(2,1)} %param.22) | copy-start | bytes 1156
  47.7 32.2 %copy-start.17 = (bf16[256]{0:T(256)(128)(2,1)S(1)}, bf16[256]{0:T(256)(128)(2,1)}, u32[]{:S(2)}) copy-start(bf16[256]{0:T(256)(128)(2,1)} %param.26) | copy-start | bytes 1540
  47.8 240.4 %all-gather.8.cloned.1.call-start = ((), (), s32[]{:S(2)}) async-start(), calls=%async_computation.8 | async-start | bytes 5242880 | tf_op jit(solution)/shard_map/all_gather | solution.py:529
  47.8 131.4 %collective-permute-start.13 = (bf16[384,2048]{1,0:T(8,128)(2,1)}, bf16[384,2048]{1,0:T(8,128)(2,1)}, u32[]{:S(2)}, u32[]{:S(2)}) collective-permute-start(bf16[384,2048]{1,0:T(8,128)(2,1)} %refs_0_.7), channel_id=1, source_target_pairs={{0,4},{1,5},{2,6},{3,7},{4,0},{5,1},{6,2},{7,3},{8,12},{9,13},{10,... | collective-permute-start | bytes 4718600 | tf_op jit(solution)/shard_map/ppermute | solution.py:42
  70.7 75.3 %collective-permute-start.12 = (bf16[384,2048]{1,0:T(8,128)(2,1)}, bf16[384,2048]{1,0:T(8,128)(2,1)}, u32[]{:S(2)}, u32[]{:S(2)}) collective-permute-start(bf16[384,2048]{1,0:T(8,128)(2,1)} %refs_0_.7), channel_id=1, source_target_pairs={{0,2},{1,3},{2,0},{3,1},{4,6},{5,7},{6,4},{7,5},{8,10},{9,11},{10,... | collective-permute-start | bytes 4718600 | tf_op jit(solution)/shard_map/ppermute | solution.py:42
  74.8 110.0 %collective-permute-start.3 = (bf16[384,2048]{1,0:T(8,128)(2,1)}, bf16[384,2048]{1,0:T(8,128)(2,1)}, u32[]{:S(2)}, u32[]{:S(2)}) collective-permute-start(bf16[384,2048]{1,0:T(8,128)(2,1)} %shard_map.255.refs_7_), channel_id=1, source_target_pairs={{0,1},{1,0},{2,3},{3,2},{4,5},{5,4},{6,7},{7,6},{8,9},{9,8},{10,11... | collective-permute-start | bytes 4718600 | tf_op jit(solution)/shard_map/ppermute | solution.py:42
  79.9 61.9 %collective-permute-start.1 = (bf16[384,2048]{1,0:T(8,128)(2,1)}, bf16[384,2048]{1,0:T(8,128)(2,1)}, u32[]{:S(2)}, u32[]{:S(2)}) collective-permute-start(bf16[384,2048]{1,0:T(8,128)(2,1)} %shard_map.255.refs_7_), channel_id=1, source_target_pairs={{0,4},{1,5},{2,6},{3,7},{4,0},{5,1},{6,2},{7,3},{8,12},{9,13},{10,... | collective-permute-start | bytes 4718600 | tf_op jit(solution)/shard_map/ppermute | solution.py:42
  80.0 5.5 collective-permute-start.7
  85.6 4.3 collective-permute-start.8
  89.9 4.3 collective-permute-start.9
  94.2 7.9 %collective-permute-start.10 = (bf16[2,2,1,1,2,8,128]{6,5,4,3,2,1,0:T(8,128)(2,1)S(1)}, bf16[2,2,1,1,2,8,128]{6,5,4,3,2,1,0:T(8,128)(2,1)S(1)}, u32[]{:S(2)}, u32[]{:S(2)}) collective-permute-start(bf16[2,2,1,1,2,8,128]{6,5,4,3,2,1,0:T(8,128)(2,1)S(1)} %maximum_select_fusion.5), channel_id=1, source_target_pairs={{0,2},{1,3},{2,0},{3,1},{4,6},{5,7},{6,4},{7,5},{8,10},{9,11},{10,... | collective-permute-start | bytes 49160 | tf_op jit(solution)/shard_map/ppermute | solution.py:42
  94.9 40.4 %copy-start = (bf16[384,2048]{1,0:T(8,128)(2,1)S(1)}, bf16[384,2048]{1,0:T(8,128)(2,1)}, u32[]{:S(2)}) copy-start(bf16[384,2048]{1,0:T(8,128)(2,1)} %shard_map.255.refs_7_) | copy-start | bytes 4718596
  96.0 393.7 %reduce-scatter.4.cloned.1.call-start = ((), (), s32[]{:S(2)}) async-start(), calls=%async_computation.9 | async-start | bytes 3932160 | tf_op jit(solution)/shard_map/reduce_scatter | solution.py:532
  102.1 33.2 %collective-permute-start.11 = (bf16[2,2,1,2,2,8,128]{6,5,4,3,2,1,0:T(8,128)(2,1)S(1)}, bf16[2,2,1,2,2,8,128]{6,5,4,3,2,1,0:T(8,128)(2,1)S(1)}, u32[]{:S(2)}, u32[]{:S(2)}) collective-permute-start(bf16[2,2,1,2,2,8,128]{6,5,4,3,2,1,0:T(8,128)(2,1)S(1)} %maximum_select_fusion.2), channel_id=1, source_target_pairs={{0,4},{1,5},{2,6},{3,7},{4,0},{5,1},{6,2},{7,3},{8,12},{9,13},{10,... | collective-permute-start | bytes 98312 | tf_op jit(solution)/shard_map/ppermute | solution.py:42
  135.3 30.7 %collective-permute-start = (bf16[384,2048]{1,0:T(8,128)(2,1)S(1)}, bf16[384,2048]{1,0:T(8,128)(2,1)S(1)}, u32[]{:S(2)}, u32[]{:S(2)}) collective-permute-start(bf16[384,2048]{1,0:T(8,128)(2,1)S(1)} %copy-done), channel_id=1, source_target_pairs={{0,2},{1,3},{2,0},{3,1},{4,6},{5,7},{6,4},{7,5},{8,10},{9,11},{10,... | collective-permute-start | bytes 4718600 | tf_op jit(solution)/shard_map/ppermute | solution.py:42
  141.7 57.9 %collective-permute-start.2 = (bf16[384,2048]{1,0:T(8,128)(2,1)}, bf16[384,2048]{1,0:T(8,128)(2,1)}, u32[]{:S(2)}, u32[]{:S(2)}) collective-permute-start(bf16[384,2048]{1,0:T(8,128)(2,1)} %collective-permute-done.1), channel_id=1, source_target_pairs={{0,2},{1,3},{2,0},{3,1},{4,6},{5,7},{6,4},{7,5},{8,10},{9,11},{10,... | collective-permute-start | bytes 4718600 | tf_op jit(solution)/shard_map/ppermute | solution.py:42
  145.9 62.7 %collective-permute-start.14 = (bf16[384,2048]{1,0:T(8,128)(2,1)}, bf16[384,2048]{1,0:T(8,128)(2,1)}, u32[]{:S(2)}, u32[]{:S(2)}) collective-permute-start(bf16[384,2048]{1,0:T(8,128)(2,1)} %collective-permute-done.12), channel_id=1, source_target_pairs={{0,4},{1,5},{2,6},{3,7},{4,0},{5,1},{6,2},{7,3},{8,12},{9,13},{10,... | collective-permute-start | bytes 4718600 | tf_op jit(solution)/shard_map/ppermute | solution.py:42
  166.0 45.4 %collective-permute-start.5 = (bf16[384,2048]{1,0:T(8,128)(2,1)}, bf16[384,2048]{1,0:T(8,128)(2,1)S(1)}, u32[]{:S(2)}, u32[]{:S(2)}) collective-permute-start(bf16[384,2048]{1,0:T(8,128)(2,1)} %collective-permute-done.1), channel_id=1, source_target_pairs={{0,1},{1,0},{2,3},{3,2},{4,5},{5,4},{6,7},{7,6},{8,9},{9,8},{10,11... | collective-permute-start | bytes 4718600 | tf_op jit(solution)/shard_map/ppermute | solution.py:42
  179.2 35.5 %collective-permute-start.4 = (bf16[384,2048]{1,0:T(8,128)(2,1)S(1)}, bf16[384,2048]{1,0:T(8,128)(2,1)S(1)}, u32[]{:S(2)}, u32[]{:S(2)}) collective-permute-start(bf16[384,2048]{1,0:T(8,128)(2,1)S(1)} %collective-permute-done), channel_id=1, source_target_pairs={{0,1},{1,0},{2,3},{3,2},{4,5},{5,4},{6,7},{7,6},{8,9},{9,8},{10,11... | collective-permute-start | bytes 4718600 | tf_op jit(solution)/shard_map/ppermute | solution.py:42
  184.7 32.5 %collective-permute-start.15 = (bf16[384,2048]{1,0:T(8,128)(2,1)}, bf16[384,2048]{1,0:T(8,128)(2,1)S(1)}, u32[]{:S(2)}, u32[]{:S(2)}) collective-permute-start(bf16[384,2048]{1,0:T(8,128)(2,1)} %refs_0_.7), channel_id=1, source_target_pairs={{0,1},{1,0},{2,3},{3,2},{4,5},{5,4},{6,7},{7,6},{8,9},{9,8},{10,11... | collective-permute-start | bytes 4718600 | tf_op jit(solution)/shard_map/ppermute | solution.py:42
  199.7 18.9 %collective-permute-start.16 = (bf16[384,2048]{1,0:T(8,128)(2,1)}, bf16[384,2048]{1,0:T(8,128)(2,1)S(1)}, u32[]{:S(2)}, u32[]{:S(2)}) collective-permute-start(bf16[384,2048]{1,0:T(8,128)(2,1)} %collective-permute-done.12), channel_id=1, source_target_pairs={{0,1},{1,0},{2,3},{3,2},{4,5},{5,4},{6,7},{7,6},{8,9},{9,8},{10,11... | collective-permute-start | bytes 4718600 | tf_op jit(solution)/shard_map/ppermute | solution.py:42
  208.7 11.2 %collective-permute-start.17 = (bf16[384,2048]{1,0:T(8,128)(2,1)}, bf16[384,2048]{1,0:T(8,128)(2,1)S(1)}, u32[]{:S(2)}, u32[]{:S(2)}) collective-permute-start(bf16[384,2048]{1,0:T(8,128)(2,1)} %collective-permute-done.13), channel_id=1, source_target_pairs={{0,1},{1,0},{2,3},{3,2},{4,5},{5,4},{6,7},{7,6},{8,9},{9,8},{10,11... | collective-permute-start | bytes 4718600 | tf_op jit(solution)/shard_map/ppermute | solution.py:42
  211.4 9.7 %collective-permute-start.6 = (bf16[384,2048]{1,0:T(8,128)(2,1)}, bf16[384,2048]{1,0:T(8,128)(2,1)S(1)}, u32[]{:S(2)}, u32[]{:S(2)}) collective-permute-start(bf16[384,2048]{1,0:T(8,128)(2,1)} %collective-permute-done.2), channel_id=1, source_target_pairs={{0,1},{1,0},{2,3},{3,2},{4,5},{5,4},{6,7},{7,6},{8,9},{9,8},{10,11... | collective-permute-start | bytes 4718600 | tf_op jit(solution)/shard_map/ppermute | solution.py:42
  214.7 7.7 %collective-permute-start.18 = (bf16[384,2048]{1,0:T(8,128)(2,1)}, bf16[384,2048]{1,0:T(8,128)(2,1)S(1)}, u32[]{:S(2)}, u32[]{:S(2)}) collective-permute-start(bf16[384,2048]{1,0:T(8,128)(2,1)} %collective-permute-done.14), channel_id=1, source_target_pairs={{0,1},{1,0},{2,3},{3,2},{4,5},{5,4},{6,7},{7,6},{8,9},{9,8},{10,11... | collective-permute-start | bytes 4718600 | tf_op jit(solution)/shard_map/ppermute | solution.py:42
  276.2 279.6 %reduce-scatter.6.cloned.1.call-start = ((), (), s32[]{:S(2)}) async-start(), calls=%async_computation.10 | async-start | bytes 5242880 | tf_op jit(solution)/shard_map/reduce_scatter | solution.py:532
  375.4 205.4 %reduce-scatter.8.cloned.1.call-start = ((), (), s32[]{:S(2)}) async-start(), calls=%async_computation.11 | async-start | bytes 6553600 | tf_op jit(solution)/shard_map/reduce_scatter | solution.py:532
  389.0 17.8 %collective-permute-start.20 = (bf16[1536,2048]{1,0:T(8,128)(2,1)}, bf16[1536,2048]{1,0:T(8,128)(2,1)}, u32[]{:S(2)}, u32[]{:S(2)}) collective-permute-start(bf16[1536,2048]{1,0:T(8,128)(2,1)} %shard_map.263.refs_6_), channel_id=1, source_target_pairs={{0,1},{1,0},{2,3},{3,2},{4,5},{5,4},{6,7},{7,6},{8,9},{9,8},{10,11... | collective-permute-start | bytes 18874376 | tf_op jit(solution)/shard_map/ppermute | solution.py:42
  406.7 17.2 %collective-permute-start.23 = (bf16[1536,2048]{1,0:T(8,128)(2,1)}, bf16[1536,2048]{1,0:T(8,128)(2,1)}, u32[]{:S(2)}, u32[]{:S(2)}) collective-permute-start(bf16[1536,2048]{1,0:T(8,128)(2,1)} %shard_map.264.refs_5_), channel_id=1, source_target_pairs={{0,1},{1,0},{2,3},{3,2},{4,5},{5,4},{6,7},{7,6},{8,9},{9,8},{10,11... | collective-permute-start | bytes 18874376 | tf_op jit(solution)/shard_map/ppermute | solution.py:42
  422.7 35.8 %collective-permute-start.22 = (bf16[384,2048]{1,0:T(8,128)(2,1)}, bf16[384,2048]{1,0:T(8,128)(2,1)S(1)}, u32[]{:S(2)}, u32[]{:S(2)}) collective-permute-start(bf16[384,2048]{1,0:T(8,128)(2,1)} %get-tuple-element.50), channel_id=1, source_target_pairs={{0,2},{1,3},{2,0},{3,1},{4,6},{5,7},{6,4},{7,5},{8,10},{9,11},{10,... | collective-permute-start | bytes 4718600 | tf_op jit(solution)/shard_map/ppermute | solution.py:42
  444.5 35.6 %collective-permute-start.25 = (bf16[384,2048]{1,0:T(8,128)(2,1)}, bf16[384,2048]{1,0:T(8,128)(2,1)}, u32[]{:S(2)}, u32[]{:S(2)}) collective-permute-start(bf16[384,2048]{1,0:T(8,128)(2,1)} %get-tuple-element.53), channel_id=1, source_target_pairs={{0,4},{1,5},{2,6},{3,7},{4,0},{5,1},{6,2},{7,3},{8,12},{9,13},{10,... | collective-permute-start | bytes 4718600 | tf_op jit(solution)/shard_map/ppermute | solution.py:42
  445.8 37.4 %collective-permute-start.28 = (f32[30,128]{1,0:T(8,128)S(1)}, f32[30,128]{1,0:T(8,128)S(1)}, u32[]{:S(2)}, u32[]{:S(2)}) collective-permute-start(f32[30,128]{1,0:T(8,128)S(1)} %bitcast.87), channel_id=1, source_target_pairs={{0,8},{1,9},{2,10},{3,11},{4,12},{5,13},{6,14},{7,15},{8,0},{9,1},... | collective-permute-start | bytes 46088 | tf_op jit(solution)/shard_map/ppermute | solution.py:42
  445.8 119.1 %collective-permute-start.21 = (bf16[384,2048]{1,0:T(8,128)(2,1)}, bf16[384,2048]{1,0:T(8,128)(2,1)}, u32[]{:S(2)}, u32[]{:S(2)}) collective-permute-start(bf16[384,2048]{1,0:T(8,128)(2,1)} %get-tuple-element.48), channel_id=1, source_target_pairs={{0,2},{1,3},{2,0},{3,1},{4,6},{5,7},{6,4},{7,5},{8,10},{9,11},{10,... | collective-permute-start | bytes 4718600 | tf_op jit(solution)/shard_map/ppermute | solution.py:42
  446.2 123.6 %collective-permute-start.26 = (bf16[384,2048]{1,0:T(8,128)(2,1)}, bf16[384,2048]{1,0:T(8,128)(2,1)S(1)}, u32[]{:S(2)}, u32[]{:S(2)}) collective-permute-start(bf16[384,2048]{1,0:T(8,128)(2,1)} %get-tuple-element.54), channel_id=1, source_target_pairs={{0,4},{1,5},{2,6},{3,7},{4,0},{5,1},{6,2},{7,3},{8,12},{9,13},{10,... | collective-permute-start | bytes 4718600 | tf_op jit(solution)/shard_map/ppermute | solution.py:42
  463.5 101.4 %collective-permute-start.24 = (bf16[384,2048]{1,0:T(8,128)(2,1)}, bf16[384,2048]{1,0:T(8,128)(2,1)}, u32[]{:S(2)}, u32[]{:S(2)}) collective-permute-start(bf16[384,2048]{1,0:T(8,128)(2,1)} %shard_map.267.refs_2_), channel_id=1, source_target_pairs={{0,4},{1,5},{2,6},{3,7},{4,0},{5,1},{6,2},{7,3},{8,12},{9,13},{10,... | collective-permute-start | bytes 4718600 | tf_op jit(solution)/shard_map/ppermute | solution.py:42
  483.0 86.8 %collective-permute-start.27 = (bf16[384,2048]{1,0:T(8,128)(2,1)}, bf16[384,2048]{1,0:T(8,128)(2,1)}, u32[]{:S(2)}, u32[]{:S(2)}) collective-permute-start(bf16[384,2048]{1,0:T(8,128)(2,1)} %shard_map.268.refs_6_), channel_id=1, source_target_pairs={{0,2},{1,3},{2,0},{3,1},{4,6},{5,7},{6,4},{7,5},{8,10},{9,11},{10,... | collective-permute-start | bytes 4718600 | tf_op jit(solution)/shard_map/ppermute | solution.py:42
  483.2 6.5 %collective-permute-start.29 = (f32[30,128]{1,0:T(8,128)S(1)}, f32[30,128]{1,0:T(8,128)S(1)}, u32[]{:S(2)}, u32[]{:S(2)}) collective-permute-start(f32[30,128]{1,0:T(8,128)S(1)} %bitcast_add_fusion), channel_id=1, source_target_pairs={{0,16},{1,17},{2,18},{3,19},{4,20},{5,21},{6,22},{7,23},{8,24},{9,... | collective-permute-start | bytes 46088 | tf_op jit(solution)/shard_map/ppermute | solution.py:42
  489.7 66.1 %all-to-all-start.1 = ((bf16[8,64,768]{2,1,0:T(8,128)(2,1)}), bf16[8,64,768]{2,1,0:T(8,128)(2,1)S(1)}, u32[]{:S(2)}, u32[]{:S(2)}) async-start(bf16[8,64,768]{2,1,0:T(8,128)(2,1)} %bitcast.77), calls=%async_computation.2 | async-start | bytes 1572864 | tf_op jit(solution)/shard_map/all_to_all | solution.py:537
  495.0 1.2 collective-permute-start.30
  496.2 38.6 %collective-permute-start.31 = (f32[1,1,2,14,128]{4,3,2,1,0:T(8,128)S(1)}, f32[1,1,2,14,128]{4,3,2,1,0:T(8,128)S(1)}, u32[]{:S(2)}, u32[]{:S(2)}) collective-permute-start(f32[1,1,2,14,128]{4,3,2,1,0:T(8,128)S(1)} %maximum_select_fusion.7), channel_id=1, source_target_pairs={{0,2},{1,3},{2,0},{3,1},{4,6},{5,7},{6,4},{7,5},{8,10},{9,11},{10,... | collective-permute-start | bytes 43016 | tf_op jit(solution)/shard_map/ppermute | solution.py:42
  534.8 29.5 %collective-permute-start.32 = (f32[1,2,2,14,128]{4,3,2,1,0:T(8,128)S(1)}, f32[1,2,2,14,128]{4,3,2,1,0:T(8,128)S(1)}, u32[]{:S(2)}, u32[]{:S(2)}) collective-permute-start(f32[1,2,2,14,128]{4,3,2,1,0:T(8,128)S(1)} %maximum_select_fusion.3), channel_id=1, source_target_pairs={{0,4},{1,5},{2,6},{3,7},{4,0},{5,1},{6,2},{7,3},{8,12},{9,13},{10,... | collective-permute-start | bytes 86024 | tf_op jit(solution)/shard_map/ppermute | solution.py:42
  555.8 35.6 %all-to-all-start.2 = ((bf16[8,64,1024]{2,1,0:T(8,128)(2,1)}), bf16[8,64,1024]{2,1,0:T(8,128)(2,1)S(1)}, u32[]{:S(2)}, u32[]{:S(2)}) async-start(bf16[8,64,1024]{2,1,0:T(8,128)(2,1)} %bitcast.76), calls=%async_computation.4 | async-start | bytes 2097152 | tf_op jit(solution)/shard_map/all_to_all | solution.py:537
  583.7 21.5 %collective-permute-start.33 = (bf16[64,2048]{1,0:T(8,128)(2,1)}, bf16[64,2048]{1,0:T(8,128)(2,1)S(1)}, u32[]{:S(2)}, u32[]{:S(2)}) collective-permute-start(bf16[64,2048]{1,0:T(8,128)(2,1)} %get-tuple-element.64), channel_id=1, source_target_pairs={{0,0},{8,1},{16,2},{24,3},{1,4},{9,5},{17,6},{25,7},{2,8},{10,9},{... | collective-permute-start | bytes 786440 | tf_op jit(solution)/shard_map/ppermute | solution.py:696
  (19 other events, 278.1 us)
Sparse Core Ops, SparseCore 0:
  38.8 69.2 all-gather.3
  110.3 97.2 all-gather.5
  209.1 78.9 all-gather.7
  290.9 58.5 reduce-scatter.3
  375.5 75.2 reduce-scatter.5
  453.1 95.0 reduce-scatter.7

commit v4 on v3

--- a/solution.py
+++ b/solution.py
@@ -57,14 +57,16 @@
     return value.reshape((-1,) + rest)
 
 
-def gather_tokens(value, plan, last):
-    pieces = {0: value}
-    for bit in (1, 2):
-        pieces[1 << bit] = swap(value, bit, plan)
-    pieces[6] = swap(pieces[1 << (3 - last)], last, plan)
+def own_pieces(value, plan):
+    return {0: value, 2: swap(value, 1, plan), 4: swap(value, 2, plan)}
+
+
+def all_pieces(pieces, passed, bit, plan):
+    pieces = dict(pieces)
+    pieces[6] = swap(passed, bit, plan)
     for mask in (0, 2, 4, 6):
         pieces[mask | 1] = swap(pieces[mask], 0, plan)
-    return jnp.concatenate([pieces[mask] for mask in ORDER])
+    return [(pieces[mask], 0) for mask in ORDER]
 
 
 class Chain:
@@ -143,13 +145,23 @@
     return lax.dot_general(left, right, PAIRED, preferred_element_type=jnp.float32)
 
 
-def over_blocks(chain, kernel, slots, blocked, known, outs, sums=(), rows=None):
-    count = blocked[0].shape[0] // slots
+def over_blocks(chain, kernel, slots, pieces, blocked, known, outs, sums=(), rows=None):
+    count = HEADS
     gathered, runs = rows or (None, [])
     extra = [gathered] if runs else []
 
     def body(*refs):
-        given = len(blocked) + len(known)
+        refs = list(refs)
+        if pieces:
+            held = refs.pop()
+            for step, piece in enumerate(refs[: len(pieces)]):
+
+                @pl.when(pl.program_id(0) == step)
+                def _(piece=piece):
+                    held[...] = piece[...]
+
+            refs = [held] + refs[len(pieces) :]
+        given = bool(pieces) + len(blocked) + len(known)
         if not runs:
             kernel(*refs)
             return
@@ -175,18 +187,31 @@
         shape = (sum(many for _, many in runs), gathered.shape[1])
         shapes.append((shape, jnp.bfloat16))
         specs.append(pl.BlockSpec(shape, lambda i: (0, 0)))
+    def once(item):
+        return pl.BlockSpec(item.shape, lambda i: (0, 0), pipeline_mode=pl.Buffered(1))
+
+    options = {}
+    if pieces:
+        item = pieces[0][0]
+        options["scratch_shapes"] = [pltpu.VMEM((slots, item.shape[1]), item.dtype)]
     return chain.launch(
         body,
-        [*blocked, *known, *extra],
-        [moving(item.shape[1]) for item in blocked]
+        [*[item for item, _ in pieces], *blocked, *known, *extra],
+        [
+            pl.BlockSpec(
+                (slots, item.shape[1]),
+                lambda i, place=place: (place, 0),
+                pipeline_mode=pl.Buffered(1),
+            )
+            for item, place in pieces
+        ]
+        + [moving(item.shape[1]) for item in blocked]
         + [whole(item) for item in known]
-        + [
-            pl.BlockSpec(item.shape, lambda i: (0, 0), pipeline_mode=pl.Buffered(1))
-            for item in extra
-        ],
+        + [once(item) for item in extra],
         shapes,
         specs,
         (count,),
+        **options,
     )
 
 
@@ -215,37 +240,59 @@
         if not split:
             outs[0][...] = total.astype(jnp.bfloat16)
             return
-        for step, out in enumerate(outs):
+        for step, out in enumerate(outs[:3]):
 
             @pl.when(pl.program_id(0) == step)
             def _(out=out):
                 out[...] = total.astype(jnp.bfloat16)
 
-    outs = 4 if split else 1
-    shape = (slots if split else 4 * slots, width)
+        @pl.when(pl.program_id(0) == 3)
+        def _():
+            outs[3][...] = total[:, : width // 2].astype(jnp.bfloat16)
+            outs[4][...] = total[:, width // 2 :].astype(jnp.bfloat16)
+
+    if split:
+        shapes = [(slots, width)] * 3 + [(slots, width // 2)] * 2
+    else:
+        shapes = [(4 * slots, width)]
     return chain.launch(
         kernel,
         [*blocked, *known, *extra],
         [pl.BlockSpec((slots, item.shape[1]), lambda i: (i + 4 * place, 0)) for item in blocked]
         + [whole(item) for item in known]
         + [pl.BlockSpec((slots, width), lambda i: (i, 0)) for _ in extra],
-        [(shape, jnp.bfloat16)] * outs,
-        [pl.BlockSpec((slots, width), lambda i: (0 if split else i, 0)) for _ in range(outs)],
+        [(shape, jnp.bfloat16) for shape in shapes],
+        [pl.BlockSpec((slots, shape[1]), lambda i: (0 if split else i, 0)) for shape in shapes],
         (4,),
     )
 
 
-def join(chain, one, two, kind):
-    rows, width = one.shape
-    tile = rows // 2 if rows % 32 == 0 else rows
-
-    def kernel(one, two, out):
-        out[...] = (one[...].astype(jnp.float32) + two[...].astype(jnp.float32)).astype(kind)
-
-    spec = pl.BlockSpec((tile, width), lambda i: (i, 0))
-    return chain.launch(
-        kernel, [one, two], [spec, spec], [((rows, width), kind)], [spec], (rows // tile,)
-    )[0]
+def pass_terms(chain, of_x, of_y, left, right):
+    rows, width = of_x.shape
+    half = width // 2
+
+    def add(one, two):
+        return (one.astype(jnp.float32) + two.astype(jnp.float32)).astype(jnp.bfloat16)
+
+    def kernel(of_x, of_y, left, right, to_x, to_y):
+        to_x[:, :half] = of_x[:, :half]
+        to_x[:, half:] = add(of_x[:, half:], right[...])
+        to_y[:, :half] = add(of_y[:, :half], left[...])
+        to_y[:, half:] = of_y[:, half:]
+
+    tile = rows // 2
+
+    def spec(columns):
+        return pl.BlockSpec((tile, columns), lambda i: (i, 0))
+
+    return chain.launch(
+        kernel,
+        [of_x, of_y, left, right],
+        [spec(width), spec(width), spec(half), spec(half)],
+        [((rows, width), jnp.bfloat16)] * 2,
+        [spec(width)] * 2,
+        (2,),
+    )
 
 
 def split_output(chain, reduced, units, rows):
@@ -308,12 +355,57 @@
     )[0]
 
 
-def norm_kernel(rows, out):
-    out[...] = norm_terms(rows[...].astype(jnp.float32))[0].astype(jnp.bfloat16)
-
-
-def scaled(normed, gain, shift):
-    return (normed[...].astype(jnp.float32) * gain[...] + shift[...]).astype(jnp.bfloat16)
+def split_columns(chain, value, split):
+    rows, width = value.shape
+    tile = rows // 4
+
+    def kernel(value, one, two):
+        one[...] = value[:, :split]
+        two[...] = value[:, split:]
+
+    def spec(columns):
+        return pl.BlockSpec((tile, columns), lambda i: (i, 0))
+
+    sizes = [split, width - split]
+    return chain.launch(
+        kernel,
+        [value],
+        [spec(width)],
+        [((rows, size), value.dtype) for size in sizes],
+        [spec(size) for size in sizes],
+        (4,),
+    )
+
+
+def laid_together(chain, values):
+    rows, width = values[0].shape
+
+    def kernel(*refs):
+        for step, value in enumerate(refs[:-1]):
+
+            @pl.when(pl.program_id(0) == step)
+            def _(value=value):
+                refs[-1][...] = value[...]
+
+    return chain.launch(
+        kernel,
+        values,
+        [
+            pl.BlockSpec((rows, width), lambda i: (0, 0), pipeline_mode=pl.Buffered(1))
+            for _ in values
+        ],
+        [((len(values) * rows, width), values[0].dtype)],
+        [pl.BlockSpec((rows, width), lambda i: (i, 0))],
+        (len(values),),
+    )[0]
+
+
+def copied(chain, value):
+    def kernel(value, out):
+        out[...] = value[...]
+
+    spec = pl.BlockSpec((value.shape[0] // 4, value.shape[1]), lambda i: (i, 0))
+    return chain.launch(kernel, [value], [spec], [(value.shape, value.dtype)], [spec], (4,))[0]
 
 
 def turn(value, cosine, sine, half):
@@ -332,8 +424,15 @@
     out[:, at + lanes : at + value.shape[1]] = value[:, lanes:].astype(jnp.bfloat16)
 
 
-def qkv_kernel(head_dim, normed, cosine, sine, gain, shift, bias, weight, out):
-    projected = times(scaled(normed, gain, shift), weight[...]) + bias[...]
+def norm_kernel(tokens, gain_one, shift_one, gain_two, shift_two, low_one, low_two, low):
+    normed, _ = norm_terms(tokens[...].astype(jnp.float32))
+    low_one[...] = (normed * gain_one[...] + shift_one[...]).astype(jnp.bfloat16)
+    low_two[...] = (normed * gain_two[...] + shift_two[...]).astype(jnp.bfloat16)
+    low[...] = normed.astype(jnp.bfloat16)
+
+
+def qkv_kernel(head_dim, x, cosine, sine, bias, weight, out):
+    projected = times(x[...], weight[...]) + bias[...]
     half = head_dim // 8
     for part in range(2):
         at = part * head_dim
@@ -341,19 +440,22 @@
     out[:, 2 * head_dim :] = projected[:, 2 * head_dim :].astype(jnp.bfloat16)
 
 
-def expand_kernel(normed, gain, shift, bias, weight, active, slope):
-    hidden = times(scaled(normed, gain, shift), weight[...]) + bias[...]
+def expand_kernel(x, bias, weight, active, slope):
+    hidden = times(x[...], weight[...]) + bias[...]
     below = 0.5 * (1.0 + lax.erf(hidden * math.sqrt(0.5)))
     density = jnp.exp(-0.5 * hidden * hidden) * (1.0 / math.sqrt(2.0 * math.pi))
     active[...] = (hidden * below).astype(jnp.bfloat16)
     slope[...] = below + hidden * density
 
 
-def grad_hidden_kernel(cotangent, slope, weight, out, out_sum, cotangent_sum):
+def grad_hidden_kernel(
+    cotangent, slope, weight, out, cotangent_out, out_sum, cotangent_sum
+):
     grad = (times_paired(cotangent[...], weight[...]) * slope[...]).astype(jnp.bfloat16)
     out[...] = grad
     add_columns(out_sum, grad)
     add_columns(cotangent_sum, cotangent[...])
+    cotangent_out[...] = cotangent[...]
 
 
 def branch_terms(attn, active, dense, contract):
@@ -365,7 +467,17 @@
 
 
 def attend_kernel(
-    head_dim, qkv, cotangent, cosine, sine, segment, segments, dense, attn, grad_qkv, grad_sum
+    head_dim,
+    qkv,
+    cotangent,
+    cosine,
+    sine,
+    segment,
+    segments,
+    dense,
+    attn,
+    grad_qkv,
+    grad_sum,
 ):
     scale = 1.0 / math.sqrt(head_dim)
     query = qkv[:, :head_dim]
@@ -539,9 +651,30 @@
     to_slot = [(d, plan.device(d % groups, d // groups)) for d in range(count)]
     from_slot = [(target, source) for source, target in to_slot]
     dense_part = lax.ppermute(dense_weight, "dp", to_slot)
-    weight_out = gather(jnp.concatenate([contract_weight, dense_part]))
+    out_part = jnp.concatenate([contract_weight, dense_part])
+    weight_out = gather(out_part)
+    chain.settle(out_part)
     contract_runs = [(group * (units + rows), units) for group in range(groups)]
     dense_runs = [(group * (units + rows) + units, rows) for group in range(groups)]
+
+    own_tokens = own_pieces(tokens, plan)
+
+    parts = [
+        ln1_gain,
+        ln1_bias,
+        ln2_gain,
+        ln2_bias,
+        dense_bias,
+        contract_bias,
+        qkv_bias,
+        expand_bias,
+        seq_lengths[0].astype(jnp.bfloat16),
+    ]
+    sizes = [item.shape[0] for item in parts]
+    lines = -(-sum(sizes) // 1024) * 8
+    small = jnp.concatenate(parts + [jnp.zeros((lines * 128 - sum(sizes),), jnp.bfloat16)])
+    every = gather_small(small.reshape(lines, 128), outer_bits + (0, 2, 1), me, plan)
+    every = every.reshape(count, lines * 128).astype(jnp.float32)
 
     expand_places = [
         (s, group * units, plan.device(group, s) * units, units)
@@ -557,38 +690,9 @@
     moves = [(s, at, 0, column, many) for s, at, column, many in qkv_places]
     moves += [(s, split + at, 1, column, many) for s, at, column, many in expand_places]
     own = exchange(pack(chain, [qkv_weight, expand_weight], moves, split + hidden_units))
-    own = own.reshape(HEADS * rows, -1)
-    weight_qkv = gather(own[:, :split])
-    weight_expand = gather(own[:, split:])
-
-    tile = slots // 4
-    own_normed = chain.launch(
-        norm_kernel,
-        [tokens],
-        [pl.BlockSpec((tile, width), lambda i: (i, 0))],
-        [((slots, width), jnp.bfloat16)],
-        [pl.BlockSpec((tile, width), lambda i: (i, 0))],
-        (slots // tile,),
-    )[0]
-    normed = gather_tokens(own_normed, plan, 1)
-    group_cotangent = gather_tokens(cotangent, plan, 2)
-
-    parts = [
-        ln1_gain,
-        ln1_bias,
-        ln2_gain,
-        ln2_bias,
-        dense_bias,
-        contract_bias,
-        qkv_bias,
-        expand_bias,
-        seq_lengths[0].astype(jnp.bfloat16),
-    ]
-    sizes = [item.shape[0] for item in parts]
-    lines = -(-sum(sizes) // 1024) * 8
-    small = jnp.concatenate(parts + [jnp.zeros((lines * 128 - sum(sizes),), jnp.bfloat16)])
-    every = gather_small(small.reshape(lines, 128), outer_bits + (0, 1, 2), me, plan)
-    every = every.reshape(count, lines * 128).astype(jnp.float32)
+    token_pieces = all_pieces(own_tokens, own_tokens[4], 1, plan)
+    own_cotangent = own_pieces(cotangent, plan)
+    early = [weight_out] + [piece for piece, _ in token_pieces[1:]]
     taken, at = [], 0
     for size in sizes:
         taken.append(every[:, at : at + size])
@@ -607,61 +711,95 @@
     ).astype(jnp.int32)
     segment, position = jax.vmap(lambda item: slot_layout(item, slots))(lengths)
     cosine, sine = rotary_tables(position.reshape(-1), rotated, head_dim // 2)
+    chain.settle(cosine, *early)
+    qkv_own, expand_own = split_columns(chain, own.reshape(HEADS * rows, -1), split)
+    weight_expand, weight_qkv = gather(expand_own), gather(qkv_own)
 
     def sum_begin(compute, blocked, known):
         terms = terms_of(chain, compute, slots, width, 1, blocked, known, None, False)[0]
         return swap(terms, 0, plan)
 
-    def sum_next(compute, blocked, known, got, near):
-        own, of_x, of_y, of_both = terms_of(
+    def sum_next(compute, blocked, known, got):
+        own, of_x, of_y, left, right = terms_of(
             chain, compute, slots, width, 0, blocked, known, got, True
         )
-        of_near, of_far = (of_x, of_y) if near == 1 else (of_y, of_x)
-        return own, swap(of_both, near, plan), swap(of_near, near, plan), of_far
-
-    def sum_last(own, from_both, from_near, of_far, near):
-        of_far = join(chain, of_far, from_both, jnp.bfloat16)
-        return own, from_near, swap(of_far, 3 - near, plan)
+        return own, of_x, of_y, swap(left, 1, plan), swap(right, 2, plan)
+
+    def sum_last(own, *parts):
+        to_x, to_y = pass_terms(chain, *parts)
+        return own, swap(to_x, 1, plan), swap(to_y, 2, plan)
+
+    low_one, low_two, normed = over_blocks(
+        chain,
+        norm_kernel,
+        slots,
+        token_pieces,
+        [],
+        [gain_one, shift_one, gain_two, shift_two],
+        [(width, jnp.bfloat16)] * 3,
+    )
+
+    passed = swap(copied(chain, own_cotangent[2]), 2, plan)
+    half = laid_together(
+        chain, [own_cotangent[0], own_cotangent[2], own_cotangent[4], passed]
+    )
+    other_half = swap(half, 0, plan)
+    cotangent_pieces = [(item, place) for item in (half, other_half) for place in range(4)]
+
+    active, slope = over_blocks(
+        chain,
+        expand_kernel,
+        slots,
+        [],
+        [low_two],
+        [bias_expand, weight_expand],
+        [(hidden_units, jnp.bfloat16), (hidden_units, jnp.float32)],
+    )
+    grad_hidden, group_cotangent, hidden_sum, cotangent_sum, weight_contract = over_blocks(
+        chain,
+        grad_hidden_kernel,
+        slots,
+        cotangent_pieces,
+        [slope],
+        [],
+        [(hidden_units, jnp.bfloat16), (width, jnp.bfloat16)],
+        [hidden_units, width],
+        (weight_out, contract_runs),
+    )
+    expand_got = reduce(input_terms(chain, normed, grad_hidden))
 
     (qkv,) = over_blocks(
         chain,
         lambda *refs: qkv_kernel(head_dim, *refs),
         slots,
-        [normed, cosine, sine],
-        [gain_one, shift_one, bias_qkv, weight_qkv],
+        [],
+        [low_one, cosine, sine],
+        [bias_qkv, weight_qkv],
         [(split, jnp.bfloat16)],
     )
     attn, grad_qkv, qkv_sum, weight_dense = over_blocks(
         chain,
         lambda *refs: attend_kernel(head_dim, *refs),
         slots,
+        [],
         [qkv, group_cotangent, cosine, sine, segment.reshape(-1, 1)],
         [segment],
         [(head_dim, jnp.bfloat16), (split, jnp.bfloat16)],
         [split],
         (weight_out, dense_runs),
     )
+
+
+    branch_of = branch_terms, [attn, active], [weight_dense, weight_contract]
+    norm_of = (
+        norm_grad_terms,
+        [grad_qkv, grad_hidden],
+        [weight_qkv, weight_expand, gain_one, gain_two],
+    )
+    branch_got = sum_begin(*branch_of)
+    norm_got = sum_begin(*norm_of)
     qkv_got = reduce(input_terms(chain, normed, grad_qkv))
-    active, slope = over_blocks(
-        chain,
-        expand_kernel,
-        slots,
-        [normed],
-        [gain_two, shift_two, bias_expand, weight_expand],
-        [(hidden_units, jnp.bfloat16), (hidden_units, jnp.float32)],
-    )
-    output_got = reduce(output_terms(chain, active, attn, groups, group_cotangent))
-    grad_hidden, hidden_sum, cotangent_sum, weight_contract = over_blocks(
-        chain,
-        grad_hidden_kernel,
-        slots,
-        [group_cotangent, slope],
-        [],
-        [(hidden_units, jnp.bfloat16)],
-        [hidden_units, width],
-        (weight_out, contract_runs),
-    )
-    expand_got = reduce(input_terms(chain, normed, grad_hidden))
+    branch = sum_next(*branch_of, branch_got)
 
     sums = jnp.concatenate([qkv_sum, hidden_sum, cotangent_sum], axis=1).reshape(-1, 128)
     for bit in outer_bits:
@@ -670,33 +808,27 @@
     bias_out_grad = lax.dynamic_slice_in_dim(
         sums[own_lines:].reshape(-1), me * (width // count), width // count
     )
-    sums = gather_small(sums[:own_lines], (0, 1, 2), me, plan).reshape(HEADS, -1)
+    sums = gather_small(sums[:own_lines], (0, 1, 2), me, plan)
+    chain.settle(sums)
+    sums = sums.reshape(HEADS, -1)
     qkv_sums, expand_sums = sums[:, :split], sums[:, split:]
 
-    branch_of = branch_terms, [attn, active], [weight_dense, weight_contract]
-    norm_of = (
-        norm_grad_terms,
-        [grad_qkv, grad_hidden],
-        [weight_qkv, weight_expand, gain_one, gain_two],
-    )
-    branch_got = sum_begin(*branch_of)
-    norm_got = sum_begin(*norm_of)
-    branch = sum_next(*branch_of, branch_got, 1)
-    norm_parts = sum_next(*norm_of, norm_got, 2)
-    branch = sum_last(*branch, 1)
-    norm_parts = sum_last(*norm_parts, 2)
+    branch = sum_last(*branch)
+    output_got = reduce(output_terms(chain, active, attn, groups, group_cotangent))
+    norm_parts = sum_next(*norm_of, norm_got)
     layer_out = finish_output(chain, tokens, *branch, bias_dense, bias_contract)
+    expand_got = exchange(expand_got.reshape(HEADS, rows, hidden_units))
+    qkv_got = exchange(qkv_got.reshape(HEADS, rows, split))
+    chain.settle(expand_got)
+    norm_parts = sum_last(*norm_parts)
+    expand_weight_grad, ln2_gain_grad, ln2_bias_grad = unpack(
+        chain, expand_places, expand_got, expand_sums, expand_weight, ln2_gain, ln2_bias
+    )
+    contract_weight_grad, dense_grad = split_output(chain, output_got, units, rows)
+    dense_weight_grad = lax.ppermute(dense_grad, "dp", from_slot).astype(jnp.float32)
     input_grad = finish_input(chain, cotangent, tokens, *norm_parts)
-
-    qkv_got = exchange(qkv_got.reshape(HEADS, rows, split))
     qkv_weight_grad, ln1_gain_grad, ln1_bias_grad = unpack(
         chain, qkv_places, qkv_got, qkv_sums, qkv_weight, ln1_gain, ln1_bias
-    )
-    contract_weight_grad, dense_grad = split_output(chain, output_got, units, rows)
-    dense_weight_grad = lax.ppermute(dense_grad, "dp", from_slot).astype(jnp.float32)
-    expand_got = exchange(expand_got.reshape(HEADS, rows, hidden_units))
-    expand_weight_grad, ln2_gain_grad, ln2_bias_grad = unpack(
-        chain, expand_places, expand_got, expand_sums, expand_weight, ln2_gain, ln2_bias
     )
     qkv_bias_grad = qkv_sums.reshape(HEADS, 3, head_dim).transpose(1, 0, 2).reshape(3 * width)
     per = qkv_bias.shape[0]

time: 618 us -> 602 us (0.974)
  Pallas kernels: 241 us -> 280 us
  blocking collectives: 27.7 us -> 0 us
  local copies, waits for them, and re-layouts: 50.9 us -> 26.8 us
  starting transfers between devices: 86.3 us -> 67.1 us
  waiting for transfers between devices: 178 us -> 185 us
    pallas_call x20 -> x23, Pallas kernels: 241 us -> 280 us  [launch(): pl.pallas_call(body, grid_spec=pltpu.PrefetchScalarGridSpec(num_scalar_pr...]
    all_to_all x1 -> x0, blocking collectives: 27.7 us -> none  [exchange(): lax.all_to_all(value, 'dp', 0, 0, tiled=True, axis_index_groups=sharing)]
    ppermute x32 -> x31, waiting for transfers between devices: 139 us -> 164 us  [swap(): return lax.ppermute(value, 'dp', plan.flip(bit))]
    ppermute x32 -> x31, starting transfers between devices: 66.1 us -> 41.9 us  [swap(): return lax.ppermute(value, 'dp', plan.flip(bit))]
    unnamed x70 -> x87, local copies, waits for them, and re-layouts: 35.3 us -> 12.9 us
    all_to_all x2 -> x3, waiting for transfers between devices: 19.8 us -> 8.49 us  [exchange(): lax.all_to_all(value, 'dp', 0, 0, tiled=True, axis_index_groups=sharing)]
    all_gather x3, waiting for transfers between devices: 9.72 us -> 0.02 us  [gather(): lax.all_gather(value, 'dp', axis=0, tiled=True, axis_index_groups=across)]
    reduce_scatter x3, waiting for transfers between devices: 0.02 us -> 9.25 us  [reduce(): lax.psum_scatter(value, 'dp', scatter_dimension=0, tiled=True, axis_index...]
  transfers between devices with their start and end apart: 42 -> 42, of which waited for: 15 -> 22; matrix products, arithmetic and copies ran while one was open for 10% -> 6% of each run, Pallas kernels for 39% -> 47%
where the time goes in v4:
time: 602 us; the launch traced here: 592 us
  Pallas kernels  280 us (47%)
  waiting for transfers between devices  185 us (31%)
  starting transfers between devices  67.1 us (11%)
  local copies, waits for them, and re-layouts  26.8 us (4%)
  other arithmetic  18.8 us (3%)
  between operations  14.9 us (2%)
    pallas_call x23, Pallas kernels, launch(): pl.pallas_call(body, grid_spec=pltpu.PrefetchScalarGridSpec(num_scalar_pr...  280 us
    ppermute x31, waiting for transfers between devices, swap(): return lax.ppermute(value, 'dp', plan.flip(bit))  164 us
    ppermute x31, starting transfers between devices, swap(): return lax.ppermute(value, 'dp', plan.flip(bit))  41.9 us
    all_to_all x3, starting transfers between devices, exchange(): lax.all_to_all(value, 'dp', 0, 0, tiled=True, axis_index_groups=sharing)  15.7 us
    unnamed x87, local copies, waits for them, and re-layouts  12.9 us
  transfers between devices with their start and end apart: 42, of which 22 were waited for; matrix products, arithmetic and copies ran while one was open for 6% of the time, Pallas kernels for 47%

profile of v4, /device:TPU:1, one launch (start us, length us, event | category | flops | bytes accessed | tf_op | source)
XLA Modules:
  0.0 592.2 jit_solution(5807152869719462805)
XLA Ops:
  7.3 4.7 collective-permute-start.12
  13.4 2.9 collective-permute-done.12
  17.4 10.4 %collective-permute-start.1 = (bf16[384,2048]{1,0:T(8,128)(2,1)S(1)}, bf16[384,2048]{1,0:T(8,128)(2,1)}, u32[]{:S(2)}, u32[]{:S(2)}) collective-permute-start(bf16[384,2048]{1,0:T(8,128)(2,1)S(1)} %copy-done), channel_id=1, source_target_pairs={{0,4},{1,5},{2,6},{3,7},{4,0},{5,1},{6,2},{7,3},{8,12},{9,13},{10,... | collective-permute-start | bytes 4718600 | tf_op jit(solution)/shard_map/ppermute | solution.py:42
  27.8 33.0 %collective-permute-done.1.refs_5_.refs_2_ = bf16[384,2048]{1,0:T(8,128)(2,1)} collective-permute-done((bf16[384,2048]{1,0:T(8,128)(2,1)S(1)}, bf16[384,2048]{1,0:T(8,128)(2,1)}, u32[]{:S(2)}, u32[]{:S(2)}) %collective-permute-start.1) | collective-permute-done | bytes 1572896 | tf_op jit(solution)/shard_map/ppermute | solution.py:42
  61.0 3.7 collective-permute-start.7
  69.2 3.2 collective-permute-done.8
  79.1 17.1 %collective-permute-done.11 = bf16[2,2,2,1,2,8,128]{6,5,4,3,2,1,0:T(8,128)(2,1)S(1)} collective-permute-done((bf16[2,2,2,1,2,8,128]{6,5,4,3,2,1,0:T(8,128)(2,1)S(1)}, bf16[2,2,2,1,2,8,128]{6,5,4,3,2,1,0:T(8,128)(2,1)S(1)}, u32[]{:S(2)}, u32[]{:S(2)}) %collective-permute-start.11) | collective-permute-done | bytes 32800 | tf_op jit(solution)/shard_map/ppermute | solution.py:42
  97.4 2.8 shard_map.254.refs_1_
  100.3 6.3 %all-to-all-start = ((bf16[8,64,1792]{2,1,0:T(8,128)(2,1)}), bf16[8,64,1792]{2,1,0:T(8,128)(2,1)S(1)}, u32[]{:S(2)}, u32[]{:S(2)}) async-start(bf16[8,64,1792]{2,1,0:T(8,128)(2,1)} %shard_map.254.refs_1_), calls=%async_computation | async-start | bytes 3670016 | tf_op jit(solution)/shard_map/all_to_all | solution.py:649
  109.9 7.8 %fusion = (f32[3072,32]{1,0:T(8,128)}, f32[3072,32]{1,0:T(8,128)}, f32[3072,32]{1,0:T(8,128)S(1)}) fusion(f32[32]{0:T(128)S(1)} %multiply_exponential_fusion, f32[3072]{0:T(1024)} %convert_element_type.49), kind=kLoop, calls=%fused_computation.4 | loop fusion | flops 196608 | bytes 1192064 | tf_op jit(solution)/shard_map/neg | solution.py:124
  119.3 7.6 %all-to-all-done = bf16[8,64,1792]{2,1,0:T(8,128)(2,1)S(1)} async-done(((bf16[8,64,1792]{2,1,0:T(8,128)(2,1)}), bf16[8,64,1792]{2,1,0:T(8,128)(2,1)S(1)}, u32[]{:S(2)}, u32[]{:S(2)}) %all-to-all-start) | async-done | bytes 1835040 | tf_op jit(solution)/shard_map/all_to_all | solution.py:649
  128.1 3.8 shard_map.255
  132.0 3.4 collective-permute-start.13
  138.8 21.8 %shard_map.256 = (bf16[3072,2048]{1,0:T(8,128)(2,1)}, bf16[3072,2048]{1,0:T(8,128)(2,1)}, bf16[3072,2048]{1,0:T(8,128)(2,1)}) custom-call(bf16[384,2048]{1,0:T(8,128)(2,1)} %refs_1_.3, bf16[384,2048]{1,0:T(8,128)(2,1)} %collective-permute-done.refs_4_.refs_1_, bf16[384,2048]{1,0:T(8,128)(2,1)} %collective-permute-done.1.refs_5_.refs_2_, ...), custom_call_target="tpu_custom_call" | custom-call | flops 1 | bytes 1 | tf_op jit(solution)/shard_map/pallas_call | solution.py:86
  160.6 8.1 %collective-permute-done.13.refs_0_.refs_1_ = bf16[384,2048]{1,0:T(8,128)(2,1)S(1)} collective-permute-done((bf16[384,2048]{1,0:T(8,128)(2,1)S(1)}, bf16[384,2048]{1,0:T(8,128)(2,1)S(1)}, u32[]{:S(2)}, u32[]{:S(2)}) %collective-permute-start.13) | collective-permute-done | bytes 1572896 | tf_op jit(solution)/shard_map/ppermute | solution.py:42
  169.8 3.6 shard_map.257.refs_4_
  173.4 34.2 %collective-permute-done.15.refs_3_ = bf16[384,2048]{1,0:T(8,128)(2,1)S(1)} collective-permute-done((bf16[384,2048]{1,0:T(8,128)(2,1)}, bf16[384,2048]{1,0:T(8,128)(2,1)S(1)}, u32[]{:S(2)}, u32[]{:S(2)}) %collective-permute-start.15) | collective-permute-done | bytes 1572896 | tf_op jit(solution)/shard_map/ppermute | solution.py:42
  208.7 5.9 shard_map.258.refs_3_.refs_0_.refs_1_.refs_2_
  214.6 2.8 collective-permute-start.16
  218.8 22.5 %shard_map.259 = (bf16[3072,1024]{1,0:T(8,128)(2,1)}, f32[3072,1024]{1,0:T(8,128)}) custom-call(bf16[3072,2048]{1,0:T(8,128)(2,1)} %get-tuple-element.55.refs_0_, f32[1,1024]{1,0:T(1,128)} %bitcast.97, bf16[2048,1024]{1,0:T(8,128)(2,1)} %all-gather.8.cloned.1.call-done.refs_2_.refs_3_, bf16[1536,2048]{1,0:T(8,128)(2,1)} %shard_map.258.refs_3_.refs_0_.refs_1_.refs_2_), custom_call_target="tpu_custom_call" | custom-call | flops 1 | bytes 1 | tf_op jit(solution)/shard_map/pallas_call | solution.py:86
  241.3 29.6 %shard_map.260 = (bf16[3072,1024]{1,0:T(8,128)(2,1)}, bf16[3072,2048]{1,0:T(8,128)(2,1)}, f32[1,1024]{1,0:T(1,128)}, f32[1,2048]{1,0:T(1,128)}, bf16[1024,2048]{1,0:T(8,128)(2,1)}) custom-call(bf16[1536,2048]{1,0:T(8,128)(2,1)} %shard_map.258.refs_3_.refs_0_.refs_1_.refs_2_, bf16[1536,2048]{1,0:T(8,128)(2,1)} %shard_map.258.refs_3_.refs_0_.refs_1_.refs_2_, ...), custom_call_target="tpu_custom_call" | custom-call | flops 1 | bytes 1 | tf_op jit(solution)/shard_map/pallas_call | solution.py:86
  270.8 18.8 %shard_map.261.refs_5_ = bf16[2048,1024]{1,0:T(8,128)(2,1)} custom-call(bf16[3072,2048]{1,0:T(8,128)(2,1)} %get-tuple-element.54.refs_0_, bf16[3072,1024]{1,0:T(8,128)(2,1)} %get-tuple-element.59.refs_1_.refs_2_, bf16[3072,1024]{1,0:T(8,128)(2,1)} %get-tuple-element.59.refs_1_.refs_2_), custom_call_target="tpu_custom_call" | custom-call | flops 1 | bytes 1 | tf_op jit(solution)/shard_map/pallas_call | solution.py:86
  294.0 16.2 %shard_map.262.refs_0_.refs_7_ = bf16[3072,768]{1,0:T(8,128)(2,1)} custom-call(bf16[3072,2048]{1,0:T(8,128)(2,1)} %get-tuple-element.53.refs_1_.refs_0_, f32[3072,128]{1,0:T(8,128)} %maximum_maximum_fusion.refs_2_.refs_1_, f32[3072,128]{1,0:T(8,128)} %maximum_maximum_fusion.1.refs_2_.refs_3_, f32[1,768]{1,0:T(1,128)} %bitcast.99, ...), custom_call_target="tpu_custom_call" | custom-call | flops 1 | bytes 1 | tf_op jit(solution)/shard_map/pallas_call | solution.py:86
  310.1 20.8 %shard_map.263 = (bf16[3072,256]{1,0:T(8,128)(2,1)}, bf16[3072,768]{1,0:T(8,128)(2,1)}, f32[1,768]{1,0:T(1,128)}, bf16[256,2048]{1,0:T(8,128)(2,1)}) custom-call(bf16[3072,768]{1,0:T(8,128)(2,1)} %shard_map.262.refs_0_.refs_7_, bf16[3072,2048]{1,0:T(8,128)(2,1)} %get-tuple-element.60.refs_1_.refs_2_, f32[3072,128]{1,0:T(8,128)} %maximum_maximum_fusion.refs_2_.refs_1_, ...), custom_call_target="tpu_custom_call" | custom-call | flops 1 | bytes 1 | tf_op jit(solution)/shard_map/pallas_call | solution.py:86
  331.0 13.0 %shard_map.264.refs_6_ = bf16[1536,2048]{1,0:T(8,128)(2,1)} custom-call(bf16[3072,256]{1,0:T(8,128)(2,1)} %get-tuple-element.61.refs_0_.refs_4_.refs_1_, bf16[3072,1024]{1,0:T(8,128)(2,1)} %get-tuple-element.58.refs_10_.refs_1_.refs_0_, bf16[256,2048]{1,0:T(8,128)(2,1)} %get-tuple-element.62.refs_2_, bf16[1024,2048]{1,0:T(8,128)(2,1)} %get-tuple-element.63.refs_3_, ...), custom_call_target="tpu_custom_call" | custom-call | flops 1 | bytes 1 | tf_op jit(solution)/shard_map/pallas_call | solution.py:86
  344.0 17.1 %shard_map.265.refs_2_ = bf16[1536,2048]{1,0:T(8,128)(2,1)} custom-call(bf16[3072,768]{1,0:T(8,128)(2,1)} %get-tuple-element.64.refs_0_.refs_1_, bf16[3072,1024]{1,0:T(8,128)(2,1)} %get-tuple-element.59.refs_1_.refs_2_, bf16[2048,768]{1,0:T(8,128)(2,1)} %all-gather.6.cloned.1.call-done.refs_4_.refs_2_, ...), custom_call_target="tpu_custom_call" | custom-call | flops 1 | bytes 1 | tf_op jit(solution)/shard_map/pallas_call | solution.py:86
  361.1 15.6 %shard_map.266.refs_5_ = bf16[2048,768]{1,0:T(8,128)(2,1)} custom-call(bf16[3072,2048]{1,0:T(8,128)(2,1)} %get-tuple-element.54.refs_0_, bf16[3072,768]{1,0:T(8,128)(2,1)} %get-tuple-element.64.refs_0_.refs_1_, bf16[1536,2048]{1,0:T(8,128)(2,1)} %shard_map.265.refs_2_), custom_call_target="tpu_custom_call" | custom-call | flops 1 | bytes 1 | tf_op jit(solution)/shard_map/pallas_call | solution.py:86
  382.8 16.4 %shard_map.267 = (bf16[384,2048]{1,0:T(8,128)(2,1)}, bf16[384,2048]{1,0:T(8,128)(2,1)}, bf16[384,2048]{1,0:T(8,128)(2,1)}, bf16[384,1024]{1,0:T(8,128)(2,1)}, bf16[384,1024]{1,0:T(8,128)(2,1)}) custom-call(bf16[3072,256]{1,0:T(8,128)(2,1)} %get-tuple-element.61.refs_0_.refs_4_.refs_1_, bf16[3072,1024]{1,0:T(8,128)(2,1)} %get-tuple-element.58.refs_10_.refs_1_.refs_0_, ...), custom_call_target="tpu_custom_call" | custom-call | flops 1 | bytes 1 | tf_op jit(solution)/shard_map/pallas_call | solution.py:86
  399.2 2.6 collective-permute-start.18
  404.8 14.3 %collective-permute-done.23 = f32[1,1,2,14,128]{4,3,2,1,0:T(8,128)S(1)} collective-permute-done((f32[1,1,2,14,128]{4,3,2,1,0:T(8,128)S(1)}, f32[1,1,2,14,128]{4,3,2,1,0:T(8,128)S(1)}, u32[]{:S(2)}, u32[]{:S(2)}) %collective-permute-start.23) | collective-permute-done | bytes 14368 | tf_op jit(solution)/shard_map/ppermute | solution.py:42
  419.2 3.2 collective-permute-done.24
  424.2 3.6 shard_map.268
  427.8 22.4 %shard_map.269.refs_7_ = bf16[1280,2048]{1,0:T(8,128)(2,1)} custom-call(bf16[3072,1024]{1,0:T(8,128)(2,1)} %get-tuple-element.58.refs_10_.refs_1_.refs_0_, bf16[3072,256]{1,0:T(8,128)(2,1)} %get-tuple-element.61.refs_0_.refs_4_.refs_1_, bf16[3072,2048]{1,0:T(8,128)(2,1)} %get-tuple-element.60.refs_1_.refs_2_, bf16[384,2048]{1,0:T(8,128)(2,1)} %get-tuple-element.73.refs_3_), custom_call_target="tpu_custom_call" | custom-call | flops 1 | bytes 1 | tf_op jit(solution)/shard_map/pallas_call | solution.py:86
  454.2 3.9 all-to-all-start.1
  458.2 4.7 collective-permute-done.27.refs_6_
  462.9 20.6 %shard_map.270 = (bf16[384,2048]{1,0:T(8,128)(2,1)}, bf16[384,2048]{1,0:T(8,128)(2,1)}, bf16[384,2048]{1,0:T(8,128)(2,1)}, bf16[384,1024]{1,0:T(8,128)(2,1)}, bf16[384,1024]{1,0:T(8,128)(2,1)}) custom-call(bf16[3072,768]{1,0:T(8,128)(2,1)} %get-tuple-element.64.refs_0_.refs_1_, bf16[3072,1024]{1,0:T(8,128)(2,1)} %get-tuple-element.59.refs_1_.refs_2_, ...), custom_call_target="tpu_custom_call" | custom-call | flops 1 | bytes 1 | tf_op jit(solution)/shard_map/pallas_call | solution.py:86
  486.3 2.8 collective-permute-done.25.refs_2_
  490.2 4.9 shard_map.271.refs_4_
  495.1 22.1 %collective-permute-done.28.refs_2_ = bf16[384,1024]{1,0:T(8,128)(2,1)S(1)} collective-permute-done((bf16[384,1024]{1,0:T(8,128)(2,1)}, bf16[384,1024]{1,0:T(8,128)(2,1)S(1)}, u32[]{:S(2)}, u32[]{:S(2)}) %collective-permute-start.28) | collective-permute-done | bytes 786464 | tf_op jit(solution)/shard_map/ppermute | solution.py:42
  519.2 3.7 shard_map.272
  523.7 5.5 all-to-all-start.2
  531.3 4.1 shard_map.273
  535.4 9.2 %reduce-scatter.6.cloned.1.call-done.refs_0_ = bf16[320,2048]{1,0:T(8,128)(2,1)} async-done(((bf16[1280,2048]{1,0:T(8,128)(2,1)}), bf16[320,2048]{1,0:T(8,128)(2,1)}) %reduce-scatter.6.cloned.1.call-update) | async-done | bytes 1310736 | tf_op jit(solution)/shard_map/reduce_scatter | solution.py:644
  544.6 2.9 shard_map.274
  547.5 3.6 collective-permute-start.32
  555.9 12.3 %collective-permute-done.30.refs_3_ = bf16[384,2048]{1,0:T(8,128)(2,1)S(1)} collective-permute-done((bf16[384,2048]{1,0:T(8,128)(2,1)}, bf16[384,2048]{1,0:T(8,128)(2,1)S(1)}, u32[]{:S(2)}, u32[]{:S(2)}) %collective-permute-start.30) | collective-permute-done | bytes 1572896 | tf_op jit(solution)/shard_map/ppermute | solution.py:42
  569.3 6.4 %shard_map.275.refs_5_ = f32[384,2048]{1,0:T(8,128)} custom-call(bf16[384,2048]{1,0:T(8,128)(2,1)} %refs_0_.9, bf16[384,2048]{1,0:T(8,128)(2,1)} %refs_1_.3, bf16[384,2048]{1,0:T(8,128)(2,1)} %get-tuple-element.75.refs_6_.refs_2_, bf16[384,2048]{1,0:T(8,128)(2,1)} %copy-done.9, bf16[384,2048]{1,0:T(8,128)(2,1)} %collective-permute-done.31.refs_4_, ...), custom_call_target="tpu_custom_call" | custom-call | flops 1 | bytes 1 | tf_op jit(solution)/shard_map/pallas_call | solution.py:86
  577.5 3.5 shard_map.276
  (221 shorter events, 68.1 us)
Async XLA Ops:
  7.2 53.6 %copy-start.33 = (bf16[64]{0:T(256)(128)(2,1)S(1)}, bf16[64]{0:T(256)(128)(2,1)}, u32[]{:S(2)}) copy-start(bf16[64]{0:T(256)(128)(2,1)} %param.17) | copy-start | bytes 388
  7.2 53.6 %copy-start.35 = (bf16[64]{0:T(256)(128)(2,1)S(1)}, bf16[64]{0:T(256)(128)(2,1)}, u32[]{:S(2)}) copy-start(bf16[64]{0:T(256)(128)(2,1)} %param.18) | copy-start | bytes 388
  7.2 53.6 %copy-start.29 = (bf16[64]{0:T(256)(128)(2,1)S(1)}, bf16[64]{0:T(256)(128)(2,1)}, u32[]{:S(2)}) copy-start(bf16[64]{0:T(256)(128)(2,1)} %param.19) | copy-start | bytes 388
  7.2 53.6 %copy-start.31 = (bf16[64]{0:T(256)(128)(2,1)S(1)}, bf16[64]{0:T(256)(128)(2,1)}, u32[]{:S(2)}) copy-start(bf16[64]{0:T(256)(128)(2,1)} %param.20) | copy-start | bytes 388
  7.3 53.6 %copy-start.27 = (bf16[192]{0:T(256)(128)(2,1)S(1)}, bf16[192]{0:T(256)(128)(2,1)}, u32[]{:S(2)}) copy-start(bf16[192]{0:T(256)(128)(2,1)} %param.22) | copy-start | bytes 1156
  7.3 119.6 %all-gather.4.cloned.1.call-start = ((), (), s32[]{:S(2)}) async-start(), calls=%async_computation.6 | async-start | bytes 6553600 | tf_op jit(solution)/shard_map/all_gather | solution.py:641
  7.3 8.9 %collective-permute-start.12 = (bf16[64,2048]{1,0:T(8,128)(2,1)}, bf16[64,2048]{1,0:T(8,128)(2,1)S(1)}, u32[]{:S(2)}, u32[]{:S(2)}) collective-permute-start(bf16[64,2048]{1,0:T(8,128)(2,1)} %param.23), channel_id=1, source_target_pairs={{0,0},{1,8},{2,16},{3,24},{4,1},{5,9},{6,17},{7,25},{8,2},{9,10},{... | collective-permute-start | bytes 786440 | tf_op jit(solution)/shard_map/ppermute | solution.py:653
  17.4 43.4 %collective-permute-start.1 = (bf16[384,2048]{1,0:T(8,128)(2,1)S(1)}, bf16[384,2048]{1,0:T(8,128)(2,1)}, u32[]{:S(2)}, u32[]{:S(2)}) collective-permute-start(bf16[384,2048]{1,0:T(8,128)(2,1)S(1)} %copy-done), channel_id=1, source_target_pairs={{0,4},{1,5},{2,6},{3,7},{4,0},{5,1},{6,2},{7,3},{8,12},{9,13},{10,... | collective-permute-start | bytes 4718600 | tf_op jit(solution)/shard_map/ppermute | solution.py:42
  27.8 79.0 %collective-permute-start = (bf16[384,2048]{1,0:T(8,128)(2,1)S(1)}, bf16[384,2048]{1,0:T(8,128)(2,1)}, u32[]{:S(2)}, u32[]{:S(2)}) collective-permute-start(bf16[384,2048]{1,0:T(8,128)(2,1)S(1)} %copy-done), channel_id=1, source_target_pairs={{0,2},{1,3},{2,0},{3,1},{4,6},{5,7},{6,4},{7,5},{8,10},{9,11},{10,... | collective-permute-start | bytes 4718600 | tf_op jit(solution)/shard_map/ppermute | solution.py:42
  60.8 46.3 %collective-permute-start.2 = (bf16[384,2048]{1,0:T(8,128)(2,1)}, bf16[384,2048]{1,0:T(8,128)(2,1)}, u32[]{:S(2)}, u32[]{:S(2)}) collective-permute-start(bf16[384,2048]{1,0:T(8,128)(2,1)} %collective-permute-done.1.refs_5_.refs_2_), channel_id=1, source_target_pairs={{0,2},{1,3},{2,0},{3,1},{4,6},{5,7},{6,4},{7,5},{8,10},{9,11},{10,... | collective-permute-start | bytes 4718600 | tf_op jit(solution)/shard_map/ppermute | solution.py:42
  61.0 7.5 %collective-permute-start.7 = (bf16[1,1,1,1,1,8,128]{6,5,4,3,2,1,0:T(8,128)(2,1)S(1)}, bf16[1,1,1,1,1,8,128]{6,5,4,3,2,1,0:T(8,128)(2,1)S(1)}, u32[]{:S(2)}, u32[]{:S(2)}) collective-permute-start(bf16[1,1,1,1,1,8,128]{6,5,4,3,2,1,0:T(8,128)(2,1)S(1)} %bitcast.94), channel_id=1, source_target_pairs={{0,8},{1,9},{2,10},{3,11},{4,12},{5,13},{6,14},{7,15},{8,0},{9,1},... | collective-permute-start | bytes 6152 | tf_op jit(solution)/shard_map/ppermute | solution.py:42
  64.7 54.6 %collective-permute-start.3 = (bf16[384,2048]{1,0:T(8,128)(2,1)S(1)}, bf16[384,2048]{1,0:T(8,128)(2,1)}, u32[]{:S(2)}, u32[]{:S(2)}) collective-permute-start(bf16[384,2048]{1,0:T(8,128)(2,1)S(1)} %copy-done), channel_id=1, source_target_pairs={{0,1},{1,0},{2,3},{3,2},{4,5},{5,4},{6,7},{7,6},{8,9},{9,8},{10,11... | collective-permute-start | bytes 4718600 | tf_op jit(solution)/shard_map/ppermute | solution.py:42
  68.5 3.9 collective-permute-start.8
  72.3 1.9 collective-permute-start.9
  74.2 3.1 collective-permute-start.10
  77.3 18.9 %collective-permute-start.11 = (bf16[2,2,2,1,2,8,128]{6,5,4,3,2,1,0:T(8,128)(2,1)S(1)}, bf16[2,2,2,1,2,8,128]{6,5,4,3,2,1,0:T(8,128)(2,1)S(1)}, u32[]{:S(2)}, u32[]{:S(2)}) collective-permute-start(bf16[2,2,2,1,2,8,128]{6,5,4,3,2,1,0:T(8,128)(2,1)S(1)} %maximum_select_fusion.2), channel_id=1, source_target_pairs={{0,2},{1,3},{2,0},{3,1},{4,6},{5,7},{6,4},{7,5},{8,10},{9,11},{10,... | collective-permute-start | bytes 98312 | tf_op jit(solution)/shard_map/ppermute | solution.py:42
  97.4 192.6 %copy-start.17 = (s32[8,384]{1,0:T(8,128)}, s32[8,384]{1,0:T(8,128)S(1)}, u32[]{:S(2)}) copy-start(s32[8,384]{1,0:T(8,128)S(1)} %get-tuple-element.90.refs_5_) | copy-start | bytes 36868
  100.3 26.6 %all-to-all-start = ((bf16[8,64,1792]{2,1,0:T(8,128)(2,1)}), bf16[8,64,1792]{2,1,0:T(8,128)(2,1)S(1)}, u32[]{:S(2)}, u32[]{:S(2)}) async-start(bf16[8,64,1792]{2,1,0:T(8,128)(2,1)} %shard_map.254.refs_1_), calls=%async_computation | async-start | bytes 3670016 | tf_op jit(solution)/shard_map/all_to_all | solution.py:649
  106.5 112.2 %all-gather.8.cloned.1.call-start = ((), (), s32[]{:S(2)}) async-start(), calls=%async_computation.8 | async-start | bytes 5242880 | tf_op jit(solution)/shard_map/all_gather | solution.py:641
  106.5 20.3 %collective-permute-start.5 = (bf16[384,2048]{1,0:T(8,128)(2,1)}, bf16[384,2048]{1,0:T(8,128)(2,1)}, u32[]{:S(2)}, u32[]{:S(2)}) collective-permute-start(bf16[384,2048]{1,0:T(8,128)(2,1)} %collective-permute-done.1.refs_5_.refs_2_), channel_id=1, source_target_pairs={{0,1},{1,0},{2,3},{3,2},{4,5},{5,4},{6,7},{7,6},{8,9},{9,8},{10,11... | collective-permute-start | bytes 4718600 | tf_op jit(solution)/shard_map/ppermute | solution.py:42
  106.8 20.1 %collective-permute-start.4 = (bf16[384,2048]{1,0:T(8,128)(2,1)}, bf16[384,2048]{1,0:T(8,128)(2,1)}, u32[]{:S(2)}, u32[]{:S(2)}) collective-permute-start(bf16[384,2048]{1,0:T(8,128)(2,1)} %collective-permute-done.refs_4_.refs_1_), channel_id=1, source_target_pairs={{0,1},{1,0},{2,3},{3,2},{4,5},{5,4},{6,7},{7,6},{8,9},{9,8},{10,11... | collective-permute-start | bytes 4718600 | tf_op jit(solution)/shard_map/ppermute | solution.py:42
  107.1 19.8 %collective-permute-start.6 = (bf16[384,2048]{1,0:T(8,128)(2,1)}, bf16[384,2048]{1,0:T(8,128)(2,1)}, u32[]{:S(2)}, u32[]{:S(2)}) collective-permute-start(bf16[384,2048]{1,0:T(8,128)(2,1)} %collective-permute-done.2.refs_6_.refs_3_), channel_id=1, source_target_pairs={{0,1},{1,0},{2,3},{3,2},{4,5},{5,4},{6,7},{7,6},{8,9},{9,8},{10,11... | collective-permute-start | bytes 4718600 | tf_op jit(solution)/shard_map/ppermute | solution.py:42
  131.9 162.0 %all-gather.6.cloned.1.call-start = ((), (), s32[]{:S(2)}) async-start(), calls=%async_computation.7 | async-start | bytes 3932160 | tf_op jit(solution)/shard_map/all_gather | solution.py:641
  132.0 36.7 %collective-permute-start.13 = (bf16[384,2048]{1,0:T(8,128)(2,1)S(1)}, bf16[384,2048]{1,0:T(8,128)(2,1)S(1)}, u32[]{:S(2)}, u32[]{:S(2)}) collective-permute-start(bf16[384,2048]{1,0:T(8,128)(2,1)S(1)} %copy-done.4), channel_id=1, source_target_pairs={{0,2},{1,3},{2,0},{3,1},{4,6},{5,7},{6,4},{7,5},{8,10},{9,11},{10,... | collective-permute-start | bytes 4718600 | tf_op jit(solution)/shard_map/ppermute | solution.py:42
  135.4 38.0 %collective-permute-start.14 = (bf16[384,2048]{1,0:T(8,128)(2,1)S(1)}, bf16[384,2048]{1,0:T(8,128)(2,1)}, u32[]{:S(2)}, u32[]{:S(2)}) collective-permute-start(bf16[384,2048]{1,0:T(8,128)(2,1)S(1)} %copy-done.4), channel_id=1, source_target_pairs={{0,4},{1,5},{2,6},{3,7},{4,0},{5,1},{6,2},{7,3},{8,12},{9,13},{10,... | collective-permute-start | bytes 4718600 | tf_op jit(solution)/shard_map/ppermute | solution.py:42
  173.4 34.2 %collective-permute-start.15 = (bf16[384,2048]{1,0:T(8,128)(2,1)}, bf16[384,2048]{1,0:T(8,128)(2,1)S(1)}, u32[]{:S(2)}, u32[]{:S(2)}) collective-permute-start(bf16[384,2048]{1,0:T(8,128)(2,1)} %shard_map.257.refs_4_), channel_id=1, source_target_pairs={{0,4},{1,5},{2,6},{3,7},{4,0},{5,1},{6,2},{7,3},{8,12},{9,13},{10,... | collective-permute-start | bytes 4718600 | tf_op jit(solution)/shard_map/ppermute | solution.py:42
  214.6 26.7 %collective-permute-start.16 = (bf16[1536,2048]{1,0:T(8,128)(2,1)}, bf16[1536,2048]{1,0:T(8,128)(2,1)}, u32[]{:S(2)}, u32[]{:S(2)}) collective-permute-start(bf16[1536,2048]{1,0:T(8,128)(2,1)} %shard_map.258.refs_3_.refs_0_.refs_1_.refs_2_), channel_id=1, source_target_pairs={{0,1},{1,0},{2,3},{3,2},{4,5},{5,4},{6,7},{7,6},{8,9},{9,8},{10,11... | collective-permute-start | bytes 18874376 | tf_op jit(solution)/shard_map/ppermute | solution.py:42
  217.5 236.7 %reduce-scatter.4.cloned.1.call-start = ((), (), s32[]{:S(2)}) async-start(), calls=%async_computation.9 | async-start | bytes 5242880 | tf_op jit(solution)/shard_map/reduce_scatter | solution.py:644
  289.7 234.0 %reduce-scatter.8.cloned.1.call-start = ((), (), s32[]{:S(2)}) async-start(), calls=%async_computation.11 | async-start | bytes 3932160 | tf_op jit(solution)/shard_map/reduce_scatter | solution.py:644
  343.9 38.9 %collective-permute-start.17 = (bf16[1536,2048]{1,0:T(8,128)(2,1)}, bf16[1536,2048]{1,0:T(8,128)(2,1)}, u32[]{:S(2)}, u32[]{:S(2)}) collective-permute-start(bf16[1536,2048]{1,0:T(8,128)(2,1)} %shard_map.264.refs_6_), channel_id=1, source_target_pairs={{0,1},{1,0},{2,3},{3,2},{4,5},{5,4},{6,7},{7,6},{8,9},{9,8},{10,11... | collective-permute-start | bytes 18874376 | tf_op jit(solution)/shard_map/ppermute | solution.py:42
  376.7 167.8 %reduce-scatter.6.cloned.1.call-start = ((), (), s32[]{:S(2)}) async-start(), calls=%async_computation.10 | async-start | bytes 6553600 | tf_op jit(solution)/shard_map/reduce_scatter | solution.py:644
  377.5 2.8 collective-permute-start.20
  380.3 21.5 %collective-permute-start.21 = (f32[30,128]{1,0:T(8,128)S(1)}, f32[30,128]{1,0:T(8,128)S(1)}, u32[]{:S(2)}, u32[]{:S(2)}) collective-permute-start(f32[30,128]{1,0:T(8,128)S(1)} %bitcast_add_fusion), channel_id=1, source_target_pairs={{0,16},{1,17},{2,18},{3,19},{4,20},{5,21},{6,22},{7,23},{8,24},{9,... | collective-permute-start | bytes 46088 | tf_op jit(solution)/shard_map/ppermute | solution.py:42
  399.2 23.8 %collective-permute-start.18 = (bf16[384,1024]{1,0:T(8,128)(2,1)}, bf16[384,1024]{1,0:T(8,128)(2,1)S(1)}, u32[]{:S(2)}, u32[]{:S(2)}) collective-permute-start(bf16[384,1024]{1,0:T(8,128)(2,1)} %get-tuple-element.68), channel_id=1, source_target_pairs={{0,2},{1,3},{2,0},{3,1},{4,6},{5,7},{6,4},{7,5},{8,10},{9,11},{10,... | collective-permute-start | bytes 2359304 | tf_op jit(solution)/shard_map/ppermute | solution.py:42
  401.8 21.2 %collective-permute-start.19 = (bf16[384,1024]{1,0:T(8,128)(2,1)}, bf16[384,1024]{1,0:T(8,128)(2,1)S(1)}, u32[]{:S(2)}, u32[]{:S(2)}) collective-permute-start(bf16[384,1024]{1,0:T(8,128)(2,1)} %get-tuple-element.69), channel_id=1, source_target_pairs={{0,4},{1,5},{2,6},{3,7},{4,0},{5,1},{6,2},{7,3},{8,12},{9,13},{10,... | collective-permute-start | bytes 2359304 | tf_op jit(solution)/shard_map/ppermute | solution.py:42
  401.9 3.0 collective-permute-start.22
  404.8 14.4 %collective-permute-start.23 = (f32[1,1,2,14,128]{4,3,2,1,0:T(8,128)S(1)}, f32[1,1,2,14,128]{4,3,2,1,0:T(8,128)S(1)}, u32[]{:S(2)}, u32[]{:S(2)}) collective-permute-start(f32[1,1,2,14,128]{4,3,2,1,0:T(8,128)S(1)} %maximum_select_fusion.7), channel_id=1, source_target_pairs={{0,2},{1,3},{2,0},{3,1},{4,6},{5,7},{6,4},{7,5},{8,10},{9,11},{10,... | collective-permute-start | bytes 43016 | tf_op jit(solution)/shard_map/ppermute | solution.py:42
  419.2 3.2 collective-permute-start.24
  450.3 12.6 %collective-permute-start.27 = (bf16[1536,2048]{1,0:T(8,128)(2,1)}, bf16[1536,2048]{1,0:T(8,128)(2,1)}, u32[]{:S(2)}, u32[]{:S(2)}) collective-permute-start(bf16[1536,2048]{1,0:T(8,128)(2,1)} %shard_map.265.refs_2_), channel_id=1, source_target_pairs={{0,1},{1,0},{2,3},{3,2},{4,5},{5,4},{6,7},{7,6},{8,9},{9,8},{10,11... | collective-permute-start | bytes 18874376 | tf_op jit(solution)/shard_map/ppermute | solution.py:42
  452.8 36.3 %collective-permute-start.25 = (bf16[384,2048]{1,0:T(8,128)(2,1)}, bf16[384,2048]{1,0:T(8,128)(2,1)S(1)}, u32[]{:S(2)}, u32[]{:S(2)}) collective-permute-start(bf16[384,2048]{1,0:T(8,128)(2,1)} %get-tuple-element.73.refs_3_), channel_id=1, source_target_pairs={{0,2},{1,3},{2,0},{3,1},{4,6},{5,7},{6,4},{7,5},{8,10},{9,11},{10,... | collective-permute-start | bytes 4718600 | tf_op jit(solution)/shard_map/ppermute | solution.py:42
  454.2 36.0 %collective-permute-start.26 = (bf16[384,2048]{1,0:T(8,128)(2,1)}, bf16[384,2048]{1,0:T(8,128)(2,1)}, u32[]{:S(2)}, u32[]{:S(2)}) collective-permute-start(bf16[384,2048]{1,0:T(8,128)(2,1)} %get-tuple-element.74), channel_id=1, source_target_pairs={{0,4},{1,5},{2,6},{3,7},{4,0},{5,1},{6,2},{7,3},{8,12},{9,13},{10,... | collective-permute-start | bytes 4718600 | tf_op jit(solution)/shard_map/ppermute | solution.py:42
  454.2 64.0 %all-to-all-start.1 = ((bf16[8,64,1024]{2,1,0:T(8,128)(2,1)}), bf16[8,64,1024]{2,1,0:T(8,128)(2,1)S(1)}, u32[]{:S(2)}, u32[]{:S(2)}) async-start(bf16[8,64,1024]{2,1,0:T(8,128)(2,1)} %bitcast.76), calls=%async_computation.2 | async-start | bytes 2097152 | tf_op jit(solution)/shard_map/all_to_all | solution.py:649
  483.5 33.8 %collective-permute-start.28 = (bf16[384,1024]{1,0:T(8,128)(2,1)}, bf16[384,1024]{1,0:T(8,128)(2,1)S(1)}, u32[]{:S(2)}, u32[]{:S(2)}) collective-permute-start(bf16[384,1024]{1,0:T(8,128)(2,1)} %get-tuple-element.78), channel_id=1, source_target_pairs={{0,2},{1,3},{2,0},{3,1},{4,6},{5,7},{6,4},{7,5},{8,10},{9,11},{10,... | collective-permute-start | bytes 2359304 | tf_op jit(solution)/shard_map/ppermute | solution.py:42
  484.9 33.3 %collective-permute-start.29 = (bf16[384,1024]{1,0:T(8,128)(2,1)}, bf16[384,1024]{1,0:T(8,128)(2,1)}, u32[]{:S(2)}, u32[]{:S(2)}) collective-permute-start(bf16[384,1024]{1,0:T(8,128)(2,1)} %get-tuple-element.79), channel_id=1, source_target_pairs={{0,4},{1,5},{2,6},{3,7},{4,0},{5,1},{6,2},{7,3},{8,12},{9,13},{10,... | collective-permute-start | bytes 2359304 | tf_op jit(solution)/shard_map/ppermute | solution.py:42
  522.9 45.3 %collective-permute-start.30 = (bf16[384,2048]{1,0:T(8,128)(2,1)}, bf16[384,2048]{1,0:T(8,128)(2,1)S(1)}, u32[]{:S(2)}, u32[]{:S(2)}) collective-permute-start(bf16[384,2048]{1,0:T(8,128)(2,1)} %get-tuple-element.80.refs_5_), channel_id=1, source_target_pairs={{0,2},{1,3},{2,0},{3,1},{4,6},{5,7},{6,4},{7,5},{8,10},{9,11},{10,... | collective-permute-start | bytes 4718600 | tf_op jit(solution)/shard_map/ppermute | solution.py:42
  523.6 44.5 %collective-permute-start.31 = (bf16[384,2048]{1,0:T(8,128)(2,1)}, bf16[384,2048]{1,0:T(8,128)(2,1)}, u32[]{:S(2)}, u32[]{:S(2)}) collective-permute-start(bf16[384,2048]{1,0:T(8,128)(2,1)} %get-tuple-element.81), channel_id=1, source_target_pairs={{0,4},{1,5},{2,6},{3,7},{4,0},{5,1},{6,2},{7,3},{8,12},{9,13},{10,... | collective-permute-start | bytes 4718600 | tf_op jit(solution)/shard_map/ppermute | solution.py:42
  523.7 52.9 %all-to-all-start.2 = ((bf16[8,64,768]{2,1,0:T(8,128)(2,1)}), bf16[8,64,768]{2,1,0:T(8,128)(2,1)S(1)}, u32[]{:S(2)}, u32[]{:S(2)}) async-start(bf16[8,64,768]{2,1,0:T(8,128)(2,1)} %bitcast.77), calls=%async_computation.5 | async-start | bytes 1572864 | tf_op jit(solution)/shard_map/all_to_all | solution.py:649
  547.5 36.3 %collective-permute-start.32 = (bf16[64,2048]{1,0:T(8,128)(2,1)}, bf16[64,2048]{1,0:T(8,128)(2,1)S(1)}, u32[]{:S(2)}, u32[]{:S(2)}) collective-permute-start(bf16[64,2048]{1,0:T(8,128)(2,1)} %get-tuple-element.89), channel_id=1, source_target_pairs={{0,0},{8,1},{16,2},{24,3},{1,4},{9,5},{17,6},{25,7},{2,8},{10,9},{... | collective-permute-start | bytes 786440 | tf_op jit(solution)/shard_map/ppermute | solution.py:828
  (34 other events, 418.8 us)
Sparse Core Ops, SparseCore 0:
  17.5 107.5 all-gather.3
  132.0 83.8 all-gather.7
  217.6 65.1 all-gather.5
  289.8 78.4 reduce-scatter.3
  376.9 62.0 reduce-scatter.7
  450.4 94.1 reduce-scatter.5

commit v5 on v4

--- a/solution.py
+++ b/solution.py
@@ -145,23 +145,26 @@
     return lax.dot_general(left, right, PAIRED, preferred_element_type=jnp.float32)
 
 
-def over_blocks(chain, kernel, slots, pieces, blocked, known, outs, sums=(), rows=None):
+def over_blocks(
+    chain, kernel, slots, pieces, blocked, known, outs, sums=(), rows=None, pair=()
+):
     count = HEADS
     gathered, runs = rows or (None, [])
     extra = [gathered] if runs else []
 
     def body(*refs):
         refs = list(refs)
-        if pieces:
+        step = pl.program_id(0)
+        if pieces or pair:
             held = refs.pop()
-            for step, piece in enumerate(refs[: len(pieces)]):
-
-                @pl.when(pl.program_id(0) == step)
+            for place, piece in enumerate(refs[: len(pieces) + len(pair)]):
+
+                @pl.when(step == place if pieces else step // (count // 2) == place)
                 def _(piece=piece):
                     held[...] = piece[...]
 
-            refs = [held] + refs[len(pieces) :]
-        given = bool(pieces) + len(blocked) + len(known)
+            refs = [held] + refs[len(pieces) + len(pair) :]
+        given = bool(pieces or pair) + len(blocked) + len(known)
         if not runs:
             kernel(*refs)
             return
@@ -187,16 +190,22 @@
         shape = (sum(many for _, many in runs), gathered.shape[1])
         shapes.append((shape, jnp.bfloat16))
         specs.append(pl.BlockSpec(shape, lambda i: (0, 0)))
+    def half_of(item, place):
+        half = count // 2
+        return pl.BlockSpec(
+            (slots, item.shape[1]), lambda i: (jnp.clip(i - place * half, 0, half - 1), 0)
+        )
+
     def once(item):
         return pl.BlockSpec(item.shape, lambda i: (0, 0), pipeline_mode=pl.Buffered(1))
 
     options = {}
-    if pieces:
-        item = pieces[0][0]
+    if pieces or pair:
+        item = pair[0] if pair else pieces[0][0]
         options["scratch_shapes"] = [pltpu.VMEM((slots, item.shape[1]), item.dtype)]
     return chain.launch(
         body,
-        [*[item for item, _ in pieces], *blocked, *known, *extra],
+        [*[item for item, _ in pieces], *pair, *blocked, *known, *extra],
         [
             pl.BlockSpec(
                 (slots, item.shape[1]),
@@ -205,6 +214,7 @@
             )
             for item, place in pieces
         ]
+        + [half_of(item, place) for place, item in enumerate(pair)]
         + [moving(item.shape[1]) for item in blocked]
         + [whole(item) for item in known]
         + [once(item) for item in extra],
@@ -229,40 +239,53 @@
 
 
 def terms_of(chain, compute, slots, width, place, blocked, known, added, split):
-    extra = [] if added is None else [added]
+    extra = list(added)
 
     def kernel(*refs):
         values = [ref[...] for ref in refs[: len(blocked) + len(known)]]
         total = compute(*values)
+        step = pl.program_id(0)
+        outs = refs[len(values) + len(extra) :]
         if extra:
-            total += refs[len(values)][...].astype(jnp.float32)
-        outs = refs[len(values) + len(extra) :]
+            one, two = [ref[...] for ref in refs[len(values) : len(values) + 2]]
+            total += jnp.where(step < 2, one, two).astype(jnp.float32)
         if not split:
-            outs[0][...] = total.astype(jnp.bfloat16)
+            for place, out in enumerate(outs):
+
+                @pl.when(step // 2 == place)
+                def _(out=out):
+                    out[...] = total.astype(jnp.bfloat16)
+
             return
-        for step, out in enumerate(outs[:3]):
-
-            @pl.when(pl.program_id(0) == step)
+        for place, out in enumerate(outs[:3]):
+
+            @pl.when(step == place)
             def _(out=out):
                 out[...] = total.astype(jnp.bfloat16)
 
-        @pl.when(pl.program_id(0) == 3)
+        @pl.when(step == 3)
         def _():
             outs[3][...] = total[:, : width // 2].astype(jnp.bfloat16)
             outs[4][...] = total[:, width // 2 :].astype(jnp.bfloat16)
 
+    def half_of(place):
+        return pl.BlockSpec((slots, width), lambda i: (jnp.clip(i - 2 * place, 0, 1), 0))
+
     if split:
         shapes = [(slots, width)] * 3 + [(slots, width // 2)] * 2
     else:
-        shapes = [(4 * slots, width)]
+        shapes = [(2 * slots, width)] * 2
     return chain.launch(
         kernel,
         [*blocked, *known, *extra],
         [pl.BlockSpec((slots, item.shape[1]), lambda i: (i + 4 * place, 0)) for item in blocked]
         + [whole(item) for item in known]
-        + [pl.BlockSpec((slots, width), lambda i: (i, 0)) for _ in extra],
+        + [half_of(place) for place in range(len(extra))],
         [(shape, jnp.bfloat16) for shape in shapes],
-        [pl.BlockSpec((slots, shape[1]), lambda i: (0 if split else i, 0)) for shape in shapes],
+        [
+            pl.BlockSpec((slots, shape[1]), lambda i: (0, 0)) if split else half_of(place)
+            for place, shape in enumerate(shapes)
+        ],
         (4,),
     )
 
@@ -448,14 +471,11 @@
     slope[...] = below + hidden * density
 
 
-def grad_hidden_kernel(
-    cotangent, slope, weight, out, cotangent_out, out_sum, cotangent_sum
-):
+def grad_hidden_kernel(cotangent, slope, weight, out, out_sum, cotangent_sum):
     grad = (times_paired(cotangent[...], weight[...]) * slope[...]).astype(jnp.bfloat16)
     out[...] = grad
     add_columns(out_sum, grad)
     add_columns(cotangent_sum, cotangent[...])
-    cotangent_out[...] = cotangent[...]
 
 
 def branch_terms(attn, active, dense, contract):
@@ -468,8 +488,8 @@
 
 def attend_kernel(
     head_dim,
+    cotangent,
     qkv,
-    cotangent,
     cosine,
     sine,
     segment,
@@ -529,17 +549,18 @@
     )[0]
 
 
-def output_terms(chain, active, attn, groups, right):
-    depth, width = right.shape
+def output_terms(chain, active, attn, groups, pair):
+    depth, width = pair[0].shape
     tile = width // 4
     lefts = [active, attn]
     own = [item.shape[1] // groups for item in lefts]
     stride = sum(own)
 
-    def kernel(active, attn, right, out):
+    def kernel(active, attn, one, two, out):
         before = 0
         for left, many in zip((active, attn), own):
-            terms = times_leading(left[...], right[...]).astype(jnp.bfloat16)
+            terms = times_leading(left[:depth], one[...]) + times_leading(left[depth:], two[...])
+            terms = terms.astype(jnp.bfloat16)
             for group in range(groups):
                 at = group * stride + before
                 out[at : at + many, :] = terms[group * many : (group + 1) * many]
@@ -547,12 +568,12 @@
 
     return chain.launch(
         kernel,
-        [active, attn, right],
+        [active, attn, *pair],
         [
             pl.BlockSpec(item.shape, lambda i: (0, 0), pipeline_mode=pl.Buffered(1))
             for item in lefts
         ]
-        + [pl.BlockSpec((depth, tile), lambda i: (0, i))],
+        + [pl.BlockSpec((depth, tile), lambda i: (0, i))] * 2,
         [((groups * stride, width), jnp.bfloat16)],
         [pl.BlockSpec((groups * stride, tile), lambda i: (0, i))],
         (width // tile,),
@@ -673,7 +694,7 @@
     sizes = [item.shape[0] for item in parts]
     lines = -(-sum(sizes) // 1024) * 8
     small = jnp.concatenate(parts + [jnp.zeros((lines * 128 - sum(sizes),), jnp.bfloat16)])
-    every = gather_small(small.reshape(lines, 128), outer_bits + (0, 2, 1), me, plan)
+    every = gather_small(small.reshape(lines, 128), (1, 2, 0) + outer_bits, me, plan)
     every = every.reshape(count, lines * 128).astype(jnp.float32)
 
     expand_places = [
@@ -692,7 +713,6 @@
     own = exchange(pack(chain, [qkv_weight, expand_weight], moves, split + hidden_units))
     token_pieces = all_pieces(own_tokens, own_tokens[4], 1, plan)
     own_cotangent = own_pieces(cotangent, plan)
-    early = [weight_out] + [piece for piece, _ in token_pieces[1:]]
     taken, at = [], 0
     for size in sizes:
         taken.append(every[:, at : at + size])
@@ -711,13 +731,14 @@
     ).astype(jnp.int32)
     segment, position = jax.vmap(lambda item: slot_layout(item, slots))(lengths)
     cosine, sine = rotary_tables(position.reshape(-1), rotated, head_dim // 2)
-    chain.settle(cosine, *early)
+    chain.settle(every, *[piece for piece, _ in token_pieces[4:7]])
     qkv_own, expand_own = split_columns(chain, own.reshape(HEADS * rows, -1), split)
     weight_expand, weight_qkv = gather(expand_own), gather(qkv_own)
+    chain.settle(cosine, weight_out)
 
     def sum_begin(compute, blocked, known):
-        terms = terms_of(chain, compute, slots, width, 1, blocked, known, None, False)[0]
-        return swap(terms, 0, plan)
+        terms = terms_of(chain, compute, slots, width, 1, blocked, known, (), False)
+        return [swap(item, 0, plan) for item in terms]
 
     def sum_next(compute, blocked, known, got):
         own, of_x, of_y, left, right = terms_of(
@@ -744,7 +765,7 @@
         chain, [own_cotangent[0], own_cotangent[2], own_cotangent[4], passed]
     )
     other_half = swap(half, 0, plan)
-    cotangent_pieces = [(item, place) for item in (half, other_half) for place in range(4)]
+    group_cotangent = (half, other_half)
 
     active, slope = over_blocks(
         chain,
@@ -755,16 +776,17 @@
         [bias_expand, weight_expand],
         [(hidden_units, jnp.bfloat16), (hidden_units, jnp.float32)],
     )
-    grad_hidden, group_cotangent, hidden_sum, cotangent_sum, weight_contract = over_blocks(
+    grad_hidden, hidden_sum, cotangent_sum, weight_contract = over_blocks(
         chain,
         grad_hidden_kernel,
         slots,
-        cotangent_pieces,
+        [],
         [slope],
         [],
-        [(hidden_units, jnp.bfloat16), (width, jnp.bfloat16)],
+        [(hidden_units, jnp.bfloat16)],
         [hidden_units, width],
         (weight_out, contract_runs),
+        group_cotangent,
     )
     expand_got = reduce(input_terms(chain, normed, grad_hidden))
 
@@ -782,11 +804,12 @@
         lambda *refs: attend_kernel(head_dim, *refs),
         slots,
         [],
-        [qkv, group_cotangent, cosine, sine, segment.reshape(-1, 1)],
+        [qkv, cosine, sine, segment.reshape(-1, 1)],
         [segment],
         [(head_dim, jnp.bfloat16), (split, jnp.bfloat16)],
         [split],
         (weight_out, dense_runs),
+        group_cotangent,
     )
 
 
@@ -796,10 +819,13 @@
         [grad_qkv, grad_hidden],
         [weight_qkv, weight_expand, gain_one, gain_two],
     )
+    qkv_got = reduce(input_terms(chain, normed, grad_qkv))
     branch_got = sum_begin(*branch_of)
     norm_got = sum_begin(*norm_of)
-    qkv_got = reduce(input_terms(chain, normed, grad_qkv))
     branch = sum_next(*branch_of, branch_got)
+    expand_got = exchange(expand_got.reshape(HEADS, rows, hidden_units))
+    chain.settle(expand_got)
+    output_got = reduce(output_terms(chain, active, attn, groups, group_cotangent))
 
     sums = jnp.concatenate([qkv_sum, hidden_sum, cotangent_sum], axis=1).reshape(-1, 128)
     for bit in outer_bits:
@@ -814,12 +840,9 @@
     qkv_sums, expand_sums = sums[:, :split], sums[:, split:]
 
     branch = sum_last(*branch)
-    output_got = reduce(output_terms(chain, active, attn, groups, group_cotangent))
     norm_parts = sum_next(*norm_of, norm_got)
     layer_out = finish_output(chain, tokens, *branch, bias_dense, bias_contract)
-    expand_got = exchange(expand_got.reshape(HEADS, rows, hidden_units))
     qkv_got = exchange(qkv_got.reshape(HEADS, rows, split))
-    chain.settle(expand_got)
     norm_parts = sum_last(*norm_parts)
     expand_weight_grad, ln2_gain_grad, ln2_bias_grad = unpack(
         chain, expand_places, expand_got, expand_sums, expand_weight, ln2_gain, ln2_bias

time: 602 us -> 584 us (0.970)
  the two profiles are of different devices: /device:TPU:1 before, /device:TPU:0 now
where the time goes in v5:
time: 584 us; the launch traced here: 577 us
  Pallas kernels  280 us (48%)
  waiting for transfers between devices  181 us (31%)
  starting transfers between devices  61 us (10%)
  local copies, waits for them, and re-layouts  23.9 us (4%)
  other arithmetic  16.1 us (3%)
  between operations  14.9 us (3%)
    pallas_call x23, Pallas kernels, launch(): pl.pallas_call(body, grid_spec=pltpu.PrefetchScalarGridSpec(num_scalar_pr...  280 us
    ppermute x33, waiting for transfers between devices, swap(): return lax.ppermute(value, 'dp', plan.flip(bit))  176 us
    ppermute x33, starting transfers between devices, swap(): return lax.ppermute(value, 'dp', plan.flip(bit))  45.6 us
    unnamed x67, local copies, waits for them, and re-layouts  12.4 us
  transfers between devices with their start and end apart: 44, of which 20 were waited for; matrix products, arithmetic and copies ran while one was open for 5% of the time, Pallas kernels for 48%

profile of v5, /device:TPU:0, one launch (start us, length us, event | category | flops | bytes accessed | tf_op | source)
XLA Modules:
  0.0 577.3 jit_solution(11027981937228930843)
XLA Ops:
  11.4 18.4 %collective-permute-start.3 = (bf16[384,2048]{1,0:T(8,128)(2,1)S(1)}, bf16[384,2048]{1,0:T(8,128)(2,1)}, u32[]{:S(2)}, u32[]{:S(2)}) collective-permute-start(bf16[384,2048]{1,0:T(8,128)(2,1)S(1)} %copy-done), channel_id=1, source_target_pairs={{0,4},{1,5},{2,6},{3,7},{4,0},{5,1},{6,2},{7,3},{8,12},{9,13},{10,... | collective-permute-start | bytes 4718600 | tf_op jit(solution)/shard_map/ppermute | solution.py:42
  29.8 2.8 shard_map.254.refs_1_
  32.7 3.8 all-to-all-start
  36.9 28.3 %collective-permute-done.3.refs_2_ = bf16[384,2048]{1,0:T(8,128)(2,1)} collective-permute-done((bf16[384,2048]{1,0:T(8,128)(2,1)S(1)}, bf16[384,2048]{1,0:T(8,128)(2,1)}, u32[]{:S(2)}, u32[]{:S(2)}) %collective-permute-start.3) | collective-permute-done | bytes 1572896 | tf_op jit(solution)/shard_map/ppermute | solution.py:42
  65.2 2.0 collective-permute-done.2.refs_1_
  67.4 16.7 %collective-permute-done.9 = bf16[1,1,1,1,1,8,128]{6,5,4,3,2,1,0:T(8,128)(2,1)S(1)} collective-permute-done((bf16[1,1,1,1,1,8,128]{6,5,4,3,2,1,0:T(8,128)(2,1)S(1)}, bf16[1,1,1,1,1,8,128]{6,5,4,3,2,1,0:T(8,128)(2,1)S(1)}, u32[]{:S(2)}, u32[]{:S(2)}) %collective-permute-start.9) | collective-permute-done | bytes 2080 | tf_op jit(solution)/shard_map/ppermute | solution.py:42
  84.5 3.2 collective-permute-done.10
  89.0 1.8 collective-permute-start.4
  90.9 2.3 collective-permute-done.12
  93.2 3.0 collective-permute-start.13
  96.2 6.6 %collective-permute-done.13 = bf16[1,2,2,2,2,8,128]{6,5,4,3,2,1,0:T(8,128)(2,1)S(1)} collective-permute-done((bf16[1,2,2,2,2,8,128]{6,5,4,3,2,1,0:T(8,128)(2,1)S(1)}, bf16[1,2,2,2,2,8,128]{6,5,4,3,2,1,0:T(8,128)(2,1)S(1)}, u32[]{:S(2)}, u32[]{:S(2)}) %collective-permute-start.13) | collective-permute-done | bytes 32800 | tf_op jit(solution)/shard_map/ppermute | solution.py:42
  104.8 3.8 shard_map.255
  112.2 14.5 %collective-permute-done.4.refs_3_ = bf16[384,2048]{1,0:T(8,128)(2,1)} collective-permute-done((bf16[384,2048]{1,0:T(8,128)(2,1)}, bf16[384,2048]{1,0:T(8,128)(2,1)}, u32[]{:S(2)}, u32[]{:S(2)}) %collective-permute-start.4) | collective-permute-done | bytes 1572896 | tf_op jit(solution)/shard_map/ppermute | solution.py:42
  129.4 7.0 %fusion = (f32[3072,32]{1,0:T(8,128)S(1)}, f32[3072,32]{1,0:T(8,128)}, f32[3072,32]{1,0:T(8,128)S(1)}) fusion(f32[32]{0:T(128)S(1)} %multiply_exponential_fusion, f32[3072]{0:T(1024)S(1)} %convert_element_type.48), kind=kLoop, calls=%fused_computation.4 | loop fusion | flops 196608 | bytes 1192064 | tf_op jit(solution)/shard_map/neg | solution.py:124
  138.0 21.3 %shard_map.256 = (bf16[3072,2048]{1,0:T(8,128)(2,1)}, bf16[3072,2048]{1,0:T(8,128)(2,1)}, bf16[3072,2048]{1,0:T(8,128)(2,1)}) custom-call(bf16[384,2048]{1,0:T(8,128)(2,1)} %refs_1_.3, bf16[384,2048]{1,0:T(8,128)(2,1)} %collective-permute-done.2.refs_1_, bf16[384,2048]{1,0:T(8,128)(2,1)} %collective-permute-done.3.refs_2_, ...), custom_call_target="tpu_custom_call" | custom-call | flops 1 | bytes 1 | tf_op jit(solution)/shard_map/pallas_call | solution.py:86
  159.6 3.6 shard_map.257.refs_4_
  164.0 36.0 %collective-permute-done.15.refs_3_ = bf16[384,2048]{1,0:T(8,128)(2,1)} collective-permute-done((bf16[384,2048]{1,0:T(8,128)(2,1)}, bf16[384,2048]{1,0:T(8,128)(2,1)}, u32[]{:S(2)}, u32[]{:S(2)}) %collective-permute-start.15) | collective-permute-done | bytes 1572896 | tf_op jit(solution)/shard_map/ppermute | solution.py:42
  200.1 6.0 %shard_map.258.refs_3_.refs_0_.refs_2_ = bf16[1536,2048]{1,0:T(8,128)(2,1)} custom-call(bf16[384,2048]{1,0:T(8,128)(2,1)} %refs_0_.9, bf16[384,2048]{1,0:T(8,128)(2,1)} %collective-permute-done.refs_0_.refs_1_, bf16[384,2048]{1,0:T(8,128)(2,1)} %collective-permute-done.1.refs_2_, bf16[384,2048]{1,0:T(8,128)(2,1)} %collective-permute-done.15.refs_3_, ...), custom_call_target="tpu_custom_call" | custom-call | flops 1 | bytes 1 | tf_op jit(solution)/shard_map/pallas_call | solution.py:86
  207.3 22.5 %shard_map.259 = (bf16[3072,1024]{1,0:T(8,128)(2,1)}, f32[3072,1024]{1,0:T(8,128)}) custom-call(bf16[3072,2048]{1,0:T(8,128)(2,1)} %get-tuple-element.58.refs_0_, f32[1,1024]{1,0:T(1,128)} %bitcast.98, bf16[2048,1024]{1,0:T(8,128)(2,1)} %all-gather.8.cloned.1.call-done.refs_2_.refs_3_, bf16[1536,2048]{1,0:T(8,128)(2,1)} %shard_map.258.refs_3_.refs_0_.refs_2_), custom_call_target="tpu_custom_call" | custom-call | flops 1 | bytes 1 | tf_op jit(solution)/shard_map/pallas_call | solution.py:86
  229.8 25.3 %shard_map.260 = (bf16[3072,1024]{1,0:T(8,128)(2,1)}, f32[1,1024]{1,0:T(1,128)}, f32[1,2048]{1,0:T(1,128)}, bf16[1024,2048]{1,0:T(8,128)(2,1)}) custom-call(bf16[1536,2048]{1,0:T(8,128)(2,1)} %shard_map.258.refs_3_.refs_0_.refs_2_, bf16[1536,2048]{1,0:T(8,128)(2,1)} %collective-permute-done.16.refs_1_.refs_3_, f32[3072,1024]{1,0:T(8,128)} %get-tuple-element.60.refs_2_, ...), custom_call_target="tpu_custom_call" | custom-call | flops 1 | bytes 1 | tf_op jit(solution)/shard_map/pallas_call | solution.py:86
  255.1 18.8 %shard_map.261.refs_5_ = bf16[2048,1024]{1,0:T(8,128)(2,1)} custom-call(bf16[3072,2048]{1,0:T(8,128)(2,1)} %get-tuple-element.57.refs_0_, bf16[3072,1024]{1,0:T(8,128)(2,1)} %get-tuple-element.62.refs_1_.refs_2_, bf16[3072,1024]{1,0:T(8,128)(2,1)} %get-tuple-element.62.refs_1_.refs_2_), custom_call_target="tpu_custom_call" | custom-call | flops 1 | bytes 1 | tf_op jit(solution)/shard_map/pallas_call | solution.py:86
  278.2 16.1 %shard_map.262.refs_2_.refs_8_ = bf16[3072,768]{1,0:T(8,128)(2,1)} custom-call(bf16[3072,2048]{1,0:T(8,128)(2,1)} %get-tuple-element.56.refs_1_.refs_0_, f32[3072,128]{1,0:T(8,128)} %maximum_maximum_fusion.refs_13_.refs_1_.refs_3_, f32[3072,128]{1,0:T(8,128)} %maximum_maximum_fusion.1.refs_2_.refs_4_, f32[1,768]{1,0:T(1,128)} %bitcast.100, ...), custom_call_target="tpu_custom_call" | custom-call | flops 1 | bytes 1 | tf_op jit(solution)/shard_map/pallas_call | solution.py:86
  294.3 21.9 %shard_map.263 = (bf16[3072,256]{1,0:T(8,128)(2,1)}, bf16[3072,768]{1,0:T(8,128)(2,1)}, f32[1,768]{1,0:T(1,128)}, bf16[256,2048]{1,0:T(8,128)(2,1)}) custom-call(bf16[1536,2048]{1,0:T(8,128)(2,1)} %shard_map.258.refs_3_.refs_0_.refs_2_, bf16[1536,2048]{1,0:T(8,128)(2,1)} %collective-permute-done.16.refs_1_.refs_3_, ...), custom_call_target="tpu_custom_call" | custom-call | flops 1 | bytes 1 | tf_op jit(solution)/shard_map/pallas_call | solution.py:86
  316.1 15.6 %shard_map.264.refs_4_ = bf16[2048,768]{1,0:T(8,128)(2,1)} custom-call(bf16[3072,2048]{1,0:T(8,128)(2,1)} %get-tuple-element.57.refs_0_, bf16[3072,768]{1,0:T(8,128)(2,1)} %get-tuple-element.66.refs_1_.refs_0_, bf16[3072,256]{1,0:T(8,128)(2,1)} %get-tuple-element.63.refs_2_.refs_0_.refs_1_), custom_call_target="tpu_custom_call" | custom-call | flops 1 | bytes 1 | tf_op jit(solution)/shard_map/pallas_call | solution.py:86
  331.7 14.1 %shard_map.265 = (bf16[768,2048]{1,0:T(8,128)(2,1)}, bf16[768,2048]{1,0:T(8,128)(2,1)}) custom-call(bf16[3072,256]{1,0:T(8,128)(2,1)} %get-tuple-element.63.refs_2_.refs_0_.refs_1_, bf16[3072,1024]{1,0:T(8,128)(2,1)} %get-tuple-element.61.refs_4_.refs_1_.refs_0_, bf16[256,2048]{1,0:T(8,128)(2,1)} %get-tuple-element.64.refs_2_, ...), custom_call_target="tpu_custom_call" | custom-call | flops 1 | bytes 1 | tf_op jit(solution)/shard_map/pallas_call | solution.py:86
  346.5 5.4 reduce-scatter.4.cloned.1.call-done
  351.9 3.6 all-to-all-start.1
  355.8 18.3 %shard_map.266 = (bf16[768,2048]{1,0:T(8,128)(2,1)}, bf16[768,2048]{1,0:T(8,128)(2,1)}) custom-call(bf16[3072,768]{1,0:T(8,128)(2,1)} %get-tuple-element.66.refs_1_.refs_0_, bf16[3072,1024]{1,0:T(8,128)(2,1)} %get-tuple-element.62.refs_1_.refs_2_, bf16[2048,768]{1,0:T(8,128)(2,1)} %all-gather.6.cloned.1.call-done.refs_4_.refs_2_, ...), custom_call_target="tpu_custom_call" | custom-call | flops 1 | bytes 1 | tf_op jit(solution)/shard_map/pallas_call | solution.py:86
  374.1 16.3 %shard_map.267 = (bf16[384,2048]{1,0:T(8,128)(2,1)}, bf16[384,2048]{1,0:T(8,128)(2,1)}, bf16[384,2048]{1,0:T(8,128)(2,1)}, bf16[384,1024]{1,0:T(8,128)(2,1)}, bf16[384,1024]{1,0:T(8,128)(2,1)}) custom-call(bf16[3072,256]{1,0:T(8,128)(2,1)} %get-tuple-element.63.refs_2_.refs_0_.refs_1_, bf16[3072,1024]{1,0:T(8,128)(2,1)} %get-tuple-element.61.refs_4_.refs_1_.refs_0_, ...), custom_call_target="tpu_custom_call" | custom-call | flops 1 | bytes 1 | tf_op jit(solution)/shard_map/pallas_call | solution.py:86
  391.4 22.5 %shard_map.268.refs_4_ = bf16[1280,2048]{1,0:T(8,128)(2,1)} custom-call(bf16[3072,1024]{1,0:T(8,128)(2,1)} %get-tuple-element.61.refs_4_.refs_1_.refs_0_, bf16[3072,256]{1,0:T(8,128)(2,1)} %get-tuple-element.63.refs_2_.refs_0_.refs_1_, bf16[1536,2048]{1,0:T(8,128)(2,1)} %shard_map.258.refs_3_.refs_0_.refs_2_, ...), custom_call_target="tpu_custom_call" | custom-call | flops 1 | bytes 1 | tf_op jit(solution)/shard_map/pallas_call | solution.py:86
  414.0 1.9 copy-done.7
  418.1 2.2 collective-permute-done.21
  420.2 3.0 collective-permute-start.22
  423.2 2.0 collective-permute-start.19
  428.5 13.8 %collective-permute-done.24 = f32[1,1,2,14,128]{4,3,2,1,0:T(8,128)S(1)} collective-permute-done((f32[1,1,2,14,128]{4,3,2,1,0:T(8,128)S(1)}, f32[1,1,2,14,128]{4,3,2,1,0:T(8,128)S(1)}, u32[]{:S(2)}, u32[]{:S(2)}) %collective-permute-start.24) | collective-permute-done | bytes 14368 | tf_op jit(solution)/shard_map/ppermute | solution.py:42
  444.0 2.3 collective-permute-done.25
  446.9 3.8 shard_map.269
  453.8 21.7 %shard_map.270 = (bf16[384,2048]{1,0:T(8,128)(2,1)}, bf16[384,2048]{1,0:T(8,128)(2,1)}, bf16[384,2048]{1,0:T(8,128)(2,1)}, bf16[384,1024]{1,0:T(8,128)(2,1)}, bf16[384,1024]{1,0:T(8,128)(2,1)}) custom-call(bf16[3072,768]{1,0:T(8,128)(2,1)} %get-tuple-element.66.refs_1_.refs_0_, bf16[3072,1024]{1,0:T(8,128)(2,1)} %get-tuple-element.62.refs_1_.refs_2_, ...), custom_call_target="tpu_custom_call" | custom-call | flops 1 | bytes 1 | tf_op jit(solution)/shard_map/pallas_call | solution.py:86
  477.8 10.5 %collective-permute-done.26.refs_2_ = bf16[384,2048]{1,0:T(8,128)(2,1)} collective-permute-done((bf16[384,2048]{1,0:T(8,128)(2,1)}, bf16[384,2048]{1,0:T(8,128)(2,1)}, u32[]{:S(2)}, u32[]{:S(2)}) %collective-permute-start.26) | collective-permute-done | bytes 1572896 | tf_op jit(solution)/shard_map/ppermute | solution.py:42
  490.0 4.9 shard_map.271.refs_4_
  494.9 6.8 %collective-permute-done.30.refs_2_ = bf16[384,1024]{1,0:T(8,128)(2,1)S(1)} collective-permute-done((bf16[384,1024]{1,0:T(8,128)(2,1)}, bf16[384,1024]{1,0:T(8,128)(2,1)S(1)}, u32[]{:S(2)}, u32[]{:S(2)}) %collective-permute-start.30) | collective-permute-done | bytes 786464 | tf_op jit(solution)/shard_map/ppermute | solution.py:42
  503.4 3.8 shard_map.272
  509.6 3.5 all-to-all-start.2
  515.2 4.1 shard_map.273
  519.3 2.9 shard_map.274
  528.5 25.6 %collective-permute-done.32.refs_3_ = bf16[384,2048]{1,0:T(8,128)(2,1)S(1)} collective-permute-done((bf16[384,2048]{1,0:T(8,128)(2,1)}, bf16[384,2048]{1,0:T(8,128)(2,1)S(1)}, u32[]{:S(2)}, u32[]{:S(2)}) %collective-permute-start.32) | collective-permute-done | bytes 1572896 | tf_op jit(solution)/shard_map/ppermute | solution.py:42
  555.3 6.4 %shard_map.275.refs_5_ = f32[384,2048]{1,0:T(8,128)} custom-call(bf16[384,2048]{1,0:T(8,128)(2,1)} %refs_0_.9, bf16[384,2048]{1,0:T(8,128)(2,1)} %refs_1_.3, bf16[384,2048]{1,0:T(8,128)(2,1)} %get-tuple-element.81.refs_6_.refs_2_, bf16[384,2048]{1,0:T(8,128)(2,1)} %copy-done.8, bf16[384,2048]{1,0:T(8,128)(2,1)} %collective-permute-done.33.refs_4_, ...), custom_call_target="tpu_custom_call" | custom-call | flops 1 | bytes 1 | tf_op jit(solution)/shard_map/pallas_call | solution.py:86
  562.6 3.5 shard_map.276
  (205 shorter events, 58.3 us)
Async XLA Ops:
  7.2 130.8 %all-gather.4.cloned.1.call-start = ((), (), s32[]{:S(2)}) async-start(), calls=%async_computation.6 | async-start | bytes 6553600 | tf_op jit(solution)/shard_map/all_gather | solution.py:662
  7.2 3.0 collective-permute-start.14
  11.4 53.8 %collective-permute-start.3 = (bf16[384,2048]{1,0:T(8,128)(2,1)S(1)}, bf16[384,2048]{1,0:T(8,128)(2,1)}, u32[]{:S(2)}, u32[]{:S(2)}) collective-permute-start(bf16[384,2048]{1,0:T(8,128)(2,1)S(1)} %copy-done), channel_id=1, source_target_pairs={{0,4},{1,5},{2,6},{3,7},{4,0},{5,1},{6,2},{7,3},{8,12},{9,13},{10,... | collective-permute-start | bytes 4718600 | tf_op jit(solution)/shard_map/ppermute | solution.py:42
  29.8 37.4 %collective-permute-start.2 = (bf16[384,2048]{1,0:T(8,128)(2,1)S(1)}, bf16[384,2048]{1,0:T(8,128)(2,1)}, u32[]{:S(2)}, u32[]{:S(2)}) collective-permute-start(bf16[384,2048]{1,0:T(8,128)(2,1)S(1)} %copy-done), channel_id=1, source_target_pairs={{0,2},{1,3},{2,0},{3,1},{4,6},{5,7},{6,4},{7,5},{8,10},{9,11},{10,... | collective-permute-start | bytes 4718600 | tf_op jit(solution)/shard_map/ppermute | solution.py:42
  32.6 34.6 %copy-start.23 = (bf16[256]{0:T(256)(128)(2,1)S(1)}, bf16[256]{0:T(256)(128)(2,1)}, u32[]{:S(2)}) copy-start(bf16[256]{0:T(256)(128)(2,1)} %param.26) | copy-start | bytes 1540
  32.7 70.9 %all-to-all-start = ((bf16[8,64,1792]{2,1,0:T(8,128)(2,1)}), bf16[8,64,1792]{2,1,0:T(8,128)(2,1)S(1)}, u32[]{:S(2)}, u32[]{:S(2)}) async-start(bf16[8,64,1792]{2,1,0:T(8,128)(2,1)} %shard_map.254.refs_1_), calls=%async_computation | async-start | bytes 3670016 | tf_op jit(solution)/shard_map/all_to_all | solution.py:670
  36.5 170.8 %all-gather.8.cloned.1.call-start = ((), (), s32[]{:S(2)}) async-start(), calls=%async_computation.8 | async-start | bytes 5242880 | tf_op jit(solution)/shard_map/all_gather | solution.py:662
  36.5 67.0 %collective-permute-start.5 = (bf16[384,2048]{1,0:T(8,128)(2,1)S(1)}, bf16[384,2048]{1,0:T(8,128)(2,1)}, u32[]{:S(2)}, u32[]{:S(2)}) collective-permute-start(bf16[384,2048]{1,0:T(8,128)(2,1)S(1)} %copy-done), channel_id=1, source_target_pairs={{0,1},{1,0},{2,3},{3,2},{4,5},{5,4},{6,7},{7,6},{8,9},{9,8},{10,11... | collective-permute-start | bytes 4718600 | tf_op jit(solution)/shard_map/ppermute | solution.py:42
  65.2 38.4 %collective-permute-start.7 = (bf16[384,2048]{1,0:T(8,128)(2,1)}, bf16[384,2048]{1,0:T(8,128)(2,1)}, u32[]{:S(2)}, u32[]{:S(2)}) collective-permute-start(bf16[384,2048]{1,0:T(8,128)(2,1)} %collective-permute-done.3.refs_2_), channel_id=1, source_target_pairs={{0,1},{1,0},{2,3},{3,2},{4,5},{5,4},{6,7},{7,6},{8,9},{9,8},{10,11... | collective-permute-start | bytes 4718600 | tf_op jit(solution)/shard_map/ppermute | solution.py:42
  67.2 36.4 %collective-permute-start.6 = (bf16[384,2048]{1,0:T(8,128)(2,1)}, bf16[384,2048]{1,0:T(8,128)(2,1)}, u32[]{:S(2)}, u32[]{:S(2)}) collective-permute-start(bf16[384,2048]{1,0:T(8,128)(2,1)} %collective-permute-done.2.refs_1_), channel_id=1, source_target_pairs={{0,1},{1,0},{2,3},{3,2},{4,5},{5,4},{6,7},{7,6},{8,9},{9,8},{10,11... | collective-permute-start | bytes 4718600 | tf_op jit(solution)/shard_map/ppermute | solution.py:42
  67.4 16.7 %collective-permute-start.9 = (bf16[1,1,1,1,1,8,128]{6,5,4,3,2,1,0:T(8,128)(2,1)S(1)}, bf16[1,1,1,1,1,8,128]{6,5,4,3,2,1,0:T(8,128)(2,1)S(1)}, u32[]{:S(2)}, u32[]{:S(2)}) collective-permute-start(bf16[1,1,1,1,1,8,128]{6,5,4,3,2,1,0:T(8,128)(2,1)S(1)} %bitcast.95), channel_id=1, source_target_pairs={{0,2},{1,3},{2,0},{3,1},{4,6},{5,7},{6,4},{7,5},{8,10},{9,11},{10,... | collective-permute-start | bytes 6152 | tf_op jit(solution)/shard_map/ppermute | solution.py:42
  84.1 3.6 collective-permute-start.10
  87.8 1.2 collective-permute-start.11
  88.9 4.2 collective-permute-start.12
  89.0 37.6 %collective-permute-start.4 = (bf16[384,2048]{1,0:T(8,128)(2,1)}, bf16[384,2048]{1,0:T(8,128)(2,1)}, u32[]{:S(2)}, u32[]{:S(2)}) collective-permute-start(bf16[384,2048]{1,0:T(8,128)(2,1)} %collective-permute-done.3.refs_2_), channel_id=1, source_target_pairs={{0,2},{1,3},{2,0},{3,1},{4,6},{5,7},{6,4},{7,5},{8,10},{9,11},{10,... | collective-permute-start | bytes 4718600 | tf_op jit(solution)/shard_map/ppermute | solution.py:42
  93.2 9.7 %collective-permute-start.13 = (bf16[1,2,2,2,2,8,128]{6,5,4,3,2,1,0:T(8,128)(2,1)S(1)}, bf16[1,2,2,2,2,8,128]{6,5,4,3,2,1,0:T(8,128)(2,1)S(1)}, u32[]{:S(2)}, u32[]{:S(2)}) collective-permute-start(bf16[1,2,2,2,2,8,128]{6,5,4,3,2,1,0:T(8,128)(2,1)S(1)} %maximum_select_fusion.2), channel_id=1, source_target_pairs={{0,16},{1,17},{2,18},{3,19},{4,20},{5,21},{6,22},{7,23},{8,24},{9,... | collective-permute-start | bytes 98312 | tf_op jit(solution)/shard_map/ppermute | solution.py:42
  108.6 169.6 %all-gather.6.cloned.1.call-start = ((), (), s32[]{:S(2)}) async-start(), calls=%async_computation.7 | async-start | bytes 3932160 | tf_op jit(solution)/shard_map/all_gather | solution.py:662
  108.7 50.9 %collective-permute-start = (bf16[384,2048]{1,0:T(8,128)(2,1)S(1)}, bf16[384,2048]{1,0:T(8,128)(2,1)}, u32[]{:S(2)}, u32[]{:S(2)}) collective-permute-start(bf16[384,2048]{1,0:T(8,128)(2,1)S(1)} %copy-done.4), channel_id=1, source_target_pairs={{0,2},{1,3},{2,0},{3,1},{4,6},{5,7},{6,4},{7,5},{8,10},{9,11},{10,... | collective-permute-start | bytes 4718600 | tf_op jit(solution)/shard_map/ppermute | solution.py:42
  110.0 54.0 %collective-permute-start.1 = (bf16[384,2048]{1,0:T(8,128)(2,1)S(1)}, bf16[384,2048]{1,0:T(8,128)(2,1)}, u32[]{:S(2)}, u32[]{:S(2)}) collective-permute-start(bf16[384,2048]{1,0:T(8,128)(2,1)S(1)} %copy-done.4), channel_id=1, source_target_pairs={{0,4},{1,5},{2,6},{3,7},{4,0},{5,1},{6,2},{7,3},{8,12},{9,13},{10,... | collective-permute-start | bytes 4718600 | tf_op jit(solution)/shard_map/ppermute | solution.py:42
  112.1 162.2 %copy-start.14 = (s32[8,384]{1,0:T(8,128)}, s32[8,384]{1,0:T(8,128)S(1)}, u32[]{:S(2)}) copy-start(s32[8,384]{1,0:T(8,128)S(1)} %get-tuple-element.96.refs_6_) | copy-start | bytes 36868
  126.7 11.3 %collective-permute-start.8 = (bf16[384,2048]{1,0:T(8,128)(2,1)}, bf16[384,2048]{1,0:T(8,128)(2,1)}, u32[]{:S(2)}, u32[]{:S(2)}) collective-permute-start(bf16[384,2048]{1,0:T(8,128)(2,1)} %collective-permute-done.4.refs_3_), channel_id=1, source_target_pairs={{0,1},{1,0},{2,3},{3,2},{4,5},{5,4},{6,7},{7,6},{8,9},{9,8},{10,11... | collective-permute-start | bytes 4718600 | tf_op jit(solution)/shard_map/ppermute | solution.py:42
  163.2 36.9 %collective-permute-start.15 = (bf16[384,2048]{1,0:T(8,128)(2,1)}, bf16[384,2048]{1,0:T(8,128)(2,1)}, u32[]{:S(2)}, u32[]{:S(2)}) collective-permute-start(bf16[384,2048]{1,0:T(8,128)(2,1)} %shard_map.257.refs_4_), channel_id=1, source_target_pairs={{0,4},{1,5},{2,6},{3,7},{4,0},{5,1},{6,2},{7,3},{8,12},{9,13},{10,... | collective-permute-start | bytes 4718600 | tf_op jit(solution)/shard_map/ppermute | solution.py:42
  206.0 23.8 %collective-permute-start.16 = (bf16[1536,2048]{1,0:T(8,128)(2,1)}, bf16[1536,2048]{1,0:T(8,128)(2,1)}, u32[]{:S(2)}, u32[]{:S(2)}) collective-permute-start(bf16[1536,2048]{1,0:T(8,128)(2,1)} %shard_map.258.refs_3_.refs_0_.refs_2_), channel_id=1, source_target_pairs={{0,1},{1,0},{2,3},{3,2},{4,5},{5,4},{6,7},{7,6},{8,9},{9,8},{10,11... | collective-permute-start | bytes 18874376 | tf_op jit(solution)/shard_map/ppermute | solution.py:42
  206.0 145.8 %reduce-scatter.4.cloned.1.call-start = ((), (), s32[]{:S(2)}) async-start(), calls=%async_computation.9 | async-start | bytes 5242880 | tf_op jit(solution)/shard_map/reduce_scatter | solution.py:665
  273.9 235.7 %reduce-scatter.8.cloned.1.call-start = ((), (), s32[]{:S(2)}) async-start(), calls=%async_computation.11 | async-start | bytes 3932160 | tf_op jit(solution)/shard_map/reduce_scatter | solution.py:665
  345.8 28.3 %collective-permute-start.17 = (bf16[768,2048]{1,0:T(8,128)(2,1)}, bf16[768,2048]{1,0:T(8,128)(2,1)}, u32[]{:S(2)}, u32[]{:S(2)}) collective-permute-start(bf16[768,2048]{1,0:T(8,128)(2,1)} %get-tuple-element.67.refs_6_), channel_id=1, source_target_pairs={{0,1},{1,0},{2,3},{3,2},{4,5},{5,4},{6,7},{7,6},{8,9},{9,8},{10,11... | collective-permute-start | bytes 9437192 | tf_op jit(solution)/shard_map/ppermute | solution.py:42
  346.4 27.7 %collective-permute-start.18 = (bf16[768,2048]{1,0:T(8,128)(2,1)}, bf16[768,2048]{1,0:T(8,128)(2,1)}, u32[]{:S(2)}, u32[]{:S(2)}) collective-permute-start(bf16[768,2048]{1,0:T(8,128)(2,1)} %get-tuple-element.68), channel_id=1, source_target_pairs={{0,1},{1,0},{2,3},{3,2},{4,5},{5,4},{6,7},{7,6},{8,9},{9,8},{10,11... | collective-permute-start | bytes 9437192 | tf_op jit(solution)/shard_map/ppermute | solution.py:42
  351.9 38.6 %all-to-all-start.1 = ((bf16[8,64,1024]{2,1,0:T(8,128)(2,1)}), bf16[8,64,1024]{2,1,0:T(8,128)(2,1)S(1)}, u32[]{:S(2)}, u32[]{:S(2)}) async-start(bf16[8,64,1024]{2,1,0:T(8,128)(2,1)} %bitcast.81), calls=%async_computation.2 | async-start | bytes 2097152 | tf_op jit(solution)/shard_map/all_to_all | solution.py:670
  355.5 163.8 %reduce-scatter.6.cloned.1.call-start = ((), (), s32[]{:S(2)}) async-start(), calls=%async_computation.10 | async-start | bytes 6553600 | tf_op jit(solution)/shard_map/reduce_scatter | solution.py:665
  415.9 37.9 %collective-permute-start.28 = (bf16[768,2048]{1,0:T(8,128)(2,1)S(1)}, bf16[768,2048]{1,0:T(8,128)(2,1)}, u32[]{:S(2)}, u32[]{:S(2)}) collective-permute-start(bf16[768,2048]{1,0:T(8,128)(2,1)S(1)} %copy-done.7), channel_id=1, source_target_pairs={{0,1},{1,0},{2,3},{3,2},{4,5},{5,4},{6,7},{7,6},{8,9},{9,8},{10,11... | collective-permute-start | bytes 9437192 | tf_op jit(solution)/shard_map/ppermute | solution.py:42
  416.4 37.4 %collective-permute-start.29 = (bf16[768,2048]{1,0:T(8,128)(2,1)}, bf16[768,2048]{1,0:T(8,128)(2,1)}, u32[]{:S(2)}, u32[]{:S(2)}) collective-permute-start(bf16[768,2048]{1,0:T(8,128)(2,1)} %get-tuple-element.80), channel_id=1, source_target_pairs={{0,1},{1,0},{2,3},{3,2},{4,5},{5,4},{6,7},{7,6},{8,9},{9,8},{10,11... | collective-permute-start | bytes 9437192 | tf_op jit(solution)/shard_map/ppermute | solution.py:42
  416.4 3.8 collective-permute-start.21
  420.2 6.4 %collective-permute-start.22 = (f32[30,128]{1,0:T(8,128)S(1)}, f32[30,128]{1,0:T(8,128)S(1)}, u32[]{:S(2)}, u32[]{:S(2)}) collective-permute-start(f32[30,128]{1,0:T(8,128)S(1)} %bitcast_add_fusion), channel_id=1, source_target_pairs={{0,16},{1,17},{2,18},{3,19},{4,20},{5,21},{6,22},{7,23},{8,24},{9,... | collective-permute-start | bytes 46088 | tf_op jit(solution)/shard_map/ppermute | solution.py:42
  423.2 23.6 %collective-permute-start.19 = (bf16[384,1024]{1,0:T(8,128)(2,1)}, bf16[384,1024]{1,0:T(8,128)(2,1)}, u32[]{:S(2)}, u32[]{:S(2)}) collective-permute-start(bf16[384,1024]{1,0:T(8,128)(2,1)} %get-tuple-element.73), channel_id=1, source_target_pairs={{0,2},{1,3},{2,0},{3,1},{4,6},{5,7},{6,4},{7,5},{8,10},{9,11},{10,... | collective-permute-start | bytes 2359304 | tf_op jit(solution)/shard_map/ppermute | solution.py:42
  425.2 21.6 %collective-permute-start.20 = (bf16[384,1024]{1,0:T(8,128)(2,1)}, bf16[384,1024]{1,0:T(8,128)(2,1)}, u32[]{:S(2)}, u32[]{:S(2)}) collective-permute-start(bf16[384,1024]{1,0:T(8,128)(2,1)} %get-tuple-element.74), channel_id=1, source_target_pairs={{0,4},{1,5},{2,6},{3,7},{4,0},{5,1},{6,2},{7,3},{8,12},{9,13},{10,... | collective-permute-start | bytes 2359304 | tf_op jit(solution)/shard_map/ppermute | solution.py:42
  426.7 1.2 collective-permute-start.23
  428.0 14.3 %collective-permute-start.24 = (f32[1,1,2,14,128]{4,3,2,1,0:T(8,128)S(1)}, f32[1,1,2,14,128]{4,3,2,1,0:T(8,128)S(1)}, u32[]{:S(2)}, u32[]{:S(2)}) collective-permute-start(f32[1,1,2,14,128]{4,3,2,1,0:T(8,128)S(1)} %maximum_select_fusion.7), channel_id=1, source_target_pairs={{0,2},{1,3},{2,0},{3,1},{4,6},{5,7},{6,4},{7,5},{8,10},{9,11},{10,... | collective-permute-start | bytes 43016 | tf_op jit(solution)/shard_map/ppermute | solution.py:42
  442.3 3.9 collective-permute-start.25
  450.7 37.7 %collective-permute-start.26 = (bf16[384,2048]{1,0:T(8,128)(2,1)}, bf16[384,2048]{1,0:T(8,128)(2,1)}, u32[]{:S(2)}, u32[]{:S(2)}) collective-permute-start(bf16[384,2048]{1,0:T(8,128)(2,1)} %get-tuple-element.78.refs_8_), channel_id=1, source_target_pairs={{0,2},{1,3},{2,0},{3,1},{4,6},{5,7},{6,4},{7,5},{8,10},{9,11},{10,... | collective-permute-start | bytes 4718600 | tf_op jit(solution)/shard_map/ppermute | solution.py:42
  452.3 37.6 %collective-permute-start.27 = (bf16[384,2048]{1,0:T(8,128)(2,1)}, bf16[384,2048]{1,0:T(8,128)(2,1)}, u32[]{:S(2)}, u32[]{:S(2)}) collective-permute-start(bf16[384,2048]{1,0:T(8,128)(2,1)} %get-tuple-element.79), channel_id=1, source_target_pairs={{0,4},{1,5},{2,6},{3,7},{4,0},{5,1},{6,2},{7,3},{8,12},{9,13},{10,... | collective-permute-start | bytes 4718600 | tf_op jit(solution)/shard_map/ppermute | solution.py:42
  475.5 26.1 %collective-permute-start.30 = (bf16[384,1024]{1,0:T(8,128)(2,1)}, bf16[384,1024]{1,0:T(8,128)(2,1)S(1)}, u32[]{:S(2)}, u32[]{:S(2)}) collective-permute-start(bf16[384,1024]{1,0:T(8,128)(2,1)} %get-tuple-element.84), channel_id=1, source_target_pairs={{0,2},{1,3},{2,0},{3,1},{4,6},{5,7},{6,4},{7,5},{8,10},{9,11},{10,... | collective-permute-start | bytes 2359304 | tf_op jit(solution)/shard_map/ppermute | solution.py:42
  476.1 26.4 %collective-permute-start.31 = (bf16[384,1024]{1,0:T(8,128)(2,1)}, bf16[384,1024]{1,0:T(8,128)(2,1)S(1)}, u32[]{:S(2)}, u32[]{:S(2)}) collective-permute-start(bf16[384,1024]{1,0:T(8,128)(2,1)} %get-tuple-element.85), channel_id=1, source_target_pairs={{0,4},{1,5},{2,6},{3,7},{4,0},{5,1},{6,2},{7,3},{8,12},{9,13},{10,... | collective-permute-start | bytes 2359304 | tf_op jit(solution)/shard_map/ppermute | solution.py:42
  507.3 46.9 %collective-permute-start.32 = (bf16[384,2048]{1,0:T(8,128)(2,1)}, bf16[384,2048]{1,0:T(8,128)(2,1)S(1)}, u32[]{:S(2)}, u32[]{:S(2)}) collective-permute-start(bf16[384,2048]{1,0:T(8,128)(2,1)} %get-tuple-element.86.refs_5_), channel_id=1, source_target_pairs={{0,2},{1,3},{2,0},{3,1},{4,6},{5,7},{6,4},{7,5},{8,10},{9,11},{10,... | collective-permute-start | bytes 4718600 | tf_op jit(solution)/shard_map/ppermute | solution.py:42
  508.1 46.0 %collective-permute-start.33 = (bf16[384,2048]{1,0:T(8,128)(2,1)}, bf16[384,2048]{1,0:T(8,128)(2,1)}, u32[]{:S(2)}, u32[]{:S(2)}) collective-permute-start(bf16[384,2048]{1,0:T(8,128)(2,1)} %get-tuple-element.87), channel_id=1, source_target_pairs={{0,4},{1,5},{2,6},{3,7},{4,0},{5,1},{6,2},{7,3},{8,12},{9,13},{10,... | collective-permute-start | bytes 4718600 | tf_op jit(solution)/shard_map/ppermute | solution.py:42
  509.6 52.1 %all-to-all-start.2 = ((bf16[8,64,768]{2,1,0:T(8,128)(2,1)}), bf16[8,64,768]{2,1,0:T(8,128)(2,1)S(1)}, u32[]{:S(2)}, u32[]{:S(2)}) async-start(bf16[8,64,768]{2,1,0:T(8,128)(2,1)} %bitcast.82), calls=%async_computation.5 | async-start | bytes 1572864 | tf_op jit(solution)/shard_map/all_to_all | solution.py:670
  522.2 46.7 %collective-permute-start.34 = (bf16[64,2048]{1,0:T(8,128)(2,1)}, bf16[64,2048]{1,0:T(8,128)(2,1)S(1)}, u32[]{:S(2)}, u32[]{:S(2)}) collective-permute-start(bf16[64,2048]{1,0:T(8,128)(2,1)} %get-tuple-element.95), channel_id=1, source_target_pairs={{0,0},{8,1},{16,2},{24,3},{1,4},{9,5},{17,6},{25,7},{2,8},{10,9},{... | collective-permute-start | bytes 786440 | tf_op jit(solution)/shard_map/ppermute | solution.py:851
  525.3 44.4 %copy-start.29 = (f32[64]{0:T(128)}, f32[64]{0:T(128)S(1)}, u32[]{:S(2)}) copy-start(f32[64]{0:T(128)S(1)} %dynamic_slice.52) | copy-start | bytes 772
  525.3 36.4 %copy-start.13 = (f32[8,768]{1,0:T(8,128)}, f32[8,768]{1,0:T(8,128)S(1)}, u32[]{:S(2)}) copy-start(f32[8,768]{1,0:T(8,128)S(1)} %slice.63.refs_1_) | copy-start | bytes 73732
  (26 other events, 334.9 us)
Sparse Core Ops, SparseCore 0:
  11.5 115.0 all-gather.3
  128.2 78.9 all-gather.7
  208.7 62.0 all-gather.5
  274.0 77.8 reduce-scatter.3
  354.7 60.7 reduce-scatter.7
  417.8 93.7 reduce-scatter.5

commit v6 on v5

--- a/solution.py
+++ b/solution.py
@@ -16,6 +16,7 @@
 LEADING = (((0,), (0,)), ((), ()))
 VMEM_LIMIT = 60 * 2**20
 ORDER = (0, 2, 4, 6, 1, 3, 5, 7)
+LONG = 400_000_000_000
 BRIEF = pl.CostEstimate(flops=1, bytes_accessed=1, transcendentals=0)
 
 
@@ -76,7 +77,18 @@
     def settle(self, *values):
         self.waits += values
 
-    def launch(self, kernel, inputs, in_specs, outs, out_specs, grid=(1,), prefetch=(), **options):
+    def launch(
+        self,
+        kernel,
+        inputs,
+        in_specs,
+        outs,
+        out_specs,
+        grid=(1,),
+        prefetch=(),
+        estimate=1,
+        **options,
+    ):
         known = len(prefetch) + len(inputs)
         waits = self.waits
 
@@ -94,7 +106,7 @@
             ),
             out_shape=[jax.ShapeDtypeStruct(shape, kind) for shape, kind in outs],
             compiler_params=pltpu.CompilerParams(vmem_limit_bytes=VMEM_LIMIT),
-            cost_estimate=BRIEF,
+            cost_estimate=pl.CostEstimate(flops=estimate, bytes_accessed=1, transcendentals=0),
         )(*prefetch, *inputs, *waits)
         self.waits = [made[0]]
         return made
@@ -375,6 +387,7 @@
         [((slots, width), jnp.bfloat16)],
         [spec],
         (slots // tile,),
+        estimate=LONG,
     )[0]
 
 
@@ -826,6 +839,15 @@
     expand_got = exchange(expand_got.reshape(HEADS, rows, hidden_units))
     chain.settle(expand_got)
     output_got = reduce(output_terms(chain, active, attn, groups, group_cotangent))
+    branch = sum_last(*branch)
+    chain.settle(qkv_got)
+    norm_parts = sum_next(*norm_of, norm_got)
+    layer_out = finish_output(chain, tokens, *branch, bias_dense, bias_contract)
+
+    norm_parts = sum_last(*norm_parts)
+    input_grad = finish_input(chain, cotangent, tokens, *norm_parts)
+    contract_weight_grad, dense_grad = split_output(chain, output_got, units, rows)
+    dense_weight_grad = lax.ppermute(dense_grad, "dp", from_slot).astype(jnp.float32)
 
     sums = jnp.concatenate([qkv_sum, hidden_sum, cotangent_sum], axis=1).reshape(-1, 128)
     for bit in outer_bits:
@@ -839,17 +861,10 @@
     sums = sums.reshape(HEADS, -1)
     qkv_sums, expand_sums = sums[:, :split], sums[:, split:]
 
-    branch = sum_last(*branch)
-    norm_parts = sum_next(*norm_of, norm_got)
-    layer_out = finish_output(chain, tokens, *branch, bias_dense, bias_contract)
-    qkv_got = exchange(qkv_got.reshape(HEADS, rows, split))
-    norm_parts = sum_last(*norm_parts)
     expand_weight_grad, ln2_gain_grad, ln2_bias_grad = unpack(
         chain, expand_places, expand_got, expand_sums, expand_weight, ln2_gain, ln2_bias
     )
-    contract_weight_grad, dense_grad = split_output(chain, output_got, units, rows)
-    dense_weight_grad = lax.ppermute(dense_grad, "dp", from_slot).astype(jnp.float32)
-    input_grad = finish_input(chain, cotangent, tokens, *norm_parts)
+    qkv_got = exchange(qkv_got.reshape(HEADS, rows, split))
     qkv_weight_grad, ln1_gain_grad, ln1_bias_grad = unpack(
         chain, qkv_places, qkv_got, qkv_sums, qkv_weight, ln1_gain, ln1_bias
     )

time: 584 us -> 564 us (0.966)
  the two profiles are of different devices: /device:TPU:0 before, /device:TPU:1 now
where the time goes in v6:
time: 564 us; the launch traced here: 557 us
  Pallas kernels  279 us (49%)
  waiting for transfers between devices  148 us (26%)
  starting transfers between devices  73.9 us (13%)
  local copies, waits for them, and re-layouts  22.1 us (4%)
  other arithmetic  18.9 us (3%)
  between operations  15 us (3%)
    pallas_call x23, Pallas kernels, launch(): pl.pallas_call(body, grid_spec=pltpu.PrefetchScalarGridSpec(num_scalar_pr...  279 us
    ppermute x33, waiting for transfers between devices, swap(): return lax.ppermute(value, 'dp', plan.flip(bit))  143 us
    ppermute x33, starting transfers between devices, swap(): return lax.ppermute(value, 'dp', plan.flip(bit))  48.9 us
    all_to_all x3, starting transfers between devices, exchange(): lax.all_to_all(value, 'dp', 0, 0, tiled=True, axis_index_groups=sharing)  13.1 us
    unnamed x79, local copies, waits for them, and re-layouts  11.9 us
  transfers between devices with their start and end apart: 44, of which 14 were waited for; matrix products, arithmetic and copies ran while one was open for 6% of the time, Pallas kernels for 50%

profile of v6, /device:TPU:1, one launch (start us, length us, event | category | flops | bytes accessed | tf_op | source)
XLA Modules:
  0.0 557.0 jit_solution(16624276257761039486)
XLA Ops:
  7.2 4.7 collective-permute-start.14
  13.3 2.9 collective-permute-done.14
  17.3 10.4 %collective-permute-start.3 = (bf16[384,2048]{1,0:T(8,128)(2,1)S(1)}, bf16[384,2048]{1,0:T(8,128)(2,1)}, u32[]{:S(2)}, u32[]{:S(2)}) collective-permute-start(bf16[384,2048]{1,0:T(8,128)(2,1)S(1)} %copy-done.3), channel_id=1, source_target_pairs={{0,4},{1,5},{2,6},{3,7},{4,0},{5,1},{6,2},{7,3},{8,12},{9,13},{10,... | collective-permute-start | bytes 4718600 | tf_op jit(solution)/shard_map/ppermute | solution.py:43
  27.7 2.8 shard_map.254.refs_1_
  30.6 5.8 %all-to-all-start = ((bf16[8,64,1792]{2,1,0:T(8,128)(2,1)}), bf16[8,64,1792]{2,1,0:T(8,128)(2,1)S(1)}, u32[]{:S(2)}, u32[]{:S(2)}) async-start(bf16[8,64,1792]{2,1,0:T(8,128)(2,1)} %shard_map.254.refs_1_), calls=%async_computation | async-start | bytes 3670016 | tf_op jit(solution)/shard_map/all_to_all | solution.py:683
  36.6 24.0 %collective-permute-done.3.refs_2_ = bf16[384,2048]{1,0:T(8,128)(2,1)} collective-permute-done((bf16[384,2048]{1,0:T(8,128)(2,1)S(1)}, bf16[384,2048]{1,0:T(8,128)(2,1)}, u32[]{:S(2)}, u32[]{:S(2)}) %collective-permute-start.3) | collective-permute-done | bytes 1572896 | tf_op jit(solution)/shard_map/ppermute | solution.py:43
  60.6 4.6 collective-permute-start.7
  65.2 2.0 collective-permute-start.6
  67.5 13.8 %collective-permute-done.9 = bf16[1,1,1,1,1,8,128]{6,5,4,3,2,1,0:T(8,128)(2,1)S(1)} collective-permute-done((bf16[1,1,1,1,1,8,128]{6,5,4,3,2,1,0:T(8,128)(2,1)S(1)}, bf16[1,1,1,1,1,8,128]{6,5,4,3,2,1,0:T(8,128)(2,1)S(1)}, u32[]{:S(2)}, u32[]{:S(2)}) %collective-permute-start.9) | collective-permute-done | bytes 2080 | tf_op jit(solution)/shard_map/ppermute | solution.py:43
  81.6 2.5 collective-permute-done.10
  84.1 3.7 collective-permute-start.11
  90.0 2.0 collective-permute-done.12
  92.0 3.4 collective-permute-start.13
  95.4 6.8 %collective-permute-done.13 = bf16[1,2,2,2,2,8,128]{6,5,4,3,2,1,0:T(8,128)(2,1)} collective-permute-done((bf16[1,2,2,2,2,8,128]{6,5,4,3,2,1,0:T(8,128)(2,1)S(1)}, bf16[1,2,2,2,2,8,128]{6,5,4,3,2,1,0:T(8,128)(2,1)}, u32[]{:S(2)}, u32[]{:S(2)}) %collective-permute-start.13) | collective-permute-done | bytes 32800 | tf_op jit(solution)/shard_map/ppermute | solution.py:43
  105.0 3.8 shard_map.255
  109.8 15.0 %collective-permute-done.4.refs_3_ = bf16[384,2048]{1,0:T(8,128)(2,1)} collective-permute-done((bf16[384,2048]{1,0:T(8,128)(2,1)}, bf16[384,2048]{1,0:T(8,128)(2,1)}, u32[]{:S(2)}, u32[]{:S(2)}) %collective-permute-start.4) | collective-permute-done | bytes 1572896 | tf_op jit(solution)/shard_map/ppermute | solution.py:43
  124.8 1.9 collective-permute-start.8
  129.4 7.0 %fusion = (f32[3072,32]{1,0:T(8,128)S(1)}, f32[3072,32]{1,0:T(8,128)}, f32[3072,32]{1,0:T(8,128)S(1)}) fusion(f32[32]{0:T(128)S(1)} %multiply_exponential_fusion, f32[3072]{0:T(1024)S(1)} %convert_element_type.48), kind=kLoop, calls=%fused_computation.4 | loop fusion | flops 196608 | bytes 1192064 | tf_op jit(solution)/shard_map/neg | solution.py:136
  138.1 21.4 %shard_map.256 = (bf16[3072,2048]{1,0:T(8,128)(2,1)}, bf16[3072,2048]{1,0:T(8,128)(2,1)}, bf16[3072,2048]{1,0:T(8,128)(2,1)}) custom-call(bf16[384,2048]{1,0:T(8,128)(2,1)} %refs_1_.3, bf16[384,2048]{1,0:T(8,128)(2,1)} %collective-permute-done.2.refs_1_, bf16[384,2048]{1,0:T(8,128)(2,1)} %collective-permute-done.3.refs_2_, ...), custom_call_target="tpu_custom_call" | custom-call | flops 1 | bytes 1 | tf_op jit(solution)/shard_map/pallas_call | solution.py:98
  159.4 3.6 shard_map.257.refs_4_
  163.9 35.3 %collective-permute-done.15.refs_3_ = bf16[384,2048]{1,0:T(8,128)(2,1)} collective-permute-done((bf16[384,2048]{1,0:T(8,128)(2,1)}, bf16[384,2048]{1,0:T(8,128)(2,1)}, u32[]{:S(2)}, u32[]{:S(2)}) %collective-permute-start.15) | collective-permute-done | bytes 1572896 | tf_op jit(solution)/shard_map/ppermute | solution.py:43
  199.1 5.9 %shard_map.258.refs_3_.refs_0_.refs_2_ = bf16[1536,2048]{1,0:T(8,128)(2,1)} custom-call(bf16[384,2048]{1,0:T(8,128)(2,1)} %refs_0_.9, bf16[384,2048]{1,0:T(8,128)(2,1)} %collective-permute-done.refs_0_.refs_1_, bf16[384,2048]{1,0:T(8,128)(2,1)} %collective-permute-done.1.refs_2_, bf16[384,2048]{1,0:T(8,128)(2,1)} %collective-permute-done.15.refs_3_, ...), custom_call_target="tpu_custom_call" | custom-call | flops 1 | bytes 1 | tf_op jit(solution)/shard_map/pallas_call | solution.py:98
  207.4 22.5 %shard_map.259 = (bf16[3072,1024]{1,0:T(8,128)(2,1)}, f32[3072,1024]{1,0:T(8,128)}) custom-call(bf16[3072,2048]{1,0:T(8,128)(2,1)} %get-tuple-element.58.refs_0_, f32[1,1024]{1,0:T(1,128)} %bitcast.96, bf16[2048,1024]{1,0:T(8,128)(2,1)} %all-gather.8.cloned.1.call-done.refs_2_.refs_3_, bf16[1536,2048]{1,0:T(8,128)(2,1)} %shard_map.258.refs_3_.refs_0_.refs_2_), custom_call_target="tpu_custom_call" | custom-call | flops 1 | bytes 1 | tf_op jit(solution)/shard_map/pallas_call | solution.py:98
  229.9 25.3 %shard_map.260 = (bf16[3072,1024]{1,0:T(8,128)(2,1)}, f32[1,1024]{1,0:T(1,128)}, f32[1,2048]{1,0:T(1,128)}, bf16[1024,2048]{1,0:T(8,128)(2,1)}) custom-call(bf16[1536,2048]{1,0:T(8,128)(2,1)} %shard_map.258.refs_3_.refs_0_.refs_2_, bf16[1536,2048]{1,0:T(8,128)(2,1)} %collective-permute-done.16.refs_1_.refs_3_, f32[3072,1024]{1,0:T(8,128)} %get-tuple-element.60.refs_2_, ...), custom_call_target="tpu_custom_call" | custom-call | flops 1 | bytes 1 | tf_op jit(solution)/shard_map/pallas_call | solution.py:98
  255.2 18.8 %shard_map.261.refs_5_ = bf16[2048,1024]{1,0:T(8,128)(2,1)} custom-call(bf16[3072,2048]{1,0:T(8,128)(2,1)} %get-tuple-element.57.refs_0_, bf16[3072,1024]{1,0:T(8,128)(2,1)} %get-tuple-element.62.refs_1_.refs_2_, bf16[3072,1024]{1,0:T(8,128)(2,1)} %get-tuple-element.62.refs_1_.refs_2_), custom_call_target="tpu_custom_call" | custom-call | flops 1 | bytes 1 | tf_op jit(solution)/shard_map/pallas_call | solution.py:98
  278.3 16.1 %shard_map.262.refs_2_.refs_8_ = bf16[3072,768]{1,0:T(8,128)(2,1)} custom-call(bf16[3072,2048]{1,0:T(8,128)(2,1)} %get-tuple-element.56.refs_1_.refs_0_, f32[3072,128]{1,0:T(8,128)} %maximum_maximum_fusion.refs_13_.refs_1_.refs_3_, f32[3072,128]{1,0:T(8,128)} %maximum_maximum_fusion.1.refs_2_.refs_4_, f32[1,768]{1,0:T(1,128)} %bitcast.98, ...), custom_call_target="tpu_custom_call" | custom-call | flops 1 | bytes 1 | tf_op jit(solution)/shard_map/pallas_call | solution.py:98
  294.4 21.8 %shard_map.263 = (bf16[3072,256]{1,0:T(8,128)(2,1)}, bf16[3072,768]{1,0:T(8,128)(2,1)}, f32[1,768]{1,0:T(1,128)}, bf16[256,2048]{1,0:T(8,128)(2,1)}) custom-call(bf16[1536,2048]{1,0:T(8,128)(2,1)} %shard_map.258.refs_3_.refs_0_.refs_2_, bf16[1536,2048]{1,0:T(8,128)(2,1)} %collective-permute-done.16.refs_1_.refs_3_, ...), custom_call_target="tpu_custom_call" | custom-call | flops 1 | bytes 1 | tf_op jit(solution)/shard_map/pallas_call | solution.py:98
  316.2 15.5 %shard_map.264.refs_4_ = bf16[2048,768]{1,0:T(8,128)(2,1)} custom-call(bf16[3072,2048]{1,0:T(8,128)(2,1)} %get-tuple-element.57.refs_0_, bf16[3072,768]{1,0:T(8,128)(2,1)} %get-tuple-element.66.refs_1_.refs_0_, bf16[3072,256]{1,0:T(8,128)(2,1)} %get-tuple-element.63.refs_2_.refs_0_.refs_1_), custom_call_target="tpu_custom_call" | custom-call | flops 1 | bytes 1 | tf_op jit(solution)/shard_map/pallas_call | solution.py:98
  331.8 14.2 %shard_map.265 = (bf16[768,2048]{1,0:T(8,128)(2,1)}, bf16[768,2048]{1,0:T(8,128)(2,1)}) custom-call(bf16[3072,256]{1,0:T(8,128)(2,1)} %get-tuple-element.63.refs_2_.refs_0_.refs_1_, bf16[3072,1024]{1,0:T(8,128)(2,1)} %get-tuple-element.61.refs_4_.refs_1_.refs_0_, bf16[256,2048]{1,0:T(8,128)(2,1)} %get-tuple-element.64.refs_2_, ...), custom_call_target="tpu_custom_call" | custom-call | flops 1 | bytes 1 | tf_op jit(solution)/shard_map/pallas_call | solution.py:98
  346.4 18.3 %shard_map.266 = (bf16[768,2048]{1,0:T(8,128)(2,1)}, bf16[768,2048]{1,0:T(8,128)(2,1)}) custom-call(bf16[3072,768]{1,0:T(8,128)(2,1)} %get-tuple-element.66.refs_1_.refs_0_, bf16[3072,1024]{1,0:T(8,128)(2,1)} %get-tuple-element.62.refs_1_.refs_2_, bf16[2048,768]{1,0:T(8,128)(2,1)} %all-gather.6.cloned.1.call-done.refs_4_.refs_2_, ...), custom_call_target="tpu_custom_call" | custom-call | flops 1 | bytes 1 | tf_op jit(solution)/shard_map/pallas_call | solution.py:98
  365.3 3.8 all-to-all-start.1
  369.2 16.3 %shard_map.267 = (bf16[384,2048]{1,0:T(8,128)(2,1)}, bf16[384,2048]{1,0:T(8,128)(2,1)}, bf16[384,2048]{1,0:T(8,128)(2,1)}, bf16[384,1024]{1,0:T(8,128)(2,1)}, bf16[384,1024]{1,0:T(8,128)(2,1)}) custom-call(bf16[3072,256]{1,0:T(8,128)(2,1)} %get-tuple-element.63.refs_2_.refs_0_.refs_1_, bf16[3072,1024]{1,0:T(8,128)(2,1)} %get-tuple-element.61.refs_4_.refs_1_.refs_0_, ...), custom_call_target="tpu_custom_call" | custom-call | flops 1 | bytes 1 | tf_op jit(solution)/shard_map/pallas_call | solution.py:98
  389.2 22.5 %shard_map.268.refs_4_ = bf16[1280,2048]{1,0:T(8,128)(2,1)} custom-call(bf16[3072,1024]{1,0:T(8,128)(2,1)} %get-tuple-element.61.refs_4_.refs_1_.refs_0_, bf16[3072,256]{1,0:T(8,128)(2,1)} %get-tuple-element.63.refs_2_.refs_0_.refs_1_, bf16[1536,2048]{1,0:T(8,128)(2,1)} %shard_map.258.refs_3_.refs_0_.refs_2_, ...), custom_call_target="tpu_custom_call" | custom-call | flops 1 | bytes 1 | tf_op jit(solution)/shard_map/pallas_call | solution.py:98
  412.9 3.7 shard_map.269
  421.3 21.5 %shard_map.270 = (bf16[384,2048]{1,0:T(8,128)(2,1)}, bf16[384,2048]{1,0:T(8,128)(2,1)}, bf16[384,2048]{1,0:T(8,128)(2,1)}, bf16[384,1024]{1,0:T(8,128)(2,1)}, bf16[384,1024]{1,0:T(8,128)(2,1)}) custom-call(bf16[3072,768]{1,0:T(8,128)(2,1)} %get-tuple-element.66.refs_1_.refs_0_, bf16[3072,1024]{1,0:T(8,128)(2,1)} %get-tuple-element.62.refs_1_.refs_2_, ...), custom_call_target="tpu_custom_call" | custom-call | flops 1 | bytes 1 | tf_op jit(solution)/shard_map/pallas_call | solution.py:98
  445.3 6.7 %collective-permute-done.21.refs_2_ = bf16[384,2048]{1,0:T(8,128)(2,1)S(1)} collective-permute-done((bf16[384,2048]{1,0:T(8,128)(2,1)}, bf16[384,2048]{1,0:T(8,128)(2,1)S(1)}, u32[]{:S(2)}, u32[]{:S(2)}) %collective-permute-start.21) | collective-permute-done | bytes 1572896 | tf_op jit(solution)/shard_map/ppermute | solution.py:43
  453.1 4.9 shard_map.271.refs_4_
  458.0 10.8 %collective-permute-done.25.refs_2_ = bf16[384,1024]{1,0:T(8,128)(2,1)} collective-permute-done((bf16[384,1024]{1,0:T(8,128)(2,1)}, bf16[384,1024]{1,0:T(8,128)(2,1)}, u32[]{:S(2)}, u32[]{:S(2)}) %collective-permute-start.25) | collective-permute-done | bytes 786464 | tf_op jit(solution)/shard_map/ppermute | solution.py:43
  468.8 3.6 shard_map.272
  474.7 3.7 collective-permute-start.30
  481.1 3.7 collective-permute-start.31
  484.8 3.5 all-to-all-start.2
  492.6 23.0 %collective-permute-done.32 = f32[1,1,2,14,128]{4,3,2,1,0:T(8,128)S(1)} collective-permute-done((f32[1,1,2,14,128]{4,3,2,1,0:T(8,128)S(1)}, f32[1,1,2,14,128]{4,3,2,1,0:T(8,128)S(1)}, u32[]{:S(2)}, u32[]{:S(2)}) %collective-permute-start.32) | collective-permute-done | bytes 14368 | tf_op jit(solution)/shard_map/ppermute | solution.py:43
  517.2 6.4 %shard_map.273.refs_1_ = f32[384,2048]{1,0:T(8,128)} custom-call(bf16[384,2048]{1,0:T(8,128)(2,1)} %refs_0_.9, bf16[384,2048]{1,0:T(8,128)(2,1)} %refs_1_.3, bf16[384,2048]{1,0:T(8,128)(2,1)} %get-tuple-element.78.refs_6_.refs_2_, bf16[384,2048]{1,0:T(8,128)(2,1)} %copy-done.7, bf16[384,2048]{1,0:T(8,128)(2,1)} %collective-permute-done.28.refs_4_, ...), custom_call_target="tpu_custom_call" | custom-call | flops 1 | bytes 1 | tf_op jit(solution)/shard_map/pallas_call | solution.py:98
  523.6 2.9 shard_map.274
  526.5 6.1 %collective-permute-start.34 = (bf16[64,2048]{1,0:T(8,128)(2,1)}, bf16[64,2048]{1,0:T(8,128)(2,1)S(1)}, u32[]{:S(2)}, u32[]{:S(2)}) collective-permute-start(bf16[64,2048]{1,0:T(8,128)(2,1)} %get-tuple-element.95), channel_id=1, source_target_pairs={{0,0},{8,1},{16,2},{24,3},{1,4},{9,5},{17,6},{25,7},{2,8},{10,9},{... | collective-permute-start | bytes 786440 | tf_op jit(solution)/shard_map/ppermute | solution.py:850
  534.0 4.1 shard_map.275
  539.1 3.5 shard_map.276
  (217 shorter events, 55.5 us)
Async XLA Ops:
  7.2 130.9 %all-gather.4.cloned.1.call-start = ((), (), s32[]{:S(2)}) async-start(), calls=%async_computation.6 | async-start | bytes 6553600 | tf_op jit(solution)/shard_map/all_gather | solution.py:675
  7.2 8.9 %collective-permute-start.14 = (bf16[64,2048]{1,0:T(8,128)(2,1)}, bf16[64,2048]{1,0:T(8,128)(2,1)S(1)}, u32[]{:S(2)}, u32[]{:S(2)}) collective-permute-start(bf16[64,2048]{1,0:T(8,128)(2,1)} %param.23), channel_id=1, source_target_pairs={{0,0},{1,8},{2,16},{3,24},{4,1},{5,9},{6,17},{7,25},{8,2},{9,10},{... | collective-permute-start | bytes 786440 | tf_op jit(solution)/shard_map/ppermute | solution.py:687
  17.3 43.4 %collective-permute-start.3 = (bf16[384,2048]{1,0:T(8,128)(2,1)S(1)}, bf16[384,2048]{1,0:T(8,128)(2,1)}, u32[]{:S(2)}, u32[]{:S(2)}) collective-permute-start(bf16[384,2048]{1,0:T(8,128)(2,1)S(1)} %copy-done.3), channel_id=1, source_target_pairs={{0,4},{1,5},{2,6},{3,7},{4,0},{5,1},{6,2},{7,3},{8,12},{9,13},{10,... | collective-permute-start | bytes 4718600 | tf_op jit(solution)/shard_map/ppermute | solution.py:43
  27.7 37.6 %collective-permute-start.2 = (bf16[384,2048]{1,0:T(8,128)(2,1)S(1)}, bf16[384,2048]{1,0:T(8,128)(2,1)}, u32[]{:S(2)}, u32[]{:S(2)}) collective-permute-start(bf16[384,2048]{1,0:T(8,128)(2,1)S(1)} %copy-done.3), channel_id=1, source_target_pairs={{0,2},{1,3},{2,0},{3,1},{4,6},{5,7},{6,4},{7,5},{8,10},{9,11},{10,... | collective-permute-start | bytes 4718600 | tf_op jit(solution)/shard_map/ppermute | solution.py:43
  30.5 36.8 %copy-start.24 = (bf16[192]{0:T(256)(128)(2,1)S(1)}, bf16[192]{0:T(256)(128)(2,1)}, u32[]{:S(2)}) copy-start(bf16[192]{0:T(256)(128)(2,1)} %param.22) | copy-start | bytes 1156
  30.5 36.8 %copy-start.25 = (bf16[256]{0:T(256)(128)(2,1)S(1)}, bf16[256]{0:T(256)(128)(2,1)}, u32[]{:S(2)}) copy-start(bf16[256]{0:T(256)(128)(2,1)} %param.26) | copy-start | bytes 1540
  30.5 36.8 %copy-start.26 = (bf16[64]{0:T(256)(128)(2,1)S(1)}, bf16[64]{0:T(256)(128)(2,1)}, u32[]{:S(2)}) copy-start(bf16[64]{0:T(256)(128)(2,1)} %param.19) | copy-start | bytes 388
  30.6 73.2 %all-to-all-start = ((bf16[8,64,1792]{2,1,0:T(8,128)(2,1)}), bf16[8,64,1792]{2,1,0:T(8,128)(2,1)S(1)}, u32[]{:S(2)}, u32[]{:S(2)}) async-start(bf16[8,64,1792]{2,1,0:T(8,128)(2,1)} %shard_map.254.refs_1_), calls=%async_computation | async-start | bytes 3670016 | tf_op jit(solution)/shard_map/all_to_all | solution.py:683
  36.4 171.0 %all-gather.8.cloned.1.call-start = ((), (), s32[]{:S(2)}) async-start(), calls=%async_computation.8 | async-start | bytes 5242880 | tf_op jit(solution)/shard_map/all_gather | solution.py:675
  36.4 67.4 %collective-permute-start.5 = (bf16[384,2048]{1,0:T(8,128)(2,1)S(1)}, bf16[384,2048]{1,0:T(8,128)(2,1)}, u32[]{:S(2)}, u32[]{:S(2)}) collective-permute-start(bf16[384,2048]{1,0:T(8,128)(2,1)S(1)} %copy-done.3), channel_id=1, source_target_pairs={{0,1},{1,0},{2,3},{3,2},{4,5},{5,4},{6,7},{7,6},{8,9},{9,8},{10,11... | collective-permute-start | bytes 4718600 | tf_op jit(solution)/shard_map/ppermute | solution.py:43
  60.6 43.1 %collective-permute-start.7 = (bf16[384,2048]{1,0:T(8,128)(2,1)}, bf16[384,2048]{1,0:T(8,128)(2,1)}, u32[]{:S(2)}, u32[]{:S(2)}) collective-permute-start(bf16[384,2048]{1,0:T(8,128)(2,1)} %collective-permute-done.3.refs_2_), channel_id=1, source_target_pairs={{0,1},{1,0},{2,3},{3,2},{4,5},{5,4},{6,7},{7,6},{8,9},{9,8},{10,11... | collective-permute-start | bytes 4718600 | tf_op jit(solution)/shard_map/ppermute | solution.py:43
  65.2 38.6 %collective-permute-start.6 = (bf16[384,2048]{1,0:T(8,128)(2,1)}, bf16[384,2048]{1,0:T(8,128)(2,1)}, u32[]{:S(2)}, u32[]{:S(2)}) collective-permute-start(bf16[384,2048]{1,0:T(8,128)(2,1)} %collective-permute-done.2.refs_1_), channel_id=1, source_target_pairs={{0,1},{1,0},{2,3},{3,2},{4,5},{5,4},{6,7},{7,6},{8,9},{9,8},{10,11... | collective-permute-start | bytes 4718600 | tf_op jit(solution)/shard_map/ppermute | solution.py:43
  67.4 13.8 %collective-permute-start.9 = (bf16[1,1,1,1,1,8,128]{6,5,4,3,2,1,0:T(8,128)(2,1)S(1)}, bf16[1,1,1,1,1,8,128]{6,5,4,3,2,1,0:T(8,128)(2,1)S(1)}, u32[]{:S(2)}, u32[]{:S(2)}) collective-permute-start(bf16[1,1,1,1,1,8,128]{6,5,4,3,2,1,0:T(8,128)(2,1)S(1)} %bitcast.93), channel_id=1, source_target_pairs={{0,2},{1,3},{2,0},{3,1},{4,6},{5,7},{6,4},{7,5},{8,10},{9,11},{10,... | collective-permute-start | bytes 6152 | tf_op jit(solution)/shard_map/ppermute | solution.py:43
  81.3 2.9 collective-permute-start.10
  84.1 4.5 collective-permute-start.11
  88.7 3.4 collective-permute-start.12
  88.8 36.0 %collective-permute-start.4 = (bf16[384,2048]{1,0:T(8,128)(2,1)}, bf16[384,2048]{1,0:T(8,128)(2,1)}, u32[]{:S(2)}, u32[]{:S(2)}) collective-permute-start(bf16[384,2048]{1,0:T(8,128)(2,1)} %collective-permute-done.3.refs_2_), channel_id=1, source_target_pairs={{0,2},{1,3},{2,0},{3,1},{4,6},{5,7},{6,4},{7,5},{8,10},{9,11},{10,... | collective-permute-start | bytes 4718600 | tf_op jit(solution)/shard_map/ppermute | solution.py:43
  92.0 10.2 %collective-permute-start.13 = (bf16[1,2,2,2,2,8,128]{6,5,4,3,2,1,0:T(8,128)(2,1)S(1)}, bf16[1,2,2,2,2,8,128]{6,5,4,3,2,1,0:T(8,128)(2,1)}, u32[]{:S(2)}, u32[]{:S(2)}) collective-permute-start(bf16[1,2,2,2,2,8,128]{6,5,4,3,2,1,0:T(8,128)(2,1)S(1)} %maximum_select_fusion.2), channel_id=1, source_target_pairs={{0,16},{1,17},{2,18},{3,19},{4,20},{5,21},{6,22},{7,23},{8,24},{9,... | collective-permute-start | bytes 98312 | tf_op jit(solution)/shard_map/ppermute | solution.py:43
  108.8 169.4 %all-gather.6.cloned.1.call-start = ((), (), s32[]{:S(2)}) async-start(), calls=%async_computation.7 | async-start | bytes 3932160 | tf_op jit(solution)/shard_map/all_gather | solution.py:675
  108.9 50.5 %collective-permute-start = (bf16[384,2048]{1,0:T(8,128)(2,1)S(1)}, bf16[384,2048]{1,0:T(8,128)(2,1)}, u32[]{:S(2)}, u32[]{:S(2)}) collective-permute-start(bf16[384,2048]{1,0:T(8,128)(2,1)S(1)} %copy-done.4), channel_id=1, source_target_pairs={{0,2},{1,3},{2,0},{3,1},{4,6},{5,7},{6,4},{7,5},{8,10},{9,11},{10,... | collective-permute-start | bytes 4718600 | tf_op jit(solution)/shard_map/ppermute | solution.py:43
  109.0 54.9 %collective-permute-start.1 = (bf16[384,2048]{1,0:T(8,128)(2,1)S(1)}, bf16[384,2048]{1,0:T(8,128)(2,1)}, u32[]{:S(2)}, u32[]{:S(2)}) collective-permute-start(bf16[384,2048]{1,0:T(8,128)(2,1)S(1)} %copy-done.4), channel_id=1, source_target_pairs={{0,4},{1,5},{2,6},{3,7},{4,0},{5,1},{6,2},{7,3},{8,12},{9,13},{10,... | collective-permute-start | bytes 4718600 | tf_op jit(solution)/shard_map/ppermute | solution.py:43
  109.7 164.7 %copy-start.15 = (s32[8,384]{1,0:T(8,128)}, s32[8,384]{1,0:T(8,128)S(1)}, u32[]{:S(2)}) copy-start(s32[8,384]{1,0:T(8,128)S(1)} %get-tuple-element.96.refs_6_) | copy-start | bytes 36868
  124.8 13.3 %collective-permute-start.8 = (bf16[384,2048]{1,0:T(8,128)(2,1)}, bf16[384,2048]{1,0:T(8,128)(2,1)}, u32[]{:S(2)}, u32[]{:S(2)}) collective-permute-start(bf16[384,2048]{1,0:T(8,128)(2,1)} %collective-permute-done.4.refs_3_), channel_id=1, source_target_pairs={{0,1},{1,0},{2,3},{3,2},{4,5},{5,4},{6,7},{7,6},{8,9},{9,8},{10,11... | collective-permute-start | bytes 4718600 | tf_op jit(solution)/shard_map/ppermute | solution.py:43
  163.0 36.1 %collective-permute-start.15 = (bf16[384,2048]{1,0:T(8,128)(2,1)}, bf16[384,2048]{1,0:T(8,128)(2,1)}, u32[]{:S(2)}, u32[]{:S(2)}) collective-permute-start(bf16[384,2048]{1,0:T(8,128)(2,1)} %shard_map.257.refs_4_), channel_id=1, source_target_pairs={{0,4},{1,5},{2,6},{3,7},{4,0},{5,1},{6,2},{7,3},{8,12},{9,13},{10,... | collective-permute-start | bytes 4718600 | tf_op jit(solution)/shard_map/ppermute | solution.py:43
  205.1 24.8 %collective-permute-start.16 = (bf16[1536,2048]{1,0:T(8,128)(2,1)}, bf16[1536,2048]{1,0:T(8,128)(2,1)}, u32[]{:S(2)}, u32[]{:S(2)}) collective-permute-start(bf16[1536,2048]{1,0:T(8,128)(2,1)} %shard_map.258.refs_3_.refs_0_.refs_2_), channel_id=1, source_target_pairs={{0,1},{1,0},{2,3},{3,2},{4,5},{5,4},{6,7},{7,6},{8,9},{9,8},{10,11... | collective-permute-start | bytes 18874376 | tf_op jit(solution)/shard_map/ppermute | solution.py:43
  206.1 159.1 %reduce-scatter.4.cloned.1.call-start = ((), (), s32[]{:S(2)}) async-start(), calls=%async_computation.9 | async-start | bytes 5242880 | tf_op jit(solution)/shard_map/reduce_scatter | solution.py:678
  274.0 147.3 %reduce-scatter.6.cloned.1.call-start = ((), (), s32[]{:S(2)}) async-start(), calls=%async_computation.10 | async-start | bytes 3932160 | tf_op jit(solution)/shard_map/reduce_scatter | solution.py:678
  345.9 23.3 %collective-permute-start.17 = (bf16[768,2048]{1,0:T(8,128)(2,1)}, bf16[768,2048]{1,0:T(8,128)(2,1)}, u32[]{:S(2)}, u32[]{:S(2)}) collective-permute-start(bf16[768,2048]{1,0:T(8,128)(2,1)} %get-tuple-element.67.refs_6_), channel_id=1, source_target_pairs={{0,1},{1,0},{2,3},{3,2},{4,5},{5,4},{6,7},{7,6},{8,9},{9,8},{10,11... | collective-permute-start | bytes 9437192 | tf_op jit(solution)/shard_map/ppermute | solution.py:43
  345.9 23.3 %collective-permute-start.18 = (bf16[768,2048]{1,0:T(8,128)(2,1)}, bf16[768,2048]{1,0:T(8,128)(2,1)}, u32[]{:S(2)}, u32[]{:S(2)}) collective-permute-start(bf16[768,2048]{1,0:T(8,128)(2,1)} %get-tuple-element.68), channel_id=1, source_target_pairs={{0,1},{1,0},{2,3},{3,2},{4,5},{5,4},{6,7},{7,6},{8,9},{9,8},{10,11... | collective-permute-start | bytes 9437192 | tf_op jit(solution)/shard_map/ppermute | solution.py:43
  364.7 56.5 %collective-permute-start.23 = (bf16[768,2048]{1,0:T(8,128)(2,1)}, bf16[768,2048]{1,0:T(8,128)(2,1)}, u32[]{:S(2)}, u32[]{:S(2)}) collective-permute-start(bf16[768,2048]{1,0:T(8,128)(2,1)} %get-tuple-element.69.refs_6_), channel_id=1, source_target_pairs={{0,1},{1,0},{2,3},{3,2},{4,5},{5,4},{6,7},{7,6},{8,9},{9,8},{10,11... | collective-permute-start | bytes 9437192 | tf_op jit(solution)/shard_map/ppermute | solution.py:43
  364.8 56.4 %collective-permute-start.24 = (bf16[768,2048]{1,0:T(8,128)(2,1)}, bf16[768,2048]{1,0:T(8,128)(2,1)}, u32[]{:S(2)}, u32[]{:S(2)}) collective-permute-start(bf16[768,2048]{1,0:T(8,128)(2,1)} %get-tuple-element.77), channel_id=1, source_target_pairs={{0,1},{1,0},{2,3},{3,2},{4,5},{5,4},{6,7},{7,6},{8,9},{9,8},{10,11... | collective-permute-start | bytes 9437192 | tf_op jit(solution)/shard_map/ppermute | solution.py:43
  365.3 22.9 %all-to-all-start.1 = ((bf16[8,64,1024]{2,1,0:T(8,128)(2,1)}), bf16[8,64,1024]{2,1,0:T(8,128)(2,1)S(1)}, u32[]{:S(2)}, u32[]{:S(2)}) async-start(bf16[8,64,1024]{2,1,0:T(8,128)(2,1)} %bitcast.81), calls=%async_computation.2 | async-start | bytes 2097152 | tf_op jit(solution)/shard_map/all_to_all | solution.py:683
  369.0 154.6 %reduce-scatter.8.cloned.1.call-start = ((), (), s32[]{:S(2)}) async-start(), calls=%async_computation.11 | async-start | bytes 6553600 | tf_op jit(solution)/shard_map/reduce_scatter | solution.py:678
  385.6 26.2 %collective-permute-start.19 = (bf16[384,1024]{1,0:T(8,128)(2,1)}, bf16[384,1024]{1,0:T(8,128)(2,1)S(1)}, u32[]{:S(2)}, u32[]{:S(2)}) collective-permute-start(bf16[384,1024]{1,0:T(8,128)(2,1)} %get-tuple-element.73), channel_id=1, source_target_pairs={{0,2},{1,3},{2,0},{3,1},{4,6},{5,7},{6,4},{7,5},{8,10},{9,11},{10,... | collective-permute-start | bytes 2359304 | tf_op jit(solution)/shard_map/ppermute | solution.py:43
  387.0 24.8 %collective-permute-start.20 = (bf16[384,1024]{1,0:T(8,128)(2,1)}, bf16[384,1024]{1,0:T(8,128)(2,1)S(1)}, u32[]{:S(2)}, u32[]{:S(2)}) collective-permute-start(bf16[384,1024]{1,0:T(8,128)(2,1)} %get-tuple-element.74), channel_id=1, source_target_pairs={{0,4},{1,5},{2,6},{3,7},{4,0},{5,1},{6,2},{7,3},{8,12},{9,13},{10,... | collective-permute-start | bytes 2359304 | tf_op jit(solution)/shard_map/ppermute | solution.py:43
  416.7 35.3 %collective-permute-start.21 = (bf16[384,2048]{1,0:T(8,128)(2,1)}, bf16[384,2048]{1,0:T(8,128)(2,1)S(1)}, u32[]{:S(2)}, u32[]{:S(2)}) collective-permute-start(bf16[384,2048]{1,0:T(8,128)(2,1)} %get-tuple-element.75.refs_8_), channel_id=1, source_target_pairs={{0,2},{1,3},{2,0},{3,1},{4,6},{5,7},{6,4},{7,5},{8,10},{9,11},{10,... | collective-permute-start | bytes 4718600 | tf_op jit(solution)/shard_map/ppermute | solution.py:43
  416.9 35.1 %collective-permute-start.22 = (bf16[384,2048]{1,0:T(8,128)(2,1)}, bf16[384,2048]{1,0:T(8,128)(2,1)}, u32[]{:S(2)}, u32[]{:S(2)}) collective-permute-start(bf16[384,2048]{1,0:T(8,128)(2,1)} %get-tuple-element.76), channel_id=1, source_target_pairs={{0,4},{1,5},{2,6},{3,7},{4,0},{5,1},{6,2},{7,3},{8,12},{9,13},{10,... | collective-permute-start | bytes 4718600 | tf_op jit(solution)/shard_map/ppermute | solution.py:43
  419.5 54.5 %collective-permute-start.29 = (f32[30,128]{1,0:T(8,128)}, f32[30,128]{1,0:T(8,128)}, u32[]{:S(2)}, u32[]{:S(2)}) collective-permute-start(f32[30,128]{1,0:T(8,128)} %bitcast.37), channel_id=1, source_target_pairs={{0,8},{1,9},{2,10},{3,11},{4,12},{5,13},{6,14},{7,15},{8,0},{9,1},... | collective-permute-start | bytes 46088 | tf_op jit(solution)/shard_map/ppermute | solution.py:43
  442.7 26.1 %collective-permute-start.25 = (bf16[384,1024]{1,0:T(8,128)(2,1)}, bf16[384,1024]{1,0:T(8,128)(2,1)}, u32[]{:S(2)}, u32[]{:S(2)}) collective-permute-start(bf16[384,1024]{1,0:T(8,128)(2,1)} %get-tuple-element.81), channel_id=1, source_target_pairs={{0,2},{1,3},{2,0},{3,1},{4,6},{5,7},{6,4},{7,5},{8,10},{9,11},{10,... | collective-permute-start | bytes 2359304 | tf_op jit(solution)/shard_map/ppermute | solution.py:43
  444.0 24.8 %collective-permute-start.26 = (bf16[384,1024]{1,0:T(8,128)(2,1)}, bf16[384,1024]{1,0:T(8,128)(2,1)}, u32[]{:S(2)}, u32[]{:S(2)}) collective-permute-start(bf16[384,1024]{1,0:T(8,128)(2,1)} %get-tuple-element.82), channel_id=1, source_target_pairs={{0,4},{1,5},{2,6},{3,7},{4,0},{5,1},{6,2},{7,3},{8,12},{9,13},{10,... | collective-permute-start | bytes 2359304 | tf_op jit(solution)/shard_map/ppermute | solution.py:43
  472.5 43.6 %collective-permute-start.27 = (bf16[384,2048]{1,0:T(8,128)(2,1)}, bf16[384,2048]{1,0:T(8,128)(2,1)S(1)}, u32[]{:S(2)}, u32[]{:S(2)}) collective-permute-start(bf16[384,2048]{1,0:T(8,128)(2,1)} %get-tuple-element.83.refs_5_), channel_id=1, source_target_pairs={{0,2},{1,3},{2,0},{3,1},{4,6},{5,7},{6,4},{7,5},{8,10},{9,11},{10,... | collective-permute-start | bytes 4718600 | tf_op jit(solution)/shard_map/ppermute | solution.py:43
  473.7 42.4 %collective-permute-start.28 = (bf16[384,2048]{1,0:T(8,128)(2,1)}, bf16[384,2048]{1,0:T(8,128)(2,1)}, u32[]{:S(2)}, u32[]{:S(2)}) collective-permute-start(bf16[384,2048]{1,0:T(8,128)(2,1)} %get-tuple-element.84), channel_id=1, source_target_pairs={{0,4},{1,5},{2,6},{3,7},{4,0},{5,1},{6,2},{7,3},{8,12},{9,13},{10,... | collective-permute-start | bytes 4718600 | tf_op jit(solution)/shard_map/ppermute | solution.py:43
  474.7 5.6 %collective-permute-start.30 = (f32[30,128]{1,0:T(8,128)S(1)}, f32[30,128]{1,0:T(8,128)S(1)}, u32[]{:S(2)}, u32[]{:S(2)}) collective-permute-start(f32[30,128]{1,0:T(8,128)S(1)} %bitcast_add_fusion), channel_id=1, source_target_pairs={{0,16},{1,17},{2,18},{3,19},{4,20},{5,21},{6,22},{7,23},{8,24},{9,... | collective-permute-start | bytes 46088 | tf_op jit(solution)/shard_map/ppermute | solution.py:43
  481.1 10.1 %collective-permute-start.31 = (f32[1,1,1,14,128]{4,3,2,1,0:T(8,128)S(1)}, f32[1,1,1,14,128]{4,3,2,1,0:T(8,128)S(1)}, u32[]{:S(2)}, u32[]{:S(2)}) collective-permute-start(f32[1,1,1,14,128]{4,3,2,1,0:T(8,128)S(1)} %get-tuple-element.105), channel_id=1, source_target_pairs={{0,1},{1,0},{2,3},{3,2},{4,5},{5,4},{6,7},{7,6},{8,9},{9,8},{10,11... | collective-permute-start | bytes 21512 | tf_op jit(solution)/shard_map/ppermute | solution.py:43
  484.8 53.3 %all-to-all-start.2 = ((bf16[8,64,768]{2,1,0:T(8,128)(2,1)}), bf16[8,64,768]{2,1,0:T(8,128)(2,1)S(1)}, u32[]{:S(2)}, u32[]{:S(2)}) async-start(bf16[8,64,768]{2,1,0:T(8,128)(2,1)} %bitcast.16), calls=%async_computation.4 | async-start | bytes 1572864 | tf_op jit(solution)/shard_map/all_to_all | solution.py:683
  491.2 24.4 %collective-permute-start.32 = (f32[1,1,2,14,128]{4,3,2,1,0:T(8,128)S(1)}, f32[1,1,2,14,128]{4,3,2,1,0:T(8,128)S(1)}, u32[]{:S(2)}, u32[]{:S(2)}) collective-permute-start(f32[1,1,2,14,128]{4,3,2,1,0:T(8,128)S(1)} %maximum_select_fusion.7), channel_id=1, source_target_pairs={{0,2},{1,3},{2,0},{3,1},{4,6},{5,7},{6,4},{7,5},{8,10},{9,11},{10,... | collective-permute-start | bytes 43016 | tf_op jit(solution)/shard_map/ppermute | solution.py:43
  515.5 17.1 %collective-permute-start.33 = (f32[1,2,2,14,128]{4,3,2,1,0:T(8,128)S(1)}, f32[1,2,2,14,128]{4,3,2,1,0:T(8,128)S(1)}, u32[]{:S(2)}, u32[]{:S(2)}) collective-permute-start(f32[1,2,2,14,128]{4,3,2,1,0:T(8,128)S(1)} %maximum_select_fusion.3), channel_id=1, source_target_pairs={{0,4},{1,5},{2,6},{3,7},{4,0},{5,1},{6,2},{7,3},{8,12},{9,13},{10,... | collective-permute-start | bytes 86024 | tf_op jit(solution)/shard_map/ppermute | solution.py:43
  526.5 22.1 %collective-permute-start.34 = (bf16[64,2048]{1,0:T(8,128)(2,1)}, bf16[64,2048]{1,0:T(8,128)(2,1)S(1)}, u32[]{:S(2)}, u32[]{:S(2)}) collective-permute-start(bf16[64,2048]{1,0:T(8,128)(2,1)} %get-tuple-element.95), channel_id=1, source_target_pairs={{0,0},{8,1},{16,2},{24,3},{1,4},{9,5},{17,6},{25,7},{2,8},{10,9},{... | collective-permute-start | bytes 786440 | tf_op jit(solution)/shard_map/ppermute | solution.py:850
  (32 other events, 355.5 us)
Sparse Core Ops, SparseCore 0:
  17.4 108.6 all-gather.3
  127.7 78.8 all-gather.7
  208.1 61.9 all-gather.5
  274.1 77.1 reduce-scatter.3
  354.1 60.5 reduce-scatter.5
  421.3 96.3 reduce-scatter.7

commit v7 on v6

--- a/solution.py
+++ b/solution.py
@@ -370,20 +370,20 @@
     )[0]
 
 
-def finish_output(chain, tokens, own, one, two, bias_one, bias_two):
+def finish_output(chain, tokens, own, one, two, bias):
     slots, width = tokens.shape
     tile = slots // 4
 
-    def kernel(tokens, own, one, two, bias_one, bias_two, out):
+    def kernel(tokens, own, one, two, bias, out):
         total = tokens[...].astype(jnp.float32) + own[...].astype(jnp.float32)
         total += one[...].astype(jnp.float32) + two[...].astype(jnp.float32)
-        out[...] = (total + bias_one[...] + bias_two[...]).astype(jnp.bfloat16)
+        out[...] = (total + bias[...]).astype(jnp.bfloat16)
 
     spec = pl.BlockSpec((tile, width), lambda i: (i, 0))
     return chain.launch(
         kernel,
-        [tokens, own, one, two, bias_one, bias_two],
-        [spec] * 4 + [whole(bias_one), whole(bias_two)],
+        [tokens, own, one, two, bias],
+        [spec] * 4 + [whole(bias)],
         [((slots, width), jnp.bfloat16)],
         [spec],
         (slots // tile,),
@@ -467,15 +467,6 @@
     low[...] = normed.astype(jnp.bfloat16)
 
 
-def qkv_kernel(head_dim, x, cosine, sine, bias, weight, out):
-    projected = times(x[...], weight[...]) + bias[...]
-    half = head_dim // 8
-    for part in range(2):
-        at = part * head_dim
-        turn_into(out, at, projected[:, at : at + head_dim], cosine[...], sine[...], half)
-    out[:, 2 * head_dim :] = projected[:, 2 * head_dim :].astype(jnp.bfloat16)
-
-
 def expand_kernel(x, bias, weight, active, slope):
     hidden = times(x[...], weight[...]) + bias[...]
     below = 0.5 * (1.0 + lax.erf(hidden * math.sqrt(0.5)))
@@ -502,20 +493,27 @@
 def attend_kernel(
     head_dim,
     cotangent,
-    qkv,
+    x,
     cosine,
     sine,
     segment,
     segments,
+    bias,
+    weight,
     dense,
     attn,
     grad_qkv,
     grad_sum,
 ):
     scale = 1.0 / math.sqrt(head_dim)
-    query = qkv[:, :head_dim]
-    key = qkv[:, head_dim : 2 * head_dim]
-    value = qkv[:, 2 * head_dim :]
+    half = head_dim // 8
+    projected = times(x[...], weight[...]) + bias[...]
+    for part in range(2):
+        at = part * head_dim
+        turn_into(grad_qkv, at, projected[:, at : at + head_dim], cosine[...], sine[...], half)
+    query = grad_qkv[:, :head_dim]
+    key = grad_qkv[:, head_dim : 2 * head_dim]
+    value = projected[:, 2 * head_dim :].astype(jnp.bfloat16)
     grad_attn = times_paired(cotangent[...], dense[...]).astype(jnp.bfloat16)
     slots = query.shape[0]
     row = lax.broadcasted_iota(jnp.int32, (slots, slots), 0)
@@ -531,7 +529,6 @@
     grad_value = times_leading(probs, grad_attn)
     inner = jnp.sum(weights * grad_probs, axis=1, keepdims=True)
     grad_score = (weights * (grad_probs - inner)).astype(jnp.bfloat16)
-    half = head_dim // 8
     back = -sine[...]
     grad_query = times(grad_score, key) * scale
     turn_into(grad_qkv, 0, grad_query, cosine[...], back, half)
@@ -615,21 +612,25 @@
     gain = gain.astype(jnp.float32).reshape(rows, 1)
     shift = shift.astype(jnp.float32).reshape(rows, 1)
 
+    lanes = min(128, places[0][3])
+
     def kernel(got, sums, weight, gain, shift, grad, gain_grad, shift_grad):
-        by_gain = jnp.zeros((rows, 1), jnp.float32)
-        by_shift = jnp.zeros((rows, 1), jnp.float32)
+        by_gain = jnp.zeros((rows, lanes), jnp.float32)
+        by_shift = jnp.zeros((rows, lanes), jnp.float32)
         for slot, start, at, many in places:
             terms = got[slot, :, start : start + many].astype(jnp.float32)
             total = sums[slot : slot + 1, start : start + many]
             parts = weight[:, at : at + many].astype(jnp.float32)
             grad[:, at : at + many] = terms * gain[...] + total * shift[...]
-            by_gain += jnp.sum(parts * terms, axis=1, keepdims=True)
-            by_shift += jnp.sum(parts * total, axis=1, keepdims=True)
-        gain_grad[...] = by_gain
-        shift_grad[...] = by_shift
+            for lane in range(0, many, lanes):
+                span = slice(lane, lane + lanes)
+                by_gain += parts[:, span] * terms[:, span]
+                by_shift += parts[:, span] * total[:, span]
+        gain_grad[...] = jnp.sum(by_gain.T, axis=0, keepdims=True)
+        shift_grad[...] = jnp.sum(by_shift.T, axis=0, keepdims=True)
 
     inputs = [got, sums, weight, gain, shift]
-    shapes = [(rows, width), (rows, 1), (rows, 1)]
+    shapes = [(rows, width), (1, rows), (1, rows)]
     grad, gain_grad, shift_grad = chain.launch(
         kernel,
         inputs,
@@ -747,6 +748,8 @@
     chain.settle(every, *[piece for piece, _ in token_pieces[4:7]])
     qkv_own, expand_own = split_columns(chain, own.reshape(HEADS * rows, -1), split)
     weight_expand, weight_qkv = gather(expand_own), gather(qkv_own)
+    bias_out = bias_dense + bias_contract
+    segment_column = segment.reshape(-1, 1)
     chain.settle(cosine, weight_out)
 
     def sum_begin(compute, blocked, known):
@@ -774,6 +777,7 @@
     )
 
     passed = swap(copied(chain, own_cotangent[2]), 2, plan)
+    chain.settle(sine, segment_column, bias_qkv, bias_out)
     half = laid_together(
         chain, [own_cotangent[0], own_cotangent[2], own_cotangent[4], passed]
     )
@@ -803,22 +807,13 @@
     )
     expand_got = reduce(input_terms(chain, normed, grad_hidden))
 
-    (qkv,) = over_blocks(
-        chain,
-        lambda *refs: qkv_kernel(head_dim, *refs),
-        slots,
-        [],
-        [low_one, cosine, sine],
-        [bias_qkv, weight_qkv],
-        [(split, jnp.bfloat16)],
-    )
     attn, grad_qkv, qkv_sum, weight_dense = over_blocks(
         chain,
         lambda *refs: attend_kernel(head_dim, *refs),
         slots,
         [],
-        [qkv, cosine, sine, segment.reshape(-1, 1)],
-        [segment],
+        [low_one, cosine, sine, segment_column],
+        [segment, bias_qkv, weight_qkv],
         [(head_dim, jnp.bfloat16), (split, jnp.bfloat16)],
         [split],
         (weight_out, dense_runs),
@@ -842,7 +837,7 @@
     branch = sum_last(*branch)
     chain.settle(qkv_got)
     norm_parts = sum_next(*norm_of, norm_got)
-    layer_out = finish_output(chain, tokens, *branch, bias_dense, bias_contract)
+    layer_out = finish_output(chain, tokens, *branch, bias_out)
 
     norm_parts = sum_last(*norm_parts)
     input_grad = finish_input(chain, cotangent, tokens, *norm_parts)

time: 564 us -> 554 us (0.982)
  Pallas kernels: 279 us -> 273 us
    ppermute x33, waiting for transfers between devices: 143 us -> 132 us  [swap(): return lax.ppermute(value, 'dp', plan.flip(bit))]
    pallas_call x23 -> x22, Pallas kernels: 279 us -> 273 us  [launch(): pl.pallas_call(body, grid_spec=pltpu.PrefetchScalarGridSpec(num_scalar_pr...]
    unnamed x79 -> x73, local copies, waits for them, and re-layouts: 11.9 us -> 12.4 us
  transfers between devices with their start and end apart: 44 -> 44, of which waited for: 14 -> 15; matrix products, arithmetic and copies ran while one was open for 6% -> 5% of each run, Pallas kernels for 50% -> 50%
where the time goes in v7:
time: 554 us; the launch traced here: 547 us
  Pallas kernels  273 us (49%)
  waiting for transfers between devices  147 us (27%)
  starting transfers between devices  74.6 us (13%)
  local copies, waits for them, and re-layouts  21.9 us (4%)
  other arithmetic  15.6 us (3%)
  between operations  15.1 us (3%)
    pallas_call x22, Pallas kernels, launch(): pl.pallas_call(body, grid_spec=pltpu.PrefetchScalarGridSpec(num_scalar_pr...  273 us
    ppermute x33, waiting for transfers between devices, swap(): return lax.ppermute(value, 'dp', plan.flip(bit))  132 us
    ppermute x33, starting transfers between devices, swap(): return lax.ppermute(value, 'dp', plan.flip(bit))  49.7 us
    all_to_all x3, starting transfers between devices, exchange(): lax.all_to_all(value, 'dp', 0, 0, tiled=True, axis_index_groups=sharing)  13.6 us
    unnamed x73, local copies, waits for them, and re-layouts  12.4 us
  transfers between devices with their start and end apart: 44, of which 15 were waited for; matrix products, arithmetic and copies ran while one was open for 5% of the time, Pallas kernels for 50%

profile of v7, /device:TPU:1, one launch (start us, length us, event | category | flops | bytes accessed | tf_op | source)
XLA Modules:
  0.0 546.8 jit_solution(8320629713474513210)
XLA Ops:
  7.2 4.7 collective-permute-start.14
  13.3 2.9 collective-permute-done.14
  17.3 10.4 %collective-permute-start.3 = (bf16[384,2048]{1,0:T(8,128)(2,1)S(1)}, bf16[384,2048]{1,0:T(8,128)(2,1)}, u32[]{:S(2)}, u32[]{:S(2)}) collective-permute-start(bf16[384,2048]{1,0:T(8,128)(2,1)S(1)} %copy-done.3), channel_id=1, source_target_pairs={{0,4},{1,5},{2,6},{3,7},{4,0},{5,1},{6,2},{7,3},{8,12},{9,13},{10,... | collective-permute-start | bytes 4718600 | tf_op jit(solution)/shard_map/ppermute | solution.py:43
  27.7 2.8 shard_map.254.refs_1_
  30.6 5.8 %all-to-all-start = ((bf16[8,64,1792]{2,1,0:T(8,128)(2,1)}), bf16[8,64,1792]{2,1,0:T(8,128)(2,1)S(1)}, u32[]{:S(2)}, u32[]{:S(2)}) async-start(bf16[8,64,1792]{2,1,0:T(8,128)(2,1)} %shard_map.254.refs_1_), calls=%async_computation | async-start | bytes 3670016 | tf_op jit(solution)/shard_map/all_to_all | solution.py:684
  36.6 24.0 %collective-permute-done.3.refs_2_ = bf16[384,2048]{1,0:T(8,128)(2,1)} collective-permute-done((bf16[384,2048]{1,0:T(8,128)(2,1)S(1)}, bf16[384,2048]{1,0:T(8,128)(2,1)}, u32[]{:S(2)}, u32[]{:S(2)}) %collective-permute-start.3) | collective-permute-done | bytes 1572896 | tf_op jit(solution)/shard_map/ppermute | solution.py:43
  60.6 4.6 collective-permute-start.7
  65.2 2.0 collective-permute-start.6
  67.5 13.8 %collective-permute-done.9 = bf16[1,1,1,1,1,8,128]{6,5,4,3,2,1,0:T(8,128)(2,1)S(1)} collective-permute-done((bf16[1,1,1,1,1,8,128]{6,5,4,3,2,1,0:T(8,128)(2,1)S(1)}, bf16[1,1,1,1,1,8,128]{6,5,4,3,2,1,0:T(8,128)(2,1)S(1)}, u32[]{:S(2)}, u32[]{:S(2)}) %collective-permute-start.9) | collective-permute-done | bytes 2080 | tf_op jit(solution)/shard_map/ppermute | solution.py:43
  81.6 2.5 collective-permute-done.10
  84.1 3.7 collective-permute-start.11
  92.0 3.3 collective-permute-start.13
  95.4 6.8 %collective-permute-done.13 = bf16[1,2,2,2,2,8,128]{6,5,4,3,2,1,0:T(8,128)(2,1)S(1)} collective-permute-done((bf16[1,2,2,2,2,8,128]{6,5,4,3,2,1,0:T(8,128)(2,1)S(1)}, bf16[1,2,2,2,2,8,128]{6,5,4,3,2,1,0:T(8,128)(2,1)S(1)}, u32[]{:S(2)}, u32[]{:S(2)}) %collective-permute-start.13) | collective-permute-done | bytes 32800 | tf_op jit(solution)/shard_map/ppermute | solution.py:43
  104.1 3.8 shard_map.255
  109.0 15.8 %collective-permute-done.4.refs_3_ = bf16[384,2048]{1,0:T(8,128)(2,1)} collective-permute-done((bf16[384,2048]{1,0:T(8,128)(2,1)}, bf16[384,2048]{1,0:T(8,128)(2,1)}, u32[]{:S(2)}, u32[]{:S(2)}) %collective-permute-start.4) | collective-permute-done | bytes 1572896 | tf_op jit(solution)/shard_map/ppermute | solution.py:43
  129.4 7.0 %fusion = (f32[3072,32]{1,0:T(8,128)S(1)}, f32[3072,32]{1,0:T(8,128)}, f32[3072,32]{1,0:T(8,128)S(1)}) fusion(f32[32]{0:T(128)S(1)} %multiply_exponential_fusion, f32[3072]{0:T(1024)S(1)} %convert_element_type.48), kind=kLoop, calls=%fused_computation.4 | loop fusion | flops 196608 | bytes 1192064 | tf_op jit(solution)/shard_map/neg | solution.py:136
  138.1 21.4 %shard_map.256 = (bf16[3072,2048]{1,0:T(8,128)(2,1)}, bf16[3072,2048]{1,0:T(8,128)(2,1)}, bf16[3072,2048]{1,0:T(8,128)(2,1)}) custom-call(bf16[384,2048]{1,0:T(8,128)(2,1)} %refs_1_.3, bf16[384,2048]{1,0:T(8,128)(2,1)} %collective-permute-done.2.refs_1_, bf16[384,2048]{1,0:T(8,128)(2,1)} %collective-permute-done.3.refs_2_, ...), custom_call_target="tpu_custom_call" | custom-call | flops 1 | bytes 1 | tf_op jit(solution)/shard_map/pallas_call | solution.py:98
  159.4 3.6 shard_map.257.refs_4_
  167.0 3.0 maximum_maximum_fusion.1.refs_5_.refs_4_
  170.0 29.1 %collective-permute-done.15.refs_3_ = bf16[384,2048]{1,0:T(8,128)(2,1)} collective-permute-done((bf16[384,2048]{1,0:T(8,128)(2,1)}, bf16[384,2048]{1,0:T(8,128)(2,1)}, u32[]{:S(2)}, u32[]{:S(2)}) %collective-permute-start.15) | collective-permute-done | bytes 1572896 | tf_op jit(solution)/shard_map/ppermute | solution.py:43
  199.1 5.9 %shard_map.258.refs_3_.refs_0_.refs_2_ = bf16[1536,2048]{1,0:T(8,128)(2,1)} custom-call(bf16[384,2048]{1,0:T(8,128)(2,1)} %refs_0_.9, bf16[384,2048]{1,0:T(8,128)(2,1)} %collective-permute-done.refs_0_.refs_1_, bf16[384,2048]{1,0:T(8,128)(2,1)} %collective-permute-done.1.refs_2_, bf16[384,2048]{1,0:T(8,128)(2,1)} %collective-permute-done.15.refs_3_, ...), custom_call_target="tpu_custom_call" | custom-call | flops 1 | bytes 1 | tf_op jit(solution)/shard_map/pallas_call | solution.py:98
  207.0 22.5 %shard_map.259 = (bf16[3072,1024]{1,0:T(8,128)(2,1)}, f32[3072,1024]{1,0:T(8,128)}) custom-call(bf16[3072,2048]{1,0:T(8,128)(2,1)} %get-tuple-element.58.refs_0_, f32[1,1024]{1,0:T(1,128)} %bitcast.103, bf16[2048,1024]{1,0:T(8,128)(2,1)} %all-gather.8.cloned.1.call-done.refs_2_.refs_3_, bf16[1536,2048]{1,0:T(8,128)(2,1)} %shard_map.258.refs_3_.refs_0_.refs_2_), custom_call_target="tpu_custom_call" | custom-call | flops 1 | bytes 1 | tf_op jit(solution)/shard_map/pallas_call | solution.py:98
  229.4 25.3 %shard_map.260 = (bf16[3072,1024]{1,0:T(8,128)(2,1)}, f32[1,1024]{1,0:T(1,128)}, f32[1,2048]{1,0:T(1,128)}, bf16[1024,2048]{1,0:T(8,128)(2,1)}) custom-call(bf16[1536,2048]{1,0:T(8,128)(2,1)} %shard_map.258.refs_3_.refs_0_.refs_2_, bf16[1536,2048]{1,0:T(8,128)(2,1)} %collective-permute-done.16.refs_1_.refs_3_, f32[3072,1024]{1,0:T(8,128)} %get-tuple-element.60.refs_2_, ...), custom_call_target="tpu_custom_call" | custom-call | flops 1 | bytes 1 | tf_op jit(solution)/shard_map/pallas_call | solution.py:98
  254.7 18.8 %shard_map.261.refs_10_ = bf16[2048,1024]{1,0:T(8,128)(2,1)} custom-call(bf16[3072,2048]{1,0:T(8,128)(2,1)} %get-tuple-element.57.refs_0_, bf16[3072,1024]{1,0:T(8,128)(2,1)} %get-tuple-element.62.refs_1_.refs_2_, bf16[3072,1024]{1,0:T(8,128)(2,1)} %get-tuple-element.62.refs_1_.refs_2_), custom_call_target="tpu_custom_call" | custom-call | flops 1 | bytes 1 | tf_op jit(solution)/shard_map/pallas_call | solution.py:98
  273.8 31.4 %shard_map.262 = (bf16[3072,256]{1,0:T(8,128)(2,1)}, bf16[3072,768]{1,0:T(8,128)(2,1)}, f32[1,768]{1,0:T(1,128)}, bf16[256,2048]{1,0:T(8,128)(2,1)}) custom-call(bf16[1536,2048]{1,0:T(8,128)(2,1)} %shard_map.258.refs_3_.refs_0_.refs_2_, bf16[1536,2048]{1,0:T(8,128)(2,1)} %collective-permute-done.16.refs_1_.refs_3_, ...), custom_call_target="tpu_custom_call" | custom-call | flops 1 | bytes 1 | tf_op jit(solution)/shard_map/pallas_call | solution.py:98
  305.2 15.6 %shard_map.263.refs_4_ = bf16[2048,768]{1,0:T(8,128)(2,1)} custom-call(bf16[3072,2048]{1,0:T(8,128)(2,1)} %get-tuple-element.57.refs_0_, bf16[3072,768]{1,0:T(8,128)(2,1)} %get-tuple-element.66.refs_1_.refs_0_, bf16[3072,256]{1,0:T(8,128)(2,1)} %get-tuple-element.63.refs_2_.refs_0_.refs_1_), custom_call_target="tpu_custom_call" | custom-call | flops 1 | bytes 1 | tf_op jit(solution)/shard_map/pallas_call | solution.py:98
  320.8 14.1 %shard_map.264 = (bf16[768,2048]{1,0:T(8,128)(2,1)}, bf16[768,2048]{1,0:T(8,128)(2,1)}) custom-call(bf16[3072,256]{1,0:T(8,128)(2,1)} %get-tuple-element.63.refs_2_.refs_0_.refs_1_, bf16[3072,1024]{1,0:T(8,128)(2,1)} %get-tuple-element.61.refs_4_.refs_1_.refs_0_, bf16[256,2048]{1,0:T(8,128)(2,1)} %get-tuple-element.64.refs_2_, ...), custom_call_target="tpu_custom_call" | custom-call | flops 1 | bytes 1 | tf_op jit(solution)/shard_map/pallas_call | solution.py:98
  335.4 18.2 %shard_map.265 = (bf16[768,2048]{1,0:T(8,128)(2,1)}, bf16[768,2048]{1,0:T(8,128)(2,1)}) custom-call(bf16[3072,768]{1,0:T(8,128)(2,1)} %get-tuple-element.66.refs_1_.refs_0_, bf16[3072,1024]{1,0:T(8,128)(2,1)} %get-tuple-element.62.refs_1_.refs_2_, bf16[2048,768]{1,0:T(8,128)(2,1)} %all-gather.6.cloned.1.call-done.refs_8_.refs_2_, ...), custom_call_target="tpu_custom_call" | custom-call | flops 1 | bytes 1 | tf_op jit(solution)/shard_map/pallas_call | solution.py:98
  354.2 4.0 all-to-all-start.1
  358.4 16.9 %shard_map.266 = (bf16[384,2048]{1,0:T(8,128)(2,1)}, bf16[384,2048]{1,0:T(8,128)(2,1)}, bf16[384,2048]{1,0:T(8,128)(2,1)}, bf16[384,1024]{1,0:T(8,128)(2,1)}, bf16[384,1024]{1,0:T(8,128)(2,1)}) custom-call(bf16[3072,256]{1,0:T(8,128)(2,1)} %get-tuple-element.63.refs_2_.refs_0_.refs_1_, bf16[3072,1024]{1,0:T(8,128)(2,1)} %get-tuple-element.61.refs_4_.refs_1_.refs_0_, ...), custom_call_target="tpu_custom_call" | custom-call | flops 1 | bytes 1 | tf_op jit(solution)/shard_map/pallas_call | solution.py:98
  378.8 22.6 %shard_map.267.refs_4_ = bf16[1280,2048]{1,0:T(8,128)(2,1)} custom-call(bf16[3072,1024]{1,0:T(8,128)(2,1)} %get-tuple-element.61.refs_4_.refs_1_.refs_0_, bf16[3072,256]{1,0:T(8,128)(2,1)} %get-tuple-element.63.refs_2_.refs_0_.refs_1_, bf16[1536,2048]{1,0:T(8,128)(2,1)} %shard_map.258.refs_3_.refs_0_.refs_2_, ...), custom_call_target="tpu_custom_call" | custom-call | flops 1 | bytes 1 | tf_op jit(solution)/shard_map/pallas_call | solution.py:98
  402.6 3.6 shard_map.268
  409.2 5.1 reduce-scatter.6.cloned.1.call-done.refs_9_
  414.3 21.5 %shard_map.269 = (bf16[384,2048]{1,0:T(8,128)(2,1)}, bf16[384,2048]{1,0:T(8,128)(2,1)}, bf16[384,2048]{1,0:T(8,128)(2,1)}, bf16[384,1024]{1,0:T(8,128)(2,1)}, bf16[384,1024]{1,0:T(8,128)(2,1)}) custom-call(bf16[3072,768]{1,0:T(8,128)(2,1)} %get-tuple-element.66.refs_1_.refs_0_, bf16[3072,1024]{1,0:T(8,128)(2,1)} %get-tuple-element.62.refs_1_.refs_2_, ...), custom_call_target="tpu_custom_call" | custom-call | flops 1 | bytes 1 | tf_op jit(solution)/shard_map/pallas_call | solution.py:98
  438.2 3.4 collective-permute-done.21.refs_2_
  443.2 4.8 shard_map.270.refs_4_
  448.0 10.4 %collective-permute-done.25.refs_2_ = bf16[384,1024]{1,0:T(8,128)(2,1)} collective-permute-done((bf16[384,1024]{1,0:T(8,128)(2,1)}, bf16[384,1024]{1,0:T(8,128)(2,1)}, u32[]{:S(2)}, u32[]{:S(2)}) %collective-permute-start.25) | collective-permute-done | bytes 786464 | tf_op jit(solution)/shard_map/ppermute | solution.py:43
  458.4 3.7 shard_map.271
  464.3 2.9 collective-permute-start.30
  469.7 5.7 %collective-permute-start.31 = (f32[1,1,1,14,128]{4,3,2,1,0:T(8,128)S(1)}, f32[1,1,1,14,128]{4,3,2,1,0:T(8,128)S(1)}, u32[]{:S(2)}, u32[]{:S(2)}) collective-permute-start(f32[1,1,1,14,128]{4,3,2,1,0:T(8,128)S(1)} %get-tuple-element.104), channel_id=1, source_target_pairs={{0,1},{1,0},{2,3},{3,2},{4,5},{5,4},{6,7},{7,6},{8,9},{9,8},{10,11... | collective-permute-start | bytes 21512 | tf_op jit(solution)/shard_map/ppermute | solution.py:43
  475.4 3.8 all-to-all-start.2
  483.5 21.8 %collective-permute-done.32 = f32[1,1,2,14,128]{4,3,2,1,0:T(8,128)S(1)} collective-permute-done((f32[1,1,2,14,128]{4,3,2,1,0:T(8,128)S(1)}, f32[1,1,2,14,128]{4,3,2,1,0:T(8,128)S(1)}, u32[]{:S(2)}, u32[]{:S(2)}) %collective-permute-start.32) | collective-permute-done | bytes 14368 | tf_op jit(solution)/shard_map/ppermute | solution.py:43
  506.9 6.5 %shard_map.272.refs_1_ = f32[384,2048]{1,0:T(8,128)} custom-call(bf16[384,2048]{1,0:T(8,128)(2,1)} %refs_0_.9, bf16[384,2048]{1,0:T(8,128)(2,1)} %refs_1_.3, bf16[384,2048]{1,0:T(8,128)(2,1)} %get-tuple-element.78.refs_5_.refs_2_, bf16[384,2048]{1,0:T(8,128)(2,1)} %copy-done.6, bf16[384,2048]{1,0:T(8,128)(2,1)} %collective-permute-done.28.refs_4_, ...), custom_call_target="tpu_custom_call" | custom-call | flops 1 | bytes 1 | tf_op jit(solution)/shard_map/pallas_call | solution.py:98
  513.4 2.9 shard_map.273
  516.2 5.7 %collective-permute-start.34 = (bf16[64,2048]{1,0:T(8,128)(2,1)}, bf16[64,2048]{1,0:T(8,128)(2,1)S(1)}, u32[]{:S(2)}, u32[]{:S(2)}) collective-permute-start(bf16[64,2048]{1,0:T(8,128)(2,1)} %get-tuple-element.95), channel_id=1, source_target_pairs={{0,0},{8,1},{16,2},{24,3},{1,4},{9,5},{17,6},{25,7},{2,8},{10,9},{... | collective-permute-start | bytes 786440 | tf_op jit(solution)/shard_map/ppermute | solution.py:845
  523.5 4.0 shard_map.274
  528.3 3.4 shard_map.275
  531.8 6.4 %collective-permute-done.34 = bf16[64,2048]{1,0:T(8,128)(2,1)S(1)} collective-permute-done((bf16[64,2048]{1,0:T(8,128)(2,1)}, bf16[64,2048]{1,0:T(8,128)(2,1)S(1)}, u32[]{:S(2)}, u32[]{:S(2)}) %collective-permute-start.34) | collective-permute-done | bytes 262176 | tf_op jit(solution)/shard_map/ppermute | solution.py:845
  (205 shorter events, 49.9 us)
Async XLA Ops:
  7.2 130.9 %all-gather.4.cloned.1.call-start = ((), (), s32[]{:S(2)}) async-start(), calls=%async_computation.6 | async-start | bytes 6553600 | tf_op jit(solution)/shard_map/all_gather | solution.py:676
  7.2 8.9 %collective-permute-start.14 = (bf16[64,2048]{1,0:T(8,128)(2,1)}, bf16[64,2048]{1,0:T(8,128)(2,1)S(1)}, u32[]{:S(2)}, u32[]{:S(2)}) collective-permute-start(bf16[64,2048]{1,0:T(8,128)(2,1)} %param.23), channel_id=1, source_target_pairs={{0,0},{1,8},{2,16},{3,24},{4,1},{5,9},{6,17},{7,25},{8,2},{9,10},{... | collective-permute-start | bytes 786440 | tf_op jit(solution)/shard_map/ppermute | solution.py:688
  17.3 43.4 %collective-permute-start.3 = (bf16[384,2048]{1,0:T(8,128)(2,1)S(1)}, bf16[384,2048]{1,0:T(8,128)(2,1)}, u32[]{:S(2)}, u32[]{:S(2)}) collective-permute-start(bf16[384,2048]{1,0:T(8,128)(2,1)S(1)} %copy-done.3), channel_id=1, source_target_pairs={{0,4},{1,5},{2,6},{3,7},{4,0},{5,1},{6,2},{7,3},{8,12},{9,13},{10,... | collective-permute-start | bytes 4718600 | tf_op jit(solution)/shard_map/ppermute | solution.py:43
  27.7 37.6 %collective-permute-start.2 = (bf16[384,2048]{1,0:T(8,128)(2,1)S(1)}, bf16[384,2048]{1,0:T(8,128)(2,1)}, u32[]{:S(2)}, u32[]{:S(2)}) collective-permute-start(bf16[384,2048]{1,0:T(8,128)(2,1)S(1)} %copy-done.3), channel_id=1, source_target_pairs={{0,2},{1,3},{2,0},{3,1},{4,6},{5,7},{6,4},{7,5},{8,10},{9,11},{10,... | collective-permute-start | bytes 4718600 | tf_op jit(solution)/shard_map/ppermute | solution.py:43
  30.5 36.8 %copy-start.20 = (bf16[192]{0:T(256)(128)(2,1)S(1)}, bf16[192]{0:T(256)(128)(2,1)}, u32[]{:S(2)}) copy-start(bf16[192]{0:T(256)(128)(2,1)} %param.22) | copy-start | bytes 1156
  30.5 36.8 %copy-start.21 = (bf16[256]{0:T(256)(128)(2,1)S(1)}, bf16[256]{0:T(256)(128)(2,1)}, u32[]{:S(2)}) copy-start(bf16[256]{0:T(256)(128)(2,1)} %param.26) | copy-start | bytes 1540
  30.5 36.8 %copy-start.22 = (bf16[64]{0:T(256)(128)(2,1)S(1)}, bf16[64]{0:T(256)(128)(2,1)}, u32[]{:S(2)}) copy-start(bf16[64]{0:T(256)(128)(2,1)} %param.19) | copy-start | bytes 388
  30.6 72.3 %all-to-all-start = ((bf16[8,64,1792]{2,1,0:T(8,128)(2,1)}), bf16[8,64,1792]{2,1,0:T(8,128)(2,1)S(1)}, u32[]{:S(2)}, u32[]{:S(2)}) async-start(bf16[8,64,1792]{2,1,0:T(8,128)(2,1)} %shard_map.254.refs_1_), calls=%async_computation | async-start | bytes 3670016 | tf_op jit(solution)/shard_map/all_to_all | solution.py:684
  36.4 170.6 %all-gather.8.cloned.1.call-start = ((), (), s32[]{:S(2)}) async-start(), calls=%async_computation.8 | async-start | bytes 5242880 | tf_op jit(solution)/shard_map/all_gather | solution.py:676
  36.4 66.5 %collective-permute-start.5 = (bf16[384,2048]{1,0:T(8,128)(2,1)S(1)}, bf16[384,2048]{1,0:T(8,128)(2,1)}, u32[]{:S(2)}, u32[]{:S(2)}) collective-permute-start(bf16[384,2048]{1,0:T(8,128)(2,1)S(1)} %copy-done.3), channel_id=1, source_target_pairs={{0,1},{1,0},{2,3},{3,2},{4,5},{5,4},{6,7},{7,6},{8,9},{9,8},{10,11... | collective-permute-start | bytes 4718600 | tf_op jit(solution)/shard_map/ppermute | solution.py:43
  60.6 42.3 %collective-permute-start.7 = (bf16[384,2048]{1,0:T(8,128)(2,1)}, bf16[384,2048]{1,0:T(8,128)(2,1)}, u32[]{:S(2)}, u32[]{:S(2)}) collective-permute-start(bf16[384,2048]{1,0:T(8,128)(2,1)} %collective-permute-done.3.refs_2_), channel_id=1, source_target_pairs={{0,1},{1,0},{2,3},{3,2},{4,5},{5,4},{6,7},{7,6},{8,9},{9,8},{10,11... | collective-permute-start | bytes 4718600 | tf_op jit(solution)/shard_map/ppermute | solution.py:43
  65.2 37.7 %collective-permute-start.6 = (bf16[384,2048]{1,0:T(8,128)(2,1)}, bf16[384,2048]{1,0:T(8,128)(2,1)}, u32[]{:S(2)}, u32[]{:S(2)}) collective-permute-start(bf16[384,2048]{1,0:T(8,128)(2,1)} %collective-permute-done.2.refs_1_), channel_id=1, source_target_pairs={{0,1},{1,0},{2,3},{3,2},{4,5},{5,4},{6,7},{7,6},{8,9},{9,8},{10,11... | collective-permute-start | bytes 4718600 | tf_op jit(solution)/shard_map/ppermute | solution.py:43
  67.4 13.8 %collective-permute-start.9 = (bf16[1,1,1,1,1,8,128]{6,5,4,3,2,1,0:T(8,128)(2,1)S(1)}, bf16[1,1,1,1,1,8,128]{6,5,4,3,2,1,0:T(8,128)(2,1)S(1)}, u32[]{:S(2)}, u32[]{:S(2)}) collective-permute-start(bf16[1,1,1,1,1,8,128]{6,5,4,3,2,1,0:T(8,128)(2,1)S(1)} %bitcast.100), channel_id=1, source_target_pairs={{0,2},{1,3},{2,0},{3,1},{4,6},{5,7},{6,4},{7,5},{8,10},{9,11},{10,... | collective-permute-start | bytes 6152 | tf_op jit(solution)/shard_map/ppermute | solution.py:43
  81.3 2.9 collective-permute-start.10
  84.1 4.5 collective-permute-start.11
  88.7 3.4 collective-permute-start.12
  88.8 36.0 %collective-permute-start.4 = (bf16[384,2048]{1,0:T(8,128)(2,1)}, bf16[384,2048]{1,0:T(8,128)(2,1)}, u32[]{:S(2)}, u32[]{:S(2)}) collective-permute-start(bf16[384,2048]{1,0:T(8,128)(2,1)} %collective-permute-done.3.refs_2_), channel_id=1, source_target_pairs={{0,2},{1,3},{2,0},{3,1},{4,6},{5,7},{6,4},{7,5},{8,10},{9,11},{10,... | collective-permute-start | bytes 4718600 | tf_op jit(solution)/shard_map/ppermute | solution.py:43
  92.0 10.1 %collective-permute-start.13 = (bf16[1,2,2,2,2,8,128]{6,5,4,3,2,1,0:T(8,128)(2,1)S(1)}, bf16[1,2,2,2,2,8,128]{6,5,4,3,2,1,0:T(8,128)(2,1)S(1)}, u32[]{:S(2)}, u32[]{:S(2)}) collective-permute-start(bf16[1,2,2,2,2,8,128]{6,5,4,3,2,1,0:T(8,128)(2,1)S(1)} %maximum_select_fusion.2), channel_id=1, source_target_pairs={{0,16},{1,17},{2,18},{3,19},{4,20},{5,21},{6,22},{7,23},{8,24},{9,... | collective-permute-start | bytes 98312 | tf_op jit(solution)/shard_map/ppermute | solution.py:43
  108.0 165.8 %all-gather.6.cloned.1.call-start = ((), (), s32[]{:S(2)}) async-start(), calls=%async_computation.7 | async-start | bytes 3932160 | tf_op jit(solution)/shard_map/all_gather | solution.py:676
  108.0 51.4 %collective-permute-start = (bf16[384,2048]{1,0:T(8,128)(2,1)S(1)}, bf16[384,2048]{1,0:T(8,128)(2,1)}, u32[]{:S(2)}, u32[]{:S(2)}) collective-permute-start(bf16[384,2048]{1,0:T(8,128)(2,1)S(1)} %copy-done.4), channel_id=1, source_target_pairs={{0,2},{1,3},{2,0},{3,1},{4,6},{5,7},{6,4},{7,5},{8,10},{9,11},{10,... | collective-permute-start | bytes 4718600 | tf_op jit(solution)/shard_map/ppermute | solution.py:43
  108.1 61.9 %collective-permute-start.1 = (bf16[384,2048]{1,0:T(8,128)(2,1)S(1)}, bf16[384,2048]{1,0:T(8,128)(2,1)}, u32[]{:S(2)}, u32[]{:S(2)}) collective-permute-start(bf16[384,2048]{1,0:T(8,128)(2,1)S(1)} %copy-done.4), channel_id=1, source_target_pairs={{0,4},{1,5},{2,6},{3,7},{4,0},{5,1},{6,2},{7,3},{8,12},{9,13},{10,... | collective-permute-start | bytes 4718600 | tf_op jit(solution)/shard_map/ppermute | solution.py:43
  108.9 55.1 %copy-start.13 = (s32[8,384]{1,0:T(8,128)}, s32[8,384]{1,0:T(8,128)S(1)}, u32[]{:S(2)}) copy-start(s32[8,384]{1,0:T(8,128)S(1)} %get-tuple-element.96.refs_6_) | copy-start | bytes 36868
  124.8 13.3 %collective-permute-start.8 = (bf16[384,2048]{1,0:T(8,128)(2,1)}, bf16[384,2048]{1,0:T(8,128)(2,1)}, u32[]{:S(2)}, u32[]{:S(2)}) collective-permute-start(bf16[384,2048]{1,0:T(8,128)(2,1)} %collective-permute-done.4.refs_3_), channel_id=1, source_target_pairs={{0,1},{1,0},{2,3},{3,2},{4,5},{5,4},{6,7},{7,6},{8,9},{9,8},{10,11... | collective-permute-start | bytes 4718600 | tf_op jit(solution)/shard_map/ppermute | solution.py:43
  163.0 36.1 %collective-permute-start.15 = (bf16[384,2048]{1,0:T(8,128)(2,1)}, bf16[384,2048]{1,0:T(8,128)(2,1)}, u32[]{:S(2)}, u32[]{:S(2)}) collective-permute-start(bf16[384,2048]{1,0:T(8,128)(2,1)} %shard_map.257.refs_4_), channel_id=1, source_target_pairs={{0,4},{1,5},{2,6},{3,7},{4,0},{5,1},{6,2},{7,3},{8,12},{9,13},{10,... | collective-permute-start | bytes 4718600 | tf_op jit(solution)/shard_map/ppermute | solution.py:43
  205.0 24.4 %collective-permute-start.16 = (bf16[1536,2048]{1,0:T(8,128)(2,1)}, bf16[1536,2048]{1,0:T(8,128)(2,1)}, u32[]{:S(2)}, u32[]{:S(2)}) collective-permute-start(bf16[1536,2048]{1,0:T(8,128)(2,1)} %shard_map.258.refs_3_.refs_0_.refs_2_), channel_id=1, source_target_pairs={{0,1},{1,0},{2,3},{3,2},{4,5},{5,4},{6,7},{7,6},{8,9},{9,8},{10,11... | collective-permute-start | bytes 18874376 | tf_op jit(solution)/shard_map/ppermute | solution.py:43
  206.1 148.1 %reduce-scatter.4.cloned.1.call-start = ((), (), s32[]{:S(2)}) async-start(), calls=%async_computation.9 | async-start | bytes 5242880 | tf_op jit(solution)/shard_map/reduce_scatter | solution.py:679
  273.5 140.8 %reduce-scatter.6.cloned.1.call-start = ((), (), s32[]{:S(2)}) async-start(), calls=%async_computation.10 | async-start | bytes 3932160 | tf_op jit(solution)/shard_map/reduce_scatter | solution.py:679
  334.9 23.5 %collective-permute-start.17 = (bf16[768,2048]{1,0:T(8,128)(2,1)}, bf16[768,2048]{1,0:T(8,128)(2,1)}, u32[]{:S(2)}, u32[]{:S(2)}) collective-permute-start(bf16[768,2048]{1,0:T(8,128)(2,1)} %get-tuple-element.67.refs_6_), channel_id=1, source_target_pairs={{0,1},{1,0},{2,3},{3,2},{4,5},{5,4},{6,7},{7,6},{8,9},{9,8},{10,11... | collective-permute-start | bytes 9437192 | tf_op jit(solution)/shard_map/ppermute | solution.py:43
  335.2 23.2 %collective-permute-start.18 = (bf16[768,2048]{1,0:T(8,128)(2,1)}, bf16[768,2048]{1,0:T(8,128)(2,1)}, u32[]{:S(2)}, u32[]{:S(2)}) collective-permute-start(bf16[768,2048]{1,0:T(8,128)(2,1)} %get-tuple-element.68), channel_id=1, source_target_pairs={{0,1},{1,0},{2,3},{3,2},{4,5},{5,4},{6,7},{7,6},{8,9},{9,8},{10,11... | collective-permute-start | bytes 9437192 | tf_op jit(solution)/shard_map/ppermute | solution.py:43
  353.6 55.6 %collective-permute-start.23 = (bf16[768,2048]{1,0:T(8,128)(2,1)}, bf16[768,2048]{1,0:T(8,128)(2,1)}, u32[]{:S(2)}, u32[]{:S(2)}) collective-permute-start(bf16[768,2048]{1,0:T(8,128)(2,1)} %get-tuple-element.69.refs_6_), channel_id=1, source_target_pairs={{0,1},{1,0},{2,3},{3,2},{4,5},{5,4},{6,7},{7,6},{8,9},{9,8},{10,11... | collective-permute-start | bytes 9437192 | tf_op jit(solution)/shard_map/ppermute | solution.py:43
  353.9 55.3 %collective-permute-start.24 = (bf16[768,2048]{1,0:T(8,128)(2,1)}, bf16[768,2048]{1,0:T(8,128)(2,1)}, u32[]{:S(2)}, u32[]{:S(2)}) collective-permute-start(bf16[768,2048]{1,0:T(8,128)(2,1)} %get-tuple-element.77), channel_id=1, source_target_pairs={{0,1},{1,0},{2,3},{3,2},{4,5},{5,4},{6,7},{7,6},{8,9},{9,8},{10,11... | collective-permute-start | bytes 9437192 | tf_op jit(solution)/shard_map/ppermute | solution.py:43
  354.2 23.7 %all-to-all-start.1 = ((bf16[8,64,1024]{2,1,0:T(8,128)(2,1)}), bf16[8,64,1024]{2,1,0:T(8,128)(2,1)S(1)}, u32[]{:S(2)}, u32[]{:S(2)}) async-start(bf16[8,64,1024]{2,1,0:T(8,128)(2,1)} %bitcast.86), calls=%async_computation.2 | async-start | bytes 2097152 | tf_op jit(solution)/shard_map/all_to_all | solution.py:684
  358.1 155.2 %reduce-scatter.8.cloned.1.call-start = ((), (), s32[]{:S(2)}) async-start(), calls=%async_computation.11 | async-start | bytes 6553600 | tf_op jit(solution)/shard_map/reduce_scatter | solution.py:679
  375.3 26.1 %collective-permute-start.19 = (bf16[384,1024]{1,0:T(8,128)(2,1)}, bf16[384,1024]{1,0:T(8,128)(2,1)S(1)}, u32[]{:S(2)}, u32[]{:S(2)}) collective-permute-start(bf16[384,1024]{1,0:T(8,128)(2,1)} %get-tuple-element.73), channel_id=1, source_target_pairs={{0,2},{1,3},{2,0},{3,1},{4,6},{5,7},{6,4},{7,5},{8,10},{9,11},{10,... | collective-permute-start | bytes 2359304 | tf_op jit(solution)/shard_map/ppermute | solution.py:43
  376.7 24.7 %collective-permute-start.20 = (bf16[384,1024]{1,0:T(8,128)(2,1)}, bf16[384,1024]{1,0:T(8,128)(2,1)S(1)}, u32[]{:S(2)}, u32[]{:S(2)}) collective-permute-start(bf16[384,1024]{1,0:T(8,128)(2,1)} %get-tuple-element.74), channel_id=1, source_target_pairs={{0,4},{1,5},{2,6},{3,7},{4,0},{5,1},{6,2},{7,3},{8,12},{9,13},{10,... | collective-permute-start | bytes 2359304 | tf_op jit(solution)/shard_map/ppermute | solution.py:43
  406.3 35.3 %collective-permute-start.21 = (bf16[384,2048]{1,0:T(8,128)(2,1)}, bf16[384,2048]{1,0:T(8,128)(2,1)S(1)}, u32[]{:S(2)}, u32[]{:S(2)}) collective-permute-start(bf16[384,2048]{1,0:T(8,128)(2,1)} %get-tuple-element.75.refs_8_), channel_id=1, source_target_pairs={{0,2},{1,3},{2,0},{3,1},{4,6},{5,7},{6,4},{7,5},{8,10},{9,11},{10,... | collective-permute-start | bytes 4718600 | tf_op jit(solution)/shard_map/ppermute | solution.py:43
  406.5 35.0 %collective-permute-start.22 = (bf16[384,2048]{1,0:T(8,128)(2,1)}, bf16[384,2048]{1,0:T(8,128)(2,1)S(1)}, u32[]{:S(2)}, u32[]{:S(2)}) collective-permute-start(bf16[384,2048]{1,0:T(8,128)(2,1)} %get-tuple-element.76), channel_id=1, source_target_pairs={{0,4},{1,5},{2,6},{3,7},{4,0},{5,1},{6,2},{7,3},{8,12},{9,13},{10,... | collective-permute-start | bytes 4718600 | tf_op jit(solution)/shard_map/ppermute | solution.py:43
  407.8 55.8 %collective-permute-start.29 = (f32[30,128]{1,0:T(8,128)}, f32[30,128]{1,0:T(8,128)}, u32[]{:S(2)}, u32[]{:S(2)}) collective-permute-start(f32[30,128]{1,0:T(8,128)} %bitcast.41), channel_id=1, source_target_pairs={{0,8},{1,9},{2,10},{3,11},{4,12},{5,13},{6,14},{7,15},{8,0},{9,1},... | collective-permute-start | bytes 46088 | tf_op jit(solution)/shard_map/ppermute | solution.py:43
  435.8 22.6 %collective-permute-start.25 = (bf16[384,1024]{1,0:T(8,128)(2,1)}, bf16[384,1024]{1,0:T(8,128)(2,1)}, u32[]{:S(2)}, u32[]{:S(2)}) collective-permute-start(bf16[384,1024]{1,0:T(8,128)(2,1)} %get-tuple-element.81), channel_id=1, source_target_pairs={{0,2},{1,3},{2,0},{3,1},{4,6},{5,7},{6,4},{7,5},{8,10},{9,11},{10,... | collective-permute-start | bytes 2359304 | tf_op jit(solution)/shard_map/ppermute | solution.py:43
  437.0 21.4 %collective-permute-start.26 = (bf16[384,1024]{1,0:T(8,128)(2,1)}, bf16[384,1024]{1,0:T(8,128)(2,1)}, u32[]{:S(2)}, u32[]{:S(2)}) collective-permute-start(bf16[384,1024]{1,0:T(8,128)(2,1)} %get-tuple-element.82), channel_id=1, source_target_pairs={{0,4},{1,5},{2,6},{3,7},{4,0},{5,1},{6,2},{7,3},{8,12},{9,13},{10,... | collective-permute-start | bytes 2359304 | tf_op jit(solution)/shard_map/ppermute | solution.py:43
  462.1 43.6 %collective-permute-start.27 = (bf16[384,2048]{1,0:T(8,128)(2,1)}, bf16[384,2048]{1,0:T(8,128)(2,1)S(1)}, u32[]{:S(2)}, u32[]{:S(2)}) collective-permute-start(bf16[384,2048]{1,0:T(8,128)(2,1)} %get-tuple-element.83.refs_5_), channel_id=1, source_target_pairs={{0,2},{1,3},{2,0},{3,1},{4,6},{5,7},{6,4},{7,5},{8,10},{9,11},{10,... | collective-permute-start | bytes 4718600 | tf_op jit(solution)/shard_map/ppermute | solution.py:43
  463.4 42.4 %collective-permute-start.28 = (bf16[384,2048]{1,0:T(8,128)(2,1)}, bf16[384,2048]{1,0:T(8,128)(2,1)}, u32[]{:S(2)}, u32[]{:S(2)}) collective-permute-start(bf16[384,2048]{1,0:T(8,128)(2,1)} %get-tuple-element.84), channel_id=1, source_target_pairs={{0,4},{1,5},{2,6},{3,7},{4,0},{5,1},{6,2},{7,3},{8,12},{9,13},{10,... | collective-permute-start | bytes 4718600 | tf_op jit(solution)/shard_map/ppermute | solution.py:43
  464.3 4.6 collective-permute-start.30
  469.7 12.4 %collective-permute-start.31 = (f32[1,1,1,14,128]{4,3,2,1,0:T(8,128)S(1)}, f32[1,1,1,14,128]{4,3,2,1,0:T(8,128)S(1)}, u32[]{:S(2)}, u32[]{:S(2)}) collective-permute-start(f32[1,1,1,14,128]{4,3,2,1,0:T(8,128)S(1)} %get-tuple-element.104), channel_id=1, source_target_pairs={{0,1},{1,0},{2,3},{3,2},{4,5},{5,4},{6,7},{7,6},{8,9},{9,8},{10,11... | collective-permute-start | bytes 21512 | tf_op jit(solution)/shard_map/ppermute | solution.py:43
  475.4 52.1 %all-to-all-start.2 = ((bf16[8,64,768]{2,1,0:T(8,128)(2,1)}), bf16[8,64,768]{2,1,0:T(8,128)(2,1)S(1)}, u32[]{:S(2)}, u32[]{:S(2)}) async-start(bf16[8,64,768]{2,1,0:T(8,128)(2,1)} %bitcast.16), calls=%async_computation.4 | async-start | bytes 1572864 | tf_op jit(solution)/shard_map/all_to_all | solution.py:684
  482.0 23.2 %collective-permute-start.32 = (f32[1,1,2,14,128]{4,3,2,1,0:T(8,128)S(1)}, f32[1,1,2,14,128]{4,3,2,1,0:T(8,128)S(1)}, u32[]{:S(2)}, u32[]{:S(2)}) collective-permute-start(f32[1,1,2,14,128]{4,3,2,1,0:T(8,128)S(1)} %maximum_select_fusion.7), channel_id=1, source_target_pairs={{0,2},{1,3},{2,0},{3,1},{4,6},{5,7},{6,4},{7,5},{8,10},{9,11},{10,... | collective-permute-start | bytes 43016 | tf_op jit(solution)/shard_map/ppermute | solution.py:43
  505.3 16.8 %collective-permute-start.33 = (f32[1,2,2,14,128]{4,3,2,1,0:T(8,128)S(1)}, f32[1,2,2,14,128]{4,3,2,1,0:T(8,128)S(1)}, u32[]{:S(2)}, u32[]{:S(2)}) collective-permute-start(f32[1,2,2,14,128]{4,3,2,1,0:T(8,128)S(1)} %maximum_select_fusion.3), channel_id=1, source_target_pairs={{0,4},{1,5},{2,6},{3,7},{4,0},{5,1},{6,2},{7,3},{8,12},{9,13},{10,... | collective-permute-start | bytes 86024 | tf_op jit(solution)/shard_map/ppermute | solution.py:43
  516.2 22.0 %collective-permute-start.34 = (bf16[64,2048]{1,0:T(8,128)(2,1)}, bf16[64,2048]{1,0:T(8,128)(2,1)S(1)}, u32[]{:S(2)}, u32[]{:S(2)}) collective-permute-start(bf16[64,2048]{1,0:T(8,128)(2,1)} %get-tuple-element.95), channel_id=1, source_target_pairs={{0,0},{8,1},{16,2},{24,3},{1,4},{9,5},{17,6},{25,7},{2,8},{10,9},{... | collective-permute-start | bytes 786440 | tf_op jit(solution)/shard_map/ppermute | solution.py:845
  (29 other events, 335.9 us)
Sparse Core Ops, SparseCore 0:
  17.4 108.6 all-gather.3
  127.7 78.8 all-gather.7
  208.2 61.9 all-gather.5
  273.6 77.2 reduce-scatter.3
  353.7 60.5 reduce-scatter.5
  416.6 94.6 reduce-scatter.7

commit v8 on v7

--- a/solution.py
+++ b/solution.py
@@ -157,12 +157,8 @@
     return lax.dot_general(left, right, PAIRED, preferred_element_type=jnp.float32)
 
 
-def over_blocks(
-    chain, kernel, slots, pieces, blocked, known, outs, sums=(), rows=None, pair=()
-):
+def over_blocks(chain, kernel, slots, pieces, blocked, known, outs, sums=(), pair=()):
     count = HEADS
-    gathered, runs = rows or (None, [])
-    extra = [gathered] if runs else []
 
     def body(*refs):
         refs = list(refs)
@@ -176,20 +172,7 @@
                     held[...] = piece[...]
 
             refs = [held] + refs[len(pieces) + len(pair) :]
-        given = bool(pieces or pair) + len(blocked) + len(known)
-        if not runs:
-            kernel(*refs)
-            return
-        weight = refs[-1]
-
-        @pl.when(pl.program_id(0) == 0)
-        def _():
-            place = 0
-            for start, many in runs:
-                weight[place : place + many, :] = refs[given][start : start + many, :]
-                place += many
-
-        kernel(*refs[:given], weight, *refs[given + 1 : -1])
+        kernel(*refs)
 
     def moving(width):
         return pl.BlockSpec((slots, width), lambda i: (i, 0))
@@ -198,26 +181,20 @@
     shapes += [((1, width), jnp.float32) for width in sums]
     specs = [moving(width) for width, _ in outs]
     specs += [pl.BlockSpec((1, width), lambda i: (0, 0)) for width in sums]
-    if runs:
-        shape = (sum(many for _, many in runs), gathered.shape[1])
-        shapes.append((shape, jnp.bfloat16))
-        specs.append(pl.BlockSpec(shape, lambda i: (0, 0)))
+
     def half_of(item, place):
         half = count // 2
         return pl.BlockSpec(
             (slots, item.shape[1]), lambda i: (jnp.clip(i - place * half, 0, half - 1), 0)
         )
 
-    def once(item):
-        return pl.BlockSpec(item.shape, lambda i: (0, 0), pipeline_mode=pl.Buffered(1))
-
     options = {}
     if pieces or pair:
         item = pair[0] if pair else pieces[0][0]
         options["scratch_shapes"] = [pltpu.VMEM((slots, item.shape[1]), item.dtype)]
     return chain.launch(
         body,
-        [*[item for item, _ in pieces], *pair, *blocked, *known, *extra],
+        [*[item for item, _ in pieces], *pair, *blocked, *known],
         [
             pl.BlockSpec(
                 (slots, item.shape[1]),
@@ -228,8 +205,7 @@
         ]
         + [half_of(item, place) for place, item in enumerate(pair)]
         + [moving(item.shape[1]) for item in blocked]
-        + [whole(item) for item in known]
-        + [once(item) for item in extra],
+        + [whole(item) for item in known],
         shapes,
         specs,
         (count,),
@@ -434,6 +410,26 @@
         [pl.BlockSpec((rows, width), lambda i: (i, 0))],
         (len(values),),
     )[0]
+
+
+def part_rows(chain, gathered, groups, units, rows):
+    width = gathered.shape[1]
+
+    def kernel(gathered, contract, dense):
+        contract[...] = gathered[:units]
+        dense[...] = gathered[units:]
+
+    def spec(many):
+        return pl.BlockSpec((many, width), lambda i: (i, 0))
+
+    return chain.launch(
+        kernel,
+        [gathered],
+        [spec(units + rows)],
+        [((groups * many, width), gathered.dtype) for many in (units, rows)],
+        [spec(units), spec(rows)],
+        (groups,),
+    )
 
 
 def copied(chain, value):
@@ -689,8 +685,6 @@
     out_part = jnp.concatenate([contract_weight, dense_part])
     weight_out = gather(out_part)
     chain.settle(out_part)
-    contract_runs = [(group * (units + rows), units) for group in range(groups)]
-    dense_runs = [(group * (units + rows) + units, rows) for group in range(groups)]
 
     own_tokens = own_pieces(tokens, plan)
 
@@ -777,6 +771,7 @@
     )
 
     passed = swap(copied(chain, own_cotangent[2]), 2, plan)
+    weight_contract, weight_dense = part_rows(chain, weight_out, groups, units, rows)
     chain.settle(sine, segment_column, bias_qkv, bias_out)
     half = laid_together(
         chain, [own_cotangent[0], own_cotangent[2], own_cotangent[4], passed]
@@ -793,31 +788,29 @@
         [bias_expand, weight_expand],
         [(hidden_units, jnp.bfloat16), (hidden_units, jnp.float32)],
     )
-    grad_hidden, hidden_sum, cotangent_sum, weight_contract = over_blocks(
+    grad_hidden, hidden_sum, cotangent_sum = over_blocks(
         chain,
         grad_hidden_kernel,
         slots,
         [],
         [slope],
-        [],
+        [weight_contract],
         [(hidden_units, jnp.bfloat16)],
         [hidden_units, width],
-        (weight_out, contract_runs),
-        group_cotangent,
+        pair=group_cotangent,
     )
     expand_got = reduce(input_terms(chain, normed, grad_hidden))
 
-    attn, grad_qkv, qkv_sum, weight_dense = over_blocks(
+    attn, grad_qkv, qkv_sum = over_blocks(
         chain,
         lambda *refs: attend_kernel(head_dim, *refs),
         slots,
         [],
         [low_one, cosine, sine, segment_column],
-        [segment, bias_qkv, weight_qkv],
+        [segment, bias_qkv, weight_qkv, weight_dense],
         [(head_dim, jnp.bfloat16), (split, jnp.bfloat16)],
         [split],
-        (weight_out, dense_runs),
-        group_cotangent,
+        pair=group_cotangent,
     )
 
 

time: 554 us -> 551 us (level)
    ppermute x33, waiting for transfers between devices: 132 us -> 125 us  [swap(): return lax.ppermute(value, 'dp', plan.flip(bit))]
    pallas_call x22 -> x23, Pallas kernels: 273 us -> 274 us  [launch(): pl.pallas_call(body, grid_spec=pltpu.PrefetchScalarGridSpec(num_scalar_pr...]
  transfers between devices with their start and end apart: 44 -> 44, of which waited for: 15 -> 16; matrix products, arithmetic and copies ran while one was open for 5% -> 5% of each run, Pallas kernels for 50% -> 50%
where the time goes in v8:
time: 551 us; the launch traced here: 544 us
  Pallas kernels  274 us (50%)
  waiting for transfers between devices  143 us (26%)
  starting transfers between devices  74.8 us (14%)
  local copies, waits for them, and re-layouts  21.8 us (4%)
  other arithmetic  15.6 us (3%)
  between operations  15.2 us (3%)
    pallas_call x23, Pallas kernels, launch(): pl.pallas_call(body, grid_spec=pltpu.PrefetchScalarGridSpec(num_scalar_pr...  274 us
    ppermute x33, waiting for transfers between devices, swap(): return lax.ppermute(value, 'dp', plan.flip(bit))  125 us
    ppermute x33, starting transfers between devices, swap(): return lax.ppermute(value, 'dp', plan.flip(bit))  50.1 us
    all_to_all x3, starting transfers between devices, exchange(): lax.all_to_all(value, 'dp', 0, 0, tiled=True, axis_index_groups=sharing)  13.4 us
    unnamed x73, local copies, waits for them, and re-layouts  12.4 us
  transfers between devices with their start and end apart: 44, of which 16 were waited for; matrix products, arithmetic and copies ran while one was open for 5% of the time, Pallas kernels for 50%

profile of v8, /device:TPU:1, one launch (start us, length us, event | category | flops | bytes accessed | tf_op | source)
XLA Modules:
  0.0 543.9 jit_solution(1232508960235454998)
XLA Ops:
  7.2 4.7 collective-permute-start.14
  13.3 2.9 collective-permute-done.14
  17.3 10.4 %collective-permute-start.3 = (bf16[384,2048]{1,0:T(8,128)(2,1)S(1)}, bf16[384,2048]{1,0:T(8,128)(2,1)}, u32[]{:S(2)}, u32[]{:S(2)}) collective-permute-start(bf16[384,2048]{1,0:T(8,128)(2,1)S(1)} %copy-done.3), channel_id=1, source_target_pairs={{0,4},{1,5},{2,6},{3,7},{4,0},{5,1},{6,2},{7,3},{8,12},{9,13},{10,... | collective-permute-start | bytes 4718600 | tf_op jit(solution)/shard_map/ppermute | solution.py:43
  27.7 2.8 shard_map.254.refs_1_
  30.6 5.8 %all-to-all-start = ((bf16[8,64,1792]{2,1,0:T(8,128)(2,1)}), bf16[8,64,1792]{2,1,0:T(8,128)(2,1)S(1)}, u32[]{:S(2)}, u32[]{:S(2)}) async-start(bf16[8,64,1792]{2,1,0:T(8,128)(2,1)} %shard_map.254.refs_1_), calls=%async_computation | async-start | bytes 3670016 | tf_op jit(solution)/shard_map/all_to_all | solution.py:680
  36.6 24.0 %collective-permute-done.3.refs_2_ = bf16[384,2048]{1,0:T(8,128)(2,1)} collective-permute-done((bf16[384,2048]{1,0:T(8,128)(2,1)S(1)}, bf16[384,2048]{1,0:T(8,128)(2,1)}, u32[]{:S(2)}, u32[]{:S(2)}) %collective-permute-start.3) | collective-permute-done | bytes 1572896 | tf_op jit(solution)/shard_map/ppermute | solution.py:43
  60.6 4.6 collective-permute-start.7
  65.2 2.0 collective-permute-start.6
  67.5 13.8 %collective-permute-done.9 = bf16[1,1,1,1,1,8,128]{6,5,4,3,2,1,0:T(8,128)(2,1)S(1)} collective-permute-done((bf16[1,1,1,1,1,8,128]{6,5,4,3,2,1,0:T(8,128)(2,1)S(1)}, bf16[1,1,1,1,1,8,128]{6,5,4,3,2,1,0:T(8,128)(2,1)S(1)}, u32[]{:S(2)}, u32[]{:S(2)}) %collective-permute-start.9) | collective-permute-done | bytes 2080 | tf_op jit(solution)/shard_map/ppermute | solution.py:43
  81.6 2.5 collective-permute-done.10
  84.1 3.7 collective-permute-start.11
  92.0 3.3 collective-permute-start.13
  95.4 6.8 %collective-permute-done.13 = bf16[1,2,2,2,2,8,128]{6,5,4,3,2,1,0:T(8,128)(2,1)S(1)} collective-permute-done((bf16[1,2,2,2,2,8,128]{6,5,4,3,2,1,0:T(8,128)(2,1)S(1)}, bf16[1,2,2,2,2,8,128]{6,5,4,3,2,1,0:T(8,128)(2,1)S(1)}, u32[]{:S(2)}, u32[]{:S(2)}) %collective-permute-start.13) | collective-permute-done | bytes 32800 | tf_op jit(solution)/shard_map/ppermute | solution.py:43
  104.1 3.8 shard_map.255
  108.9 15.9 %collective-permute-done.4.refs_3_ = bf16[384,2048]{1,0:T(8,128)(2,1)} collective-permute-done((bf16[384,2048]{1,0:T(8,128)(2,1)}, bf16[384,2048]{1,0:T(8,128)(2,1)}, u32[]{:S(2)}, u32[]{:S(2)}) %collective-permute-start.4) | collective-permute-done | bytes 1572896 | tf_op jit(solution)/shard_map/ppermute | solution.py:43
  129.4 7.0 %fusion = (f32[3072,32]{1,0:T(8,128)S(1)}, f32[3072,32]{1,0:T(8,128)}, f32[3072,32]{1,0:T(8,128)S(1)}) fusion(f32[32]{0:T(128)S(1)} %multiply_exponential_fusion, f32[3072]{0:T(1024)S(1)} %convert_element_type.48), kind=kLoop, calls=%fused_computation.4 | loop fusion | flops 196608 | bytes 1192064 | tf_op jit(solution)/shard_map/neg | solution.py:136
  138.1 21.4 %shard_map.256 = (bf16[3072,2048]{1,0:T(8,128)(2,1)}, bf16[3072,2048]{1,0:T(8,128)(2,1)}, bf16[3072,2048]{1,0:T(8,128)(2,1)}) custom-call(bf16[384,2048]{1,0:T(8,128)(2,1)} %refs_1_.3, bf16[384,2048]{1,0:T(8,128)(2,1)} %collective-permute-done.2.refs_1_, bf16[384,2048]{1,0:T(8,128)(2,1)} %collective-permute-done.3.refs_2_, ...), custom_call_target="tpu_custom_call" | custom-call | flops 1 | bytes 1 | tf_op jit(solution)/shard_map/pallas_call | solution.py:98
  159.4 3.6 shard_map.257.refs_1_
  167.0 3.0 maximum_maximum_fusion.1.refs_5_.refs_4_
  170.0 5.3 shard_map.258
  175.3 23.8 %collective-permute-done.15.refs_3_ = bf16[384,2048]{1,0:T(8,128)(2,1)} collective-permute-done((bf16[384,2048]{1,0:T(8,128)(2,1)}, bf16[384,2048]{1,0:T(8,128)(2,1)}, u32[]{:S(2)}, u32[]{:S(2)}) %collective-permute-start.15) | collective-permute-done | bytes 1572896 | tf_op jit(solution)/shard_map/ppermute | solution.py:43
  199.1 5.9 %shard_map.259.refs_3_.refs_0_.refs_2_ = bf16[1536,2048]{1,0:T(8,128)(2,1)} custom-call(bf16[384,2048]{1,0:T(8,128)(2,1)} %refs_0_.9, bf16[384,2048]{1,0:T(8,128)(2,1)} %collective-permute-done.refs_0_.refs_1_, bf16[384,2048]{1,0:T(8,128)(2,1)} %collective-permute-done.1.refs_2_, bf16[384,2048]{1,0:T(8,128)(2,1)} %collective-permute-done.15.refs_3_, ...), custom_call_target="tpu_custom_call" | custom-call | flops 1 | bytes 1 | tf_op jit(solution)/shard_map/pallas_call | solution.py:98
  207.0 22.5 %shard_map.260 = (bf16[3072,1024]{1,0:T(8,128)(2,1)}, f32[3072,1024]{1,0:T(8,128)}) custom-call(bf16[3072,2048]{1,0:T(8,128)(2,1)} %get-tuple-element.60.refs_0_, f32[1,1024]{1,0:T(1,128)} %bitcast.103, bf16[2048,1024]{1,0:T(8,128)(2,1)} %all-gather.8.cloned.1.call-done.refs_2_.refs_3_, bf16[1536,2048]{1,0:T(8,128)(2,1)} %shard_map.259.refs_3_.refs_0_.refs_2_), custom_call_target="tpu_custom_call" | custom-call | flops 1 | bytes 1 | tf_op jit(solution)/shard_map/pallas_call | solution.py:98
  229.4 23.3 %shard_map.261 = (bf16[3072,1024]{1,0:T(8,128)(2,1)}, f32[1,1024]{1,0:T(1,128)}, f32[1,2048]{1,0:T(1,128)}) custom-call(bf16[1536,2048]{1,0:T(8,128)(2,1)} %shard_map.259.refs_3_.refs_0_.refs_2_, bf16[1536,2048]{1,0:T(8,128)(2,1)} %collective-permute-done.16.refs_1_.refs_3_, f32[3072,1024]{1,0:T(8,128)} %get-tuple-element.62.refs_2_, ...), custom_call_target="tpu_custom_call" | custom-call | flops 1 | bytes 1 | tf_op jit(solution)/shard_map/pallas_call | solution.py:98
  252.7 18.8 %shard_map.262.refs_10_ = bf16[2048,1024]{1,0:T(8,128)(2,1)} custom-call(bf16[3072,2048]{1,0:T(8,128)(2,1)} %get-tuple-element.59.refs_0_, bf16[3072,1024]{1,0:T(8,128)(2,1)} %get-tuple-element.64.refs_1_.refs_2_, bf16[3072,1024]{1,0:T(8,128)(2,1)} %get-tuple-element.64.refs_1_.refs_2_), custom_call_target="tpu_custom_call" | custom-call | flops 1 | bytes 1 | tf_op jit(solution)/shard_map/pallas_call | solution.py:98
  271.8 29.6 %shard_map.263 = (bf16[3072,256]{1,0:T(8,128)(2,1)}, bf16[3072,768]{1,0:T(8,128)(2,1)}, f32[1,768]{1,0:T(1,128)}) custom-call(bf16[1536,2048]{1,0:T(8,128)(2,1)} %shard_map.259.refs_3_.refs_0_.refs_2_, bf16[1536,2048]{1,0:T(8,128)(2,1)} %collective-permute-done.16.refs_1_.refs_3_, bf16[3072,2048]{1,0:T(8,128)(2,1)} %get-tuple-element.56.refs_1_.refs_2_, ...), custom_call_target="tpu_custom_call" | custom-call | flops 1 | bytes 1 | tf_op jit(solution)/shard_map/pallas_call | solution.py:98
  301.4 15.5 %shard_map.264.refs_4_ = bf16[2048,768]{1,0:T(8,128)(2,1)} custom-call(bf16[3072,2048]{1,0:T(8,128)(2,1)} %get-tuple-element.59.refs_0_, bf16[3072,768]{1,0:T(8,128)(2,1)} %get-tuple-element.66.refs_1_.refs_0_, bf16[3072,256]{1,0:T(8,128)(2,1)} %get-tuple-element.65.refs_2_.refs_0_.refs_1_), custom_call_target="tpu_custom_call" | custom-call | flops 1 | bytes 1 | tf_op jit(solution)/shard_map/pallas_call | solution.py:98
  317.0 14.2 %shard_map.265 = (bf16[768,2048]{1,0:T(8,128)(2,1)}, bf16[768,2048]{1,0:T(8,128)(2,1)}) custom-call(bf16[3072,256]{1,0:T(8,128)(2,1)} %get-tuple-element.65.refs_2_.refs_0_.refs_1_, bf16[3072,1024]{1,0:T(8,128)(2,1)} %get-tuple-element.63.refs_4_.refs_1_.refs_0_, bf16[256,2048]{1,0:T(8,128)(2,1)} %get-tuple-element.58.refs_9_.refs_2_, ...), custom_call_target="tpu_custom_call" | custom-call | flops 1 | bytes 1 | tf_op jit(solution)/shard_map/pallas_call | solution.py:98
  331.7 18.3 %shard_map.266 = (bf16[768,2048]{1,0:T(8,128)(2,1)}, bf16[768,2048]{1,0:T(8,128)(2,1)}) custom-call(bf16[3072,768]{1,0:T(8,128)(2,1)} %get-tuple-element.66.refs_1_.refs_0_, bf16[3072,1024]{1,0:T(8,128)(2,1)} %get-tuple-element.64.refs_1_.refs_2_, bf16[2048,768]{1,0:T(8,128)(2,1)} %all-gather.6.cloned.1.call-done.refs_8_.refs_2_, ...), custom_call_target="tpu_custom_call" | custom-call | flops 1 | bytes 1 | tf_op jit(solution)/shard_map/pallas_call | solution.py:98
  350.5 4.0 all-to-all-start.1
  354.8 16.4 %shard_map.267 = (bf16[384,2048]{1,0:T(8,128)(2,1)}, bf16[384,2048]{1,0:T(8,128)(2,1)}, bf16[384,2048]{1,0:T(8,128)(2,1)}, bf16[384,1024]{1,0:T(8,128)(2,1)}, bf16[384,1024]{1,0:T(8,128)(2,1)}) custom-call(bf16[3072,256]{1,0:T(8,128)(2,1)} %get-tuple-element.65.refs_2_.refs_0_.refs_1_, bf16[3072,1024]{1,0:T(8,128)(2,1)} %get-tuple-element.63.refs_4_.refs_1_.refs_0_, ...), custom_call_target="tpu_custom_call" | custom-call | flops 1 | bytes 1 | tf_op jit(solution)/shard_map/pallas_call | solution.py:98
  374.7 22.5 %shard_map.268.refs_4_ = bf16[1280,2048]{1,0:T(8,128)(2,1)} custom-call(bf16[3072,1024]{1,0:T(8,128)(2,1)} %get-tuple-element.63.refs_4_.refs_1_.refs_0_, bf16[3072,256]{1,0:T(8,128)(2,1)} %get-tuple-element.65.refs_2_.refs_0_.refs_1_, bf16[1536,2048]{1,0:T(8,128)(2,1)} %shard_map.259.refs_3_.refs_0_.refs_2_, ...), custom_call_target="tpu_custom_call" | custom-call | flops 1 | bytes 1 | tf_op jit(solution)/shard_map/pallas_call | solution.py:98
  398.4 3.8 shard_map.269
  404.8 7.7 %reduce-scatter.6.cloned.1.call-done.refs_9_ = bf16[512,768]{1,0:T(8,128)(2,1)} async-done(((bf16[2048,768]{1,0:T(8,128)(2,1)}), bf16[512,768]{1,0:T(8,128)(2,1)}) %reduce-scatter.6.cloned.1.call-update) | async-done | bytes 786448 | tf_op jit(solution)/shard_map/reduce_scatter | solution.py:675
  412.5 21.4 %shard_map.270 = (bf16[384,2048]{1,0:T(8,128)(2,1)}, bf16[384,2048]{1,0:T(8,128)(2,1)}, bf16[384,2048]{1,0:T(8,128)(2,1)}, bf16[384,1024]{1,0:T(8,128)(2,1)}, bf16[384,1024]{1,0:T(8,128)(2,1)}) custom-call(bf16[3072,768]{1,0:T(8,128)(2,1)} %get-tuple-element.66.refs_1_.refs_0_, bf16[3072,1024]{1,0:T(8,128)(2,1)} %get-tuple-element.64.refs_1_.refs_2_, ...), custom_call_target="tpu_custom_call" | custom-call | flops 1 | bytes 1 | tf_op jit(solution)/shard_map/pallas_call | solution.py:98
  439.1 4.9 shard_map.271.refs_4_
  443.9 10.3 %collective-permute-done.25.refs_2_ = bf16[384,1024]{1,0:T(8,128)(2,1)} collective-permute-done((bf16[384,1024]{1,0:T(8,128)(2,1)}, bf16[384,1024]{1,0:T(8,128)(2,1)}, u32[]{:S(2)}, u32[]{:S(2)}) %collective-permute-start.25) | collective-permute-done | bytes 786464 | tf_op jit(solution)/shard_map/ppermute | solution.py:43
  455.0 3.6 shard_map.272
  461.0 2.6 collective-permute-start.30
  466.1 7.2 %collective-permute-start.31 = (f32[1,1,1,14,128]{4,3,2,1,0:T(8,128)S(1)}, f32[1,1,1,14,128]{4,3,2,1,0:T(8,128)S(1)}, u32[]{:S(2)}, u32[]{:S(2)}) collective-permute-start(f32[1,1,1,14,128]{4,3,2,1,0:T(8,128)S(1)} %get-tuple-element.104), channel_id=1, source_target_pairs={{0,1},{1,0},{2,3},{3,2},{4,5},{5,4},{6,7},{7,6},{8,9},{9,8},{10,11... | collective-permute-start | bytes 21512 | tf_op jit(solution)/shard_map/ppermute | solution.py:43
  473.2 3.5 all-to-all-start.2
  481.0 21.4 %collective-permute-done.32 = f32[1,1,2,14,128]{4,3,2,1,0:T(8,128)S(1)} collective-permute-done((f32[1,1,2,14,128]{4,3,2,1,0:T(8,128)S(1)}, f32[1,1,2,14,128]{4,3,2,1,0:T(8,128)S(1)}, u32[]{:S(2)}, u32[]{:S(2)}) %collective-permute-start.32) | collective-permute-done | bytes 14368 | tf_op jit(solution)/shard_map/ppermute | solution.py:43
  503.5 6.4 %shard_map.273.refs_1_ = f32[384,2048]{1,0:T(8,128)} custom-call(bf16[384,2048]{1,0:T(8,128)(2,1)} %refs_0_.9, bf16[384,2048]{1,0:T(8,128)(2,1)} %refs_1_.3, bf16[384,2048]{1,0:T(8,128)(2,1)} %get-tuple-element.78.refs_5_.refs_2_, bf16[384,2048]{1,0:T(8,128)(2,1)} %copy-done.6, bf16[384,2048]{1,0:T(8,128)(2,1)} %collective-permute-done.28.refs_4_, ...), custom_call_target="tpu_custom_call" | custom-call | flops 1 | bytes 1 | tf_op jit(solution)/shard_map/pallas_call | solution.py:98
  509.9 2.9 shard_map.274
  512.8 5.8 %collective-permute-start.34 = (bf16[64,2048]{1,0:T(8,128)(2,1)}, bf16[64,2048]{1,0:T(8,128)(2,1)S(1)}, u32[]{:S(2)}, u32[]{:S(2)}) collective-permute-start(bf16[64,2048]{1,0:T(8,128)(2,1)} %get-tuple-element.95), channel_id=1, source_target_pairs={{0,0},{8,1},{16,2},{24,3},{1,4},{9,5},{17,6},{25,7},{2,8},{10,9},{... | collective-permute-start | bytes 786440 | tf_op jit(solution)/shard_map/ppermute | solution.py:838
  520.1 4.0 shard_map.275
  525.0 3.4 shard_map.276
  528.4 6.9 %collective-permute-done.34 = bf16[64,2048]{1,0:T(8,128)(2,1)S(1)} collective-permute-done((bf16[64,2048]{1,0:T(8,128)(2,1)}, bf16[64,2048]{1,0:T(8,128)(2,1)S(1)}, u32[]{:S(2)}, u32[]{:S(2)}) %collective-permute-start.34) | collective-permute-done | bytes 262176 | tf_op jit(solution)/shard_map/ppermute | solution.py:838
  (206 shorter events, 51.1 us)
Async XLA Ops:
  7.2 130.9 %all-gather.4.cloned.1.call-start = ((), (), s32[]{:S(2)}) async-start(), calls=%async_computation.6 | async-start | bytes 6553600 | tf_op jit(solution)/shard_map/all_gather | solution.py:672
  7.2 8.9 %collective-permute-start.14 = (bf16[64,2048]{1,0:T(8,128)(2,1)}, bf16[64,2048]{1,0:T(8,128)(2,1)S(1)}, u32[]{:S(2)}, u32[]{:S(2)}) collective-permute-start(bf16[64,2048]{1,0:T(8,128)(2,1)} %param.23), channel_id=1, source_target_pairs={{0,0},{1,8},{2,16},{3,24},{4,1},{5,9},{6,17},{7,25},{8,2},{9,10},{... | collective-permute-start | bytes 786440 | tf_op jit(solution)/shard_map/ppermute | solution.py:684
  17.3 43.4 %collective-permute-start.3 = (bf16[384,2048]{1,0:T(8,128)(2,1)S(1)}, bf16[384,2048]{1,0:T(8,128)(2,1)}, u32[]{:S(2)}, u32[]{:S(2)}) collective-permute-start(bf16[384,2048]{1,0:T(8,128)(2,1)S(1)} %copy-done.3), channel_id=1, source_target_pairs={{0,4},{1,5},{2,6},{3,7},{4,0},{5,1},{6,2},{7,3},{8,12},{9,13},{10,... | collective-permute-start | bytes 4718600 | tf_op jit(solution)/shard_map/ppermute | solution.py:43
  27.7 37.6 %collective-permute-start.2 = (bf16[384,2048]{1,0:T(8,128)(2,1)S(1)}, bf16[384,2048]{1,0:T(8,128)(2,1)}, u32[]{:S(2)}, u32[]{:S(2)}) collective-permute-start(bf16[384,2048]{1,0:T(8,128)(2,1)S(1)} %copy-done.3), channel_id=1, source_target_pairs={{0,2},{1,3},{2,0},{3,1},{4,6},{5,7},{6,4},{7,5},{8,10},{9,11},{10,... | collective-permute-start | bytes 4718600 | tf_op jit(solution)/shard_map/ppermute | solution.py:43
  30.5 36.8 %copy-start.20 = (bf16[192]{0:T(256)(128)(2,1)S(1)}, bf16[192]{0:T(256)(128)(2,1)}, u32[]{:S(2)}) copy-start(bf16[192]{0:T(256)(128)(2,1)} %param.22) | copy-start | bytes 1156
  30.5 36.8 %copy-start.21 = (bf16[256]{0:T(256)(128)(2,1)S(1)}, bf16[256]{0:T(256)(128)(2,1)}, u32[]{:S(2)}) copy-start(bf16[256]{0:T(256)(128)(2,1)} %param.26) | copy-start | bytes 1540
  30.5 36.8 %copy-start.22 = (bf16[64]{0:T(256)(128)(2,1)S(1)}, bf16[64]{0:T(256)(128)(2,1)}, u32[]{:S(2)}) copy-start(bf16[64]{0:T(256)(128)(2,1)} %param.19) | copy-start | bytes 388
  30.6 72.3 %all-to-all-start = ((bf16[8,64,1792]{2,1,0:T(8,128)(2,1)}), bf16[8,64,1792]{2,1,0:T(8,128)(2,1)S(1)}, u32[]{:S(2)}, u32[]{:S(2)}) async-start(bf16[8,64,1792]{2,1,0:T(8,128)(2,1)} %shard_map.254.refs_1_), calls=%async_computation | async-start | bytes 3670016 | tf_op jit(solution)/shard_map/all_to_all | solution.py:680
  36.4 170.6 %all-gather.8.cloned.1.call-start = ((), (), s32[]{:S(2)}) async-start(), calls=%async_computation.8 | async-start | bytes 5242880 | tf_op jit(solution)/shard_map/all_gather | solution.py:672
  36.4 66.5 %collective-permute-start.5 = (bf16[384,2048]{1,0:T(8,128)(2,1)S(1)}, bf16[384,2048]{1,0:T(8,128)(2,1)}, u32[]{:S(2)}, u32[]{:S(2)}) collective-permute-start(bf16[384,2048]{1,0:T(8,128)(2,1)S(1)} %copy-done.3), channel_id=1, source_target_pairs={{0,1},{1,0},{2,3},{3,2},{4,5},{5,4},{6,7},{7,6},{8,9},{9,8},{10,11... | collective-permute-start | bytes 4718600 | tf_op jit(solution)/shard_map/ppermute | solution.py:43
  60.6 42.3 %collective-permute-start.7 = (bf16[384,2048]{1,0:T(8,128)(2,1)}, bf16[384,2048]{1,0:T(8,128)(2,1)}, u32[]{:S(2)}, u32[]{:S(2)}) collective-permute-start(bf16[384,2048]{1,0:T(8,128)(2,1)} %collective-permute-done.3.refs_2_), channel_id=1, source_target_pairs={{0,1},{1,0},{2,3},{3,2},{4,5},{5,4},{6,7},{7,6},{8,9},{9,8},{10,11... | collective-permute-start | bytes 4718600 | tf_op jit(solution)/shard_map/ppermute | solution.py:43
  65.2 37.7 %collective-permute-start.6 = (bf16[384,2048]{1,0:T(8,128)(2,1)}, bf16[384,2048]{1,0:T(8,128)(2,1)}, u32[]{:S(2)}, u32[]{:S(2)}) collective-permute-start(bf16[384,2048]{1,0:T(8,128)(2,1)} %collective-permute-done.2.refs_1_), channel_id=1, source_target_pairs={{0,1},{1,0},{2,3},{3,2},{4,5},{5,4},{6,7},{7,6},{8,9},{9,8},{10,11... | collective-permute-start | bytes 4718600 | tf_op jit(solution)/shard_map/ppermute | solution.py:43
  67.4 13.8 %collective-permute-start.9 = (bf16[1,1,1,1,1,8,128]{6,5,4,3,2,1,0:T(8,128)(2,1)S(1)}, bf16[1,1,1,1,1,8,128]{6,5,4,3,2,1,0:T(8,128)(2,1)S(1)}, u32[]{:S(2)}, u32[]{:S(2)}) collective-permute-start(bf16[1,1,1,1,1,8,128]{6,5,4,3,2,1,0:T(8,128)(2,1)S(1)} %bitcast.100), channel_id=1, source_target_pairs={{0,2},{1,3},{2,0},{3,1},{4,6},{5,7},{6,4},{7,5},{8,10},{9,11},{10,... | collective-permute-start | bytes 6152 | tf_op jit(solution)/shard_map/ppermute | solution.py:43
  81.3 2.9 collective-permute-start.10
  84.1 4.5 collective-permute-start.11
  88.7 3.4 collective-permute-start.12
  88.8 36.0 %collective-permute-start.4 = (bf16[384,2048]{1,0:T(8,128)(2,1)}, bf16[384,2048]{1,0:T(8,128)(2,1)}, u32[]{:S(2)}, u32[]{:S(2)}) collective-permute-start(bf16[384,2048]{1,0:T(8,128)(2,1)} %collective-permute-done.3.refs_2_), channel_id=1, source_target_pairs={{0,2},{1,3},{2,0},{3,1},{4,6},{5,7},{6,4},{7,5},{8,10},{9,11},{10,... | collective-permute-start | bytes 4718600 | tf_op jit(solution)/shard_map/ppermute | solution.py:43
  92.0 10.1 %collective-permute-start.13 = (bf16[1,2,2,2,2,8,128]{6,5,4,3,2,1,0:T(8,128)(2,1)S(1)}, bf16[1,2,2,2,2,8,128]{6,5,4,3,2,1,0:T(8,128)(2,1)S(1)}, u32[]{:S(2)}, u32[]{:S(2)}) collective-permute-start(bf16[1,2,2,2,2,8,128]{6,5,4,3,2,1,0:T(8,128)(2,1)S(1)} %maximum_select_fusion.2), channel_id=1, source_target_pairs={{0,16},{1,17},{2,18},{3,19},{4,20},{5,21},{6,22},{7,23},{8,24},{9,... | collective-permute-start | bytes 98312 | tf_op jit(solution)/shard_map/ppermute | solution.py:43
  107.9 163.9 %all-gather.6.cloned.1.call-start = ((), (), s32[]{:S(2)}) async-start(), calls=%async_computation.7 | async-start | bytes 3932160 | tf_op jit(solution)/shard_map/all_gather | solution.py:672
  108.0 51.4 %collective-permute-start = (bf16[384,2048]{1,0:T(8,128)(2,1)S(1)}, bf16[384,2048]{1,0:T(8,128)(2,1)}, u32[]{:S(2)}, u32[]{:S(2)}) collective-permute-start(bf16[384,2048]{1,0:T(8,128)(2,1)S(1)} %copy-done.4), channel_id=1, source_target_pairs={{0,2},{1,3},{2,0},{3,1},{4,6},{5,7},{6,4},{7,5},{8,10},{9,11},{10,... | collective-permute-start | bytes 4718600 | tf_op jit(solution)/shard_map/ppermute | solution.py:43
  108.1 67.3 %collective-permute-start.1 = (bf16[384,2048]{1,0:T(8,128)(2,1)S(1)}, bf16[384,2048]{1,0:T(8,128)(2,1)}, u32[]{:S(2)}, u32[]{:S(2)}) collective-permute-start(bf16[384,2048]{1,0:T(8,128)(2,1)S(1)} %copy-done.4), channel_id=1, source_target_pairs={{0,4},{1,5},{2,6},{3,7},{4,0},{5,1},{6,2},{7,3},{8,12},{9,13},{10,... | collective-permute-start | bytes 4718600 | tf_op jit(solution)/shard_map/ppermute | solution.py:43
  108.8 55.1 %copy-start.13 = (s32[8,384]{1,0:T(8,128)}, s32[8,384]{1,0:T(8,128)S(1)}, u32[]{:S(2)}) copy-start(s32[8,384]{1,0:T(8,128)S(1)} %get-tuple-element.96.refs_6_) | copy-start | bytes 36868
  124.8 13.3 %collective-permute-start.8 = (bf16[384,2048]{1,0:T(8,128)(2,1)}, bf16[384,2048]{1,0:T(8,128)(2,1)}, u32[]{:S(2)}, u32[]{:S(2)}) collective-permute-start(bf16[384,2048]{1,0:T(8,128)(2,1)} %collective-permute-done.4.refs_3_), channel_id=1, source_target_pairs={{0,1},{1,0},{2,3},{3,2},{4,5},{5,4},{6,7},{7,6},{8,9},{9,8},{10,11... | collective-permute-start | bytes 4718600 | tf_op jit(solution)/shard_map/ppermute | solution.py:43
  163.0 36.1 %collective-permute-start.15 = (bf16[384,2048]{1,0:T(8,128)(2,1)}, bf16[384,2048]{1,0:T(8,128)(2,1)}, u32[]{:S(2)}, u32[]{:S(2)}) collective-permute-start(bf16[384,2048]{1,0:T(8,128)(2,1)} %shard_map.257.refs_1_), channel_id=1, source_target_pairs={{0,4},{1,5},{2,6},{3,7},{4,0},{5,1},{6,2},{7,3},{8,12},{9,13},{10,... | collective-permute-start | bytes 4718600 | tf_op jit(solution)/shard_map/ppermute | solution.py:43
  205.0 24.4 %collective-permute-start.16 = (bf16[1536,2048]{1,0:T(8,128)(2,1)}, bf16[1536,2048]{1,0:T(8,128)(2,1)}, u32[]{:S(2)}, u32[]{:S(2)}) collective-permute-start(bf16[1536,2048]{1,0:T(8,128)(2,1)} %shard_map.259.refs_3_.refs_0_.refs_2_), channel_id=1, source_target_pairs={{0,1},{1,0},{2,3},{3,2},{4,5},{5,4},{6,7},{7,6},{8,9},{9,8},{10,11... | collective-permute-start | bytes 18874376 | tf_op jit(solution)/shard_map/ppermute | solution.py:43
  206.1 144.4 %reduce-scatter.4.cloned.1.call-start = ((), (), s32[]{:S(2)}) async-start(), calls=%async_computation.9 | async-start | bytes 5242880 | tf_op jit(solution)/shard_map/reduce_scatter | solution.py:675
  271.5 141.0 %reduce-scatter.6.cloned.1.call-start = ((), (), s32[]{:S(2)}) async-start(), calls=%async_computation.10 | async-start | bytes 3932160 | tf_op jit(solution)/shard_map/reduce_scatter | solution.py:675
  331.2 23.6 %collective-permute-start.17 = (bf16[768,2048]{1,0:T(8,128)(2,1)}, bf16[768,2048]{1,0:T(8,128)(2,1)}, u32[]{:S(2)}, u32[]{:S(2)}) collective-permute-start(bf16[768,2048]{1,0:T(8,128)(2,1)} %get-tuple-element.67.refs_6_), channel_id=1, source_target_pairs={{0,1},{1,0},{2,3},{3,2},{4,5},{5,4},{6,7},{7,6},{8,9},{9,8},{10,11... | collective-permute-start | bytes 9437192 | tf_op jit(solution)/shard_map/ppermute | solution.py:43
  331.5 23.3 %collective-permute-start.18 = (bf16[768,2048]{1,0:T(8,128)(2,1)}, bf16[768,2048]{1,0:T(8,128)(2,1)}, u32[]{:S(2)}, u32[]{:S(2)}) collective-permute-start(bf16[768,2048]{1,0:T(8,128)(2,1)} %get-tuple-element.68), channel_id=1, source_target_pairs={{0,1},{1,0},{2,3},{3,2},{4,5},{5,4},{6,7},{7,6},{8,9},{9,8},{10,11... | collective-permute-start | bytes 9437192 | tf_op jit(solution)/shard_map/ppermute | solution.py:43
  350.0 54.9 %collective-permute-start.23 = (bf16[768,2048]{1,0:T(8,128)(2,1)}, bf16[768,2048]{1,0:T(8,128)(2,1)}, u32[]{:S(2)}, u32[]{:S(2)}) collective-permute-start(bf16[768,2048]{1,0:T(8,128)(2,1)} %get-tuple-element.69.refs_6_), channel_id=1, source_target_pairs={{0,1},{1,0},{2,3},{3,2},{4,5},{5,4},{6,7},{7,6},{8,9},{9,8},{10,11... | collective-permute-start | bytes 9437192 | tf_op jit(solution)/shard_map/ppermute | solution.py:43
  350.3 54.5 %collective-permute-start.24 = (bf16[768,2048]{1,0:T(8,128)(2,1)}, bf16[768,2048]{1,0:T(8,128)(2,1)}, u32[]{:S(2)}, u32[]{:S(2)}) collective-permute-start(bf16[768,2048]{1,0:T(8,128)(2,1)} %get-tuple-element.77), channel_id=1, source_target_pairs={{0,1},{1,0},{2,3},{3,2},{4,5},{5,4},{6,7},{7,6},{8,9},{9,8},{10,11... | collective-permute-start | bytes 9437192 | tf_op jit(solution)/shard_map/ppermute | solution.py:43
  350.5 23.2 %all-to-all-start.1 = ((bf16[8,64,1024]{2,1,0:T(8,128)(2,1)}), bf16[8,64,1024]{2,1,0:T(8,128)(2,1)S(1)}, u32[]{:S(2)}, u32[]{:S(2)}) async-start(bf16[8,64,1024]{2,1,0:T(8,128)(2,1)} %bitcast.86), calls=%async_computation.2 | async-start | bytes 2097152 | tf_op jit(solution)/shard_map/all_to_all | solution.py:680
  354.5 155.4 %reduce-scatter.8.cloned.1.call-start = ((), (), s32[]{:S(2)}) async-start(), calls=%async_computation.11 | async-start | bytes 6553600 | tf_op jit(solution)/shard_map/reduce_scatter | solution.py:675
  371.2 26.0 %collective-permute-start.19 = (bf16[384,1024]{1,0:T(8,128)(2,1)}, bf16[384,1024]{1,0:T(8,128)(2,1)S(1)}, u32[]{:S(2)}, u32[]{:S(2)}) collective-permute-start(bf16[384,1024]{1,0:T(8,128)(2,1)} %get-tuple-element.73), channel_id=1, source_target_pairs={{0,2},{1,3},{2,0},{3,1},{4,6},{5,7},{6,4},{7,5},{8,10},{9,11},{10,... | collective-permute-start | bytes 2359304 | tf_op jit(solution)/shard_map/ppermute | solution.py:43
  372.5 24.7 %collective-permute-start.20 = (bf16[384,1024]{1,0:T(8,128)(2,1)}, bf16[384,1024]{1,0:T(8,128)(2,1)S(1)}, u32[]{:S(2)}, u32[]{:S(2)}) collective-permute-start(bf16[384,1024]{1,0:T(8,128)(2,1)} %get-tuple-element.74), channel_id=1, source_target_pairs={{0,4},{1,5},{2,6},{3,7},{4,0},{5,1},{6,2},{7,3},{8,12},{9,13},{10,... | collective-permute-start | bytes 2359304 | tf_op jit(solution)/shard_map/ppermute | solution.py:43
  402.1 35.3 %collective-permute-start.21 = (bf16[384,2048]{1,0:T(8,128)(2,1)}, bf16[384,2048]{1,0:T(8,128)(2,1)S(1)}, u32[]{:S(2)}, u32[]{:S(2)}) collective-permute-start(bf16[384,2048]{1,0:T(8,128)(2,1)} %get-tuple-element.75.refs_8_), channel_id=1, source_target_pairs={{0,2},{1,3},{2,0},{3,1},{4,6},{5,7},{6,4},{7,5},{8,10},{9,11},{10,... | collective-permute-start | bytes 4718600 | tf_op jit(solution)/shard_map/ppermute | solution.py:43
  402.4 35.0 %collective-permute-start.22 = (bf16[384,2048]{1,0:T(8,128)(2,1)}, bf16[384,2048]{1,0:T(8,128)(2,1)S(1)}, u32[]{:S(2)}, u32[]{:S(2)}) collective-permute-start(bf16[384,2048]{1,0:T(8,128)(2,1)} %get-tuple-element.76), channel_id=1, source_target_pairs={{0,4},{1,5},{2,6},{3,7},{4,0},{5,1},{6,2},{7,3},{8,12},{9,13},{10,... | collective-permute-start | bytes 4718600 | tf_op jit(solution)/shard_map/ppermute | solution.py:43
  403.7 56.6 %collective-permute-start.29 = (f32[30,128]{1,0:T(8,128)}, f32[30,128]{1,0:T(8,128)}, u32[]{:S(2)}, u32[]{:S(2)}) collective-permute-start(f32[30,128]{1,0:T(8,128)} %bitcast.41), channel_id=1, source_target_pairs={{0,8},{1,9},{2,10},{3,11},{4,12},{5,13},{6,14},{7,15},{8,0},{9,1},... | collective-permute-start | bytes 46088 | tf_op jit(solution)/shard_map/ppermute | solution.py:43
  433.9 20.3 %collective-permute-start.25 = (bf16[384,1024]{1,0:T(8,128)(2,1)}, bf16[384,1024]{1,0:T(8,128)(2,1)}, u32[]{:S(2)}, u32[]{:S(2)}) collective-permute-start(bf16[384,1024]{1,0:T(8,128)(2,1)} %get-tuple-element.81), channel_id=1, source_target_pairs={{0,2},{1,3},{2,0},{3,1},{4,6},{5,7},{6,4},{7,5},{8,10},{9,11},{10,... | collective-permute-start | bytes 2359304 | tf_op jit(solution)/shard_map/ppermute | solution.py:43
  435.1 19.9 %collective-permute-start.26 = (bf16[384,1024]{1,0:T(8,128)(2,1)}, bf16[384,1024]{1,0:T(8,128)(2,1)}, u32[]{:S(2)}, u32[]{:S(2)}) collective-permute-start(bf16[384,1024]{1,0:T(8,128)(2,1)} %get-tuple-element.82), channel_id=1, source_target_pairs={{0,4},{1,5},{2,6},{3,7},{4,0},{5,1},{6,2},{7,3},{8,12},{9,13},{10,... | collective-permute-start | bytes 2359304 | tf_op jit(solution)/shard_map/ppermute | solution.py:43
  458.7 43.7 %collective-permute-start.27 = (bf16[384,2048]{1,0:T(8,128)(2,1)}, bf16[384,2048]{1,0:T(8,128)(2,1)S(1)}, u32[]{:S(2)}, u32[]{:S(2)}) collective-permute-start(bf16[384,2048]{1,0:T(8,128)(2,1)} %get-tuple-element.83.refs_5_), channel_id=1, source_target_pairs={{0,2},{1,3},{2,0},{3,1},{4,6},{5,7},{6,4},{7,5},{8,10},{9,11},{10,... | collective-permute-start | bytes 4718600 | tf_op jit(solution)/shard_map/ppermute | solution.py:43
  459.1 43.3 %collective-permute-start.28 = (bf16[384,2048]{1,0:T(8,128)(2,1)}, bf16[384,2048]{1,0:T(8,128)(2,1)}, u32[]{:S(2)}, u32[]{:S(2)}) collective-permute-start(bf16[384,2048]{1,0:T(8,128)(2,1)} %get-tuple-element.84), channel_id=1, source_target_pairs={{0,4},{1,5},{2,6},{3,7},{4,0},{5,1},{6,2},{7,3},{8,12},{9,13},{10,... | collective-permute-start | bytes 4718600 | tf_op jit(solution)/shard_map/ppermute | solution.py:43
  461.0 4.3 collective-permute-start.30
  466.1 13.5 %collective-permute-start.31 = (f32[1,1,1,14,128]{4,3,2,1,0:T(8,128)S(1)}, f32[1,1,1,14,128]{4,3,2,1,0:T(8,128)S(1)}, u32[]{:S(2)}, u32[]{:S(2)}) collective-permute-start(f32[1,1,1,14,128]{4,3,2,1,0:T(8,128)S(1)} %get-tuple-element.104), channel_id=1, source_target_pairs={{0,1},{1,0},{2,3},{3,2},{4,5},{5,4},{6,7},{7,6},{8,9},{9,8},{10,11... | collective-permute-start | bytes 21512 | tf_op jit(solution)/shard_map/ppermute | solution.py:43
  473.2 50.9 %all-to-all-start.2 = ((bf16[8,64,768]{2,1,0:T(8,128)(2,1)}), bf16[8,64,768]{2,1,0:T(8,128)(2,1)S(1)}, u32[]{:S(2)}, u32[]{:S(2)}) async-start(bf16[8,64,768]{2,1,0:T(8,128)(2,1)} %bitcast.16), calls=%async_computation.4 | async-start | bytes 1572864 | tf_op jit(solution)/shard_map/all_to_all | solution.py:680
  479.5 22.8 %collective-permute-start.32 = (f32[1,1,2,14,128]{4,3,2,1,0:T(8,128)S(1)}, f32[1,1,2,14,128]{4,3,2,1,0:T(8,128)S(1)}, u32[]{:S(2)}, u32[]{:S(2)}) collective-permute-start(f32[1,1,2,14,128]{4,3,2,1,0:T(8,128)S(1)} %maximum_select_fusion.7), channel_id=1, source_target_pairs={{0,2},{1,3},{2,0},{3,1},{4,6},{5,7},{6,4},{7,5},{8,10},{9,11},{10,... | collective-permute-start | bytes 43016 | tf_op jit(solution)/shard_map/ppermute | solution.py:43
  502.4 16.3 %collective-permute-start.33 = (f32[1,2,2,14,128]{4,3,2,1,0:T(8,128)S(1)}, f32[1,2,2,14,128]{4,3,2,1,0:T(8,128)S(1)}, u32[]{:S(2)}, u32[]{:S(2)}) collective-permute-start(f32[1,2,2,14,128]{4,3,2,1,0:T(8,128)S(1)} %maximum_select_fusion.3), channel_id=1, source_target_pairs={{0,4},{1,5},{2,6},{3,7},{4,0},{5,1},{6,2},{7,3},{8,12},{9,13},{10,... | collective-permute-start | bytes 86024 | tf_op jit(solution)/shard_map/ppermute | solution.py:43
  512.8 22.5 %collective-permute-start.34 = (bf16[64,2048]{1,0:T(8,128)(2,1)}, bf16[64,2048]{1,0:T(8,128)(2,1)S(1)}, u32[]{:S(2)}, u32[]{:S(2)}) collective-permute-start(bf16[64,2048]{1,0:T(8,128)(2,1)} %get-tuple-element.95), channel_id=1, source_target_pairs={{0,0},{8,1},{16,2},{24,3},{1,4},{9,5},{17,6},{25,7},{2,8},{10,9},{... | collective-permute-start | bytes 786440 | tf_op jit(solution)/shard_map/ppermute | solution.py:838
  (29 other events, 338.1 us)
Sparse Core Ops, SparseCore 0:
  17.4 108.6 all-gather.3
  127.7 78.8 all-gather.7
  208.2 61.9 all-gather.5
  272.3 76.5 reduce-scatter.3
  351.8 60.6 reduce-scatter.5
  414.8 94.4 reduce-scatter.7

commit v9 on v8

--- a/solution.py
+++ b/solution.py
@@ -833,7 +833,6 @@
     layer_out = finish_output(chain, tokens, *branch, bias_out)
 
     norm_parts = sum_last(*norm_parts)
-    input_grad = finish_input(chain, cotangent, tokens, *norm_parts)
     contract_weight_grad, dense_grad = split_output(chain, output_got, units, rows)
     dense_weight_grad = lax.ppermute(dense_grad, "dp", from_slot).astype(jnp.float32)
 
@@ -852,6 +851,7 @@
     expand_weight_grad, ln2_gain_grad, ln2_bias_grad = unpack(
         chain, expand_places, expand_got, expand_sums, expand_weight, ln2_gain, ln2_bias
     )
+    input_grad = finish_input(chain, cotangent, tokens, *norm_parts)
     qkv_got = exchange(qkv_got.reshape(HEADS, rows, split))
     qkv_weight_grad, ln1_gain_grad, ln1_bias_grad = unpack(
         chain, qkv_places, qkv_got, qkv_sums, qkv_weight, ln1_gain, ln1_bias

time: 551 us -> 550 us (level)
  starting transfers between devices: 74.8 us -> 67.3 us
  waiting for transfers between devices: 143 us -> 149 us
    ppermute x33, waiting for transfers between devices: 125 us -> 136 us  [swap(): return lax.ppermute(value, 'dp', plan.flip(bit))]
    ppermute x1, waiting for transfers between devices: 6.88 us -> 0.42 us  [per_device(): lax.ppermute(dense_grad, 'dp', from_slot).astype(jnp.float32)]
    ppermute x33, starting transfers between devices: 50.1 us -> 44.5 us  [swap(): return lax.ppermute(value, 'dp', plan.flip(bit))]
    unnamed x73 -> x81, local copies, waits for them, and re-layouts: 12.4 us -> 12.4 us
  transfers between devices with their start and end apart: 44 -> 44, of which waited for: 16 -> 17; matrix products, arithmetic and copies ran while one was open for 5% -> 5% of each run, Pallas kernels for 50% -> 51%
where the time goes in v9:
time: 550 us; the launch traced here: 542 us
  Pallas kernels  274 us (50%)
  waiting for transfers between devices  149 us (27%)
  starting transfers between devices  67.3 us (12%)
  local copies, waits for them, and re-layouts  21.8 us (4%)
  other arithmetic  15.3 us (3%)
  between operations  15 us (3%)
    pallas_call x23, Pallas kernels, launch(): pl.pallas_call(body, grid_spec=pltpu.PrefetchScalarGridSpec(num_scalar_pr...  274 us
    ppermute x33, waiting for transfers between devices, swap(): return lax.ppermute(value, 'dp', plan.flip(bit))  136 us
    ppermute x33, starting transfers between devices, swap(): return lax.ppermute(value, 'dp', plan.flip(bit))  44.5 us
    all_to_all x3, starting transfers between devices, exchange(): lax.all_to_all(value, 'dp', 0, 0, tiled=True, axis_index_groups=sharing)  13.1 us
    unnamed x81, local copies, waits for them, and re-layouts  12.4 us
  transfers between devices with their start and end apart: 44, of which 17 were waited for; matrix products, arithmetic and copies ran while one was open for 5% of the time, Pallas kernels for 51%

profile of v9, /device:TPU:1, one launch (start us, length us, event | category | flops | bytes accessed | tf_op | source)
XLA Modules:
  0.0 542.4 jit_solution(11553317487951781157)
XLA Ops:
  7.2 4.7 collective-permute-start.14
  13.3 2.9 collective-permute-done.14
  17.3 10.4 %collective-permute-start.3 = (bf16[384,2048]{1,0:T(8,128)(2,1)S(1)}, bf16[384,2048]{1,0:T(8,128)(2,1)}, u32[]{:S(2)}, u32[]{:S(2)}) collective-permute-start(bf16[384,2048]{1,0:T(8,128)(2,1)S(1)} %copy-done.3), channel_id=1, source_target_pairs={{0,4},{1,5},{2,6},{3,7},{4,0},{5,1},{6,2},{7,3},{8,12},{9,13},{10,... | collective-permute-start | bytes 4718600 | tf_op jit(solution)/shard_map/ppermute | solution.py:43
  27.7 2.8 shard_map.254.refs_1_
  30.6 5.8 %all-to-all-start = ((bf16[8,64,1792]{2,1,0:T(8,128)(2,1)}), bf16[8,64,1792]{2,1,0:T(8,128)(2,1)S(1)}, u32[]{:S(2)}, u32[]{:S(2)}) async-start(bf16[8,64,1792]{2,1,0:T(8,128)(2,1)} %shard_map.254.refs_1_), calls=%async_computation | async-start | bytes 3670016 | tf_op jit(solution)/shard_map/all_to_all | solution.py:680
  36.6 24.0 %collective-permute-done.3.refs_2_ = bf16[384,2048]{1,0:T(8,128)(2,1)} collective-permute-done((bf16[384,2048]{1,0:T(8,128)(2,1)S(1)}, bf16[384,2048]{1,0:T(8,128)(2,1)}, u32[]{:S(2)}, u32[]{:S(2)}) %collective-permute-start.3) | collective-permute-done | bytes 1572896 | tf_op jit(solution)/shard_map/ppermute | solution.py:43
  60.6 4.6 collective-permute-start.7
  65.2 2.0 collective-permute-start.6
  67.5 13.8 %collective-permute-done.9 = bf16[1,1,1,1,1,8,128]{6,5,4,3,2,1,0:T(8,128)(2,1)S(1)} collective-permute-done((bf16[1,1,1,1,1,8,128]{6,5,4,3,2,1,0:T(8,128)(2,1)S(1)}, bf16[1,1,1,1,1,8,128]{6,5,4,3,2,1,0:T(8,128)(2,1)S(1)}, u32[]{:S(2)}, u32[]{:S(2)}) %collective-permute-start.9) | collective-permute-done | bytes 2080 | tf_op jit(solution)/shard_map/ppermute | solution.py:43
  81.6 2.5 collective-permute-done.10
  84.1 3.7 collective-permute-start.11
  92.0 3.3 collective-permute-start.13
  95.4 6.8 %collective-permute-done.13 = bf16[1,2,2,2,2,8,128]{6,5,4,3,2,1,0:T(8,128)(2,1)S(1)} collective-permute-done((bf16[1,2,2,2,2,8,128]{6,5,4,3,2,1,0:T(8,128)(2,1)S(1)}, bf16[1,2,2,2,2,8,128]{6,5,4,3,2,1,0:T(8,128)(2,1)S(1)}, u32[]{:S(2)}, u32[]{:S(2)}) %collective-permute-start.13) | collective-permute-done | bytes 32800 | tf_op jit(solution)/shard_map/ppermute | solution.py:43
  104.1 3.8 shard_map.255
  108.9 15.9 %collective-permute-done.4.refs_3_ = bf16[384,2048]{1,0:T(8,128)(2,1)} collective-permute-done((bf16[384,2048]{1,0:T(8,128)(2,1)}, bf16[384,2048]{1,0:T(8,128)(2,1)}, u32[]{:S(2)}, u32[]{:S(2)}) %collective-permute-start.4) | collective-permute-done | bytes 1572896 | tf_op jit(solution)/shard_map/ppermute | solution.py:43
  129.4 7.0 %fusion = (f32[3072,32]{1,0:T(8,128)S(1)}, f32[3072,32]{1,0:T(8,128)}, f32[3072,32]{1,0:T(8,128)S(1)}) fusion(f32[32]{0:T(128)S(1)} %multiply_exponential_fusion, f32[3072]{0:T(1024)S(1)} %convert_element_type.48), kind=kLoop, calls=%fused_computation.4 | loop fusion | flops 196608 | bytes 1192064 | tf_op jit(solution)/shard_map/neg | solution.py:136
  138.1 21.3 %shard_map.256 = (bf16[3072,2048]{1,0:T(8,128)(2,1)}, bf16[3072,2048]{1,0:T(8,128)(2,1)}, bf16[3072,2048]{1,0:T(8,128)(2,1)}) custom-call(bf16[384,2048]{1,0:T(8,128)(2,1)} %refs_1_.3, bf16[384,2048]{1,0:T(8,128)(2,1)} %collective-permute-done.2.refs_1_, bf16[384,2048]{1,0:T(8,128)(2,1)} %collective-permute-done.3.refs_2_, ...), custom_call_target="tpu_custom_call" | custom-call | flops 1 | bytes 1 | tf_op jit(solution)/shard_map/pallas_call | solution.py:98
  159.4 3.6 shard_map.257.refs_1_
  166.9 3.0 maximum_maximum_fusion.1.refs_5_.refs_4_
  170.0 5.3 shard_map.258
  175.3 23.8 %collective-permute-done.15.refs_3_ = bf16[384,2048]{1,0:T(8,128)(2,1)} collective-permute-done((bf16[384,2048]{1,0:T(8,128)(2,1)}, bf16[384,2048]{1,0:T(8,128)(2,1)}, u32[]{:S(2)}, u32[]{:S(2)}) %collective-permute-start.15) | collective-permute-done | bytes 1572896 | tf_op jit(solution)/shard_map/ppermute | solution.py:43
  199.0 5.9 %shard_map.259.refs_3_.refs_0_.refs_2_ = bf16[1536,2048]{1,0:T(8,128)(2,1)} custom-call(bf16[384,2048]{1,0:T(8,128)(2,1)} %refs_0_.9, bf16[384,2048]{1,0:T(8,128)(2,1)} %collective-permute-done.refs_0_.refs_1_, bf16[384,2048]{1,0:T(8,128)(2,1)} %collective-permute-done.1.refs_2_, bf16[384,2048]{1,0:T(8,128)(2,1)} %collective-permute-done.15.refs_3_, ...), custom_call_target="tpu_custom_call" | custom-call | flops 1 | bytes 1 | tf_op jit(solution)/shard_map/pallas_call | solution.py:98
  207.3 22.5 %shard_map.260 = (bf16[3072,1024]{1,0:T(8,128)(2,1)}, f32[3072,1024]{1,0:T(8,128)}) custom-call(bf16[3072,2048]{1,0:T(8,128)(2,1)} %get-tuple-element.60.refs_0_, f32[1,1024]{1,0:T(1,128)} %bitcast.104, bf16[2048,1024]{1,0:T(8,128)(2,1)} %all-gather.8.cloned.1.call-done.refs_2_.refs_3_, bf16[1536,2048]{1,0:T(8,128)(2,1)} %shard_map.259.refs_3_.refs_0_.refs_2_), custom_call_target="tpu_custom_call" | custom-call | flops 1 | bytes 1 | tf_op jit(solution)/shard_map/pallas_call | solution.py:98
  229.8 23.3 %shard_map.261 = (bf16[3072,1024]{1,0:T(8,128)(2,1)}, f32[1,1024]{1,0:T(1,128)}, f32[1,2048]{1,0:T(1,128)}) custom-call(bf16[1536,2048]{1,0:T(8,128)(2,1)} %shard_map.259.refs_3_.refs_0_.refs_2_, bf16[1536,2048]{1,0:T(8,128)(2,1)} %collective-permute-done.16.refs_1_.refs_3_, f32[3072,1024]{1,0:T(8,128)} %get-tuple-element.62.refs_2_, ...), custom_call_target="tpu_custom_call" | custom-call | flops 1 | bytes 1 | tf_op jit(solution)/shard_map/pallas_call | solution.py:98
  253.1 18.8 %shard_map.262.refs_10_ = bf16[2048,1024]{1,0:T(8,128)(2,1)} custom-call(bf16[3072,2048]{1,0:T(8,128)(2,1)} %get-tuple-element.59.refs_0_, bf16[3072,1024]{1,0:T(8,128)(2,1)} %get-tuple-element.64.refs_1_.refs_2_, bf16[3072,1024]{1,0:T(8,128)(2,1)} %get-tuple-element.64.refs_1_.refs_2_), custom_call_target="tpu_custom_call" | custom-call | flops 1 | bytes 1 | tf_op jit(solution)/shard_map/pallas_call | solution.py:98
  272.1 29.6 %shard_map.263 = (bf16[3072,256]{1,0:T(8,128)(2,1)}, bf16[3072,768]{1,0:T(8,128)(2,1)}, f32[1,768]{1,0:T(1,128)}) custom-call(bf16[1536,2048]{1,0:T(8,128)(2,1)} %shard_map.259.refs_3_.refs_0_.refs_2_, bf16[1536,2048]{1,0:T(8,128)(2,1)} %collective-permute-done.16.refs_1_.refs_3_, bf16[3072,2048]{1,0:T(8,128)(2,1)} %get-tuple-element.56.refs_1_.refs_2_, ...), custom_call_target="tpu_custom_call" | custom-call | flops 1 | bytes 1 | tf_op jit(solution)/shard_map/pallas_call | solution.py:98
  301.7 15.5 %shard_map.264.refs_4_ = bf16[2048,768]{1,0:T(8,128)(2,1)} custom-call(bf16[3072,2048]{1,0:T(8,128)(2,1)} %get-tuple-element.59.refs_0_, bf16[3072,768]{1,0:T(8,128)(2,1)} %get-tuple-element.66.refs_1_.refs_0_, bf16[3072,256]{1,0:T(8,128)(2,1)} %get-tuple-element.65.refs_2_.refs_0_.refs_1_), custom_call_target="tpu_custom_call" | custom-call | flops 1 | bytes 1 | tf_op jit(solution)/shard_map/pallas_call | solution.py:98
  317.3 14.2 %shard_map.265 = (bf16[768,2048]{1,0:T(8,128)(2,1)}, bf16[768,2048]{1,0:T(8,128)(2,1)}) custom-call(bf16[3072,256]{1,0:T(8,128)(2,1)} %get-tuple-element.65.refs_2_.refs_0_.refs_1_, bf16[3072,1024]{1,0:T(8,128)(2,1)} %get-tuple-element.63.refs_4_.refs_1_.refs_0_, bf16[256,2048]{1,0:T(8,128)(2,1)} %get-tuple-element.58.refs_9_.refs_2_, ...), custom_call_target="tpu_custom_call" | custom-call | flops 1 | bytes 1 | tf_op jit(solution)/shard_map/pallas_call | solution.py:98
  332.0 18.3 %shard_map.266 = (bf16[768,2048]{1,0:T(8,128)(2,1)}, bf16[768,2048]{1,0:T(8,128)(2,1)}) custom-call(bf16[3072,768]{1,0:T(8,128)(2,1)} %get-tuple-element.66.refs_1_.refs_0_, bf16[3072,1024]{1,0:T(8,128)(2,1)} %get-tuple-element.64.refs_1_.refs_2_, bf16[2048,768]{1,0:T(8,128)(2,1)} %all-gather.6.cloned.1.call-done.refs_8_.refs_2_, ...), custom_call_target="tpu_custom_call" | custom-call | flops 1 | bytes 1 | tf_op jit(solution)/shard_map/pallas_call | solution.py:98
  350.8 3.8 all-to-all-start.1
  354.8 16.3 %shard_map.267 = (bf16[384,2048]{1,0:T(8,128)(2,1)}, bf16[384,2048]{1,0:T(8,128)(2,1)}, bf16[384,2048]{1,0:T(8,128)(2,1)}, bf16[384,1024]{1,0:T(8,128)(2,1)}, bf16[384,1024]{1,0:T(8,128)(2,1)}) custom-call(bf16[3072,256]{1,0:T(8,128)(2,1)} %get-tuple-element.65.refs_2_.refs_0_.refs_1_, bf16[3072,1024]{1,0:T(8,128)(2,1)} %get-tuple-element.63.refs_4_.refs_1_.refs_0_, ...), custom_call_target="tpu_custom_call" | custom-call | flops 1 | bytes 1 | tf_op jit(solution)/shard_map/pallas_call | solution.py:98
  374.7 22.5 %shard_map.268.refs_4_ = bf16[1280,2048]{1,0:T(8,128)(2,1)} custom-call(bf16[3072,1024]{1,0:T(8,128)(2,1)} %get-tuple-element.63.refs_4_.refs_1_.refs_0_, bf16[3072,256]{1,0:T(8,128)(2,1)} %get-tuple-element.65.refs_2_.refs_0_.refs_1_, bf16[1536,2048]{1,0:T(8,128)(2,1)} %shard_map.259.refs_3_.refs_0_.refs_2_, ...), custom_call_target="tpu_custom_call" | custom-call | flops 1 | bytes 1 | tf_op jit(solution)/shard_map/pallas_call | solution.py:98
  398.4 3.7 shard_map.269
  405.0 3.4 collective-permute-done.29
  410.8 2.2 reduce-scatter.6.cloned.1.call-done.refs_9_
  413.0 21.4 %shard_map.270 = (bf16[384,2048]{1,0:T(8,128)(2,1)}, bf16[384,2048]{1,0:T(8,128)(2,1)}, bf16[384,2048]{1,0:T(8,128)(2,1)}, bf16[384,1024]{1,0:T(8,128)(2,1)}, bf16[384,1024]{1,0:T(8,128)(2,1)}) custom-call(bf16[3072,768]{1,0:T(8,128)(2,1)} %get-tuple-element.66.refs_1_.refs_0_, bf16[3072,1024]{1,0:T(8,128)(2,1)} %get-tuple-element.64.refs_1_.refs_2_, ...), custom_call_target="tpu_custom_call" | custom-call | flops 1 | bytes 1 | tf_op jit(solution)/shard_map/pallas_call | solution.py:98
  439.1 4.8 shard_map.271.refs_4_
  443.9 10.5 %collective-permute-done.25.refs_2_ = bf16[384,1024]{1,0:T(8,128)(2,1)} collective-permute-done((bf16[384,1024]{1,0:T(8,128)(2,1)}, bf16[384,1024]{1,0:T(8,128)(2,1)}, u32[]{:S(2)}, u32[]{:S(2)}) %collective-permute-start.25) | collective-permute-done | bytes 786464 | tf_op jit(solution)/shard_map/ppermute | solution.py:43
  454.7 3.7 shard_map.272
  460.7 2.2 collective-permute-start.31
  462.9 3.5 all-to-all-start.2
  470.6 31.2 %collective-permute-done.32 = f32[1,1,2,14,128]{4,3,2,1,0:T(8,128)S(1)} collective-permute-done((f32[1,1,2,14,128]{4,3,2,1,0:T(8,128)S(1)}, f32[1,1,2,14,128]{4,3,2,1,0:T(8,128)S(1)}, u32[]{:S(2)}, u32[]{:S(2)}) %collective-permute-start.32) | collective-permute-done | bytes 14368 | tf_op jit(solution)/shard_map/ppermute | solution.py:43
  501.9 7.6 %reduce-scatter.8.cloned.1.call-done.refs_0_ = bf16[320,2048]{1,0:T(8,128)(2,1)} async-done(((bf16[1280,2048]{1,0:T(8,128)(2,1)}), bf16[320,2048]{1,0:T(8,128)(2,1)}) %reduce-scatter.8.cloned.1.call-update) | async-done | bytes 1310736 | tf_op jit(solution)/shard_map/reduce_scatter | solution.py:675
  509.5 2.9 shard_map.273
  512.4 3.9 collective-permute-start.34
  517.7 4.0 shard_map.274
  522.9 6.4 %shard_map.275.refs_5_ = f32[384,2048]{1,0:T(8,128)} custom-call(bf16[384,2048]{1,0:T(8,128)(2,1)} %refs_0_.9, bf16[384,2048]{1,0:T(8,128)(2,1)} %refs_1_.3, bf16[384,2048]{1,0:T(8,128)(2,1)} %get-tuple-element.78.refs_5_.refs_2_, bf16[384,2048]{1,0:T(8,128)(2,1)} %copy-done.6, bf16[384,2048]{1,0:T(8,128)(2,1)} %collective-permute-done.28.refs_4_, ...), custom_call_target="tpu_custom_call" | custom-call | flops 1 | bytes 1 | tf_op jit(solution)/shard_map/pallas_call | solution.py:98
  530.1 3.4 shard_map.276
  (214 shorter events, 50.8 us)
Async XLA Ops:
  7.2 130.9 %all-gather.4.cloned.1.call-start = ((), (), s32[]{:S(2)}) async-start(), calls=%async_computation.6 | async-start | bytes 6553600 | tf_op jit(solution)/shard_map/all_gather | solution.py:672
  7.2 8.9 %collective-permute-start.14 = (bf16[64,2048]{1,0:T(8,128)(2,1)}, bf16[64,2048]{1,0:T(8,128)(2,1)S(1)}, u32[]{:S(2)}, u32[]{:S(2)}) collective-permute-start(bf16[64,2048]{1,0:T(8,128)(2,1)} %param.23), channel_id=1, source_target_pairs={{0,0},{1,8},{2,16},{3,24},{4,1},{5,9},{6,17},{7,25},{8,2},{9,10},{... | collective-permute-start | bytes 786440 | tf_op jit(solution)/shard_map/ppermute | solution.py:684
  17.3 43.4 %collective-permute-start.3 = (bf16[384,2048]{1,0:T(8,128)(2,1)S(1)}, bf16[384,2048]{1,0:T(8,128)(2,1)}, u32[]{:S(2)}, u32[]{:S(2)}) collective-permute-start(bf16[384,2048]{1,0:T(8,128)(2,1)S(1)} %copy-done.3), channel_id=1, source_target_pairs={{0,4},{1,5},{2,6},{3,7},{4,0},{5,1},{6,2},{7,3},{8,12},{9,13},{10,... | collective-permute-start | bytes 4718600 | tf_op jit(solution)/shard_map/ppermute | solution.py:43
  27.7 37.6 %collective-permute-start.2 = (bf16[384,2048]{1,0:T(8,128)(2,1)S(1)}, bf16[384,2048]{1,0:T(8,128)(2,1)}, u32[]{:S(2)}, u32[]{:S(2)}) collective-permute-start(bf16[384,2048]{1,0:T(8,128)(2,1)S(1)} %copy-done.3), channel_id=1, source_target_pairs={{0,2},{1,3},{2,0},{3,1},{4,6},{5,7},{6,4},{7,5},{8,10},{9,11},{10,... | collective-permute-start | bytes 4718600 | tf_op jit(solution)/shard_map/ppermute | solution.py:43
  30.5 36.8 %copy-start.25 = (bf16[192]{0:T(256)(128)(2,1)S(1)}, bf16[192]{0:T(256)(128)(2,1)}, u32[]{:S(2)}) copy-start(bf16[192]{0:T(256)(128)(2,1)} %param.22) | copy-start | bytes 1156
  30.5 36.8 %copy-start.26 = (bf16[256]{0:T(256)(128)(2,1)S(1)}, bf16[256]{0:T(256)(128)(2,1)}, u32[]{:S(2)}) copy-start(bf16[256]{0:T(256)(128)(2,1)} %param.26) | copy-start | bytes 1540
  30.5 36.8 %copy-start.27 = (bf16[64]{0:T(256)(128)(2,1)S(1)}, bf16[64]{0:T(256)(128)(2,1)}, u32[]{:S(2)}) copy-start(bf16[64]{0:T(256)(128)(2,1)} %param.19) | copy-start | bytes 388
  30.6 72.3 %all-to-all-start = ((bf16[8,64,1792]{2,1,0:T(8,128)(2,1)}), bf16[8,64,1792]{2,1,0:T(8,128)(2,1)S(1)}, u32[]{:S(2)}, u32[]{:S(2)}) async-start(bf16[8,64,1792]{2,1,0:T(8,128)(2,1)} %shard_map.254.refs_1_), calls=%async_computation | async-start | bytes 3670016 | tf_op jit(solution)/shard_map/all_to_all | solution.py:680
  36.4 170.9 %all-gather.8.cloned.1.call-start = ((), (), s32[]{:S(2)}) async-start(), calls=%async_computation.8 | async-start | bytes 5242880 | tf_op jit(solution)/shard_map/all_gather | solution.py:672
  36.4 66.5 %collective-permute-start.5 = (bf16[384,2048]{1,0:T(8,128)(2,1)S(1)}, bf16[384,2048]{1,0:T(8,128)(2,1)}, u32[]{:S(2)}, u32[]{:S(2)}) collective-permute-start(bf16[384,2048]{1,0:T(8,128)(2,1)S(1)} %copy-done.3), channel_id=1, source_target_pairs={{0,1},{1,0},{2,3},{3,2},{4,5},{5,4},{6,7},{7,6},{8,9},{9,8},{10,11... | collective-permute-start | bytes 4718600 | tf_op jit(solution)/shard_map/ppermute | solution.py:43
  60.6 42.3 %collective-permute-start.7 = (bf16[384,2048]{1,0:T(8,128)(2,1)}, bf16[384,2048]{1,0:T(8,128)(2,1)}, u32[]{:S(2)}, u32[]{:S(2)}) collective-permute-start(bf16[384,2048]{1,0:T(8,128)(2,1)} %collective-permute-done.3.refs_2_), channel_id=1, source_target_pairs={{0,1},{1,0},{2,3},{3,2},{4,5},{5,4},{6,7},{7,6},{8,9},{9,8},{10,11... | collective-permute-start | bytes 4718600 | tf_op jit(solution)/shard_map/ppermute | solution.py:43
  65.2 37.7 %collective-permute-start.6 = (bf16[384,2048]{1,0:T(8,128)(2,1)}, bf16[384,2048]{1,0:T(8,128)(2,1)}, u32[]{:S(2)}, u32[]{:S(2)}) collective-permute-start(bf16[384,2048]{1,0:T(8,128)(2,1)} %collective-permute-done.2.refs_1_), channel_id=1, source_target_pairs={{0,1},{1,0},{2,3},{3,2},{4,5},{5,4},{6,7},{7,6},{8,9},{9,8},{10,11... | collective-permute-start | bytes 4718600 | tf_op jit(solution)/shard_map/ppermute | solution.py:43
  67.4 13.8 %collective-permute-start.9 = (bf16[1,1,1,1,1,8,128]{6,5,4,3,2,1,0:T(8,128)(2,1)S(1)}, bf16[1,1,1,1,1,8,128]{6,5,4,3,2,1,0:T(8,128)(2,1)S(1)}, u32[]{:S(2)}, u32[]{:S(2)}) collective-permute-start(bf16[1,1,1,1,1,8,128]{6,5,4,3,2,1,0:T(8,128)(2,1)S(1)} %bitcast.101), channel_id=1, source_target_pairs={{0,2},{1,3},{2,0},{3,1},{4,6},{5,7},{6,4},{7,5},{8,10},{9,11},{10,... | collective-permute-start | bytes 6152 | tf_op jit(solution)/shard_map/ppermute | solution.py:43
  81.3 2.9 collective-permute-start.10
  84.1 4.5 collective-permute-start.11
  88.7 3.4 collective-permute-start.12
  88.8 36.0 %collective-permute-start.4 = (bf16[384,2048]{1,0:T(8,128)(2,1)}, bf16[384,2048]{1,0:T(8,128)(2,1)}, u32[]{:S(2)}, u32[]{:S(2)}) collective-permute-start(bf16[384,2048]{1,0:T(8,128)(2,1)} %collective-permute-done.3.refs_2_), channel_id=1, source_target_pairs={{0,2},{1,3},{2,0},{3,1},{4,6},{5,7},{6,4},{7,5},{8,10},{9,11},{10,... | collective-permute-start | bytes 4718600 | tf_op jit(solution)/shard_map/ppermute | solution.py:43
  92.0 10.1 %collective-permute-start.13 = (bf16[1,2,2,2,2,8,128]{6,5,4,3,2,1,0:T(8,128)(2,1)S(1)}, bf16[1,2,2,2,2,8,128]{6,5,4,3,2,1,0:T(8,128)(2,1)S(1)}, u32[]{:S(2)}, u32[]{:S(2)}) collective-permute-start(bf16[1,2,2,2,2,8,128]{6,5,4,3,2,1,0:T(8,128)(2,1)S(1)} %maximum_select_fusion.2), channel_id=1, source_target_pairs={{0,16},{1,17},{2,18},{3,19},{4,20},{5,21},{6,22},{7,23},{8,24},{9,... | collective-permute-start | bytes 98312 | tf_op jit(solution)/shard_map/ppermute | solution.py:43
  107.9 164.2 %all-gather.6.cloned.1.call-start = ((), (), s32[]{:S(2)}) async-start(), calls=%async_computation.7 | async-start | bytes 3932160 | tf_op jit(solution)/shard_map/all_gather | solution.py:672
  108.0 51.4 %collective-permute-start = (bf16[384,2048]{1,0:T(8,128)(2,1)S(1)}, bf16[384,2048]{1,0:T(8,128)(2,1)}, u32[]{:S(2)}, u32[]{:S(2)}) collective-permute-start(bf16[384,2048]{1,0:T(8,128)(2,1)S(1)} %copy-done.4), channel_id=1, source_target_pairs={{0,2},{1,3},{2,0},{3,1},{4,6},{5,7},{6,4},{7,5},{8,10},{9,11},{10,... | collective-permute-start | bytes 4718600 | tf_op jit(solution)/shard_map/ppermute | solution.py:43
  108.1 67.2 %collective-permute-start.1 = (bf16[384,2048]{1,0:T(8,128)(2,1)S(1)}, bf16[384,2048]{1,0:T(8,128)(2,1)}, u32[]{:S(2)}, u32[]{:S(2)}) collective-permute-start(bf16[384,2048]{1,0:T(8,128)(2,1)S(1)} %copy-done.4), channel_id=1, source_target_pairs={{0,4},{1,5},{2,6},{3,7},{4,0},{5,1},{6,2},{7,3},{8,12},{9,13},{10,... | collective-permute-start | bytes 4718600 | tf_op jit(solution)/shard_map/ppermute | solution.py:43
  108.8 55.1 %copy-start.15 = (s32[8,384]{1,0:T(8,128)}, s32[8,384]{1,0:T(8,128)S(1)}, u32[]{:S(2)}) copy-start(s32[8,384]{1,0:T(8,128)S(1)} %get-tuple-element.96.refs_6_) | copy-start | bytes 36868
  124.8 13.3 %collective-permute-start.8 = (bf16[384,2048]{1,0:T(8,128)(2,1)}, bf16[384,2048]{1,0:T(8,128)(2,1)}, u32[]{:S(2)}, u32[]{:S(2)}) collective-permute-start(bf16[384,2048]{1,0:T(8,128)(2,1)} %collective-permute-done.4.refs_3_), channel_id=1, source_target_pairs={{0,1},{1,0},{2,3},{3,2},{4,5},{5,4},{6,7},{7,6},{8,9},{9,8},{10,11... | collective-permute-start | bytes 4718600 | tf_op jit(solution)/shard_map/ppermute | solution.py:43
  163.0 36.1 %collective-permute-start.15 = (bf16[384,2048]{1,0:T(8,128)(2,1)}, bf16[384,2048]{1,0:T(8,128)(2,1)}, u32[]{:S(2)}, u32[]{:S(2)}) collective-permute-start(bf16[384,2048]{1,0:T(8,128)(2,1)} %shard_map.257.refs_1_), channel_id=1, source_target_pairs={{0,4},{1,5},{2,6},{3,7},{4,0},{5,1},{6,2},{7,3},{8,12},{9,13},{10,... | collective-permute-start | bytes 4718600 | tf_op jit(solution)/shard_map/ppermute | solution.py:43
  204.9 24.9 %collective-permute-start.16 = (bf16[1536,2048]{1,0:T(8,128)(2,1)}, bf16[1536,2048]{1,0:T(8,128)(2,1)}, u32[]{:S(2)}, u32[]{:S(2)}) collective-permute-start(bf16[1536,2048]{1,0:T(8,128)(2,1)} %shard_map.259.refs_3_.refs_0_.refs_2_), channel_id=1, source_target_pairs={{0,1},{1,0},{2,3},{3,2},{4,5},{5,4},{6,7},{7,6},{8,9},{9,8},{10,11... | collective-permute-start | bytes 18874376 | tf_op jit(solution)/shard_map/ppermute | solution.py:43
  206.0 144.8 %reduce-scatter.4.cloned.1.call-start = ((), (), s32[]{:S(2)}) async-start(), calls=%async_computation.9 | async-start | bytes 5242880 | tf_op jit(solution)/shard_map/reduce_scatter | solution.py:675
  271.9 141.1 %reduce-scatter.6.cloned.1.call-start = ((), (), s32[]{:S(2)}) async-start(), calls=%async_computation.10 | async-start | bytes 3932160 | tf_op jit(solution)/shard_map/reduce_scatter | solution.py:675
  331.5 23.3 %collective-permute-start.17 = (bf16[768,2048]{1,0:T(8,128)(2,1)}, bf16[768,2048]{1,0:T(8,128)(2,1)}, u32[]{:S(2)}, u32[]{:S(2)}) collective-permute-start(bf16[768,2048]{1,0:T(8,128)(2,1)} %get-tuple-element.67.refs_6_), channel_id=1, source_target_pairs={{0,1},{1,0},{2,3},{3,2},{4,5},{5,4},{6,7},{7,6},{8,9},{9,8},{10,11... | collective-permute-start | bytes 9437192 | tf_op jit(solution)/shard_map/ppermute | solution.py:43
  331.5 23.3 %collective-permute-start.18 = (bf16[768,2048]{1,0:T(8,128)(2,1)}, bf16[768,2048]{1,0:T(8,128)(2,1)}, u32[]{:S(2)}, u32[]{:S(2)}) collective-permute-start(bf16[768,2048]{1,0:T(8,128)(2,1)} %get-tuple-element.68), channel_id=1, source_target_pairs={{0,1},{1,0},{2,3},{3,2},{4,5},{5,4},{6,7},{7,6},{8,9},{9,8},{10,11... | collective-permute-start | bytes 9437192 | tf_op jit(solution)/shard_map/ppermute | solution.py:43
  350.3 60.5 %collective-permute-start.23 = (bf16[768,2048]{1,0:T(8,128)(2,1)}, bf16[768,2048]{1,0:T(8,128)(2,1)}, u32[]{:S(2)}, u32[]{:S(2)}) collective-permute-start(bf16[768,2048]{1,0:T(8,128)(2,1)} %get-tuple-element.69.refs_6_), channel_id=1, source_target_pairs={{0,1},{1,0},{2,3},{3,2},{4,5},{5,4},{6,7},{7,6},{8,9},{9,8},{10,11... | collective-permute-start | bytes 9437192 | tf_op jit(solution)/shard_map/ppermute | solution.py:43
  350.4 60.4 %collective-permute-start.24 = (bf16[768,2048]{1,0:T(8,128)(2,1)}, bf16[768,2048]{1,0:T(8,128)(2,1)}, u32[]{:S(2)}, u32[]{:S(2)}) collective-permute-start(bf16[768,2048]{1,0:T(8,128)(2,1)} %get-tuple-element.77), channel_id=1, source_target_pairs={{0,1},{1,0},{2,3},{3,2},{4,5},{5,4},{6,7},{7,6},{8,9},{9,8},{10,11... | collective-permute-start | bytes 9437192 | tf_op jit(solution)/shard_map/ppermute | solution.py:43
  350.8 22.9 %all-to-all-start.1 = ((bf16[8,64,1024]{2,1,0:T(8,128)(2,1)}), bf16[8,64,1024]{2,1,0:T(8,128)(2,1)S(1)}, u32[]{:S(2)}, u32[]{:S(2)}) async-start(bf16[8,64,1024]{2,1,0:T(8,128)(2,1)} %bitcast.86), calls=%async_computation.2 | async-start | bytes 2097152 | tf_op jit(solution)/shard_map/all_to_all | solution.py:680
  354.6 154.9 %reduce-scatter.8.cloned.1.call-start = ((), (), s32[]{:S(2)}) async-start(), calls=%async_computation.11 | async-start | bytes 6553600 | tf_op jit(solution)/shard_map/reduce_scatter | solution.py:675
  371.1 26.0 %collective-permute-start.19 = (bf16[384,1024]{1,0:T(8,128)(2,1)}, bf16[384,1024]{1,0:T(8,128)(2,1)S(1)}, u32[]{:S(2)}, u32[]{:S(2)}) collective-permute-start(bf16[384,1024]{1,0:T(8,128)(2,1)} %get-tuple-element.73), channel_id=1, source_target_pairs={{0,2},{1,3},{2,0},{3,1},{4,6},{5,7},{6,4},{7,5},{8,10},{9,11},{10,... | collective-permute-start | bytes 2359304 | tf_op jit(solution)/shard_map/ppermute | solution.py:43
  372.5 24.7 %collective-permute-start.20 = (bf16[384,1024]{1,0:T(8,128)(2,1)}, bf16[384,1024]{1,0:T(8,128)(2,1)S(1)}, u32[]{:S(2)}, u32[]{:S(2)}) collective-permute-start(bf16[384,1024]{1,0:T(8,128)(2,1)} %get-tuple-element.74), channel_id=1, source_target_pairs={{0,4},{1,5},{2,6},{3,7},{4,0},{5,1},{6,2},{7,3},{8,12},{9,13},{10,... | collective-permute-start | bytes 2359304 | tf_op jit(solution)/shard_map/ppermute | solution.py:43
  402.1 35.3 %collective-permute-start.21 = (bf16[384,2048]{1,0:T(8,128)(2,1)}, bf16[384,2048]{1,0:T(8,128)(2,1)S(1)}, u32[]{:S(2)}, u32[]{:S(2)}) collective-permute-start(bf16[384,2048]{1,0:T(8,128)(2,1)} %get-tuple-element.75.refs_8_), channel_id=1, source_target_pairs={{0,2},{1,3},{2,0},{3,1},{4,6},{5,7},{6,4},{7,5},{8,10},{9,11},{10,... | collective-permute-start | bytes 4718600 | tf_op jit(solution)/shard_map/ppermute | solution.py:43
  402.3 35.1 %collective-permute-start.22 = (bf16[384,2048]{1,0:T(8,128)(2,1)}, bf16[384,2048]{1,0:T(8,128)(2,1)S(1)}, u32[]{:S(2)}, u32[]{:S(2)}) collective-permute-start(bf16[384,2048]{1,0:T(8,128)(2,1)} %get-tuple-element.76), channel_id=1, source_target_pairs={{0,4},{1,5},{2,6},{3,7},{4,0},{5,1},{6,2},{7,3},{8,12},{9,13},{10,... | collective-permute-start | bytes 4718600 | tf_op jit(solution)/shard_map/ppermute | solution.py:43
  403.0 5.4 collective-permute-start.29
  409.1 50.8 %collective-permute-start.30 = (f32[30,128]{1,0:T(8,128)}, f32[30,128]{1,0:T(8,128)}, u32[]{:S(2)}, u32[]{:S(2)}) collective-permute-start(f32[30,128]{1,0:T(8,128)} %bitcast_add_fusion), channel_id=1, source_target_pairs={{0,16},{1,17},{2,18},{3,19},{4,20},{5,21},{6,22},{7,23},{8,24},{9,... | collective-permute-start | bytes 46088 | tf_op jit(solution)/shard_map/ppermute | solution.py:43
  434.4 19.9 %collective-permute-start.25 = (bf16[384,1024]{1,0:T(8,128)(2,1)}, bf16[384,1024]{1,0:T(8,128)(2,1)}, u32[]{:S(2)}, u32[]{:S(2)}) collective-permute-start(bf16[384,1024]{1,0:T(8,128)(2,1)} %get-tuple-element.81), channel_id=1, source_target_pairs={{0,2},{1,3},{2,0},{3,1},{4,6},{5,7},{6,4},{7,5},{8,10},{9,11},{10,... | collective-permute-start | bytes 2359304 | tf_op jit(solution)/shard_map/ppermute | solution.py:43
  435.6 19.2 %collective-permute-start.26 = (bf16[384,1024]{1,0:T(8,128)(2,1)}, bf16[384,1024]{1,0:T(8,128)(2,1)}, u32[]{:S(2)}, u32[]{:S(2)}) collective-permute-start(bf16[384,1024]{1,0:T(8,128)(2,1)} %get-tuple-element.82), channel_id=1, source_target_pairs={{0,4},{1,5},{2,6},{3,7},{4,0},{5,1},{6,2},{7,3},{8,12},{9,13},{10,... | collective-permute-start | bytes 2359304 | tf_op jit(solution)/shard_map/ppermute | solution.py:43
  458.4 63.3 %collective-permute-start.27 = (bf16[384,2048]{1,0:T(8,128)(2,1)}, bf16[384,2048]{1,0:T(8,128)(2,1)S(1)}, u32[]{:S(2)}, u32[]{:S(2)}) collective-permute-start(bf16[384,2048]{1,0:T(8,128)(2,1)} %get-tuple-element.83.refs_1_), channel_id=1, source_target_pairs={{0,2},{1,3},{2,0},{3,1},{4,6},{5,7},{6,4},{7,5},{8,10},{9,11},{10,... | collective-permute-start | bytes 4718600 | tf_op jit(solution)/shard_map/ppermute | solution.py:43
  459.6 62.1 %collective-permute-start.28 = (bf16[384,2048]{1,0:T(8,128)(2,1)}, bf16[384,2048]{1,0:T(8,128)(2,1)}, u32[]{:S(2)}, u32[]{:S(2)}) collective-permute-start(bf16[384,2048]{1,0:T(8,128)(2,1)} %get-tuple-element.84), channel_id=1, source_target_pairs={{0,4},{1,5},{2,6},{3,7},{4,0},{5,1},{6,2},{7,3},{8,12},{9,13},{10,... | collective-permute-start | bytes 4718600 | tf_op jit(solution)/shard_map/ppermute | solution.py:43
  460.7 8.5 %collective-permute-start.31 = (f32[1,1,1,14,128]{4,3,2,1,0:T(8,128)S(1)}, f32[1,1,1,14,128]{4,3,2,1,0:T(8,128)S(1)}, u32[]{:S(2)}, u32[]{:S(2)}) collective-permute-start(f32[1,1,1,14,128]{4,3,2,1,0:T(8,128)S(1)} %get-tuple-element.104), channel_id=1, source_target_pairs={{0,1},{1,0},{2,3},{3,2},{4,5},{5,4},{6,7},{7,6},{8,9},{9,8},{10,11... | collective-permute-start | bytes 21512 | tf_op jit(solution)/shard_map/ppermute | solution.py:43
  462.9 66.4 %all-to-all-start.2 = ((bf16[8,64,768]{2,1,0:T(8,128)(2,1)}), bf16[8,64,768]{2,1,0:T(8,128)(2,1)S(1)}, u32[]{:S(2)}, u32[]{:S(2)}) async-start(bf16[8,64,768]{2,1,0:T(8,128)(2,1)} %bitcast.23), calls=%async_computation.5 | async-start | bytes 1572864 | tf_op jit(solution)/shard_map/all_to_all | solution.py:680
  469.2 32.6 %collective-permute-start.32 = (f32[1,1,2,14,128]{4,3,2,1,0:T(8,128)S(1)}, f32[1,1,2,14,128]{4,3,2,1,0:T(8,128)S(1)}, u32[]{:S(2)}, u32[]{:S(2)}) collective-permute-start(f32[1,1,2,14,128]{4,3,2,1,0:T(8,128)S(1)} %maximum_select_fusion.7), channel_id=1, source_target_pairs={{0,2},{1,3},{2,0},{3,1},{4,6},{5,7},{6,4},{7,5},{8,10},{9,11},{10,... | collective-permute-start | bytes 43016 | tf_op jit(solution)/shard_map/ppermute | solution.py:43
  501.8 14.5 %collective-permute-start.33 = (f32[1,2,2,14,128]{4,3,2,1,0:T(8,128)S(1)}, f32[1,2,2,14,128]{4,3,2,1,0:T(8,128)S(1)}, u32[]{:S(2)}, u32[]{:S(2)}) collective-permute-start(f32[1,2,2,14,128]{4,3,2,1,0:T(8,128)S(1)} %maximum_select_fusion.3), channel_id=1, source_target_pairs={{0,4},{1,5},{2,6},{3,7},{4,0},{5,1},{6,2},{7,3},{8,12},{9,13},{10,... | collective-permute-start | bytes 86024 | tf_op jit(solution)/shard_map/ppermute | solution.py:43
  512.4 21.6 %collective-permute-start.34 = (bf16[64,2048]{1,0:T(8,128)(2,1)}, bf16[64,2048]{1,0:T(8,128)(2,1)S(1)}, u32[]{:S(2)}, u32[]{:S(2)}) collective-permute-start(bf16[64,2048]{1,0:T(8,128)(2,1)} %get-tuple-element.95), channel_id=1, source_target_pairs={{0,0},{8,1},{16,2},{24,3},{1,4},{9,5},{17,6},{25,7},{2,8},{10,9},{... | collective-permute-start | bytes 786440 | tf_op jit(solution)/shard_map/ppermute | solution.py:837
  (33 other events, 335.6 us)
Sparse Core Ops, SparseCore 0:
  17.4 108.6 all-gather.3
  127.7 78.8 all-gather.7
  208.1 61.9 all-gather.5
  272.3 76.8 reduce-scatter.3
  352.1 60.8 reduce-scatter.5
  415.3 94.1 reduce-scatter.7
